TPU v7x, 32 devices: a whole 2x2x4 slice. The times are simulated.
32 devices in a mesh: frame: 16 (over z, x, core), space: 2 (over y).
Axes of the slice: x: 2, y: 2, z: 4, core: 2. Of those that a mesh axis runs over, the one named last changes fastest.
Arguments:
- queries: bfloat16 [2560, 3072], P('frame', 'space'), may hold values from -24 to 24
- keys: bfloat16 [2560, 3072], P('frame', 'space'), may hold values from -24 to 24
- values: bfloat16 [2560, 3072], P('frame', 'space'), may hold values from -6 to 6
- grad_out: bfloat16 [2560, 3072], P('frame', 'space'), may hold values from -24 to 24
- proj_weight: bfloat16 [3072, 3072], P('space', 'frame'), may hold values from -0.109375 to 0.109375
Outputs:
- grad_queries: bfloat16 [2560, 3072], P('frame', 'space')
- grad_keys: bfloat16 [2560, 3072], P('frame', 'space')
- grad_values: bfloat16 [2560, 3072], P('frame', 'space')
- grad_proj: float32 [3072, 3072], P('space', 'frame')
All inputs are finite; a program needn't handle non-finite values.
Results may differ from a plain program's by a relative error of at most 0.03.
Values may be sent and summed in bfloat16 or wider, within the bound.
No kernel may reach another device: no remote copies, remote signals or barrier semaphores. Data moves between devices by JAX's collectives and lax.ppermute only.
A program may use at most 128 MiB of HBM per device.

v0:
```python
import math

import jax
import jax.numpy as jnp
from jax import lax
from jax.sharding import PartitionSpec as P

HD = 128


def largest_divisor(count, limit):
    best = 1
    for candidate in range(1, min(count, limit) + 1):
        if count % candidate == 0:
            best = candidate
    return best


def local(queries, keys, values, grad_out, proj_weight):
    tok_rows = queries.shape[0]
    width = queries.shape[1]
    heads_loc = width // HD
    factor = 1.0 / math.sqrt(HD)
    grad_rows = lax.all_gather(grad_out, "space", axis=1, tiled=True)
    grad_attn = lax.dot_general(
        grad_rows,
        lax.all_gather(proj_weight, "frame", axis=1, tiled=True),
        (((1,), (1,)), ((), ())),
        preferred_element_type=jnp.float32,
    ).astype(jnp.bfloat16)
    key_all, value_all = (
        lax.all_gather(keys, "frame", axis=0, tiled=True),
        lax.all_gather(values, "frame", axis=0, tiled=True),
    )
    seq_len = key_all.shape[0]
    key_block = math.gcd(seq_len, 512)
    nblocks = seq_len // key_block
    query3 = queries.reshape(tok_rows, heads_loc, HD)
    grad3 = grad_attn.reshape(tok_rows, heads_loc, HD)

    def block_of(source, offset, size):
        return lax.dynamic_slice_in_dim(source, offset, size, 0).reshape(size, heads_loc, HD)

    def scores_at(offset, size):
        key_blk = block_of(key_all, offset, size)
        logits = (
            jnp.einsum("qhd,khd->hqk", query3, key_blk, preferred_element_type=jnp.float32) * factor
        )
        return (logits, key_blk)

    def stats_step(index, carry):
        run_max, run_sum = carry
        logits, unused = scores_at(index * key_block, key_block)
        new_max = jnp.maximum(run_max, jnp.max(logits, axis=2))
        run_sum = run_sum * jnp.exp(run_max - new_max) + jnp.sum(
            jnp.exp(logits - new_max[:, :, None]), axis=2
        )
        return (new_max, run_sum)

    start_max = jnp.full((heads_loc, tok_rows), -jnp.inf, jnp.float32)
    start_sum = jnp.zeros((heads_loc, tok_rows), jnp.float32)
    run_max, run_sum = lax.fori_loop(0, nblocks, stats_step, (start_max, start_sum))
    log_norm = run_max + jnp.log(run_sum)

    def forward_step(index, accum):
        offset = index * key_block
        logits, unused = scores_at(offset, key_block)
        probs_low = jnp.exp(logits - log_norm[:, :, None]).astype(jnp.bfloat16)
        return accum + jnp.einsum(
            "hqk,khd->hqd",
            probs_low,
            block_of(value_all, offset, key_block),
            preferred_element_type=jnp.float32,
        )

    attn_acc = lax.fori_loop(
        0, nblocks, forward_step, jnp.zeros((heads_loc, tok_rows, HD), jnp.float32)
    )
    attn_out = attn_acc.astype(jnp.bfloat16)
    attn_rows = attn_out.transpose(1, 0, 2).reshape(tok_rows, width)
    row_delta = jnp.sum(
        grad3.astype(jnp.float32).transpose(1, 0, 2) * attn_out.astype(jnp.float32), axis=2
    )
    weight_term = lax.dot_general(
        attn_rows, grad_rows, (((0,), (0,)), ((), ())), preferred_element_type=jnp.float32
    )
    grad_proj = lax.psum_scatter(
        weight_term.astype(jnp.bfloat16), "frame", scatter_dimension=1, tiled=True
    ).astype(jnp.float32)

    def block_grads(offset, size):
        logits, key_blk = scores_at(offset, size)
        value_blk = block_of(value_all, offset, size)
        probs = jnp.exp(logits - log_norm[:, :, None])
        grad_probs = jnp.einsum(
            "qhd,khd->hqk", grad3, value_blk, preferred_element_type=jnp.float32
        )
        grad_logits = (probs * (grad_probs - row_delta[:, :, None])).astype(jnp.bfloat16)
        return (probs, grad_logits, key_blk)

    def key_value_rows(probs, grad_logits, size):
        value_grad = jnp.einsum(
            "hqk,qhd->khd", probs.astype(jnp.bfloat16), grad3, preferred_element_type=jnp.float32
        )
        key_grad = factor * jnp.einsum(
            "hqk,qhd->khd", grad_logits, query3, preferred_element_type=jnp.float32
        )
        return (
            key_grad.reshape(size, width).astype(jnp.bfloat16),
            value_grad.reshape(size, width).astype(jnp.bfloat16),
        )

    def query_step(index, grad_query):
        probs, grad_logits, key_blk = block_grads(index * key_block, key_block)
        return grad_query + jnp.einsum(
            "hqk,khd->hqd", grad_logits, key_blk, preferred_element_type=jnp.float32
        )

    grad_query = lax.fori_loop(
        0, nblocks, query_step, jnp.zeros((heads_loc, tok_rows, HD), jnp.float32)
    )
    start = jnp.int32(0)
    inner = largest_divisor(lax.axis_size("frame") * tok_rows, 1024)

    def term_step(index, buffer):
        probs, grad_logits, unused = block_grads(start + index * inner, inner)
        key_low, value_low = key_value_rows(probs, grad_logits, inner)
        joined = jnp.concatenate([key_low, value_low], axis=1)
        return lax.dynamic_update_slice_in_dim(buffer, joined, index * inner, 0)

    buffer = lax.fori_loop(
        0,
        lax.axis_size("frame") * tok_rows // inner,
        term_step,
        jnp.zeros((lax.axis_size("frame") * tok_rows, 2 * width), jnp.bfloat16),
    )
    summed = lax.psum_scatter(
        lax.optimization_barrier(buffer).astype(jnp.float32).astype(jnp.bfloat16),
        "frame",
        scatter_dimension=0,
        tiled=True,
    ).astype(jnp.float32)
    grad_keys = summed[:, :width].astype(jnp.bfloat16)
    grad_values = summed[:, width:].astype(jnp.bfloat16)
    grad_queries = (
        (factor * grad_query).transpose(1, 0, 2).reshape(tok_rows, width).astype(jnp.bfloat16)
    )
    return (grad_queries, grad_keys, grad_values, grad_proj)


def solution(mesh):
    in_specs = (
        P("frame", "space"),
        P("frame", "space"),
        P("frame", "space"),
        P("frame", "space"),
        P("space", "frame"),
    )
    out_specs = (P("frame", "space"), P("frame", "space"), P("frame", "space"), P("space", "frame"))
    return jax.shard_map(local, mesh=mesh, in_specs=in_specs, out_specs=out_specs, check_vma=False)
```

profile of v0, /device:TPU:0, one launch (start us, length us, event | category | flops | bytes accessed | tf_op | source)
XLA Modules:
  0.0 606.3 jit_solution(8163499004449636193)
XLA Ops:
  9.5 15.1 %all_gather.14 = bf16[160,3072]{1,0:T(8,128)(2,1)S(1)} all-gather(bf16[160,1536]{1,0:T(8,128)(2,1)} %param.16), channel_id=1, replica_groups=mesh['frame'=16,'space'=2] {'space'}, dimensions={1}, use_global_device_ids=true | all-gather | bytes 1474560 | tf_op jit(solution)/shard_map/all_gather | solution.py:24
  24.6 60.0 %all-gather.4.cloned.1.call-done = bf16[2560,1536]{1,0:T(8,128)(2,1)} async-done(((bf16[160,1536]{1,0:T(8,128)(2,1)}), bf16[2560,1536]{1,0:T(8,128)(2,1)}) %all-gather.4.cloned.1.call-update) | async-done | bytes 7864336 | tf_op jit(solution)/shard_map/all_gather | solution.py:32
  84.6 10.5 %copy.41 = bf16[2560,1536]{0,1:T(8,128)(2,1)} copy(bf16[2560,1536]{1,0:T(8,128)(2,1)} %all-gather.4.cloned.1.call-done) | data formatting | bytes 15728640
  95.2 61.7 %all-gather.6.cloned.1.call-done = bf16[2560,1536]{1,0:T(8,128)(2,1)} async-done(((bf16[160,1536]{1,0:T(8,128)(2,1)}), bf16[2560,1536]{1,0:T(8,128)(2,1)}) %all-gather.6.cloned.1.call-update) | async-done | bytes 7864336 | tf_op jit(solution)/shard_map/all_gather | solution.py:33
  156.9 10.5 %copy.43 = bf16[2560,1536]{0,1:T(8,128)(2,1)} copy(bf16[2560,1536]{1,0:T(8,128)(2,1)} %all-gather.6.cloned.1.call-done) | data formatting | bytes 15728640
  167.3 71.6 %all-gather.8.cloned.1.call-done = bf16[1536,3072]{0,1:T(8,128)(2,1)} async-done(((bf16[1536,192]{0,1:T(8,128)(2,1)}), bf16[1536,3072]{0,1:T(8,128)(2,1)}) %all-gather.8.cloned.1.call-update) | async-done | bytes 9437200 | tf_op jit(solution)/shard_map/all_gather | solution.py:27
  239.0 5.4 convolution_convert_fusion.1
  245.7 36.2 %while.58 = (s32[]{:T(128)}, f32[12,160]{1,0:T(8,128)S(1)}, f32[12,160]{1,0:T(8,128)S(1)}, bf16[2560,1536]{0,1:T(8,128)(2,1)}, bf16[160,12,128]{2,0,1:T(8,128)(2...) while((s32[]{:T(128)}, f32[12,160]{1,0:T(8,128)S(1)}, f32[12,160]{1,0:T(8,128)S(1)}, ...), condition=%wide.region_3.0_spmd.clone, body=%wide.region_0.0_spmd.clone.sunk | while | flops 256583040 | bytes 13174426 | solution.py:62
  247.2 2.5 bitcast_reduce_fusion.2
  249.8 3.2 fusion.89
  254.5 2.5 bitcast_reduce_fusion.2
  257.0 3.2 fusion.89
  264.2 3.2 fusion.89
  269.0 2.5 bitcast_reduce_fusion.2
  271.5 3.2 fusion.89
  278.7 3.2 fusion.89
  282.0 36.2 %while.59 = (s32[]{:T(128)}, f32[12,160,128]{2,1,0:T(8,128)}, bf16[2560,1536]{0,1:T(8,128)(2,1)}, bf16[160,12,128]{2,0,1:T(8,128)(2,1)S(1)}, f32[12,160]{1,0:T(8...) while((s32[]{:T(128)}, f32[12,160,128]{2,1,0:T(8,128)}, ...), condition=%wide.region_5.0_spmd.clone, body=%wide.region_4.0_spmd.clone.sunk | while | flops 506757120 | bytes 11902625 | solution.py:76
  282.0 3.3 constant_dynamic-slice_fusion.13
  285.2 3.8 fusion.94
  289.0 3.3 constant_dynamic-slice_fusion.13
  292.3 4.0 fusion.94
  296.3 3.3 constant_dynamic-slice_fusion.13
  299.6 4.0 fusion.94
  303.6 3.3 constant_dynamic-slice_fusion.13
  306.9 4.0 fusion.94
  310.9 3.3 constant_dynamic-slice_fusion.13
  314.1 4.0 fusion.94
  320.3 6.5 %convolution_convert_fusion = bf16[1536,3072]{0,1:T(8,128)(2,1)} fusion(bf16[160,3072]{1,0:T(8,128)(2,1)} %copy-done.3, bf16[20,8,12,128]{3,2,1,0:T(8,128)(2,1)S(1)} %bitcast.128), kind=kOutput, calls=%fused_computation.38 | convolution fusion | flops 1514668032 | bytes 10911744 | tf_op jit(solution)/shard_map/dot_general | solution.py:84
  327.1 7.6 %broadcast_in_dim.29 = bf16[2560,3072]{0,1:T(8,128)(2,1)} broadcast(bf16[]{:T(256)} %constant.160.clone.1), dimensions={} | broadcast | bytes 15728642 | tf_op jit(solution)/shard_map/broadcast_in_dim | solution.py:135
  334.7 81.6 %while.57 = (s32[]{:T(128)}, bf16[2560,3072]{0,1:T(8,128)(2,1)}, bf16[2560,1536]{0,1:T(8,128)(2,1)}, bf16[160,12,128]{2,0,1:T(8,128)(2,1)S(1)}, f32[12,160]{1,0:...) while((s32[]{:T(128)}, bf16[2560,3072]{0,1:T(8,128)(2,1)}, ...), condition=%wide.region_10.0_spmd, body=%wide.region_9.0_spmd.sunk | while | flops 1278935040 | bytes 48192196 | solution.py:131
  334.7 4.3 constant_dynamic-slice_fusion.11
  339.0 3.0 fusion.85
  342.0 7.4 %multiply_convert_fusion.10 = bf16[12,640,128]{1,2,0:T(8,128)(2,1)} fusion(bf16[160,12,128]{2,0,1:T(8,128)(2,1)S(1)} %get-tuple-element.980, f32[12,640,160]{1,2,0:T(8,128)} %fusion.85, bf16[160,12,128]{2,0,1:T(8,128)(2,1)S(1)} %get-tuple-element.983, bf16[640,12,128]{0,2,1:T(8,128)(2,1)} %bitcast.125, f32[12,160]{1,0:T(8,128)S(1)} %get-tuple-element.984, ...), kind=kOutput, calls=%fused_computation.4.clone.1 | convolution fusion | flops 637255680 | bytes 9845760 | tf_op jit(solution)/shard_map/while/body/eval_jaxpr/hqk,qhd->khd/dot_general | solution.py:105
  349.5 3.9 fusion.86
  355.8 4.5 constant_dynamic-slice_fusion.11
  360.2 3.0 fusion.85
  363.2 6.7 %multiply_convert_fusion.10 = bf16[12,640,128]{1,2,0:T(8,128)(2,1)} fusion(bf16[160,12,128]{2,0,1:T(8,128)(2,1)S(1)} %get-tuple-element.980, f32[12,640,160]{1,2,0:T(8,128)} %fusion.85, bf16[160,12,128]{2,0,1:T(8,128)(2,1)S(1)} %get-tuple-element.983, bf16[640,12,128]{0,2,1:T(8,128)(2,1)} %bitcast.125, f32[12,160]{1,0:T(8,128)S(1)} %get-tuple-element.984, ...), kind=kOutput, calls=%fused_computation.4.clone.1 | convolution fusion | flops 637255680 | bytes 9845760 | tf_op jit(solution)/shard_map/while/body/eval_jaxpr/hqk,qhd->khd/dot_general | solution.py:105
  370.0 3.9 fusion.86
  376.3 3.9 constant_dynamic-slice_fusion.11
  380.2 3.0 fusion.85
  383.2 6.8 %multiply_convert_fusion.10 = bf16[12,640,128]{1,2,0:T(8,128)(2,1)} fusion(bf16[160,12,128]{2,0,1:T(8,128)(2,1)S(1)} %get-tuple-element.980, f32[12,640,160]{1,2,0:T(8,128)} %fusion.85, bf16[160,12,128]{2,0,1:T(8,128)(2,1)S(1)} %get-tuple-element.983, bf16[640,12,128]{0,2,1:T(8,128)(2,1)} %bitcast.125, f32[12,160]{1,0:T(8,128)S(1)} %get-tuple-element.984, ...), kind=kOutput, calls=%fused_computation.4.clone.1 | convolution fusion | flops 637255680 | bytes 9845760 | tf_op jit(solution)/shard_map/while/body/eval_jaxpr/hqk,qhd->khd/dot_general | solution.py:105
  390.0 4.0 fusion.86
  396.4 4.0 constant_dynamic-slice_fusion.11
  400.4 3.0 fusion.85
  403.4 6.7 %multiply_convert_fusion.10 = bf16[12,640,128]{1,2,0:T(8,128)(2,1)} fusion(bf16[160,12,128]{2,0,1:T(8,128)(2,1)S(1)} %get-tuple-element.980, f32[12,640,160]{1,2,0:T(8,128)} %fusion.85, bf16[160,12,128]{2,0,1:T(8,128)(2,1)S(1)} %get-tuple-element.983, bf16[640,12,128]{0,2,1:T(8,128)(2,1)} %bitcast.125, f32[12,160]{1,0:T(8,128)S(1)} %get-tuple-element.984, ...), kind=kOutput, calls=%fused_computation.4.clone.1 | convolution fusion | flops 637255680 | bytes 9845760 | tf_op jit(solution)/shard_map/while/body/eval_jaxpr/hqk,qhd->khd/dot_general | solution.py:105
  410.1 3.9 fusion.86
  416.3 20.7 %copy.52 = bf16[2560,3072]{1,0:T(8,128)(2,1)} copy(bf16[2560,3072]{0,1:T(8,128)(2,1)} %get-tuple-element.490) | data formatting | bytes 31457280 | tf_op jit(solution)/shard_map/optimization_barrier | solution.py:138
  437.1 58.1 %while.60 = (s32[]{:T(128)}, f32[12,160,128]{2,1,0:T(8,128)}, bf16[2560,1536]{0,1:T(8,128)(2,1)}, bf16[160,12,128]{2,0,1:T(8,128)(2,1)S(1)}, f32[12,160]{1,0:T(8...) while((s32[]{:T(128)}, f32[12,160,128]{2,1,0:T(8,128)}, ...), condition=%wide.region_8.0_spmd.clone, body=%wide.region_7.0_spmd.clone.sunk | while | flops 760381440 | bytes 21839024 | solution.py:119
  437.1 3.2 constant_dynamic-slice_fusion.14
  440.3 2.6 fusion.100
  442.9 5.1 fusion.101
  448.0 3.9 constant_dynamic-slice_fusion.14
  451.8 2.7 fusion.100
  454.6 6.4 %fusion.101 = f32[12,160,128]{2,1,0:T(8,128)} fusion(bf16[512,12,128]{0,2,1:T(8,128)(2,1)S(1)} %bitcast.119, f32[12,512,160]{1,2,0:T(8,128)} %fusion.100, bf16[160,12,128]{2,0,1:T(8,128)(2,1)S(1)} %get-tuple-element.947, bf16[512,12,128]{0,2,1:T(8,128)(2,1)} %bitcast.122, f32[12,160]{1,0:T(8,128)S(1)} %get-tuple-element.948, ...), kind=kOutput, calls=%fused_computation.34.clone.1 | convolution fusion | flops 508723200 | bytes 9550849 | tf_op jit(solution)/shard_map/while/body/eval_jaxpr/hqk,khd->hqd/dot_general | solution.py:115
  461.0 3.9 constant_dynamic-slice_fusion.14
  464.9 2.6 fusion.100
  467.4 5.4 fusion.101
  472.9 3.2 constant_dynamic-slice_fusion.14
  476.1 2.6 fusion.100
  478.7 5.3 fusion.101
  484.0 3.2 constant_dynamic-slice_fusion.14
  487.3 2.6 fusion.100
  489.8 5.3 fusion.101
  499.5 98.1 %reduce-scatter.3.cloned.1.call-done = bf16[160,3072]{1,0:T(8,128)(2,1)} async-done(((bf16[2560,3072]{1,0:T(8,128)(2,1)}), bf16[160,3072]{1,0:T(8,128)(2,1)}) %reduce-scatter.3.cloned.1.call-update) | async-done | bytes 983056 | tf_op jit(solution)/shard_map/reduce_scatter | solution.py:137
  (63 shorter events, 34.9 us)
Async XLA Ops:
  7.2 238.4 %copy-start = (bf16[160,1536]{1,0:T(8,128)(2,1)S(1)}, bf16[160,1536]{1,0:T(8,128)(2,1)}, u32[]{:S(2)}) copy-start(bf16[160,1536]{1,0:T(8,128)(2,1)} %param.13) | copy-start | bytes 1474564
  7.2 77.4 %all-gather.4.cloned.1.call-start = ((), (), s32[]{:S(2)}) async-start(), calls=%async_computation.2 | async-start | bytes 8355840 | tf_op jit(solution)/shard_map/all_gather | solution.py:32
  7.9 148.9 %all-gather.6.cloned.1.call-start = ((), (), s32[]{:S(2)}) async-start(), calls=%async_computation.3 | async-start | bytes 8355840 | tf_op jit(solution)/shard_map/all_gather | solution.py:33
  8.7 230.3 %all-gather.8.cloned.1.call-start = ((), (), s32[]{:S(2)}) async-start(), calls=%async_computation.4 | async-start | bytes 10027008 | tf_op jit(solution)/shard_map/all_gather | solution.py:27
  9.4 487.9 %reduce-scatter.5.cloned.1.call-start = ((), (), s32[]{:S(2)}) async-start(), calls=%async_computation.6 | async-start | bytes 10027008 | tf_op jit(solution)/shard_map/reduce_scatter | solution.py:87
  24.6 214.4 %copy-start.3 = (bf16[160,3072]{1,0:T(8,128)(2,1)}, bf16[160,3072]{1,0:T(8,128)(2,1)S(1)}, u32[]{:S(2)}) copy-start(bf16[160,3072]{1,0:T(8,128)(2,1)S(1)} %all_gather.14) | copy-start | bytes 2949124
  326.8 270.7 %reduce-scatter.3.cloned.1.call-start = ((), (), s32[]{:S(2)}) async-start(), calls=%async_computation.5 | async-start | bytes 16711680 | tf_op jit(solution)/shard_map/reduce_scatter | solution.py:137
  349.5 3.9 copy-start.2
  370.0 3.9 copy-start.2
  390.0 4.0 copy-start.2
  410.1 3.9 copy-start.2
  495.1 104.6 %copy-start.1 = (bf16[160,1536]{1,0:T(8,128)(2,1)S(1)}, bf16[160,1536]{1,0:T(8,128)(2,1)}, u32[]{:S(2)}) copy-start(bf16[160,1536]{1,0:T(8,128)(2,1)} %param.13) | copy-start | bytes 1474564
Sparse Core Ops, SparseCore 0:
  10.3 74.2 all-gather.3
  86.9 69.9 all-gather.5
  159.1 79.7 all-gather.7
  327.0 109.4 reduce-scatter.4
  441.0 156.5 reduce-scatter.2
where the time goes:
time: 608 us; the launch traced here: 606 us
  waiting for transfers between devices  294 us (48%)
  matrix products  140 us (23%)
  local copies, waits for them, and re-layouts  111 us (18%)
  other arithmetic  32 us (5%)
  blocking collectives  15.1 us (2%)
  between operations  13.9 us (2%)
    reduce_scatter x1, waiting for transfers between devices, local(): lax.psum_scatter(lax.optimization_barrier(buffer).astype(jnp.float32).ast...  98.1 us
    all_gather x1, waiting for transfers between devices, local(): lax.all_gather(proj_weight, 'frame', axis=1, tiled=True)  71.6 us
    all_gather x1, waiting for transfers between devices, local(): lax.all_gather(values, 'frame', axis=0, tiled=True)  61.7 us
    all_gather x1, waiting for transfers between devices, local(): lax.all_gather(keys, 'frame', axis=0, tiled=True)  60 us
    dynamic_slice x19, local copies, waits for them, and re-layouts, block_of(): lax.dynamic_slice_in_dim(source, offset, size, 0)  57.9 us
    dot_general x14, matrix products, scores_at(): jnp.einsum('qhd,khd->hqk', query3, key_blk, preferred_element_type=jnp.fl...  37.6 us
    dot_general x4, matrix products, key_value_rows(): jnp.einsum('hqk,qhd->khd', grad_logits, query3, preferred_element_type=jn...  27.7 us
    dot_general x5, matrix products, query_step(): jnp.einsum('hqk,khd->hqd', grad_logits, key_blk, preferred_element_type=j...  27.5 us
  transfers between devices with their start and end apart: 5, of which 4 were waited for; matrix products, arithmetic and copies ran while one was open for 32% of the time, Pallas kernels for 0%

commit v1 on v0

v1 whole, which is shorter than its diff:
```python
import functools
import math

import jax
import jax.numpy as jnp
from jax import lax
from jax.experimental import pallas as pl
from jax.experimental.pallas import tpu as pltpu
from jax.sharding import PartitionSpec as P

HD = 128
VMEM_BYTES = 50 * 1024 * 1024
BF16 = jnp.bfloat16
F32 = jnp.float32


def bits_of(count):
    found = []
    bit = 1
    while bit < count:
        found.append(bit)
        bit *= 2
    return found


def relative_of(position, bits):
    total = 0
    for place, bit in enumerate(reversed(bits)):
        if position >> place & 1:
            total |= bit
    return total


def shift_pairs(n_groups, n_tok, step):
    return [
        (g * n_tok + t, (g + step) % n_groups * n_tok + t)
        for g in range(n_groups)
        for t in range(n_tok)
    ]


def xor_pairs(count, bit):
    return [(i, i ^ bit) for i in range(count)]


def gather_bits(block, axis, count, bits):
    for bit in reversed(bits):
        other = lax.ppermute(block, axis, xor_pairs(count, bit))
        block = jnp.concatenate([block, other], axis=0)
    return block


def scatter_bits(block, axis, count, bits):
    for bit in bits:
        half = block.shape[0] // 2
        other = lax.ppermute(block[half:], axis, xor_pairs(count, bit))
        block = (block[:half].astype(F32) + other.astype(F32)).astype(BF16)
    return block


def params():
    return pltpu.CompilerParams(vmem_limit_bytes=VMEM_BYTES)


def smem():
    return pl.BlockSpec(memory_space=pltpu.SMEM)


def vmem():
    return pl.BlockSpec(memory_space=pltpu.VMEM)


def aligned(value, unit):
    return pl.multiple_of(value, unit)


def dot(a, b, dims):
    return lax.dot_general(a, b, (dims, ((), ())), preferred_element_type=F32)


def pack_kernel(n_groups, ids, q, k, v, w, *outs):
    group_width = q.shape[1] // n_groups
    for s in range(n_groups):
        dest = lax.rem(ids[0] + s, n_groups)
        start = dest * group_width
        cols = pl.ds(aligned(start, HD), group_width)
        outs[s][...] = q[:, cols]
        for h in range(group_width // HD):
            head = pl.ds(aligned(start + h * HD, HD), HD)
            outs[n_groups + s][:, 2 * h * HD : (2 * h + 1) * HD] = k[:, head]
            outs[n_groups + s][:, (2 * h + 1) * HD : (2 * h + 2) * HD] = v[:, head]
        outs[2 * n_groups + s][...] = w[:, cols]


def pack(ids, q, k, v, w, n_groups):
    rows, width = q.shape
    gw = width // n_groups
    shapes = (
        [jax.ShapeDtypeStruct((rows, gw), BF16)] * n_groups
        + [jax.ShapeDtypeStruct((rows, 2 * gw), BF16)] * n_groups
        + [jax.ShapeDtypeStruct((w.shape[0], gw), BF16)] * n_groups
    )
    outs = pl.pallas_call(
        functools.partial(pack_kernel, n_groups),
        out_shape=shapes,
        in_specs=[smem()] + [vmem()] * 4,
        out_specs=[vmem()] * len(shapes),
        compiler_params=params(),
        name="pack",
    )(ids, q, k, v, w)
    return outs[:n_groups], outs[n_groups : 2 * n_groups], outs[2 * n_groups :]


def place_queries(n_groups, ids, pieces, scratch):
    rows = pieces[0].shape[0]
    for s in range(n_groups):
        src = lax.rem(ids[0] - s + n_groups, n_groups)
        scratch[pl.ds(aligned(src * rows, 16), rows), :] = pieces[s][...]


def forward_kernel(n_groups, chunk, scale, ids, *refs):
    pieces, (kv, p_out, o_out, il_out, q_all, logits) = refs[:n_groups], refs[n_groups:]
    seq_len = kv.shape[0]
    place_queries(n_groups, ids, pieces, q_all)
    q = q_all[...]
    top = None
    for c in range(0, seq_len, chunk):
        block = dot(kv[c : c + chunk, :HD], q, ((1,), (1,)))
        logits[c : c + chunk, :] = block
        here = jnp.max(block, axis=0, keepdims=True)
        top = here if top is None else jnp.maximum(top, here)
    top = top * scale
    total = jnp.zeros_like(top)
    out = jnp.zeros((HD, q.shape[0]), F32)
    for c in range(0, seq_len, chunk):
        prob = jnp.exp2(logits[c : c + chunk, :] * scale - top)
        total = total + jnp.sum(prob, axis=0, keepdims=True)
        low = prob.astype(BF16)
        p_out[0, c : c + chunk, :] = low
        out = out + dot(kv[c : c + chunk, HD:], low, ((0,), (0,)))
    inverse = 1.0 / total
    il_out[0] = inverse
    o_out[...] = (out * inverse).T.astype(BF16)


def forward(ids, pieces, kv, n_groups):
    rows, gw = pieces[0].shape
    heads = gw // HD
    n_q = rows * n_groups
    seq_len = kv.shape[0]
    chunk = math.gcd(seq_len, 512)
    scale = math.log2(math.e) / math.sqrt(HD)
    return pl.pallas_call(
        functools.partial(forward_kernel, n_groups, chunk, scale),
        grid=(heads,),
        out_shape=[
            jax.ShapeDtypeStruct((heads, seq_len, n_q), BF16),
            jax.ShapeDtypeStruct((n_q, gw), BF16),
            jax.ShapeDtypeStruct((heads, 1, n_q), F32),
        ],
        in_specs=[smem()]
        + [pl.BlockSpec((rows, HD), lambda h: (0, h))] * n_groups
        + [pl.BlockSpec((seq_len, 2 * HD), lambda h: (0, h))],
        out_specs=[
            pl.BlockSpec((1, seq_len, n_q), lambda h: (h, 0, 0)),
            pl.BlockSpec((n_q, HD), lambda h: (0, h)),
            pl.BlockSpec((1, 1, n_q), lambda h: (h, 0, 0)),
        ],
        scratch_shapes=[pltpu.VMEM((n_q, HD), BF16), pltpu.VMEM((seq_len, n_q), F32)],
        compiler_params=params(),
        cost_estimate=pl.CostEstimate(
            flops=4 * heads * seq_len * n_q * HD,
            bytes_accessed=2 * heads * seq_len * n_q,
            transcendentals=heads * seq_len * n_q,
        ),
        name="forward",
    )(ids, *pieces, kv)


def backward_kernel(n_groups, chunk, factor, ids, *refs):
    pieces = refs[:n_groups]
    kv, p_in, o_in, il_in, da_in = refs[n_groups : n_groups + 5]
    dq_outs = refs[n_groups + 5 : 2 * n_groups + 5]
    dkv_out, q_all, dq_all = refs[2 * n_groups + 5 :]
    seq_len = kv.shape[0]
    rows = pieces[0].shape[0]
    place_queries(n_groups, ids, pieces, q_all)
    q = q_all[...]
    n_q = q.shape[0]
    inverse = jnp.broadcast_to(il_in[0], (HD, n_q)).T
    da = (da_in[...].astype(F32) * inverse).astype(BF16)
    delta = jnp.sum((da.astype(F32) * o_in[...].astype(F32)).T, axis=0, keepdims=True)
    dq = jnp.zeros((HD, n_q), F32)
    for c in range(0, seq_len, chunk):
        low = p_in[0, c : c + chunk, :]
        dp = dot(kv[c : c + chunk, HD:], da, ((1,), (1,)))
        ds = (low.astype(F32) * (dp - delta)).astype(BF16)
        dkv_out[c : c + chunk, :HD] = (factor * dot(ds, q, ((1,), (0,)))).astype(BF16)
        dkv_out[c : c + chunk, HD:] = dot(low, da, ((1,), (0,))).astype(BF16)
        dq = dq + dot(kv[c : c + chunk, :HD], ds, ((0,), (0,)))
    dq_all[...] = (factor * dq).T.astype(BF16)
    for s in range(n_groups):
        src = lax.rem(ids[0] - s + n_groups, n_groups)
        dq_outs[s][...] = dq_all[pl.ds(aligned(src * rows, 16), rows), :]


def backward(ids, pieces, kv, probs, out, inverse, grad_attn, n_groups):
    rows, gw = pieces[0].shape
    heads = gw // HD
    n_q = rows * n_groups
    seq_len = kv.shape[0]
    chunk = math.gcd(seq_len, 512)
    outs = pl.pallas_call(
        functools.partial(backward_kernel, n_groups, chunk, 1.0 / math.sqrt(HD)),
        grid=(heads,),
        out_shape=[jax.ShapeDtypeStruct((rows, gw), BF16)] * n_groups
        + [jax.ShapeDtypeStruct((seq_len, 2 * gw), BF16)],
        in_specs=[smem()]
        + [pl.BlockSpec((rows, HD), lambda h: (0, h))] * n_groups
        + [
            pl.BlockSpec((seq_len, 2 * HD), lambda h: (0, h)),
            pl.BlockSpec((1, seq_len, n_q), lambda h: (h, 0, 0)),
            pl.BlockSpec((n_q, HD), lambda h: (0, h)),
            pl.BlockSpec((1, 1, n_q), lambda h: (h, 0, 0)),
            pl.BlockSpec((n_q, HD), lambda h: (0, h)),
        ],
        out_specs=[pl.BlockSpec((rows, HD), lambda h: (0, h))] * n_groups
        + [pl.BlockSpec((seq_len, 2 * HD), lambda h: (0, h))],
        scratch_shapes=[pltpu.VMEM((n_q, HD), BF16), pltpu.VMEM((n_q, HD), BF16)],
        compiler_params=params(),
        cost_estimate=pl.CostEstimate(
            flops=8 * heads * seq_len * n_q * HD,
            bytes_accessed=2 * heads * seq_len * n_q,
            transcendentals=0,
        ),
        name="backward",
    )(ids, *pieces, kv, probs, out, inverse, grad_attn)
    return outs[:n_groups], outs[n_groups]


def frame_block(ids, sign, s, position, n_groups, n_tok):
    group = lax.rem(ids[0] + sign * s + n_groups, n_groups)
    return group * n_tok + jnp.bitwise_xor(ids[1], relative_of(position, bits_of(n_tok)))


def attn_kernel(n_groups, n_tok, n_space, ids, *refs):
    grads, (w_rel, out, weight) = refs[:n_space], refs[n_space:]
    depth = w_rel.shape[0] // (n_groups * n_tok)
    for j in range(n_tok):
        for s in range(n_groups):
            place = frame_block(ids, -1, s, j, n_groups, n_tok) * depth
            at = (j * n_groups + s) * depth
            weight[pl.ds(aligned(place, 16), depth), :] = w_rel[at : at + depth, :]
    part = grads[0].shape[1]
    total = None
    for r in range(n_space):
        start = jnp.bitwise_xor(ids[2], relative_of(r, bits_of(n_space))) * part
        term = dot(grads[r][...], weight[pl.ds(aligned(start, 16), part), :], ((1,), (0,)))
        total = term if total is None else total + term
    out[...] = total.astype(BF16)


def attn_gradient(ids, grads, w_rel, n_groups, n_tok, n_space):
    n_q = grads[0].shape[0]
    depth, gw = w_rel.shape
    return pl.pallas_call(
        functools.partial(attn_kernel, n_groups, n_tok, n_space),
        out_shape=jax.ShapeDtypeStruct((n_q, gw), BF16),
        in_specs=[smem()] + [vmem()] * (n_space + 1),
        out_specs=vmem(),
        scratch_shapes=[pltpu.VMEM((depth, gw), BF16)],
        compiler_params=params(),
        cost_estimate=pl.CostEstimate(
            flops=2 * n_q * depth * gw,
            bytes_accessed=2 * (n_q * depth + depth * gw + n_q * gw),
            transcendentals=0,
        ),
        name="attn_gradient",
    )(ids, *grads, w_rel)


def proj_kernel(n_groups, n_tok, n_space, ids, *refs):
    grads, (attn, out, whole) = refs[:n_space], refs[n_space:]
    part = grads[0].shape[1]
    for r in range(n_space):
        start = jnp.bitwise_xor(ids[2], relative_of(r, bits_of(n_space))) * part
        term = dot(grads[r][...], attn[...], ((0,), (0,)))
        whole[pl.ds(aligned(start, 16), part), :] = term.astype(BF16)
    depth = out.shape[0] // (n_groups * n_tok)
    for j in range(n_tok):
        for s in range(n_groups):
            place = frame_block(ids, 1, s, j, n_groups, n_tok) * depth
            at = (j * n_groups + s) * depth
            out[at : at + depth, :] = whole[pl.ds(aligned(place, 16), depth), :]


def proj_gradient(ids, grads, attn, n_groups, n_tok, n_space):
    n_q, part = grads[0].shape
    depth = part * n_space
    gw = attn.shape[1]
    return pl.pallas_call(
        functools.partial(proj_kernel, n_groups, n_tok, n_space),
        out_shape=jax.ShapeDtypeStruct((depth, gw), BF16),
        in_specs=[smem()] + [vmem()] * (n_space + 1),
        out_specs=vmem(),
        scratch_shapes=[pltpu.VMEM((depth, gw), BF16)],
        compiler_params=params(),
        cost_estimate=pl.CostEstimate(
            flops=2 * n_q * depth * gw,
            bytes_accessed=2 * (n_q * depth + depth * gw + n_q * gw),
            transcendentals=0,
        ),
        name="proj_gradient",
    )(ids, *grads, attn)


def unpack_kernel(n_groups, ids, *refs):
    dq_in, dkv_in, (dq, dk, dv) = refs[:n_groups], refs[n_groups : 2 * n_groups], refs[2 * n_groups :]
    gw = dq_in[0].shape[1]
    for s in range(n_groups):
        start = lax.rem(ids[0] + s, n_groups) * gw
        dq[:, pl.ds(aligned(start, HD), gw)] = dq_in[s][...]
        for h in range(gw // HD):
            head = pl.ds(aligned(start + h * HD, HD), HD)
            dk[:, head] = dkv_in[s][:, 2 * h * HD : (2 * h + 1) * HD]
            dv[:, head] = dkv_in[s][:, (2 * h + 1) * HD : (2 * h + 2) * HD]


def unpack(ids, dq_in, dkv_in, n_groups):
    rows, gw = dq_in[0].shape
    return pl.pallas_call(
        functools.partial(unpack_kernel, n_groups),
        out_shape=[jax.ShapeDtypeStruct((rows, gw * n_groups), BF16)] * 3,
        in_specs=[smem()] + [vmem()] * (2 * n_groups),
        out_specs=[vmem()] * 3,
        compiler_params=params(),
        name="unpack",
    )(ids, *dq_in, *dkv_in)


def join_kernel(n_groups, ids, *refs):
    pieces, out = refs[:n_groups], refs[n_groups]
    gw = pieces[0].shape[1]
    for s in range(n_groups):
        start = lax.rem(ids[0] - s + n_groups, n_groups) * gw
        out[:, pl.ds(aligned(start, HD), gw)] = pieces[s][...].astype(F32)


def join(ids, pieces, n_groups):
    rows, gw = pieces[0].shape
    return pl.pallas_call(
        functools.partial(join_kernel, n_groups),
        out_shape=jax.ShapeDtypeStruct((rows, gw * n_groups), F32),
        in_specs=[smem()] + [vmem()] * n_groups,
        out_specs=vmem(),
        compiler_params=params(),
        name="join",
    )(ids, *pieces)


def exchange(pieces, n_groups, n_tok, sign):
    return [pieces[0]] + [
        lax.ppermute(pieces[s], "frame", shift_pairs(n_groups, n_tok, sign * s))
        for s in range(1, n_groups)
    ]


def local(queries, keys, values, grad_out, proj_weight):
    n_frame = lax.axis_size("frame")
    n_space = lax.axis_size("space")
    rows, width = queries.shape
    n_groups = math.gcd(width // HD, n_frame)
    n_tok = n_frame // n_groups
    tok_bits = bits_of(n_tok)
    gw = width // n_groups
    frame = lax.axis_index("frame")
    ids = jnp.stack([frame // n_tok, frame % n_tok, lax.axis_index("space")]).astype(jnp.int32)

    q_send, kv_send, w_send = pack(ids, queries, keys, values, proj_weight.T, n_groups)
    q_pieces = exchange(q_send, n_groups, n_tok, 1)
    kv = jnp.concatenate(exchange(kv_send, n_groups, n_tok, 1), axis=0)
    kv = gather_bits(kv, "frame", n_frame, tok_bits)
    weight = jnp.concatenate(exchange(w_send, n_groups, n_tok, 1), axis=0)
    weight = gather_bits(weight, "frame", n_frame, tok_bits)

    own = grad_out
    if n_groups > 1:
        groups = [[g * n_tok + t for g in range(n_groups)] for t in range(n_tok)]
        own = lax.all_gather(grad_out, "frame", axis=0, tiled=True, axis_index_groups=groups)
    grads = [own]
    for bit in reversed(bits_of(n_space)):
        grads = grads + [lax.ppermute(g, "space", xor_pairs(n_space, bit)) for g in grads]

    probs, out, inverse = forward(ids, q_pieces, kv, n_groups)
    proj = proj_gradient(ids, grads, out, n_groups, n_tok, n_space)
    grad_attn = attn_gradient(ids, grads, weight, n_groups, n_tok, n_space)
    dq_send, dkv = backward(ids, q_pieces, kv, probs, out, inverse, grad_attn, n_groups)

    proj = scatter_bits(proj, "frame", n_frame, tok_bits)
    depth = proj.shape[0] // n_groups
    proj_pieces = exchange(
        [proj[s * depth : (s + 1) * depth] for s in range(n_groups)], n_groups, n_tok, 1
    )
    grad_proj = join(ids, proj_pieces, n_groups).T

    dq_pieces = exchange(dq_send, n_groups, n_tok, -1)
    dkv = scatter_bits(dkv, "frame", n_frame, tok_bits)
    dkv_pieces = exchange(
        [dkv[s * rows : (s + 1) * rows] for s in range(n_groups)], n_groups, n_tok, -1
    )
    grad_queries, grad_keys, grad_values = unpack(ids, dq_pieces, dkv_pieces, n_groups)
    return (grad_queries, grad_keys, grad_values, grad_proj)


def solution(mesh):
    in_specs = (
        P("frame", "space"),
        P("frame", "space"),
        P("frame", "space"),
        P("frame", "space"),
        P("space", "frame"),
    )
    out_specs = (P("frame", "space"), P("frame", "space"), P("frame", "space"), P("space", "frame"))
    return jax.shard_map(local, mesh=mesh, in_specs=in_specs, out_specs=out_specs, check_vma=False)
```

time: 608 us -> 256 us (0.42)
  waiting for transfers between devices: 294 us -> 104 us
  matrix products: 140 us -> 0 us
  local copies, waits for them, and re-layouts: 111 us -> 21.5 us
  starting transfers between devices: 0.37 us -> 71.3 us
  Pallas kernels: 0 us -> 42.8 us
  other arithmetic: 32 us -> 1.61 us
  blocking collectives: 15.1 us -> 0 us
    all_gather x3 -> x1, waiting for transfers between devices: 193 us -> 0.01 us  [local(): lax.all_gather(grad_out, 'frame', axis=0, tiled=True, axis_index_groups=g...]
    dot_general x34 -> x0, matrix products: 140 us -> none  [the longest x14 37.6 us: scores_at(): jnp.einsum('qhd,khd->hqk', query3, key_blk, preferred_element_type=jnp.fl...]
    ppermute x0 -> x27, waiting for transfers between devices: none -> 103 us  [the longest x18 57.3 us: exchange(): lax.ppermute(pieces[s], 'frame', shift_pairs(n_groups, n_tok, sign * s))]
    reduce_scatter x2 -> x0, waiting for transfers between devices: 98.1 us -> none  [the longest x1 98.1 us: local(): lax.psum_scatter(lax.optimization_barrier(buffer).astype(jnp.float32).ast...]
    ppermute x0 -> x27, starting transfers between devices: none -> 71.3 us  [the longest x18 64.6 us: exchange(): lax.ppermute(pieces[s], 'frame', shift_pairs(n_groups, n_tok, sign * s))]
    dynamic_slice x19 -> x0, local copies, waits for them, and re-layouts: 57.9 us -> none  [block_of(): lax.dynamic_slice_in_dim(source, offset, size, 0)]
    pallas_call x0 -> x7, Pallas kernels: none -> 42.8 us  [the longest x1 14.8 us: backward(): pl.pallas_call(functools.partial(backward_kernel, n_groups, chunk, 1.0 /...]
    optimization_barrier x1 -> x0, local copies, waits for them, and re-layouts: 20.7 us -> none  [local(): lax.optimization_barrier(buffer).astype(jnp.float32).astype(jnp.bfloat16)]
  transfers between devices with their start and end apart: 5 -> 28, of which waited for: 4 -> 11; matrix products, arithmetic and copies ran while one was open for 32% -> 7% of each run, Pallas kernels for 0% -> 8%
where the time goes in v1:
time: 256 us; the launch traced here: 255 us
  waiting for transfers between devices  104 us (41%)
  starting transfers between devices  71.3 us (28%)
  Pallas kernels  42.8 us (17%)
  local copies, waits for them, and re-layouts  21.5 us (8%)
  between operations  14.2 us (6%)
    ppermute x18, starting transfers between devices, exchange(): lax.ppermute(pieces[s], 'frame', shift_pairs(n_groups, n_tok, sign * s))  64.6 us
    ppermute x18, waiting for transfers between devices, exchange(): lax.ppermute(pieces[s], 'frame', shift_pairs(n_groups, n_tok, sign * s))  57.3 us
    ppermute x4, waiting for transfers between devices, scatter_bits(): other = lax.ppermute(block[half:], axis, xor_pairs(count, bit))  22.7 us
    ppermute x1, waiting for transfers between devices, local(): lax.ppermute(g, 'space', xor_pairs(n_space, bit))  16 us
    pallas_call x1, Pallas kernels, backward(): pl.pallas_call(functools.partial(backward_kernel, n_groups, chunk, 1.0 /...  14.8 us
    pallas_call x1, Pallas kernels, forward(): pl.pallas_call(functools.partial(forward_kernel, n_groups, chunk, scale),...  12.7 us
    unnamed x26, local copies, waits for them, and re-layouts  10.7 us
    concatenate x4, local copies, waits for them, and re-layouts, gather_bits(): block = jnp.concatenate([block, other], axis=0)  7.33 us
  transfers between devices with their start and end apart: 28, of which 11 were waited for; matrix products, arithmetic and copies ran while one was open for 7% of the time, Pallas kernels for 8%

profile of v1, /device:TPU:0, one launch (start us, length us, event | category | flops | bytes accessed | tf_op | source)
XLA Modules:
  0.0 255.3 jit_solution(2212582516460278382)
XLA Ops:
  7.2 0.7 all-gather.2.cloned.1.call-update
  7.9 0.1 pad_add_fusion.ids
  8.0 1.0 copy-done.1
  9.0 1.0 copy-done.2
  10.1 1.0 copy-done.3
  11.1 1.3 pack.1
  12.4 3.1 %collective-permute-start.3 = (bf16[160,768]{1,0:T(8,128)(2,1)S(1)}, bf16[160,768]{1,0:T(8,128)(2,1)S(1)}, u32[]{:S(2)}, u32[]{:S(2)}) collective-permute-start(bf16[160,768]{1,0:T(8,128)(2,1)S(1)} %get-tuple-element.32), channel_id=1, source_target_pairs={{0,8},{2,10},{4,12},{6,14},{8,16},{10,18},{12,20},{14,22},{16,24},... | collective-permute-start | bytes 737288 | tf_op jit(solution)/shard_map/ppermute | solution.py:363
  15.5 2.6 %collective-permute-start.4 = (bf16[160,768]{1,0:T(8,128)(2,1)S(1)}, bf16[160,768]{1,0:T(8,128)(2,1)S(1)}, u32[]{:S(2)}, u32[]{:S(2)}) collective-permute-start(bf16[160,768]{1,0:T(8,128)(2,1)S(1)} %get-tuple-element.33), channel_id=1, source_target_pairs={{0,16},{2,18},{4,20},{6,22},{8,24},{10,26},{12,28},{14,30},{16,0},... | collective-permute-start | bytes 737288 | tf_op jit(solution)/shard_map/ppermute | solution.py:363
  18.1 1.3 collective-permute-start.5
  19.5 5.0 %collective-permute-done.3 = bf16[160,768]{1,0:T(8,128)(2,1)S(1)} collective-permute-done((bf16[160,768]{1,0:T(8,128)(2,1)S(1)}, bf16[160,768]{1,0:T(8,128)(2,1)S(1)}, u32[]{:S(2)}, u32[]{:S(2)}) %collective-permute-start.3) | collective-permute-done | bytes 245792 | tf_op jit(solution)/shard_map/ppermute | solution.py:363
  24.5 20.2 %collective-permute-done.4 = bf16[160,768]{1,0:T(8,128)(2,1)S(1)} collective-permute-done((bf16[160,768]{1,0:T(8,128)(2,1)S(1)}, bf16[160,768]{1,0:T(8,128)(2,1)S(1)}, u32[]{:S(2)}, u32[]{:S(2)}) %collective-permute-start.4) | collective-permute-done | bytes 245792 | tf_op jit(solution)/shard_map/ppermute | solution.py:363
  44.8 1.6 collective-permute-start.6
  46.3 21.2 %collective-permute-start.9 = (bf16[192,384]{1,0:T(8,128)(2,1)S(1)}, bf16[192,384]{1,0:T(8,128)(2,1)S(1)}, u32[]{:S(2)}, u32[]{:S(2)}) collective-permute-start(bf16[192,384]{1,0:T(8,128)(2,1)S(1)} %get-tuple-element.39), channel_id=1, source_target_pairs={{0,8},{2,10},{4,12},{6,14},{8,16},{10,18},{12,20},{14,22},{16,24},... | collective-permute-start | bytes 442376 | tf_op jit(solution)/shard_map/ppermute | solution.py:363
  67.6 2.4 collective-permute-start.11
  69.9 0.7 constant_dynamic-update-slice_fusion.4
  70.7 1.2 collective-permute-done.9
  71.9 8.8 %collective-permute-done.10 = bf16[192,384]{1,0:T(8,128)(2,1)S(1)} collective-permute-done((bf16[192,384]{1,0:T(8,128)(2,1)S(1)}, bf16[192,384]{1,0:T(8,128)(2,1)S(1)}, u32[]{:S(2)}, u32[]{:S(2)}) %collective-permute-start.10) | collective-permute-done | bytes 147488 | tf_op jit(solution)/shard_map/ppermute | solution.py:363
  80.7 0.7 collective-permute-start.12
  81.4 0.8 constant_dynamic-update-slice_fusion.3
  82.1 0.7 constant_dynamic-update-slice_fusion.2
  82.9 0.7 constant_dynamic-update-slice_fusion.1
  83.6 1.1 constant_dynamic-update-slice_fusion
  84.7 0.8 constant_dynamic-update-slice_fusion.15
  85.5 1.3 constant_dynamic-update-slice_fusion.14
  86.7 0.7 constant_dynamic-update-slice_fusion.13
  87.4 0.7 constant_dynamic-update-slice_fusion.12
  88.1 7.2 %collective-permute-done.12 = bf16[768,384]{1,0:T(8,128)(2,1)S(1)} collective-permute-done((bf16[768,384]{1,0:T(8,128)(2,1)S(1)}, bf16[768,384]{1,0:T(8,128)(2,1)S(1)}, u32[]{:S(2)}, u32[]{:S(2)}) %collective-permute-start.12) | collective-permute-done | bytes 589856 | tf_op jit(solution)/shard_map/ppermute | solution.py:48
  95.3 0.9 constant_dynamic-update-slice_fusion.11
  96.2 1.6 collective-permute-start.8
  97.8 6.6 %collective-permute-start = (bf16[160,384]{1,0:T(8,128)(2,1)S(1)}, bf16[160,384]{1,0:T(8,128)(2,1)S(1)}, u32[]{:S(2)}, u32[]{:S(2)}) collective-permute-start(bf16[160,384]{1,0:T(8,128)(2,1)S(1)} %get-tuple-element.28), channel_id=1, source_target_pairs={{0,8},{2,10},{4,12},{6,14},{8,16},{10,18},{12,20},{14,22},{16,24},... | collective-permute-start | bytes 368648 | tf_op jit(solution)/shard_map/ppermute | solution.py:363
  104.5 2.4 collective-permute-start.2
  106.8 1.5 constant_dynamic-update-slice_fusion.16.refs_2_
  108.4 3.8 %constant_dynamic-update-slice_fusion.5.refs_4_ = bf16[2560,768]{1,0:T(8,128)(2,1)} fusion(bf16[2560,768]{1,0:T(8,128)(2,1)} %copy-done.8, bf16[1280,768]{1,0:T(8,128)(2,1)} %collective-permute-done.7), kind=kLoop, calls=%fused_computation.11 | loop fusion | bytes 3932160 | tf_op jit(solution)/shard_map/concatenate | solution.py:49
  112.2 0.7 collective-permute-done.1.refs_2_
  112.9 12.7 %forward.1 = (bf16[3,2560,640]{2,1,0:T(8,128)(2,1)}, bf16[640,384]{1,0:T(8,128)(2,1)S(1)}, f32[3,1,640]{2,1,0:T(1,128)S(1)}) custom-call(s32[3]{0:T(128)S(1)} %pad_add_fusion.ids, bf16[160,384]{1,0:T(8,128)(2,1)S(1)} %get-tuple-element.27.refs_0_, bf16[160,384]{1,0:T(8,128)(2,1)S(1)} %collective-permute-done.refs_1_, ...), custom_call_target="tpu_custom_call" | custom-call | flops 2516582400 | bytes 9830400 | tf_op jit(solution)/shard_map/forward/pallas_call | solution.py:153
  125.6 16.0 %collective-permute-done.8.refs_1_ = bf16[640,1536]{1,0:T(8,128)(2,1)S(1)} collective-permute-done((bf16[640,1536]{1,0:T(8,128)(2,1)}, bf16[640,1536]{1,0:T(8,128)(2,1)S(1)}, u32[]{:S(2)}, u32[]{:S(2)}) %collective-permute-start.8) | collective-permute-done | bytes 1966112 | tf_op jit(solution)/shard_map/ppermute | solution.py:392
  141.7 1.3 copy-done.5
  142.9 4.7 %attn_gradient.1.refs_8_ = bf16[640,384]{1,0:T(8,128)(2,1)S(1)} custom-call(s32[3]{0:T(128)S(1)} %pad_add_fusion.ids, bf16[640,1536]{1,0:T(8,128)(2,1)S(1)} %copy-done, bf16[640,1536]{1,0:T(8,128)(2,1)} %copy-done.5, bf16[3072,384]{1,0:T(8,128)(2,1)} %copy-done.7), custom_call_target="tpu_custom_call" | custom-call | flops 1509949440 | bytes 6782976 | tf_op jit(solution)/shard_map/attn_gradient/pallas_call | solution.py:266
  147.6 14.8 %backward.1 = (bf16[160,384]{1,0:T(8,128)(2,1)S(1)}, bf16[160,384]{1,0:T(8,128)(2,1)S(1)}, bf16[160,384]{1,0:T(8,128)(2,1)S(1)}, bf16[160,384]{1,0:T(8,128)(2,1)S(1)}, bf16[2560,768]{1,0:T(8,128)(2,1)}) custom-call(s32[3]{0:T(128)S(1)} %pad_add_fusion.ids, bf16[160,384]{1,0:T(8,128)(2,1)S(1)} %get-tuple-element.27.refs_0_, ...), custom_call_target="tpu_custom_call" | custom-call | flops 5033164800 | bytes 9830400 | tf_op jit(solution)/shard_map/backward/pallas_call | solution.py:213
  162.4 1.7 slice.49
  164.1 0.1 collective-permute-start.17
  164.2 5.6 %proj_gradient.1 = bf16[3072,384]{1,0:T(8,128)(2,1)} custom-call(s32[3]{0:T(128)S(1)} %pad_add_fusion.ids, bf16[640,1536]{1,0:T(8,128)(2,1)S(1)} %copy-done, bf16[640,1536]{1,0:T(8,128)(2,1)} %copy-done.5, bf16[640,384]{1,0:T(8,128)(2,1)S(1)} %get-tuple-element.36.refs_6_.refs_2_), custom_call_target="tpu_custom_call" | custom-call | flops 1509949440 | bytes 6782976 | tf_op jit(solution)/shard_map/proj_gradient/pallas_call | solution.py:301
  169.8 1.5 slice.71
  171.4 0.6 collective-permute-start.22
  171.9 2.5 collective-permute-done.22
  174.4 0.3 add_convert_fusion.1
  174.8 1.6 collective-permute-start.23
  176.5 0.6 add_convert_fusion
  177.2 0.5 collective-permute-start.18
  177.7 5.2 %collective-permute-start.14 = (bf16[160,384]{1,0:T(8,128)(2,1)S(1)}, bf16[160,384]{1,0:T(8,128)(2,1)S(1)}, u32[]{:S(2)}, u32[]{:S(2)}) collective-permute-start(bf16[160,384]{1,0:T(8,128)(2,1)S(1)} %get-tuple-element.43), channel_id=1, source_target_pairs={{0,24},{2,26},{4,28},{6,30},{8,0},{10,2},{12,4},{14,6},{16,8},{18,... | collective-permute-start | bytes 368648 | tf_op jit(solution)/shard_map/ppermute | solution.py:363
  182.9 8.1 %collective-permute-done.23 = bf16[768,384]{1,0:T(8,128)(2,1)S(1)} collective-permute-done((bf16[768,384]{1,0:T(8,128)(2,1)S(1)}, bf16[768,384]{1,0:T(8,128)(2,1)S(1)}, u32[]{:S(2)}, u32[]{:S(2)}) %collective-permute-start.23) | collective-permute-done | bytes 589856 | tf_op jit(solution)/shard_map/ppermute | solution.py:56
  191.0 0.2 add_convert_fusion.3
  191.3 5.3 %collective-permute-start.26 = (bf16[192,384]{1,0:T(8,128)(2,1)S(1)}, bf16[192,384]{1,0:T(8,128)(2,1)S(1)}, u32[]{:S(2)}, u32[]{:S(2)}) collective-permute-start(bf16[192,384]{1,0:T(8,128)(2,1)S(1)} %get-tuple-element.56), channel_id=1, source_target_pairs={{0,24},{2,26},{4,28},{6,30},{8,0},{10,2},{12,4},{14,6},{16,8},{18,... | collective-permute-start | bytes 442376 | tf_op jit(solution)/shard_map/ppermute | solution.py:363
  196.5 2.9 %collective-permute-start.25 = (bf16[192,384]{1,0:T(8,128)(2,1)S(1)}, bf16[192,384]{1,0:T(8,128)(2,1)S(1)}, u32[]{:S(2)}, u32[]{:S(2)}) collective-permute-start(bf16[192,384]{1,0:T(8,128)(2,1)S(1)} %get-tuple-element.57), channel_id=1, source_target_pairs={{0,16},{2,18},{4,20},{6,22},{8,24},{10,26},{12,28},{14,30},{16,0},... | collective-permute-start | bytes 442376 | tf_op jit(solution)/shard_map/ppermute | solution.py:363
  199.4 12.1 %collective-permute-done.18 = bf16[640,768]{1,0:T(8,128)(2,1)S(1)} collective-permute-done((bf16[640,768]{1,0:T(8,128)(2,1)S(1)}, bf16[640,768]{1,0:T(8,128)(2,1)S(1)}, u32[]{:S(2)}, u32[]{:S(2)}) %collective-permute-start.18) | collective-permute-done | bytes 983072 | tf_op jit(solution)/shard_map/ppermute | solution.py:56
  211.6 0.3 add_convert_fusion.2
  211.8 0.1 fusion
  211.9 6.7 %collective-permute-start.21 = (bf16[160,768]{1,0:T(8,128)(2,1)S(1)}, bf16[160,768]{1,0:T(8,128)(2,1)S(1)}, u32[]{:S(2)}, u32[]{:S(2)}) collective-permute-start(bf16[160,768]{1,0:T(8,128)(2,1)S(1)} %get-tuple-element.50), channel_id=1, source_target_pairs={{0,8},{2,10},{4,12},{6,14},{8,16},{10,18},{12,20},{14,22},{16,24},... | collective-permute-start | bytes 737288 | tf_op jit(solution)/shard_map/ppermute | solution.py:363
  218.6 2.4 collective-permute-start.19
  221.1 0.5 collective-permute-start.15
  221.6 2.0 collective-permute-start.16
  223.6 1.7 join.1
  225.2 21.3 %collective-permute-done.15.refs_2_ = bf16[160,384]{1,0:T(8,128)(2,1)S(1)} collective-permute-done((bf16[160,384]{1,0:T(8,128)(2,1)S(1)}, bf16[160,384]{1,0:T(8,128)(2,1)S(1)}, u32[]{:S(2)}, u32[]{:S(2)}) %collective-permute-start.15) | collective-permute-done | bytes 122912 | tf_op jit(solution)/shard_map/ppermute | solution.py:363
  246.6 1.9 unpack.1
  (43 shorter events, 0.4 us)
Async XLA Ops:
  7.2 89.0 %all-gather.2.cloned.1.call-start = ((), (), s32[]{:S(2)}) async-start(), calls=%async_computation | async-start | bytes 2457600 | tf_op jit(solution)/shard_map/all_gather | solution.py:389
  8.0 1.0 copy-start.1
  9.0 1.0 copy-start.2
  10.1 1.0 copy-start.3
  12.4 12.0 %collective-permute-start.3 = (bf16[160,768]{1,0:T(8,128)(2,1)S(1)}, bf16[160,768]{1,0:T(8,128)(2,1)S(1)}, u32[]{:S(2)}, u32[]{:S(2)}) collective-permute-start(bf16[160,768]{1,0:T(8,128)(2,1)S(1)} %get-tuple-element.32), channel_id=1, source_target_pairs={{0,8},{2,10},{4,12},{6,14},{8,16},{10,18},{12,20},{14,22},{16,24},... | collective-permute-start | bytes 737288 | tf_op jit(solution)/shard_map/ppermute | solution.py:363
  15.5 29.2 %collective-permute-start.4 = (bf16[160,768]{1,0:T(8,128)(2,1)S(1)}, bf16[160,768]{1,0:T(8,128)(2,1)S(1)}, u32[]{:S(2)}, u32[]{:S(2)}) collective-permute-start(bf16[160,768]{1,0:T(8,128)(2,1)S(1)} %get-tuple-element.33), channel_id=1, source_target_pairs={{0,16},{2,18},{4,20},{6,22},{8,24},{10,26},{12,28},{14,30},{16,0},... | collective-permute-start | bytes 737288 | tf_op jit(solution)/shard_map/ppermute | solution.py:363
  18.1 26.6 %collective-permute-start.5 = (bf16[160,768]{1,0:T(8,128)(2,1)S(1)}, bf16[160,768]{1,0:T(8,128)(2,1)S(1)}, u32[]{:S(2)}, u32[]{:S(2)}) collective-permute-start(bf16[160,768]{1,0:T(8,128)(2,1)S(1)} %get-tuple-element.34), channel_id=1, source_target_pairs={{0,24},{2,26},{4,28},{6,30},{8,0},{10,2},{12,4},{14,6},{16,8},{18,... | collective-permute-start | bytes 737288 | tf_op jit(solution)/shard_map/ppermute | solution.py:363
  44.8 38.8 %collective-permute-start.6 = (bf16[640,768]{1,0:T(8,128)(2,1)S(1)}, bf16[640,768]{1,0:T(8,128)(2,1)S(1)}, u32[]{:S(2)}, u32[]{:S(2)}) collective-permute-start(bf16[640,768]{1,0:T(8,128)(2,1)S(1)} %pad_maximum_fusion), channel_id=1, source_target_pairs={{0,4},{2,6},{4,0},{6,2},{8,12},{10,14},{12,8},{14,10},{16,20},{18,... | collective-permute-start | bytes 2949128 | tf_op jit(solution)/shard_map/ppermute | solution.py:48
  46.3 25.5 %collective-permute-start.9 = (bf16[192,384]{1,0:T(8,128)(2,1)S(1)}, bf16[192,384]{1,0:T(8,128)(2,1)S(1)}, u32[]{:S(2)}, u32[]{:S(2)}) collective-permute-start(bf16[192,384]{1,0:T(8,128)(2,1)S(1)} %get-tuple-element.39), channel_id=1, source_target_pairs={{0,8},{2,10},{4,12},{6,14},{8,16},{10,18},{12,20},{14,22},{16,24},... | collective-permute-start | bytes 442376 | tf_op jit(solution)/shard_map/ppermute | solution.py:363
  67.6 13.1 %collective-permute-start.10 = (bf16[192,384]{1,0:T(8,128)(2,1)S(1)}, bf16[192,384]{1,0:T(8,128)(2,1)S(1)}, u32[]{:S(2)}, u32[]{:S(2)}) collective-permute-start(bf16[192,384]{1,0:T(8,128)(2,1)S(1)} %get-tuple-element.40), channel_id=1, source_target_pairs={{0,16},{2,18},{4,20},{6,22},{8,24},{10,26},{12,28},{14,30},{16,0},... | collective-permute-start | bytes 442376 | tf_op jit(solution)/shard_map/ppermute | solution.py:363
  67.6 13.1 %collective-permute-start.11 = (bf16[192,384]{1,0:T(8,128)(2,1)S(1)}, bf16[192,384]{1,0:T(8,128)(2,1)S(1)}, u32[]{:S(2)}, u32[]{:S(2)}) collective-permute-start(bf16[192,384]{1,0:T(8,128)(2,1)S(1)} %get-tuple-element.41), channel_id=1, source_target_pairs={{0,24},{2,26},{4,28},{6,30},{8,0},{10,2},{12,4},{14,6},{16,8},{18,... | collective-permute-start | bytes 442376 | tf_op jit(solution)/shard_map/ppermute | solution.py:363
  80.7 14.5 %collective-permute-start.12 = (bf16[768,384]{1,0:T(8,128)(2,1)S(1)}, bf16[768,384]{1,0:T(8,128)(2,1)S(1)}, u32[]{:S(2)}, u32[]{:S(2)}) collective-permute-start(bf16[768,384]{1,0:T(8,128)(2,1)S(1)} %pad_maximum_fusion.1), channel_id=1, source_target_pairs={{0,4},{2,6},{4,0},{6,2},{8,12},{10,14},{12,8},{14,10},{16,20},{18,... | collective-permute-start | bytes 1769480 | tf_op jit(solution)/shard_map/ppermute | solution.py:48
  84.7 11.5 %copy-start.8 = (bf16[2560,768]{1,0:T(8,128)(2,1)}, bf16[2560,768]{1,0:T(8,128)(2,1)S(1)}, u32[]{:S(2)}) copy-start(bf16[2560,768]{1,0:T(8,128)(2,1)S(1)} %get-tuple-element.55) | copy-start | bytes 11796484
  84.7 23.6 %collective-permute-start.7 = (bf16[1280,768]{1,0:T(8,128)(2,1)}, bf16[1280,768]{1,0:T(8,128)(2,1)}, u32[]{:S(2)}, u32[]{:S(2)}) collective-permute-start(bf16[1280,768]{1,0:T(8,128)(2,1)} %get-tuple-element.54), channel_id=1, source_target_pairs={{0,2},{2,0},{4,6},{6,4},{8,10},{10,8},{12,14},{14,12},{16,18},{18,... | collective-permute-start | bytes 5898248 | tf_op jit(solution)/shard_map/ppermute | solution.py:48
  96.2 8.3 %collective-permute-start.13 = (bf16[1536,384]{1,0:T(8,128)(2,1)}, bf16[1536,384]{1,0:T(8,128)(2,1)}, u32[]{:S(2)}, u32[]{:S(2)}) collective-permute-start(bf16[1536,384]{1,0:T(8,128)(2,1)} %get-tuple-element.60), channel_id=1, source_target_pairs={{0,2},{2,0},{4,6},{6,4},{8,10},{10,8},{12,14},{14,12},{16,18},{18,... | collective-permute-start | bytes 3538952 | tf_op jit(solution)/shard_map/ppermute | solution.py:48
  96.2 45.4 %collective-permute-start.8 = (bf16[640,1536]{1,0:T(8,128)(2,1)}, bf16[640,1536]{1,0:T(8,128)(2,1)S(1)}, u32[]{:S(2)}, u32[]{:S(2)}) collective-permute-start(bf16[640,1536]{1,0:T(8,128)(2,1)} %all-gather.2.cloned.1.call-done.refs_0_), channel_id=1, source_target_pairs={{0,1},{1,0},{2,3},{3,2},{4,5},{5,4},{6,7},{7,6},{8,9},{9,8},{10,11... | collective-permute-start | bytes 5898248 | tf_op jit(solution)/shard_map/ppermute | solution.py:392
  97.8 14.4 %collective-permute-start = (bf16[160,384]{1,0:T(8,128)(2,1)S(1)}, bf16[160,384]{1,0:T(8,128)(2,1)S(1)}, u32[]{:S(2)}, u32[]{:S(2)}) collective-permute-start(bf16[160,384]{1,0:T(8,128)(2,1)S(1)} %get-tuple-element.28), channel_id=1, source_target_pairs={{0,8},{2,10},{4,12},{6,14},{8,16},{10,18},{12,20},{14,22},{16,24},... | collective-permute-start | bytes 368648 | tf_op jit(solution)/shard_map/ppermute | solution.py:363
  104.5 8.5 %collective-permute-start.1 = (bf16[160,384]{1,0:T(8,128)(2,1)S(1)}, bf16[160,384]{1,0:T(8,128)(2,1)S(1)}, u32[]{:S(2)}, u32[]{:S(2)}) collective-permute-start(bf16[160,384]{1,0:T(8,128)(2,1)S(1)} %get-tuple-element.29), channel_id=1, source_target_pairs={{0,16},{2,18},{4,20},{6,22},{8,24},{10,26},{12,28},{14,30},{16,0},... | collective-permute-start | bytes 368648 | tf_op jit(solution)/shard_map/ppermute | solution.py:363
  104.5 8.5 %collective-permute-start.2 = (bf16[160,384]{1,0:T(8,128)(2,1)S(1)}, bf16[160,384]{1,0:T(8,128)(2,1)S(1)}, u32[]{:S(2)}, u32[]{:S(2)}) collective-permute-start(bf16[160,384]{1,0:T(8,128)(2,1)S(1)} %get-tuple-element.30), channel_id=1, source_target_pairs={{0,24},{2,26},{4,28},{6,30},{8,0},{10,2},{12,4},{14,6},{16,8},{18,... | collective-permute-start | bytes 368648 | tf_op jit(solution)/shard_map/ppermute | solution.py:363
  108.3 3.8 %copy-start.7 = (bf16[3072,384]{1,0:T(8,128)(2,1)}, bf16[3072,384]{1,0:T(8,128)(2,1)S(1)}, u32[]{:S(2)}) copy-start(bf16[3072,384]{1,0:T(8,128)(2,1)S(1)} %constant_dynamic-update-slice_fusion.16.refs_2_) | copy-start | bytes 7077892
  112.9 30.0 %copy-start = (bf16[640,1536]{1,0:T(8,128)(2,1)S(1)}, bf16[640,1536]{1,0:T(8,128)(2,1)}, u32[]{:S(2)}) copy-start(bf16[640,1536]{1,0:T(8,128)(2,1)} %all-gather.2.cloned.1.call-done.refs_0_) | copy-start | bytes 5898244
  141.7 1.3 copy-start.5
  164.1 12.4 %collective-permute-start.17 = (bf16[1280,768]{1,0:T(8,128)(2,1)S(1)}, bf16[1280,768]{1,0:T(8,128)(2,1)S(1)}, u32[]{:S(2)}, u32[]{:S(2)}) collective-permute-start(bf16[1280,768]{1,0:T(8,128)(2,1)S(1)} %slice.49), channel_id=1, source_target_pairs={{0,2},{2,0},{4,6},{6,4},{8,10},{10,8},{12,14},{14,12},{16,18},{18,... | collective-permute-start | bytes 5898248 | tf_op jit(solution)/shard_map/ppermute | solution.py:56
  169.8 4.6 %copy-start.4 = (bf16[3072,384]{1,0:T(8,128)(2,1)S(1)}, bf16[3072,384]{1,0:T(8,128)(2,1)}, u32[]{:S(2)}) copy-start(bf16[3072,384]{1,0:T(8,128)(2,1)} %proj_gradient.1) | copy-start | bytes 7077892
  171.4 5.1 %copy-start.6 = (bf16[2560,768]{1,0:T(8,128)(2,1)S(1)}, bf16[2560,768]{1,0:T(8,128)(2,1)}, u32[]{:S(2)}) copy-start(bf16[2560,768]{1,0:T(8,128)(2,1)} %get-tuple-element.46) | copy-start | bytes 11796484
  171.4 3.0 %collective-permute-start.22 = (bf16[1536,384]{1,0:T(8,128)(2,1)S(1)}, bf16[1536,384]{1,0:T(8,128)(2,1)S(1)}, u32[]{:S(2)}, u32[]{:S(2)}) collective-permute-start(bf16[1536,384]{1,0:T(8,128)(2,1)S(1)} %slice.71), channel_id=1, source_target_pairs={{0,2},{2,0},{4,6},{6,4},{8,10},{10,8},{12,14},{14,12},{16,18},{18,... | collective-permute-start | bytes 3538952 | tf_op jit(solution)/shard_map/ppermute | solution.py:56
  174.8 16.2 %collective-permute-start.23 = (bf16[768,384]{1,0:T(8,128)(2,1)S(1)}, bf16[768,384]{1,0:T(8,128)(2,1)S(1)}, u32[]{:S(2)}, u32[]{:S(2)}) collective-permute-start(bf16[768,384]{1,0:T(8,128)(2,1)S(1)} %slice.73), channel_id=1, source_target_pairs={{0,4},{2,6},{4,0},{6,2},{8,12},{10,14},{12,8},{14,10},{16,20},{18,... | collective-permute-start | bytes 1769480 | tf_op jit(solution)/shard_map/ppermute | solution.py:56
  177.2 34.4 %collective-permute-start.18 = (bf16[640,768]{1,0:T(8,128)(2,1)S(1)}, bf16[640,768]{1,0:T(8,128)(2,1)S(1)}, u32[]{:S(2)}, u32[]{:S(2)}) collective-permute-start(bf16[640,768]{1,0:T(8,128)(2,1)S(1)} %slice.65), channel_id=1, source_target_pairs={{0,4},{2,6},{4,0},{6,2},{8,12},{10,14},{12,8},{14,10},{16,20},{18,... | collective-permute-start | bytes 2949128 | tf_op jit(solution)/shard_map/ppermute | solution.py:56
  177.7 40.9 %collective-permute-start.14 = (bf16[160,384]{1,0:T(8,128)(2,1)S(1)}, bf16[160,384]{1,0:T(8,128)(2,1)S(1)}, u32[]{:S(2)}, u32[]{:S(2)}) collective-permute-start(bf16[160,384]{1,0:T(8,128)(2,1)S(1)} %get-tuple-element.43), channel_id=1, source_target_pairs={{0,24},{2,26},{4,28},{6,30},{8,0},{10,2},{12,4},{14,6},{16,8},{18,... | collective-permute-start | bytes 368648 | tf_op jit(solution)/shard_map/ppermute | solution.py:363
  191.3 27.4 %collective-permute-start.26 = (bf16[192,384]{1,0:T(8,128)(2,1)S(1)}, bf16[192,384]{1,0:T(8,128)(2,1)S(1)}, u32[]{:S(2)}, u32[]{:S(2)}) collective-permute-start(bf16[192,384]{1,0:T(8,128)(2,1)S(1)} %get-tuple-element.56), channel_id=1, source_target_pairs={{0,24},{2,26},{4,28},{6,30},{8,0},{10,2},{12,4},{14,6},{16,8},{18,... | collective-permute-start | bytes 442376 | tf_op jit(solution)/shard_map/ppermute | solution.py:363
  196.5 24.5 %collective-permute-start.25 = (bf16[192,384]{1,0:T(8,128)(2,1)S(1)}, bf16[192,384]{1,0:T(8,128)(2,1)S(1)}, u32[]{:S(2)}, u32[]{:S(2)}) collective-permute-start(bf16[192,384]{1,0:T(8,128)(2,1)S(1)} %get-tuple-element.57), channel_id=1, source_target_pairs={{0,16},{2,18},{4,20},{6,22},{8,24},{10,26},{12,28},{14,30},{16,0},... | collective-permute-start | bytes 442376 | tf_op jit(solution)/shard_map/ppermute | solution.py:363
  199.4 22.2 %collective-permute-start.24 = (bf16[192,384]{1,0:T(8,128)(2,1)S(1)}, bf16[192,384]{1,0:T(8,128)(2,1)S(1)}, u32[]{:S(2)}, u32[]{:S(2)}) collective-permute-start(bf16[192,384]{1,0:T(8,128)(2,1)S(1)} %get-tuple-element.58), channel_id=1, source_target_pairs={{0,8},{2,10},{4,12},{6,14},{8,16},{10,18},{12,20},{14,22},{16,24},... | collective-permute-start | bytes 442376 | tf_op jit(solution)/shard_map/ppermute | solution.py:363
  211.9 34.6 %collective-permute-start.21 = (bf16[160,768]{1,0:T(8,128)(2,1)S(1)}, bf16[160,768]{1,0:T(8,128)(2,1)S(1)}, u32[]{:S(2)}, u32[]{:S(2)}) collective-permute-start(bf16[160,768]{1,0:T(8,128)(2,1)S(1)} %get-tuple-element.50), channel_id=1, source_target_pairs={{0,8},{2,10},{4,12},{6,14},{8,16},{10,18},{12,20},{14,22},{16,24},... | collective-permute-start | bytes 737288 | tf_op jit(solution)/shard_map/ppermute | solution.py:363
  218.6 27.9 %collective-permute-start.20 = (bf16[160,768]{1,0:T(8,128)(2,1)S(1)}, bf16[160,768]{1,0:T(8,128)(2,1)S(1)}, u32[]{:S(2)}, u32[]{:S(2)}) collective-permute-start(bf16[160,768]{1,0:T(8,128)(2,1)S(1)} %get-tuple-element.51), channel_id=1, source_target_pairs={{0,16},{2,18},{4,20},{6,22},{8,24},{10,26},{12,28},{14,30},{16,0},... | collective-permute-start | bytes 737288 | tf_op jit(solution)/shard_map/ppermute | solution.py:363
  218.6 27.9 %collective-permute-start.19 = (bf16[160,768]{1,0:T(8,128)(2,1)S(1)}, bf16[160,768]{1,0:T(8,128)(2,1)S(1)}, u32[]{:S(2)}, u32[]{:S(2)}) collective-permute-start(bf16[160,768]{1,0:T(8,128)(2,1)S(1)} %get-tuple-element.52), channel_id=1, source_target_pairs={{0,24},{2,26},{4,28},{6,30},{8,0},{10,2},{12,4},{14,6},{16,8},{18,... | collective-permute-start | bytes 737288 | tf_op jit(solution)/shard_map/ppermute | solution.py:363
  221.1 25.5 %collective-permute-start.15 = (bf16[160,384]{1,0:T(8,128)(2,1)S(1)}, bf16[160,384]{1,0:T(8,128)(2,1)S(1)}, u32[]{:S(2)}, u32[]{:S(2)}) collective-permute-start(bf16[160,384]{1,0:T(8,128)(2,1)S(1)} %get-tuple-element.44), channel_id=1, source_target_pairs={{0,16},{2,18},{4,20},{6,22},{8,24},{10,26},{12,28},{14,30},{16,0},... | collective-permute-start | bytes 368648 | tf_op jit(solution)/shard_map/ppermute | solution.py:363
  221.6 24.9 %collective-permute-start.16 = (bf16[160,384]{1,0:T(8,128)(2,1)S(1)}, bf16[160,384]{1,0:T(8,128)(2,1)S(1)}, u32[]{:S(2)}, u32[]{:S(2)}) collective-permute-start(bf16[160,384]{1,0:T(8,128)(2,1)S(1)} %get-tuple-element.45), channel_id=1, source_target_pairs={{0,8},{2,10},{4,12},{6,14},{8,16},{10,18},{12,20},{14,22},{16,24},... | collective-permute-start | bytes 368648 | tf_op jit(solution)/shard_map/ppermute | solution.py:363
Sparse Core Ops, SparseCore 0:
  9.6 71.3 all-gather.1

commit v2 on v1

v2 whole, which is shorter than its diff:
```python
import functools
import math

import jax
import jax.numpy as jnp
from jax import lax
from jax.experimental import pallas as pl
from jax.experimental.pallas import tpu as pltpu
from jax.sharding import PartitionSpec as P

HD = 128
VMEM_BYTES = 40 * 1024 * 1024
GRAD_CHUNKS = 2
BF16 = jnp.bfloat16
F32 = jnp.float32


def bits_of(count):
    found = []
    bit = 1
    while bit < count:
        found.append(bit)
        bit *= 2
    return found


def relative_of(position, bits):
    total = 0
    for place, bit in enumerate(reversed(bits)):
        if position >> place & 1:
            total |= bit
    return total


def shift_pairs(n_groups, n_tok, step):
    return [
        (g * n_tok + t, (g + step) % n_groups * n_tok + t)
        for g in range(n_groups)
        for t in range(n_tok)
    ]


def xor_pairs(count, bit):
    return [(i, i ^ bit) for i in range(count)]


def gather_blocks(block, axis, count, bits):
    blocks = [block]
    for bit in reversed(bits):
        blocks = blocks + [lax.ppermute(b, axis, xor_pairs(count, bit)) for b in blocks]
    return blocks


def params():
    return pltpu.CompilerParams(vmem_limit_bytes=VMEM_BYTES)


def smem():
    return pl.BlockSpec(memory_space=pltpu.SMEM)


def vmem():
    return pl.BlockSpec(memory_space=pltpu.VMEM)


def aligned(value, unit):
    return pl.multiple_of(value, unit)


def dot(a, b, dims):
    return lax.dot_general(a, b, (dims, ((), ())), preferred_element_type=F32)


def whole_call(body, out_shape, args, name, scratch=(), cost=None):
    single = not isinstance(out_shape, list)
    return pl.pallas_call(
        body,
        out_shape=out_shape,
        in_specs=[smem()] + [vmem()] * (len(args) - 1),
        out_specs=vmem() if single else [vmem()] * len(out_shape),
        scratch_shapes=list(scratch),
        compiler_params=params(),
        cost_estimate=cost,
        name=name,
    )(*args)


def pack_kernel(n_groups, ids, q, k, v, *outs):
    rows = q.shape[0]
    gw = q.shape[1] // n_groups
    for s in range(n_groups):
        cols = pl.ds(aligned(lax.rem(ids[0] + s, n_groups) * gw, HD), gw)
        for i, source in enumerate((q, k, v)):
            outs[s][i * rows : (i + 1) * rows, :] = source[:, cols]


def pack(ids, q, k, v, n_groups):
    rows, width = q.shape
    shape = jax.ShapeDtypeStruct((3 * rows, width // n_groups), BF16)
    return whole_call(
        functools.partial(pack_kernel, n_groups), [shape] * n_groups, (ids, q, k, v), "pack"
    )


def cut_kernel(n_groups, ids, w, *outs):
    gw = w.shape[1] // n_groups
    for s in range(n_groups):
        outs[s][...] = w[:, pl.ds(aligned(lax.rem(ids[0] + s, n_groups) * gw, HD), gw)]


def cut(ids, w, n_groups):
    depth, width = w.shape
    shape = jax.ShapeDtypeStruct((depth, width // n_groups), BF16)
    return whole_call(functools.partial(cut_kernel, n_groups), [shape] * n_groups, (ids, w), "cut")


def split_kernel(n_groups, ids, *refs):
    pieces, (q_out, kv_out) = refs[:n_groups], refs[n_groups:]
    rows = pieces[0].shape[0] // 3
    half = n_groups * rows
    for s in range(n_groups):
        src = lax.rem(ids[0] - s + n_groups, n_groups)
        q_out[pl.ds(aligned(src * rows, 16), rows), :] = pieces[s][:rows, :]
        kv_out[s * rows : (s + 1) * rows, :] = pieces[s][rows : 2 * rows, :]
        kv_out[half + s * rows : half + (s + 1) * rows, :] = pieces[s][2 * rows :, :]


def split(ids, pieces, n_groups):
    rows, gw = pieces[0].shape[0] // 3, pieces[0].shape[1]
    shapes = [
        jax.ShapeDtypeStruct((n_groups * rows, gw), BF16),
        jax.ShapeDtypeStruct((2 * n_groups * rows, gw), BF16),
    ]
    return whole_call(functools.partial(split_kernel, n_groups), shapes, (ids, *pieces), "split")


def stack_kernel(ids, *refs):
    pieces, out = refs[:-1], refs[-1]
    rows = pieces[0].shape[0]
    for s, piece in enumerate(pieces):
        out[s * rows : (s + 1) * rows, :] = piece[...]


def stack(ids, pieces):
    rows, gw = pieces[0].shape
    shape = jax.ShapeDtypeStruct((rows * len(pieces), gw), BF16)
    return whole_call(stack_kernel, shape, (ids, *pieces), "stack")


def forward_kernel(chunk, scale, q_in, *refs):
    blocks, (p_out, o_out, il_out, logits) = refs[:-4], refs[-4:]
    part = blocks[0].shape[0] // 2
    q = q_in[...]
    top = None
    for j, kv in enumerate(blocks):
        for c in range(0, part, chunk):
            at = j * part + c
            block = dot(kv[c : c + chunk, :], q, ((1,), (1,)))
            logits[at : at + chunk, :] = block
            here = jnp.max(block, axis=0, keepdims=True)
            top = here if top is None else jnp.maximum(top, here)
    top = top * scale
    total = jnp.zeros_like(top)
    out = jnp.zeros((HD, q.shape[0]), F32)
    for j, kv in enumerate(blocks):
        for c in range(0, part, chunk):
            at = j * part + c
            prob = jnp.exp2(logits[at : at + chunk, :] * scale - top)
            total = total + jnp.sum(prob, axis=0, keepdims=True)
            low = prob.astype(BF16)
            p_out[0, at : at + chunk, :] = low
            out = out + dot(kv[part + c : part + c + chunk, :], low, ((0,), (0,)))
    inverse = 1.0 / total
    il_out[0] = inverse
    o_out[...] = (out * inverse).T.astype(BF16)


def forward(q, blocks):
    n_q, gw = q.shape
    heads = gw // HD
    part = blocks[0].shape[0] // 2
    seq_len = part * len(blocks)
    chunk = part if part <= 640 else math.gcd(part, 512)
    scale = math.log2(math.e) / math.sqrt(HD)
    return pl.pallas_call(
        functools.partial(forward_kernel, chunk, scale),
        grid=(heads,),
        out_shape=[
            jax.ShapeDtypeStruct((heads, seq_len, n_q), BF16),
            jax.ShapeDtypeStruct((n_q, gw), BF16),
            jax.ShapeDtypeStruct((heads, 1, n_q), F32),
        ],
        in_specs=[pl.BlockSpec((n_q, HD), lambda h: (0, h))]
        + [pl.BlockSpec((2 * part, HD), lambda h: (0, h))] * len(blocks),
        out_specs=[
            pl.BlockSpec((1, seq_len, n_q), lambda h: (h, 0, 0)),
            pl.BlockSpec((n_q, HD), lambda h: (0, h)),
            pl.BlockSpec((1, 1, n_q), lambda h: (h, 0, 0)),
        ],
        scratch_shapes=[pltpu.VMEM((seq_len, n_q), F32)],
        compiler_params=params(),
        cost_estimate=pl.CostEstimate(
            flops=4 * heads * seq_len * n_q * HD,
            bytes_accessed=2 * heads * seq_len * n_q,
            transcendentals=heads * seq_len * n_q,
        ),
        name="forward",
    )(q, *blocks)


def backward_kernel(n_groups, chunk, factor, ids, *refs):
    q_in, p_in, o_in, il_in, da_in = refs[:5]
    dq_outs, halves, dq_all = refs[-n_groups - 3 : -3], refs[-3:-1], refs[-1]
    blocks = refs[5 : -n_groups - 3]
    part = blocks[0].shape[0] // 2
    rows = dq_outs[0].shape[0]
    q = q_in[...]
    n_q = q.shape[0]
    inverse = jnp.broadcast_to(il_in[0], (HD, n_q)).T
    da = (da_in[...].astype(F32) * inverse).astype(BF16)
    delta = jnp.sum((da.astype(F32) * o_in[...].astype(F32)).T, axis=0, keepdims=True)
    dq = jnp.zeros((HD, n_q), F32)
    per_half = max(1, len(blocks) // 2)
    for j, kv in enumerate(blocks):
        out = halves[j // per_half]
        base = j % per_half * 2 * part
        for c in range(0, part, chunk):
            at = j * part + c
            low = p_in[0, at : at + chunk, :]
            dp = dot(kv[part + c : part + c + chunk, :], da, ((1,), (1,)))
            ds = (low.astype(F32) * (dp - delta)).astype(BF16)
            dk = (factor * dot(ds, q, ((1,), (0,)))).astype(BF16)
            out[base + c : base + c + chunk, :] = dk
            dv = dot(low, da, ((1,), (0,))).astype(BF16)
            out[base + part + c : base + part + c + chunk, :] = dv
            dq = dq + dot(kv[c : c + chunk, :], ds, ((0,), (0,)))
    dq_all[...] = (factor * dq).T.astype(BF16)
    for s in range(n_groups):
        src = lax.rem(ids[0] - s + n_groups, n_groups)
        dq_outs[s][...] = dq_all[pl.ds(aligned(src * rows, 16), rows), :]


def backward(ids, head, q, blocks, probs, out, inverse, grad_attn, n_groups):
    n_q = q.shape[0]
    rows = n_q // n_groups
    part = blocks[0].shape[0] // 2
    seq_len = part * len(blocks)
    chunk = part if part <= 640 else math.gcd(part, 512)
    per_half = max(1, len(blocks) // 2)
    column = pl.BlockSpec((n_q, HD), lambda i: (0, head))
    results = pl.pallas_call(
        functools.partial(backward_kernel, n_groups, chunk, 1.0 / math.sqrt(HD)),
        grid=(1,),
        out_shape=[jax.ShapeDtypeStruct((rows, HD), BF16)] * n_groups
        + [jax.ShapeDtypeStruct((per_half * 2 * part, HD), BF16)] * 2,
        in_specs=[
            smem(),
            column,
            pl.BlockSpec((1, seq_len, n_q), lambda i: (head, 0, 0)),
            column,
            pl.BlockSpec((1, 1, n_q), lambda i: (head, 0, 0)),
            column,
        ]
        + [pl.BlockSpec((2 * part, HD), lambda i: (0, head))] * len(blocks),
        out_specs=[vmem()] * (n_groups + 2),
        scratch_shapes=[pltpu.VMEM((n_q, HD), BF16)],
        compiler_params=params(),
        cost_estimate=pl.CostEstimate(
            flops=8 * seq_len * n_q * HD,
            bytes_accessed=2 * seq_len * n_q,
            transcendentals=0,
        ),
        name="backward",
    )(ids, q, probs, out, inverse, grad_attn, *blocks)
    return results[:n_groups], results[n_groups:]


def frame_block(ids, sign, s, position, n_groups, n_tok):
    group = lax.rem(ids[0] + sign * s + n_groups, n_groups)
    return group * n_tok + jnp.bitwise_xor(ids[1], relative_of(position, bits_of(n_tok)))


def column_starts(ids, grads, n_space):
    part = sum(g.shape[1] for g in grads[0])
    for r in range(n_space):
        start = jnp.bitwise_xor(ids[2], relative_of(r, bits_of(n_space))) * part
        for grad in grads[r]:
            yield grad, aligned(start, 16)
            start = start + grad.shape[1]


def by_space(refs, n_space):
    count = len(refs) // n_space
    return [refs[r * count : (r + 1) * count] for r in range(n_space)]


def attn_kernel(n_groups, n_tok, n_space, ids, *refs):
    weights, (out, weight) = refs[:n_tok], refs[-2:]
    grads = by_space(refs[n_tok:-2], n_space)
    depth = weights[0].shape[0] // n_groups
    for j in range(n_tok):
        for s in range(n_groups):
            place = frame_block(ids, -1, s, j, n_groups, n_tok) * depth
            weight[pl.ds(aligned(place, 16), depth), :] = weights[j][s * depth : (s + 1) * depth, :]
    total = None
    for grad, start in column_starts(ids, grads, n_space):
        term = dot(grad[...], weight[pl.ds(start, grad.shape[1]), :], ((1,), (0,)))
        total = term if total is None else total + term
    out[...] = total.astype(BF16)


def projection_cost(n_q, depth, gw):
    return pl.CostEstimate(
        flops=2 * n_q * depth * gw,
        bytes_accessed=2 * (n_q * depth + depth * gw + n_q * gw),
        transcendentals=0,
    )


def attn_gradient(ids, grads, weights, n_groups, n_tok, n_space):
    n_q = grads[0][0].shape[0]
    depth, gw = n_tok * weights[0].shape[0], weights[0].shape[1]
    return whole_call(
        functools.partial(attn_kernel, n_groups, n_tok, n_space),
        jax.ShapeDtypeStruct((n_q, gw), BF16),
        (ids, *weights, *[g for part in grads for g in part]),
        "attn_gradient",
        [pltpu.VMEM((depth, gw), BF16)],
        projection_cost(n_q, depth, gw),
    )


def proj_kernel(n_groups, n_tok, n_space, ids, *refs):
    attn, halves, whole = refs[0], refs[-3:-1], refs[-1]
    grads = by_space(refs[1:-3], n_space)
    for grad, start in column_starts(ids, grads, n_space):
        term = dot(grad[...], attn[...], ((0,), (0,)))
        whole[pl.ds(start, grad.shape[1]), :] = term.astype(BF16)
    depth = whole.shape[0] // (n_groups * n_tok)
    per_half = max(1, n_tok // 2)
    for j in range(n_tok):
        for s in range(n_groups):
            place = frame_block(ids, 1, s, j, n_groups, n_tok) * depth
            at = (j % per_half * n_groups + s) * depth
            halves[j // per_half][at : at + depth, :] = whole[pl.ds(aligned(place, 16), depth), :]


def proj_gradient(ids, grads, attn, n_groups, n_tok, n_space):
    n_q, gw = attn.shape
    depth = n_space * sum(g.shape[1] for g in grads[0])
    half = depth // n_tok * max(1, n_tok // 2)
    return whole_call(
        functools.partial(proj_kernel, n_groups, n_tok, n_space),
        [jax.ShapeDtypeStruct((half, gw), BF16)] * 2,
        (ids, attn, *[g for part in grads for g in part]),
        "proj_gradient",
        [pltpu.VMEM((depth, gw), BF16)],
        projection_cost(n_q, depth, gw),
    )


def add_kernel(ids, kept, other, *outs):
    rows = outs[0].shape[0]
    for i, out in enumerate(outs):
        total = kept[i * rows : (i + 1) * rows, :].astype(F32)
        total = total + other[i * rows : (i + 1) * rows, :].astype(F32)
        out[...] = total.astype(BF16)


def add_parts(ids, kept, other, count):
    rows, gw = kept.shape
    shape = jax.ShapeDtypeStruct((rows // count, gw), BF16)
    return whole_call(add_kernel, [shape] * count, (ids, kept, other), "add_parts")


def reduce_halves(ids, kept, sent, n_frame, bits):
    for place, bit in enumerate(bits):
        other = lax.ppermute(sent, "frame", xor_pairs(n_frame, bit))
        if place == len(bits) - 1:
            return kept, other
        kept, sent = add_parts(ids, kept, other, 2)


def finish_kernel(n_groups, ids, kept, other, *refs):
    dq, outs = refs[:n_groups], refs[n_groups:]
    rows = dq[0].shape[0]
    for s in range(n_groups):
        outs[s][:rows, :] = dq[s][...]
        for i in range(2):
            at = (i * n_groups + s) * rows
            total = kept[at : at + rows, :].astype(F32) + other[at : at + rows, :].astype(F32)
            outs[s][(i + 1) * rows : (i + 2) * rows, :] = total.astype(BF16)


def finish(ids, kept, other, dq, n_groups):
    rows = dq[0].shape[0]
    return whole_call(
        functools.partial(finish_kernel, n_groups),
        [jax.ShapeDtypeStruct((3 * rows, HD), BF16)] * n_groups,
        (ids, kept, other, *dq),
        "finish",
    )


def unpack_kernel(n_groups, heads, ids, *refs):
    rows = refs[-1].shape[0]
    for h in range(heads):
        for s in range(n_groups):
            start = (lax.rem(ids[0] + s, n_groups) * heads + h) * HD
            for i, out in enumerate(refs[-3:]):
                piece = refs[h * n_groups + s][i * rows : (i + 1) * rows, :]
                out[:, pl.ds(aligned(start, HD), HD)] = piece


def unpack(ids, pieces, n_groups):
    heads = len(pieces)
    rows = pieces[0][0].shape[0] // 3
    shape = jax.ShapeDtypeStruct((rows, HD * heads * n_groups), BF16)
    return whole_call(
        functools.partial(unpack_kernel, n_groups, heads),
        [shape] * 3,
        (ids, *[p for per_head in pieces for p in per_head]),
        "unpack",
    )


def join_kernel(n_groups, ids, *refs):
    pieces, out = refs[:n_groups], refs[n_groups]
    gw = pieces[0].shape[1]
    for s in range(n_groups):
        start = lax.rem(ids[0] - s + n_groups, n_groups) * gw
        out[:, pl.ds(aligned(start, HD), gw)] = pieces[s][...].astype(F32)


def join(ids, pieces, n_groups):
    rows, gw = pieces[0].shape
    return whole_call(
        functools.partial(join_kernel, n_groups),
        jax.ShapeDtypeStruct((rows, gw * n_groups), F32),
        (ids, *pieces),
        "join",
    )


def exchange(pieces, n_groups, n_tok, sign):
    return [pieces[0]] + [
        lax.ppermute(pieces[s], "frame", shift_pairs(n_groups, n_tok, sign * s))
        for s in range(1, n_groups)
    ]


def local(queries, keys, values, grad_out, proj_weight):
    n_frame = lax.axis_size("frame")
    n_space = lax.axis_size("space")
    width = queries.shape[1]
    n_groups = math.gcd(width // HD, n_frame)
    n_tok = n_frame // n_groups
    tok_bits = bits_of(n_tok)
    heads = width // n_groups // HD
    frame = lax.axis_index("frame")
    ids = jnp.stack([frame // n_tok, frame % n_tok, lax.axis_index("space")]).astype(jnp.int32)

    pieces = exchange(pack(ids, queries, keys, values, n_groups), n_groups, n_tok, 1)
    q, kv = split(ids, pieces, n_groups)
    kv = gather_blocks(kv, "frame", n_frame, tok_bits)
    weight = exchange(cut(ids, proj_weight.T, n_groups), n_groups, n_tok, 1)
    weights = gather_blocks(stack(ids, weight), "frame", n_frame, tok_bits)

    n_chunk = math.gcd(grad_out.shape[1] // HD, GRAD_CHUNKS)
    chunk_cols = grad_out.shape[1] // n_chunk
    lines = [[g * n_tok + t for g in range(n_groups)] for t in range(n_tok)]
    grads = [[] for _ in range(n_space)]
    for c in range(n_chunk):
        own = grad_out[:, c * chunk_cols : (c + 1) * chunk_cols]
        if n_groups > 1:
            own = lax.all_gather(own, "frame", axis=0, tiled=True, axis_index_groups=lines)
        gathered = gather_blocks(own, "space", n_space, bits_of(n_space))
        for r in range(n_space):
            grads[r].append(gathered[r])

    probs, out, inverse = forward(q, kv)
    kept, sent = proj_gradient(ids, grads, out, n_groups, n_tok, n_space)
    grad_attn = attn_gradient(ids, grads, weights, n_groups, n_tok, n_space)
    grad_attn, kept, sent = lax.optimization_barrier((grad_attn, kept, sent))
    proj = reduce_halves(ids, kept, sent, n_frame, tok_bits)
    proj = exchange(add_parts(ids, *proj, n_groups), n_groups, n_tok, 1)
    grad_proj = join(ids, proj, n_groups).T

    returned = []
    for h in range(heads):
        dq, halves = backward(ids, h, q, kv, probs, out, inverse, grad_attn, n_groups)
        kept, other = reduce_halves(ids, *halves, n_frame, tok_bits)
        returned.append(exchange(finish(ids, kept, other, dq, n_groups), n_groups, n_tok, -1))
    grad_queries, grad_keys, grad_values = unpack(ids, returned, n_groups)
    return (grad_queries, grad_keys, grad_values, grad_proj)


def solution(mesh):
    in_specs = (
        P("frame", "space"),
        P("frame", "space"),
        P("frame", "space"),
        P("frame", "space"),
        P("space", "frame"),
    )
    out_specs = (P("frame", "space"), P("frame", "space"), P("frame", "space"), P("space", "frame"))
    return jax.shard_map(local, mesh=mesh, in_specs=in_specs, out_specs=out_specs, check_vma=False)
```

time: 256 us -> 235 us (0.918)
  blocking collectives: 0 us -> 44.1 us
  starting transfers between devices: 71.3 us -> 40 us
  local copies, waits for them, and re-layouts: 21.5 us -> 3.19 us
  between operations: 14.2 us -> 0.87 us
  waiting for transfers between devices: 104 us -> 99.6 us
  Pallas kernels: 42.8 us -> 46.4 us
    all_gather x0 -> x2, blocking collectives: none -> 44.1 us  [local(): lax.all_gather(own, 'frame', axis=0, tiled=True, axis_index_groups=lines)]
    ppermute x18, starting transfers between devices: 64.6 us -> 28.5 us  [exchange(): lax.ppermute(pieces[s], 'frame', shift_pairs(n_groups, n_tok, sign * s))]
    unnamed x26 -> x10, local copies, waits for them, and re-layouts: 10.7 us -> 3.16 us
    concatenate x4 -> x0, local copies, waits for them, and re-layouts: 7.33 us -> none  [gather_bits(): block = jnp.concatenate([block, other], axis=0)]
    ppermute x18, waiting for transfers between devices: 57.3 us -> 51.1 us  [exchange(): lax.ppermute(pieces[s], 'frame', shift_pairs(n_groups, n_tok, sign * s))]
    ppermute x9 -> x16, starting transfers between devices: 6.63 us -> 11.5 us  [the longest x8 5.97 us: gather_blocks(): lax.ppermute(b, axis, xor_pairs(count, bit))]
    slice x6 -> x1, local copies, waits for them, and re-layouts: 3.46 us -> 0.03 us  [local(): own = grad_out[:, c * chunk_cols:(c + 1) * chunk_cols]]
    ppermute x9 -> x16, waiting for transfers between devices: 45.9 us -> 48.5 us  [the longest x8 26.9 us: reduce_halves(): other = lax.ppermute(sent, 'frame', xor_pairs(n_frame, bit))]
  transfers between devices with their start and end apart: 28 -> 34, of which waited for: 11 -> 10; matrix products, arithmetic and copies ran while one was open for 7% -> 0% of each run, Pallas kernels for 8% -> 13%
where the time goes in v2:
time: 235 us; the launch traced here: 234 us
  waiting for transfers between devices  99.6 us (42%)
  Pallas kernels  46.4 us (20%)
  blocking collectives  44.1 us (19%)
  starting transfers between devices  40 us (17%)
  local copies, waits for them, and re-layouts  3.19 us (1%)
    ppermute x18, waiting for transfers between devices, exchange(): lax.ppermute(pieces[s], 'frame', shift_pairs(n_groups, n_tok, sign * s))  51.1 us
    all_gather x2, blocking collectives, local(): lax.all_gather(own, 'frame', axis=0, tiled=True, axis_index_groups=lines)  44.1 us
    ppermute x18, starting transfers between devices, exchange(): lax.ppermute(pieces[s], 'frame', shift_pairs(n_groups, n_tok, sign * s))  28.5 us
    ppermute x8, waiting for transfers between devices, reduce_halves(): other = lax.ppermute(sent, 'frame', xor_pairs(n_frame, bit))  26.9 us
    ppermute x8, waiting for transfers between devices, gather_blocks(): lax.ppermute(b, axis, xor_pairs(count, bit))  21.7 us
    pallas_call x16, Pallas kernels, whole_call(): pl.pallas_call(body, out_shape=out_shape, in_specs=[smem()] + [vmem()] *...  17.9 us
    pallas_call x3, Pallas kernels, backward(): pl.pallas_call(functools.partial(backward_kernel, n_groups, chunk, 1.0 /...  17.1 us
    pallas_call x1, Pallas kernels, forward(): pl.pallas_call(functools.partial(forward_kernel, chunk, scale), grid=(hea...  11.4 us
  transfers between devices with their start and end apart: 34, of which 10 were waited for; matrix products, arithmetic and copies ran while one was open for 0% of the time, Pallas kernels for 13%

profile of v2, /device:TPU:0, one launch (start us, length us, event | category | flops | bytes accessed | tf_op | source)
XLA Modules:
  0.0 234.2 jit_solution(3456162489008927574)
XLA Ops:
  0.7 0.1 pad_add_fusion.ids
  0.7 1.1 copy-done.1
  1.8 1.0 copy-done.2
  2.9 1.0 copy-done.3
  3.9 0.7 pack.1
  4.6 3.1 %collective-permute-start = (bf16[480,384]{1,0:T(8,128)(2,1)S(1)}, bf16[480,384]{1,0:T(8,128)(2,1)S(1)}, u32[]{:S(2)}, u32[]{:S(2)}) collective-permute-start(bf16[480,384]{1,0:T(8,128)(2,1)S(1)} %get-tuple-element.68), channel_id=1, source_target_pairs={{0,8},{2,10},{4,12},{6,14},{8,16},{10,18},{12,20},{14,22},{16,24},... | collective-permute-start | bytes 1105928 | tf_op jit(solution)/shard_map/ppermute | solution.py:447
  7.7 2.6 %collective-permute-start.1 = (bf16[480,384]{1,0:T(8,128)(2,1)S(1)}, bf16[480,384]{1,0:T(8,128)(2,1)S(1)}, u32[]{:S(2)}, u32[]{:S(2)}) collective-permute-start(bf16[480,384]{1,0:T(8,128)(2,1)S(1)} %get-tuple-element.69), channel_id=1, source_target_pairs={{0,16},{2,18},{4,20},{6,22},{8,24},{10,26},{12,28},{14,30},{16,0},... | collective-permute-start | bytes 1105928 | tf_op jit(solution)/shard_map/ppermute | solution.py:447
  10.3 1.3 collective-permute-start.2
  11.6 0.6 cut.1
  12.2 0.7 collective-permute-start.6
  12.9 0.3 collective-permute-start.7
  13.3 6.0 %collective-permute-done.refs_1_ = bf16[480,384]{1,0:T(8,128)(2,1)S(1)} collective-permute-done((bf16[480,384]{1,0:T(8,128)(2,1)S(1)}, bf16[480,384]{1,0:T(8,128)(2,1)S(1)}, u32[]{:S(2)}, u32[]{:S(2)}) %collective-permute-start) | collective-permute-done | bytes 368672 | tf_op jit(solution)/shard_map/ppermute | solution.py:447
  19.3 2.5 %collective-permute-start.8 = (bf16[192,384]{1,0:T(8,128)(2,1)S(1)}, bf16[192,384]{1,0:T(8,128)(2,1)S(1)}, u32[]{:S(2)}, u32[]{:S(2)}) collective-permute-start(bf16[192,384]{1,0:T(8,128)(2,1)S(1)} %get-tuple-element.79), channel_id=1, source_target_pairs={{0,24},{2,26},{4,28},{6,30},{8,0},{10,2},{12,4},{14,6},{16,8},{18,... | collective-permute-start | bytes 442376 | tf_op jit(solution)/shard_map/ppermute | solution.py:447
  21.7 13.4 %collective-permute-done.1.refs_2_ = bf16[480,384]{1,0:T(8,128)(2,1)S(1)} collective-permute-done((bf16[480,384]{1,0:T(8,128)(2,1)S(1)}, bf16[480,384]{1,0:T(8,128)(2,1)S(1)}, u32[]{:S(2)}, u32[]{:S(2)}) %collective-permute-start.1) | collective-permute-done | bytes 368672 | tf_op jit(solution)/shard_map/ppermute | solution.py:447
  35.1 0.7 split.1
  35.8 1.8 collective-permute-start.3
  37.6 0.6 collective-permute-done.6.refs_1_
  38.3 13.4 %collective-permute-done.7.refs_2_ = bf16[192,384]{1,0:T(8,128)(2,1)S(1)} collective-permute-done((bf16[192,384]{1,0:T(8,128)(2,1)S(1)}, bf16[192,384]{1,0:T(8,128)(2,1)S(1)}, u32[]{:S(2)}, u32[]{:S(2)}) %collective-permute-start.7) | collective-permute-done | bytes 147488 | tf_op jit(solution)/shard_map/ppermute | solution.py:447
  51.6 0.6 stack.17.refs_0_
  52.2 1.6 collective-permute-start.9
  53.8 23.1 %all_gather.6.refs_4_.refs_1_ = bf16[640,768]{1,0:T(8,128)(2,1)S(1)} all-gather(bf16[160,768]{1,0:T(8,128)(2,1)S(1)} %get-tuple-element.131), channel_id=1, replica_groups={{0,8,16,24},{2,10,18,26},{4,12,20,28},{6,14,22,30},{1,9,17,25},{3,11,19..., dimensions={0}, use_global_device_ids=true | all-gather | bytes 1228800 | tf_op jit(solution)/shard_map/all_gather | solution.py:476
  76.9 1.5 collective-permute-start.12
  78.4 21.0 %all_gather.7.refs_5_.refs_2_ = bf16[640,768]{1,0:T(8,128)(2,1)S(1)} all-gather(bf16[160,768]{1,0:T(8,128)(2,1)S(1)} %get-tuple-element.130), channel_id=1, replica_groups={{0,8,16,24},{2,10,18,26},{4,12,20,28},{6,14,22,30},{1,9,17,25},{3,11,19..., dimensions={0}, use_global_device_ids=true | all-gather | bytes 1228800 | tf_op jit(solution)/shard_map/all_gather | solution.py:476
  99.4 0.5 collective-permute-start.13
  99.9 0.5 collective-permute-start.5
  100.4 0.1 collective-permute-start.11
  100.5 21.7 %collective-permute-done.13.refs_7_.refs_4_ = bf16[640,768]{1,0:T(8,128)(2,1)S(1)} collective-permute-done((bf16[640,768]{1,0:T(8,128)(2,1)S(1)}, bf16[640,768]{1,0:T(8,128)(2,1)S(1)}, u32[]{:S(2)}, u32[]{:S(2)}) %collective-permute-start.13) | collective-permute-done | bytes 983072 | tf_op jit(solution)/shard_map/ppermute | solution.py:50
  122.2 3.0 %attn_gradient.1.refs_4_ = bf16[640,384]{1,0:T(8,128)(2,1)S(1)} custom-call(s32[3]{0:T(128)S(1)} %pad_add_fusion.ids, bf16[768,384]{1,0:T(8,128)(2,1)S(1)} %stack.17.refs_0_, bf16[768,384]{1,0:T(8,128)(2,1)S(1)} %collective-permute-done.9.refs_1_, bf16[768,384]{1,0:T(8,128)(2,1)S(1)} %collective-permute-done.10.refs_2_, ...), custom_call_target="tpu_custom_call" | custom-call | flops 1509949440 | bytes 6782976 | tf_op jit(solution)/shard_map/attn_gradient/pallas_call | solution.py:76
  125.1 11.4 %forward.1 = (bf16[3,2560,640]{2,1,0:T(8,128)(2,1)}, bf16[640,384]{1,0:T(8,128)(2,1)S(1)}, f32[3,1,640]{2,1,0:T(1,128)S(1)}) custom-call(bf16[640,384]{1,0:T(8,128)(2,1)S(1)} %get-tuple-element.71.q_in.refs_0_, bf16[1280,384]{1,0:T(8,128)(2,1)S(1)} %get-tuple-element.72.refs_0_.refs_5_, bf16[1280,384]{1,0:T(8,128)(2,1)S(1)} %collective-permute-done.3.refs_1_.refs_6_, ...), custom_call_target="tpu_custom_call" | custom-call | flops 2516582400 | bytes 9830400 | tf_op jit(solution)/shard_map/forward/pallas_call | solution.py:185
  136.5 3.2 %proj_gradient.1 = (bf16[1536,384]{1,0:T(8,128)(2,1)S(1)}, bf16[1536,384]{1,0:T(8,128)(2,1)S(1)}) custom-call(s32[3]{0:T(128)S(1)} %pad_add_fusion.ids, bf16[640,384]{1,0:T(8,128)(2,1)S(1)} %get-tuple-element.74.refs_0_.refs_2_, bf16[640,768]{1,0:T(8,128)(2,1)S(1)} %all_gather.6.refs_4_.refs_1_, bf16[640,768]{1,0:T(8,128)(2,1)S(1)} %all_gather.7.refs_5_.refs_2_, ...), custom_call_target="tpu_custom_call" | custom-call | flops 1509949440 | bytes 6782976 | tf_op jit(solution)/shard_map/proj_gradient/pallas_call | solution.py:76
  139.8 0.1 collective-permute-start.29
  139.8 5.6 %backward.3 = (bf16[160,128]{1,0:T(8,128)(2,1)S(1)}, bf16[160,128]{1,0:T(8,128)(2,1)S(1)}, bf16[160,128]{1,0:T(8,128)(2,1)S(1)}, bf16[160,128]{1,0:T(8,128)(2,1)...) custom-call(s32[3]{0:T(128)S(1)} %pad_add_fusion.ids, ...), custom_call_target="tpu_custom_call" | custom-call | flops 1677721600 | bytes 3276800 | tf_op jit(solution)/shard_map/backward/pallas_call | solution.py:251
  145.5 0.6 collective-permute-start.14
  146.0 5.6 %backward.4 = (bf16[160,128]{1,0:T(8,128)(2,1)S(1)}, bf16[160,128]{1,0:T(8,128)(2,1)S(1)}, bf16[160,128]{1,0:T(8,128)(2,1)S(1)}, bf16[160,128]{1,0:T(8,128)(2,1)...) custom-call(s32[3]{0:T(128)S(1)} %pad_add_fusion.ids, ...), custom_call_target="tpu_custom_call" | custom-call | flops 1677721600 | bytes 3276800 | tf_op jit(solution)/shard_map/backward/pallas_call | solution.py:251
  151.7 0.1 collective-permute-start.19
  151.7 5.9 %backward.5 = (bf16[160,128]{1,0:T(8,128)(2,1)S(1)}, bf16[160,128]{1,0:T(8,128)(2,1)S(1)}, bf16[160,128]{1,0:T(8,128)(2,1)S(1)}, bf16[160,128]{1,0:T(8,128)(2,1)...) custom-call(s32[3]{0:T(128)S(1)} %pad_add_fusion.ids, ...), custom_call_target="tpu_custom_call" | custom-call | flops 1677721600 | bytes 3276800 | tf_op jit(solution)/shard_map/backward/pallas_call | solution.py:251
  157.6 0.6 collective-permute-start.24
  158.2 0.8 add_parts.8
  159.0 0.6 collective-permute-start.30
  159.6 0.7 add_parts.5
  160.3 1.6 collective-permute-start.15
  161.9 0.7 add_parts.6
  162.6 0.6 collective-permute-start.20
  163.2 0.7 add_parts.7
  163.9 1.6 collective-permute-start.25
  165.4 16.9 %collective-permute-done.15.other = bf16[1280,128]{1,0:T(8,128)(2,1)S(1)} collective-permute-done((bf16[1280,128]{1,0:T(8,128)(2,1)S(1)}, bf16[1280,128]{1,0:T(8,128)(2,1)S(1)}, u32[]{:S(2)}, u32[]{:S(2)}) %collective-permute-start.15) | collective-permute-done | bytes 327712 | tf_op jit(solution)/shard_map/ppermute | solution.py:378
  182.3 0.6 finish.3
  182.9 1.8 collective-permute-start.16
  184.8 4.5 %collective-permute-done.20.other = bf16[1280,128]{1,0:T(8,128)(2,1)S(1)} collective-permute-done((bf16[1280,128]{1,0:T(8,128)(2,1)S(1)}, bf16[1280,128]{1,0:T(8,128)(2,1)S(1)}, u32[]{:S(2)}, u32[]{:S(2)}) %collective-permute-start.20) | collective-permute-done | bytes 327712 | tf_op jit(solution)/shard_map/ppermute | solution.py:378
  189.3 0.6 finish.4
  189.9 5.5 %collective-permute-done.25.other = bf16[1280,128]{1,0:T(8,128)(2,1)S(1)} collective-permute-done((bf16[1280,128]{1,0:T(8,128)(2,1)S(1)}, bf16[1280,128]{1,0:T(8,128)(2,1)S(1)}, u32[]{:S(2)}, u32[]{:S(2)}) %collective-permute-start.25) | collective-permute-done | bytes 327712 | tf_op jit(solution)/shard_map/ppermute | solution.py:378
  195.4 1.8 collective-permute-start.21
  197.2 0.6 finish.5
  197.8 1.5 collective-permute-start.23
  199.3 2.4 %collective-permute-start.26 = (bf16[480,128]{1,0:T(8,128)(2,1)S(1)}, bf16[480,128]{1,0:T(8,128)(2,1)S(1)}, u32[]{:S(2)}, u32[]{:S(2)}) collective-permute-start(bf16[480,128]{1,0:T(8,128)(2,1)S(1)} %get-tuple-element.116), channel_id=1, source_target_pairs={{0,24},{2,26},{4,28},{6,30},{8,0},{10,2},{12,4},{14,6},{16,8},{18,... | collective-permute-start | bytes 368648 | tf_op jit(solution)/shard_map/ppermute | solution.py:447
  201.7 0.7 add_parts.9
  202.5 1.3 collective-permute-start.32
  203.8 5.9 %collective-permute-done.22.refs_6_ = bf16[480,128]{1,0:T(8,128)(2,1)S(1)} collective-permute-done((bf16[480,128]{1,0:T(8,128)(2,1)S(1)}, bf16[480,128]{1,0:T(8,128)(2,1)S(1)}, u32[]{:S(2)}, u32[]{:S(2)}) %collective-permute-start.22) | collective-permute-done | bytes 122912 | tf_op jit(solution)/shard_map/ppermute | solution.py:447
  209.7 0.5 collective-permute-start.33
  210.1 4.5 %collective-permute-start.27 = (bf16[480,128]{1,0:T(8,128)(2,1)S(1)}, bf16[480,128]{1,0:T(8,128)(2,1)S(1)}, u32[]{:S(2)}, u32[]{:S(2)}) collective-permute-start(bf16[480,128]{1,0:T(8,128)(2,1)S(1)} %get-tuple-element.117), channel_id=1, source_target_pairs={{0,16},{2,18},{4,20},{6,22},{8,24},{10,26},{12,28},{14,30},{16,0},... | collective-permute-start | bytes 368648 | tf_op jit(solution)/shard_map/ppermute | solution.py:447
  214.6 4.1 %collective-permute-start.28 = (bf16[480,128]{1,0:T(8,128)(2,1)S(1)}, bf16[480,128]{1,0:T(8,128)(2,1)S(1)}, u32[]{:S(2)}, u32[]{:S(2)}) collective-permute-start(bf16[480,128]{1,0:T(8,128)(2,1)S(1)} %get-tuple-element.118), channel_id=1, source_target_pairs={{0,8},{2,10},{4,12},{6,14},{8,16},{10,18},{12,20},{14,22},{16,24},... | collective-permute-start | bytes 368648 | tf_op jit(solution)/shard_map/ppermute | solution.py:447
  218.7 11.9 %collective-permute-done.27.refs_10_ = bf16[480,128]{1,0:T(8,128)(2,1)S(1)} collective-permute-done((bf16[480,128]{1,0:T(8,128)(2,1)S(1)}, bf16[480,128]{1,0:T(8,128)(2,1)S(1)}, u32[]{:S(2)}, u32[]{:S(2)}) %collective-permute-start.27) | collective-permute-done | bytes 122912 | tf_op jit(solution)/shard_map/ppermute | solution.py:447
  230.5 2.0 unpack.1
  232.6 1.7 join.1
  (38 shorter events, 0.2 us)
Async XLA Ops:
  0.6 11.0 %copy-start = (bf16[1536,192]{0,1:T(8,128)(2,1)S(1)}, bf16[1536,192]{0,1:T(8,128)(2,1)}, u32[]{:S(2)}) copy-start(bf16[1536,192]{0,1:T(8,128)(2,1)} %param.9) | copy-start | bytes 1769476
  0.7 1.1 copy-start.1
  1.8 1.0 copy-start.2
  2.9 1.0 copy-start.3
  4.6 33.0 %copy-start.4 = (bf16[160,1536]{1,0:T(8,128)(2,1)S(1)}, bf16[160,1536]{1,0:T(8,128)(2,1)}, u32[]{:S(2)}) copy-start(bf16[160,1536]{1,0:T(8,128)(2,1)} %param.8) | copy-start | bytes 1474564
  4.6 14.7 %collective-permute-start = (bf16[480,384]{1,0:T(8,128)(2,1)S(1)}, bf16[480,384]{1,0:T(8,128)(2,1)S(1)}, u32[]{:S(2)}, u32[]{:S(2)}) collective-permute-start(bf16[480,384]{1,0:T(8,128)(2,1)S(1)} %get-tuple-element.68), channel_id=1, source_target_pairs={{0,8},{2,10},{4,12},{6,14},{8,16},{10,18},{12,20},{14,22},{16,24},... | collective-permute-start | bytes 1105928 | tf_op jit(solution)/shard_map/ppermute | solution.py:447
  7.7 27.4 %collective-permute-start.1 = (bf16[480,384]{1,0:T(8,128)(2,1)S(1)}, bf16[480,384]{1,0:T(8,128)(2,1)S(1)}, u32[]{:S(2)}, u32[]{:S(2)}) collective-permute-start(bf16[480,384]{1,0:T(8,128)(2,1)S(1)} %get-tuple-element.69), channel_id=1, source_target_pairs={{0,16},{2,18},{4,20},{6,22},{8,24},{10,26},{12,28},{14,30},{16,0},... | collective-permute-start | bytes 1105928 | tf_op jit(solution)/shard_map/ppermute | solution.py:447
  10.3 24.8 %collective-permute-start.2 = (bf16[480,384]{1,0:T(8,128)(2,1)S(1)}, bf16[480,384]{1,0:T(8,128)(2,1)S(1)}, u32[]{:S(2)}, u32[]{:S(2)}) collective-permute-start(bf16[480,384]{1,0:T(8,128)(2,1)S(1)} %get-tuple-element.70), channel_id=1, source_target_pairs={{0,24},{2,26},{4,28},{6,30},{8,0},{10,2},{12,4},{14,6},{16,8},{18,... | collective-permute-start | bytes 1105928 | tf_op jit(solution)/shard_map/ppermute | solution.py:447
  12.2 26.0 %collective-permute-start.6 = (bf16[192,384]{1,0:T(8,128)(2,1)S(1)}, bf16[192,384]{1,0:T(8,128)(2,1)S(1)}, u32[]{:S(2)}, u32[]{:S(2)}) collective-permute-start(bf16[192,384]{1,0:T(8,128)(2,1)S(1)} %get-tuple-element.77), channel_id=1, source_target_pairs={{0,8},{2,10},{4,12},{6,14},{8,16},{10,18},{12,20},{14,22},{16,24},... | collective-permute-start | bytes 442376 | tf_op jit(solution)/shard_map/ppermute | solution.py:447
  12.9 38.7 %collective-permute-start.7 = (bf16[192,384]{1,0:T(8,128)(2,1)S(1)}, bf16[192,384]{1,0:T(8,128)(2,1)S(1)}, u32[]{:S(2)}, u32[]{:S(2)}) collective-permute-start(bf16[192,384]{1,0:T(8,128)(2,1)S(1)} %get-tuple-element.78), channel_id=1, source_target_pairs={{0,16},{2,18},{4,20},{6,22},{8,24},{10,26},{12,28},{14,30},{16,0},... | collective-permute-start | bytes 442376 | tf_op jit(solution)/shard_map/ppermute | solution.py:447
  19.3 32.4 %collective-permute-start.8 = (bf16[192,384]{1,0:T(8,128)(2,1)S(1)}, bf16[192,384]{1,0:T(8,128)(2,1)S(1)}, u32[]{:S(2)}, u32[]{:S(2)}) collective-permute-start(bf16[192,384]{1,0:T(8,128)(2,1)S(1)} %get-tuple-element.79), channel_id=1, source_target_pairs={{0,24},{2,26},{4,28},{6,30},{8,0},{10,2},{12,4},{14,6},{16,8},{18,... | collective-permute-start | bytes 442376 | tf_op jit(solution)/shard_map/ppermute | solution.py:447
  35.8 64.1 %collective-permute-start.3 = (bf16[1280,384]{1,0:T(8,128)(2,1)S(1)}, bf16[1280,384]{1,0:T(8,128)(2,1)S(1)}, u32[]{:S(2)}, u32[]{:S(2)}) collective-permute-start(bf16[1280,384]{1,0:T(8,128)(2,1)S(1)} %get-tuple-element.72.refs_0_.refs_5_), channel_id=1, source_target_pairs={{0,4},{2,6},{4,0},{6,2},{8,12},{10,14},{12,8},{14,10},{16,20},{18,... | collective-permute-start | bytes 2949128 | tf_op jit(solution)/shard_map/ppermute | solution.py:50
  52.2 47.7 %collective-permute-start.9 = (bf16[768,384]{1,0:T(8,128)(2,1)S(1)}, bf16[768,384]{1,0:T(8,128)(2,1)S(1)}, u32[]{:S(2)}, u32[]{:S(2)}) collective-permute-start(bf16[768,384]{1,0:T(8,128)(2,1)S(1)} %stack.17.refs_0_), channel_id=1, source_target_pairs={{0,4},{2,6},{4,0},{6,2},{8,12},{10,14},{12,8},{14,10},{16,20},{18,... | collective-permute-start | bytes 1769480 | tf_op jit(solution)/shard_map/ppermute | solution.py:50
  76.9 23.6 %collective-permute-start.12 = (bf16[640,768]{1,0:T(8,128)(2,1)S(1)}, bf16[640,768]{1,0:T(8,128)(2,1)S(1)}, u32[]{:S(2)}, u32[]{:S(2)}) collective-permute-start(bf16[640,768]{1,0:T(8,128)(2,1)S(1)} %all_gather.6.refs_4_.refs_1_), channel_id=1, source_target_pairs={{0,1},{1,0},{2,3},{3,2},{4,5},{5,4},{6,7},{7,6},{8,9},{9,8},{10,11... | collective-permute-start | bytes 2949128 | tf_op jit(solution)/shard_map/ppermute | solution.py:50
  78.4 22.0 %collective-permute-start.10 = (bf16[768,384]{1,0:T(8,128)(2,1)S(1)}, bf16[768,384]{1,0:T(8,128)(2,1)S(1)}, u32[]{:S(2)}, u32[]{:S(2)}) collective-permute-start(bf16[768,384]{1,0:T(8,128)(2,1)S(1)} %stack.17.refs_0_), channel_id=1, source_target_pairs={{0,2},{2,0},{4,6},{6,4},{8,10},{10,8},{12,14},{14,12},{16,18},{18,... | collective-permute-start | bytes 1769480 | tf_op jit(solution)/shard_map/ppermute | solution.py:50
  99.4 22.8 %collective-permute-start.13 = (bf16[640,768]{1,0:T(8,128)(2,1)S(1)}, bf16[640,768]{1,0:T(8,128)(2,1)S(1)}, u32[]{:S(2)}, u32[]{:S(2)}) collective-permute-start(bf16[640,768]{1,0:T(8,128)(2,1)S(1)} %all_gather.7.refs_5_.refs_2_), channel_id=1, source_target_pairs={{0,1},{1,0},{2,3},{3,2},{4,5},{5,4},{6,7},{7,6},{8,9},{9,8},{10,11... | collective-permute-start | bytes 2949128 | tf_op jit(solution)/shard_map/ppermute | solution.py:50
  99.9 25.2 %collective-permute-start.4 = (bf16[1280,384]{1,0:T(8,128)(2,1)S(1)}, bf16[1280,384]{1,0:T(8,128)(2,1)S(1)}, u32[]{:S(2)}, u32[]{:S(2)}) collective-permute-start(bf16[1280,384]{1,0:T(8,128)(2,1)S(1)} %get-tuple-element.72.refs_0_.refs_5_), channel_id=1, source_target_pairs={{0,2},{2,0},{4,6},{6,4},{8,10},{10,8},{12,14},{14,12},{16,18},{18,... | collective-permute-start | bytes 2949128 | tf_op jit(solution)/shard_map/ppermute | solution.py:50
  99.9 25.2 %collective-permute-start.5 = (bf16[1280,384]{1,0:T(8,128)(2,1)S(1)}, bf16[1280,384]{1,0:T(8,128)(2,1)S(1)}, u32[]{:S(2)}, u32[]{:S(2)}) collective-permute-start(bf16[1280,384]{1,0:T(8,128)(2,1)S(1)} %collective-permute-done.3.refs_1_.refs_6_), channel_id=1, source_target_pairs={{0,2},{2,0},{4,6},{6,4},{8,10},{10,8},{12,14},{14,12},{16,18},{18,... | collective-permute-start | bytes 2949128 | tf_op jit(solution)/shard_map/ppermute | solution.py:50
  100.4 21.7 %collective-permute-start.11 = (bf16[768,384]{1,0:T(8,128)(2,1)S(1)}, bf16[768,384]{1,0:T(8,128)(2,1)S(1)}, u32[]{:S(2)}, u32[]{:S(2)}) collective-permute-start(bf16[768,384]{1,0:T(8,128)(2,1)S(1)} %collective-permute-done.9.refs_1_), channel_id=1, source_target_pairs={{0,2},{2,0},{4,6},{6,4},{8,10},{10,8},{12,14},{14,12},{16,18},{18,... | collective-permute-start | bytes 1769480 | tf_op jit(solution)/shard_map/ppermute | solution.py:50
  139.8 18.4 %collective-permute-start.29 = (bf16[1536,384]{1,0:T(8,128)(2,1)S(1)}, bf16[1536,384]{1,0:T(8,128)(2,1)S(1)}, u32[]{:S(2)}, u32[]{:S(2)}) collective-permute-start(bf16[1536,384]{1,0:T(8,128)(2,1)S(1)} %get-tuple-element.123), channel_id=1, source_target_pairs={{0,2},{2,0},{4,6},{6,4},{8,10},{10,8},{12,14},{14,12},{16,18},{18,... | collective-permute-start | bytes 3538952 | tf_op jit(solution)/shard_map/ppermute | solution.py:378
  145.5 14.1 %collective-permute-start.14 = (bf16[2560,128]{1,0:T(8,128)(2,1)S(1)}, bf16[2560,128]{1,0:T(8,128)(2,1)S(1)}, u32[]{:S(2)}, u32[]{:S(2)}) collective-permute-start(bf16[2560,128]{1,0:T(8,128)(2,1)S(1)} %get-tuple-element.84), channel_id=1, source_target_pairs={{0,2},{2,0},{4,6},{6,4},{8,10},{10,8},{12,14},{14,12},{16,18},{18,... | collective-permute-start | bytes 1966088 | tf_op jit(solution)/shard_map/ppermute | solution.py:378
  151.7 10.2 %collective-permute-start.19 = (bf16[2560,128]{1,0:T(8,128)(2,1)S(1)}, bf16[2560,128]{1,0:T(8,128)(2,1)S(1)}, u32[]{:S(2)}, u32[]{:S(2)}) collective-permute-start(bf16[2560,128]{1,0:T(8,128)(2,1)S(1)} %get-tuple-element.96), channel_id=1, source_target_pairs={{0,2},{2,0},{4,6},{6,4},{8,10},{10,8},{12,14},{14,12},{16,18},{18,... | collective-permute-start | bytes 1966088 | tf_op jit(solution)/shard_map/ppermute | solution.py:378
  157.6 5.5 %collective-permute-start.24 = (bf16[2560,128]{1,0:T(8,128)(2,1)S(1)}, bf16[2560,128]{1,0:T(8,128)(2,1)S(1)}, u32[]{:S(2)}, u32[]{:S(2)}) collective-permute-start(bf16[2560,128]{1,0:T(8,128)(2,1)S(1)} %get-tuple-element.108), channel_id=1, source_target_pairs={{0,2},{2,0},{4,6},{6,4},{8,10},{10,8},{12,14},{14,12},{16,18},{18,... | collective-permute-start | bytes 1966088 | tf_op jit(solution)/shard_map/ppermute | solution.py:378
  159.0 40.3 %collective-permute-start.30 = (bf16[768,384]{1,0:T(8,128)(2,1)S(1)}, bf16[768,384]{1,0:T(8,128)(2,1)S(1)}, u32[]{:S(2)}, u32[]{:S(2)}) collective-permute-start(bf16[768,384]{1,0:T(8,128)(2,1)S(1)} %get-tuple-element.125), channel_id=1, source_target_pairs={{0,4},{2,6},{4,0},{6,2},{8,12},{10,14},{12,8},{14,10},{16,20},{18,... | collective-permute-start | bytes 1769480 | tf_op jit(solution)/shard_map/ppermute | solution.py:378
  160.3 22.0 %collective-permute-start.15 = (bf16[1280,128]{1,0:T(8,128)(2,1)S(1)}, bf16[1280,128]{1,0:T(8,128)(2,1)S(1)}, u32[]{:S(2)}, u32[]{:S(2)}) collective-permute-start(bf16[1280,128]{1,0:T(8,128)(2,1)S(1)} %get-tuple-element.86), channel_id=1, source_target_pairs={{0,4},{2,6},{4,0},{6,2},{8,12},{10,14},{12,8},{14,10},{16,20},{18,... | collective-permute-start | bytes 983048 | tf_op jit(solution)/shard_map/ppermute | solution.py:378
  162.6 26.7 %collective-permute-start.20 = (bf16[1280,128]{1,0:T(8,128)(2,1)S(1)}, bf16[1280,128]{1,0:T(8,128)(2,1)S(1)}, u32[]{:S(2)}, u32[]{:S(2)}) collective-permute-start(bf16[1280,128]{1,0:T(8,128)(2,1)S(1)} %get-tuple-element.98), channel_id=1, source_target_pairs={{0,4},{2,6},{4,0},{6,2},{8,12},{10,14},{12,8},{14,10},{16,20},{18,... | collective-permute-start | bytes 983048 | tf_op jit(solution)/shard_map/ppermute | solution.py:378
  163.9 31.5 %collective-permute-start.25 = (bf16[1280,128]{1,0:T(8,128)(2,1)S(1)}, bf16[1280,128]{1,0:T(8,128)(2,1)S(1)}, u32[]{:S(2)}, u32[]{:S(2)}) collective-permute-start(bf16[1280,128]{1,0:T(8,128)(2,1)S(1)} %get-tuple-element.110), channel_id=1, source_target_pairs={{0,4},{2,6},{4,0},{6,2},{8,12},{10,14},{12,8},{14,10},{16,20},{18,... | collective-permute-start | bytes 983048 | tf_op jit(solution)/shard_map/ppermute | solution.py:378
  182.9 14.3 %collective-permute-start.16 = (bf16[480,128]{1,0:T(8,128)(2,1)S(1)}, bf16[480,128]{1,0:T(8,128)(2,1)S(1)}, u32[]{:S(2)}, u32[]{:S(2)}) collective-permute-start(bf16[480,128]{1,0:T(8,128)(2,1)S(1)} %get-tuple-element.92), channel_id=1, source_target_pairs={{0,24},{2,26},{4,28},{6,30},{8,0},{10,2},{12,4},{14,6},{16,8},{18,... | collective-permute-start | bytes 368648 | tf_op jit(solution)/shard_map/ppermute | solution.py:447
  184.8 13.1 %collective-permute-start.17 = (bf16[480,128]{1,0:T(8,128)(2,1)S(1)}, bf16[480,128]{1,0:T(8,128)(2,1)S(1)}, u32[]{:S(2)}, u32[]{:S(2)}) collective-permute-start(bf16[480,128]{1,0:T(8,128)(2,1)S(1)} %get-tuple-element.93), channel_id=1, source_target_pairs={{0,16},{2,18},{4,20},{6,22},{8,24},{10,26},{12,28},{14,30},{16,0},... | collective-permute-start | bytes 368648 | tf_op jit(solution)/shard_map/ppermute | solution.py:447
  189.3 13.1 %collective-permute-start.18 = (bf16[480,128]{1,0:T(8,128)(2,1)S(1)}, bf16[480,128]{1,0:T(8,128)(2,1)S(1)}, u32[]{:S(2)}, u32[]{:S(2)}) collective-permute-start(bf16[480,128]{1,0:T(8,128)(2,1)S(1)} %get-tuple-element.94), channel_id=1, source_target_pairs={{0,8},{2,10},{4,12},{6,14},{8,16},{10,18},{12,20},{14,22},{16,24},... | collective-permute-start | bytes 368648 | tf_op jit(solution)/shard_map/ppermute | solution.py:447
  195.4 7.1 %collective-permute-start.21 = (bf16[480,128]{1,0:T(8,128)(2,1)S(1)}, bf16[480,128]{1,0:T(8,128)(2,1)S(1)}, u32[]{:S(2)}, u32[]{:S(2)}) collective-permute-start(bf16[480,128]{1,0:T(8,128)(2,1)S(1)} %get-tuple-element.104), channel_id=1, source_target_pairs={{0,24},{2,26},{4,28},{6,30},{8,0},{10,2},{12,4},{14,6},{16,8},{18,... | collective-permute-start | bytes 368648 | tf_op jit(solution)/shard_map/ppermute | solution.py:447
  197.2 12.5 %collective-permute-start.22 = (bf16[480,128]{1,0:T(8,128)(2,1)S(1)}, bf16[480,128]{1,0:T(8,128)(2,1)S(1)}, u32[]{:S(2)}, u32[]{:S(2)}) collective-permute-start(bf16[480,128]{1,0:T(8,128)(2,1)S(1)} %get-tuple-element.105), channel_id=1, source_target_pairs={{0,16},{2,18},{4,20},{6,22},{8,24},{10,26},{12,28},{14,30},{16,0},... | collective-permute-start | bytes 368648 | tf_op jit(solution)/shard_map/ppermute | solution.py:447
  197.8 12.3 %collective-permute-start.23 = (bf16[480,128]{1,0:T(8,128)(2,1)S(1)}, bf16[480,128]{1,0:T(8,128)(2,1)S(1)}, u32[]{:S(2)}, u32[]{:S(2)}) collective-permute-start(bf16[480,128]{1,0:T(8,128)(2,1)S(1)} %get-tuple-element.106), channel_id=1, source_target_pairs={{0,8},{2,10},{4,12},{6,14},{8,16},{10,18},{12,20},{14,22},{16,24},... | collective-permute-start | bytes 368648 | tf_op jit(solution)/shard_map/ppermute | solution.py:447
  199.3 15.3 %collective-permute-start.26 = (bf16[480,128]{1,0:T(8,128)(2,1)S(1)}, bf16[480,128]{1,0:T(8,128)(2,1)S(1)}, u32[]{:S(2)}, u32[]{:S(2)}) collective-permute-start(bf16[480,128]{1,0:T(8,128)(2,1)S(1)} %get-tuple-element.116), channel_id=1, source_target_pairs={{0,24},{2,26},{4,28},{6,30},{8,0},{10,2},{12,4},{14,6},{16,8},{18,... | collective-permute-start | bytes 368648 | tf_op jit(solution)/shard_map/ppermute | solution.py:447
  202.4 30.2 %collective-permute-start.31 = (bf16[192,384]{1,0:T(8,128)(2,1)S(1)}, bf16[192,384]{1,0:T(8,128)(2,1)S(1)}, u32[]{:S(2)}, u32[]{:S(2)}) collective-permute-start(bf16[192,384]{1,0:T(8,128)(2,1)S(1)} %get-tuple-element.127), channel_id=1, source_target_pairs={{0,8},{2,10},{4,12},{6,14},{8,16},{10,18},{12,20},{14,22},{16,24},... | collective-permute-start | bytes 442376 | tf_op jit(solution)/shard_map/ppermute | solution.py:447
  202.5 30.1 %collective-permute-start.32 = (bf16[192,384]{1,0:T(8,128)(2,1)S(1)}, bf16[192,384]{1,0:T(8,128)(2,1)S(1)}, u32[]{:S(2)}, u32[]{:S(2)}) collective-permute-start(bf16[192,384]{1,0:T(8,128)(2,1)S(1)} %get-tuple-element.128), channel_id=1, source_target_pairs={{0,16},{2,18},{4,20},{6,22},{8,24},{10,26},{12,28},{14,30},{16,0},... | collective-permute-start | bytes 442376 | tf_op jit(solution)/shard_map/ppermute | solution.py:447
  209.7 22.9 %collective-permute-start.33 = (bf16[192,384]{1,0:T(8,128)(2,1)S(1)}, bf16[192,384]{1,0:T(8,128)(2,1)S(1)}, u32[]{:S(2)}, u32[]{:S(2)}) collective-permute-start(bf16[192,384]{1,0:T(8,128)(2,1)S(1)} %get-tuple-element.129), channel_id=1, source_target_pairs={{0,24},{2,26},{4,28},{6,30},{8,0},{10,2},{12,4},{14,6},{16,8},{18,... | collective-permute-start | bytes 442376 | tf_op jit(solution)/shard_map/ppermute | solution.py:447
  210.1 20.4 %collective-permute-start.27 = (bf16[480,128]{1,0:T(8,128)(2,1)S(1)}, bf16[480,128]{1,0:T(8,128)(2,1)S(1)}, u32[]{:S(2)}, u32[]{:S(2)}) collective-permute-start(bf16[480,128]{1,0:T(8,128)(2,1)S(1)} %get-tuple-element.117), channel_id=1, source_target_pairs={{0,16},{2,18},{4,20},{6,22},{8,24},{10,26},{12,28},{14,30},{16,0},... | collective-permute-start | bytes 368648 | tf_op jit(solution)/shard_map/ppermute | solution.py:447
  214.6 15.9 %collective-permute-start.28 = (bf16[480,128]{1,0:T(8,128)(2,1)S(1)}, bf16[480,128]{1,0:T(8,128)(2,1)S(1)}, u32[]{:S(2)}, u32[]{:S(2)}) collective-permute-start(bf16[480,128]{1,0:T(8,128)(2,1)S(1)} %get-tuple-element.118), channel_id=1, source_target_pairs={{0,8},{2,10},{4,12},{6,14},{8,16},{10,18},{12,20},{14,22},{16,24},... | collective-permute-start | bytes 368648 | tf_op jit(solution)/shard_map/ppermute | solution.py:447

commit v3 on v2

--- a/solution.py
+++ b/solution.py
@@ -9,8 +9,7 @@
 from jax.sharding import PartitionSpec as P
 
 HD = 128
-VMEM_BYTES = 40 * 1024 * 1024
-GRAD_CHUNKS = 2
+VMEM_BYTES = 32 * 1024 * 1024
 BF16 = jnp.bfloat16
 F32 = jnp.float32
 
@@ -85,66 +84,66 @@
     )(*args)
 
 
-def pack_kernel(n_groups, ids, q, k, v, *outs):
-    rows = q.shape[0]
+def pack_kernel(n_groups, ids, q, k, v, w, *outs):
+    rows, depth = q.shape[0], w.shape[0]
     gw = q.shape[1] // n_groups
     for s in range(n_groups):
         cols = pl.ds(aligned(lax.rem(ids[0] + s, n_groups) * gw, HD), gw)
-        for i, source in enumerate((q, k, v)):
-            outs[s][i * rows : (i + 1) * rows, :] = source[:, cols]
-
-
-def pack(ids, q, k, v, n_groups):
+        outs[s][:rows, :] = k[:, cols]
+        outs[s][rows : 2 * rows, :] = v[:, cols]
+        outs[s][2 * rows : 2 * rows + depth, :] = w[:, cols]
+        if s == 0:
+            outs[n_groups][...] = q[:, cols]
+        else:
+            outs[s][2 * rows + depth :, :] = q[:, cols]
+
+
+def pack(ids, q, k, v, w, n_groups):
     rows, width = q.shape
-    shape = jax.ShapeDtypeStruct((3 * rows, width // n_groups), BF16)
+    gw = width // n_groups
+    shared = 2 * rows + w.shape[0]
+    shapes = (
+        [jax.ShapeDtypeStruct((shared, gw), BF16)]
+        + [jax.ShapeDtypeStruct((shared + rows, gw), BF16)] * (n_groups - 1)
+        + [jax.ShapeDtypeStruct((rows, gw), BF16)]
+    )
+    return whole_call(functools.partial(pack_kernel, n_groups), shapes, (ids, q, k, v, w), "pack")
+
+
+def stack_kernel(n_groups, rows, ids, *refs):
+    pieces, out = refs[:n_groups], refs[n_groups]
+    shared = out.shape[0] // n_groups
+    depth = shared - 2 * rows
+    for s, piece in enumerate(pieces):
+        for i in range(2):
+            at = (i * n_groups + s) * rows
+            out[at : at + rows, :] = piece[i * rows : (i + 1) * rows, :]
+        at = 2 * n_groups * rows + s * depth
+        out[at : at + depth, :] = piece[2 * rows : shared, :]
+
+
+def stack(ids, pieces, rows):
+    shared, gw = pieces[0].shape
     return whole_call(
-        functools.partial(pack_kernel, n_groups), [shape] * n_groups, (ids, q, k, v), "pack"
-    )
-
-
-def cut_kernel(n_groups, ids, w, *outs):
-    gw = w.shape[1] // n_groups
-    for s in range(n_groups):
-        outs[s][...] = w[:, pl.ds(aligned(lax.rem(ids[0] + s, n_groups) * gw, HD), gw)]
-
-
-def cut(ids, w, n_groups):
-    depth, width = w.shape
-    shape = jax.ShapeDtypeStruct((depth, width // n_groups), BF16)
-    return whole_call(functools.partial(cut_kernel, n_groups), [shape] * n_groups, (ids, w), "cut")
-
-
-def split_kernel(n_groups, ids, *refs):
-    pieces, (q_out, kv_out) = refs[:n_groups], refs[n_groups:]
-    rows = pieces[0].shape[0] // 3
-    half = n_groups * rows
-    for s in range(n_groups):
-        src = lax.rem(ids[0] - s + n_groups, n_groups)
-        q_out[pl.ds(aligned(src * rows, 16), rows), :] = pieces[s][:rows, :]
-        kv_out[s * rows : (s + 1) * rows, :] = pieces[s][rows : 2 * rows, :]
-        kv_out[half + s * rows : half + (s + 1) * rows, :] = pieces[s][2 * rows :, :]
-
-
-def split(ids, pieces, n_groups):
-    rows, gw = pieces[0].shape[0] // 3, pieces[0].shape[1]
-    shapes = [
-        jax.ShapeDtypeStruct((n_groups * rows, gw), BF16),
-        jax.ShapeDtypeStruct((2 * n_groups * rows, gw), BF16),
-    ]
-    return whole_call(functools.partial(split_kernel, n_groups), shapes, (ids, *pieces), "split")
-
-
-def stack_kernel(ids, *refs):
+        functools.partial(stack_kernel, len(pieces), rows),
+        jax.ShapeDtypeStruct((shared * len(pieces), gw), BF16),
+        (ids, *pieces),
+        "stack",
+    )
+
+
+def stack_queries_kernel(ids, own, *refs):
     pieces, out = refs[:-1], refs[-1]
-    rows = pieces[0].shape[0]
+    rows = own.shape[0]
+    out[:rows, :] = own[...]
     for s, piece in enumerate(pieces):
-        out[s * rows : (s + 1) * rows, :] = piece[...]
-
-
-def stack(ids, pieces):
-    rows, gw = pieces[0].shape
-    shape = jax.ShapeDtypeStruct((rows * len(pieces), gw), BF16)
-    return whole_call(stack_kernel, shape, (ids, *pieces), "stack")
+        out[(s + 1) * rows : (s + 2) * rows, :] = piece[piece.shape[0] - rows :, :]
+
+
+def stack_queries(ids, own, pieces):
+    rows, gw = own.shape
+    shape = jax.ShapeDtypeStruct((rows * (len(pieces) + 1), gw), BF16)
+    return whole_call(stack_queries_kernel, shape, (ids, own, *pieces), "stack_queries")
 
 
 def forward_kernel(chunk, scale, q_in, *refs):
@@ -175,10 +174,9 @@
     o_out[...] = (out * inverse).T.astype(BF16)
 
 
-def forward(q, blocks):
+def forward(q, blocks, part):
     n_q, gw = q.shape
     heads = gw // HD
-    part = blocks[0].shape[0] // 2
     seq_len = part * len(blocks)
     chunk = part if part <= 640 else math.gcd(part, 512)
     scale = math.log2(math.e) / math.sqrt(HD)
@@ -208,7 +206,7 @@
     )(q, *blocks)
 
 
-def backward_kernel(n_groups, chunk, factor, ids, *refs):
+def backward_kernel(n_groups, chunk, factor, *refs):
     q_in, p_in, o_in, il_in, da_in = refs[:5]
     dq_outs, halves, dq_all = refs[-n_groups - 3 : -3], refs[-3:-1], refs[-1]
     blocks = refs[5 : -n_groups - 3]
@@ -236,14 +234,12 @@
             dq = dq + dot(kv[c : c + chunk, :], ds, ((0,), (0,)))
     dq_all[...] = (factor * dq).T.astype(BF16)
     for s in range(n_groups):
-        src = lax.rem(ids[0] - s + n_groups, n_groups)
-        dq_outs[s][...] = dq_all[pl.ds(aligned(src * rows, 16), rows), :]
-
-
-def backward(ids, head, q, blocks, probs, out, inverse, grad_attn, n_groups):
+        dq_outs[s][...] = dq_all[s * rows : (s + 1) * rows, :]
+
+
+def backward(head, q, blocks, part, probs, out, inverse, grad_attn, n_groups):
     n_q = q.shape[0]
     rows = n_q // n_groups
-    part = blocks[0].shape[0] // 2
     seq_len = part * len(blocks)
     chunk = part if part <= 640 else math.gcd(part, 512)
     per_half = max(1, len(blocks) // 2)
@@ -254,7 +250,6 @@
         out_shape=[jax.ShapeDtypeStruct((rows, HD), BF16)] * n_groups
         + [jax.ShapeDtypeStruct((per_half * 2 * part, HD), BF16)] * 2,
         in_specs=[
-            smem(),
             column,
             pl.BlockSpec((1, seq_len, n_q), lambda i: (head, 0, 0)),
             column,
@@ -266,12 +261,12 @@
         scratch_shapes=[pltpu.VMEM((n_q, HD), BF16)],
         compiler_params=params(),
         cost_estimate=pl.CostEstimate(
-            flops=8 * seq_len * n_q * HD,
-            bytes_accessed=2 * seq_len * n_q,
+            flops=n_q * HD,
+            bytes_accessed=2 * n_q * HD,
             transcendentals=0,
         ),
         name="backward",
-    )(ids, q, probs, out, inverse, grad_attn, *blocks)
+    )(q, probs, out, inverse, grad_attn, *blocks)
     return results[:n_groups], results[n_groups:]
 
 
@@ -280,82 +275,57 @@
     return group * n_tok + jnp.bitwise_xor(ids[1], relative_of(position, bits_of(n_tok)))
 
 
-def column_starts(ids, grads, n_space):
-    part = sum(g.shape[1] for g in grads[0])
-    for r in range(n_space):
-        start = jnp.bitwise_xor(ids[2], relative_of(r, bits_of(n_space))) * part
-        for grad in grads[r]:
-            yield grad, aligned(start, 16)
-            start = start + grad.shape[1]
-
-
-def by_space(refs, n_space):
-    count = len(refs) // n_space
-    return [refs[r * count : (r + 1) * count] for r in range(n_space)]
-
-
-def attn_kernel(n_groups, n_tok, n_space, ids, *refs):
-    weights, (out, weight) = refs[:n_tok], refs[-2:]
-    grads = by_space(refs[n_tok:-2], n_space)
-    depth = weights[0].shape[0] // n_groups
+def project_kernel(n_groups, n_tok, n_space, ids, attn, *refs):
+    blocks, grads = refs[:n_tok], refs[n_tok : n_tok + n_groups * n_space]
+    grad_attn, kept, sent, weight, whole, tokens = refs[n_tok + n_groups * n_space :]
+    rows, part = grads[0].shape
+    depth = weight.shape[0] // (n_groups * n_tok)
+    first = blocks[0].shape[0] - n_groups * depth
     for j in range(n_tok):
         for s in range(n_groups):
             place = frame_block(ids, -1, s, j, n_groups, n_tok) * depth
-            weight[pl.ds(aligned(place, 16), depth), :] = weights[j][s * depth : (s + 1) * depth, :]
+            at = first + s * depth
+            weight[pl.ds(aligned(place, 16), depth), :] = blocks[j][at : at + depth, :]
     total = None
-    for grad, start in column_starts(ids, grads, n_space):
-        term = dot(grad[...], weight[pl.ds(start, grad.shape[1]), :], ((1,), (0,)))
+    for r in range(n_space):
+        for s in range(n_groups):
+            tokens[s * rows : (s + 1) * rows, :] = grads[r * n_groups + s][...]
+        start = jnp.bitwise_xor(ids[2], relative_of(r, bits_of(n_space))) * part
+        block = tokens[...]
+        here = pl.ds(aligned(start, 16), part)
+        term = dot(block, weight[here, :], ((1,), (0,)))
         total = term if total is None else total + term
-    out[...] = total.astype(BF16)
-
-
-def projection_cost(n_q, depth, gw):
-    return pl.CostEstimate(
-        flops=2 * n_q * depth * gw,
-        bytes_accessed=2 * (n_q * depth + depth * gw + n_q * gw),
-        transcendentals=0,
-    )
-
-
-def attn_gradient(ids, grads, weights, n_groups, n_tok, n_space):
-    n_q = grads[0][0].shape[0]
-    depth, gw = n_tok * weights[0].shape[0], weights[0].shape[1]
-    return whole_call(
-        functools.partial(attn_kernel, n_groups, n_tok, n_space),
-        jax.ShapeDtypeStruct((n_q, gw), BF16),
-        (ids, *weights, *[g for part in grads for g in part]),
-        "attn_gradient",
-        [pltpu.VMEM((depth, gw), BF16)],
-        projection_cost(n_q, depth, gw),
-    )
-
-
-def proj_kernel(n_groups, n_tok, n_space, ids, *refs):
-    attn, halves, whole = refs[0], refs[-3:-1], refs[-1]
-    grads = by_space(refs[1:-3], n_space)
-    for grad, start in column_starts(ids, grads, n_space):
-        term = dot(grad[...], attn[...], ((0,), (0,)))
-        whole[pl.ds(start, grad.shape[1]), :] = term.astype(BF16)
-    depth = whole.shape[0] // (n_groups * n_tok)
+        whole[here, :] = dot(block, attn[...], ((0,), (0,))).astype(BF16)
+    grad_attn[...] = total.astype(BF16)
     per_half = max(1, n_tok // 2)
     for j in range(n_tok):
+        half = sent if j >= per_half else kept
         for s in range(n_groups):
             place = frame_block(ids, 1, s, j, n_groups, n_tok) * depth
             at = (j % per_half * n_groups + s) * depth
-            halves[j // per_half][at : at + depth, :] = whole[pl.ds(aligned(place, 16), depth), :]
-
-
-def proj_gradient(ids, grads, attn, n_groups, n_tok, n_space):
+            half[at : at + depth, :] = whole[pl.ds(aligned(place, 16), depth), :]
+
+
+def project(ids, attn, blocks, grads, depth, n_groups, n_tok, n_space):
     n_q, gw = attn.shape
-    depth = n_space * sum(g.shape[1] for g in grads[0])
-    half = depth // n_tok * max(1, n_tok // 2)
+    part = grads[0].shape[1]
+    half = n_groups * depth * max(1, n_tok // 2)
+    total = n_groups * n_tok * depth
     return whole_call(
-        functools.partial(proj_kernel, n_groups, n_tok, n_space),
-        [jax.ShapeDtypeStruct((half, gw), BF16)] * 2,
-        (ids, attn, *[g for part in grads for g in part]),
-        "proj_gradient",
-        [pltpu.VMEM((depth, gw), BF16)],
-        projection_cost(n_q, depth, gw),
+        functools.partial(project_kernel, n_groups, n_tok, n_space),
+        [jax.ShapeDtypeStruct((n_q, gw), BF16)] + [jax.ShapeDtypeStruct((half, gw), BF16)] * 2,
+        (ids, attn, *blocks, *grads),
+        "project",
+        [
+            pltpu.VMEM((total, gw), BF16),
+            pltpu.VMEM((total, gw), BF16),
+            pltpu.VMEM((n_q, part), BF16),
+        ],
+        pl.CostEstimate(
+            flops=4 * n_q * total * gw,
+            bytes_accessed=2 * (n_q * total + 2 * total * gw + 2 * n_q * gw),
+            transcendentals=0,
+        ),
     )
 
 
@@ -373,12 +343,11 @@
     return whole_call(add_kernel, [shape] * count, (ids, kept, other), "add_parts")
 
 
-def reduce_halves(ids, kept, sent, n_frame, bits):
-    for place, bit in enumerate(bits):
+def halve(ids, kept, sent, n_frame, bits):
+    for bit in bits[:-1]:
         other = lax.ppermute(sent, "frame", xor_pairs(n_frame, bit))
-        if place == len(bits) - 1:
-            return kept, other
         kept, sent = add_parts(ids, kept, other, 2)
+    return kept, sent
 
 
 def finish_kernel(n_groups, ids, kept, other, *refs):
@@ -452,45 +421,62 @@
 def local(queries, keys, values, grad_out, proj_weight):
     n_frame = lax.axis_size("frame")
     n_space = lax.axis_size("space")
-    width = queries.shape[1]
+    rows, width = queries.shape
+    depth = proj_weight.shape[1]
     n_groups = math.gcd(width // HD, n_frame)
     n_tok = n_frame // n_groups
     tok_bits = bits_of(n_tok)
+    space_bits = bits_of(n_space)
     heads = width // n_groups // HD
+    shared = 2 * rows + depth
     frame = lax.axis_index("frame")
     ids = jnp.stack([frame // n_tok, frame % n_tok, lax.axis_index("space")]).astype(jnp.int32)
 
-    pieces = exchange(pack(ids, queries, keys, values, n_groups), n_groups, n_tok, 1)
-    q, kv = split(ids, pieces, n_groups)
-    kv = gather_blocks(kv, "frame", n_frame, tok_bits)
-    weight = exchange(cut(ids, proj_weight.T, n_groups), n_groups, n_tok, 1)
-    weights = gather_blocks(stack(ids, weight), "frame", n_frame, tok_bits)
-
-    n_chunk = math.gcd(grad_out.shape[1] // HD, GRAD_CHUNKS)
-    chunk_cols = grad_out.shape[1] // n_chunk
-    lines = [[g * n_tok + t for g in range(n_groups)] for t in range(n_tok)]
-    grads = [[] for _ in range(n_space)]
-    for c in range(n_chunk):
-        own = grad_out[:, c * chunk_cols : (c + 1) * chunk_cols]
-        if n_groups > 1:
-            own = lax.all_gather(own, "frame", axis=0, tiled=True, axis_index_groups=lines)
-        gathered = gather_blocks(own, "space", n_space, bits_of(n_space))
-        for r in range(n_space):
-            grads[r].append(gathered[r])
-
-    probs, out, inverse = forward(q, kv)
-    kept, sent = proj_gradient(ids, grads, out, n_groups, n_tok, n_space)
-    grad_attn = attn_gradient(ids, grads, weights, n_groups, n_tok, n_space)
-    grad_attn, kept, sent = lax.optimization_barrier((grad_attn, kept, sent))
-    proj = reduce_halves(ids, kept, sent, n_frame, tok_bits)
-    proj = exchange(add_parts(ids, *proj, n_groups), n_groups, n_tok, 1)
+    *pieces, own_q = pack(ids, queries, keys, values, proj_weight.T, n_groups)
+    pieces = exchange(pieces, n_groups, n_tok, 1)
+    q_pieces = pieces[1:]
+    first = xor_pairs(n_frame, tok_bits[-1])
+    own, others, by_piece = [pieces[0]], [lax.ppermute(pieces[0], "frame", first)], []
+    ring = grad_out
+    for s in range(n_groups):
+        across = gather_blocks(ring, "space", n_space, space_bits)
+        if s + 1 < n_groups:
+            ring = lax.ppermute(ring, "frame", shift_pairs(n_groups, n_tok, 1))
+            ring, piece, *across = lax.optimization_barrier((ring, pieces[s + 1][:shared], *across))
+            own.append(piece)
+            others.append(lax.ppermute(piece, "frame", first))
+        by_piece.append(across)
+    grads = [by_piece[s][r] for r in range(n_space) for s in range(n_groups)]
+
+    q = stack_queries(ids, own_q, q_pieces)
+    blocks = [stack(ids, own, rows), stack(ids, others, rows)]
+    for bit in reversed(tok_bits[:-1]):
+        blocks = blocks + [lax.ppermute(b, "frame", xor_pairs(n_frame, bit)) for b in blocks]
+
+    part = n_groups * rows
+    probs, out, inverse = forward(q, blocks, part)
+    grad_attn, kept, sent = project(ids, out, blocks, grads, depth, n_groups, n_tok, n_space)
+    last = xor_pairs(n_frame, tok_bits[-1])
+    proj_kept, proj_sent = halve(ids, kept, sent, n_frame, tok_bits)
+    here, sums, finished = q, (), []
+    for h in range(heads):
+        if h > 0:
+            here, kept, sent, *sums = lax.optimization_barrier((q, kept, sent, *sums))
+        if h > 1:
+            finished[-1] = sums
+        if h > 0:
+            other = lax.ppermute(sent, "frame", last)
+            kept_dq = (kept, other, dq)
+        dq, halves = backward(h, here, blocks, part, probs, out, inverse, grad_attn, n_groups)
+        if h > 0:
+            sums = finish(ids, *kept_dq, n_groups)
+            finished.append(sums)
+        kept, sent = halve(ids, *halves, n_frame, tok_bits)
+    finished.append(finish(ids, kept, lax.ppermute(sent, "frame", last), dq, n_groups))
+    proj = add_parts(ids, proj_kept, lax.ppermute(proj_sent, "frame", last), n_groups)
+    proj = exchange(proj, n_groups, n_tok, 1)
     grad_proj = join(ids, proj, n_groups).T
-
-    returned = []
-    for h in range(heads):
-        dq, halves = backward(ids, h, q, kv, probs, out, inverse, grad_attn, n_groups)
-        kept, other = reduce_halves(ids, *halves, n_frame, tok_bits)
-        returned.append(exchange(finish(ids, kept, other, dq, n_groups), n_groups, n_tok, -1))
+    returned = [exchange(sums, n_groups, n_tok, -1) for sums in finished]
     grad_queries, grad_keys, grad_values = unpack(ids, returned, n_groups)
     return (grad_queries, grad_keys, grad_values, grad_proj)
 

time: 235 us -> 219 us (0.932)
  blocking collectives: 44.1 us -> 0 us
  starting transfers between devices: 40 us -> 62.4 us
  waiting for transfers between devices: 99.6 us -> 111 us
  Pallas kernels: 46.4 us -> 39.7 us
    all_gather x2 -> x0, blocking collectives: 44.1 us -> none  [local(): lax.all_gather(own, 'frame', axis=0, tiled=True, axis_index_groups=lines)]
    ppermute x8 -> x17, waiting for transfers between devices: 26.9 us -> 62 us  [the longest x3 22.1 us: local(): others.append(lax.ppermute(piece, 'frame', first))]
    ppermute x8 -> x17, starting transfers between devices: 5.58 us -> 32.2 us  [the longest x3 20.9 us: local(): ring = lax.ppermute(ring, 'frame', shift_pairs(n_groups, n_tok, 1))]
    ppermute x8 -> x4, waiting for transfers between devices: 21.7 us -> 2.21 us  [gather_blocks(): lax.ppermute(b, axis, xor_pairs(count, bit))]
    pallas_call x3, Pallas kernels: 17.1 us -> 12 us  [backward(): pl.pallas_call(functools.partial(backward_kernel, n_groups, chunk, 1.0 /...]
    ppermute x18 -> x15, waiting for transfers between devices: 51.1 us -> 46.7 us  [exchange(): lax.ppermute(pieces[s], 'frame', shift_pairs(n_groups, n_tok, sign * s))]
    ppermute x18 -> x15, starting transfers between devices: 28.5 us -> 25.1 us  [exchange(): lax.ppermute(pieces[s], 'frame', shift_pairs(n_groups, n_tok, sign * s))]
    ppermute x8 -> x4, starting transfers between devices: 5.97 us -> 5.13 us  [gather_blocks(): lax.ppermute(b, axis, xor_pairs(count, bit))]
  transfers between devices with their start and end apart: 34 -> 36, of which waited for: 10 -> 18; matrix products, arithmetic and copies ran while one was open for 0% -> 0% of each run, Pallas kernels for 13% -> 13%
where the time goes in v3:
time: 219 us; the launch traced here: 218 us
  waiting for transfers between devices  111 us (51%)
  starting transfers between devices  62.4 us (28%)
  Pallas kernels  39.7 us (18%)
  local copies, waits for them, and re-layouts  4.28 us (2%)
    ppermute x15, waiting for transfers between devices, exchange(): lax.ppermute(pieces[s], 'frame', shift_pairs(n_groups, n_tok, sign * s))  46.7 us
    ppermute x15, starting transfers between devices, exchange(): lax.ppermute(pieces[s], 'frame', shift_pairs(n_groups, n_tok, sign * s))  25.1 us
    ppermute x3, waiting for transfers between devices, local(): others.append(lax.ppermute(piece, 'frame', first))  22.1 us
    ppermute x3, starting transfers between devices, local(): ring = lax.ppermute(ring, 'frame', shift_pairs(n_groups, n_tok, 1))  20.9 us
    pallas_call x15, Pallas kernels, whole_call(): pl.pallas_call(body, out_shape=out_shape, in_specs=[smem()] + [vmem()] *...  17.3 us
    ppermute x3, waiting for transfers between devices, local(): ring = lax.ppermute(ring, 'frame', shift_pairs(n_groups, n_tok, 1))  12.4 us
    ppermute x2, waiting for transfers between devices, local(): other = lax.ppermute(sent, 'frame', last)  12.3 us
    pallas_call x3, Pallas kernels, backward(): pl.pallas_call(functools.partial(backward_kernel, n_groups, chunk, 1.0 /...  12 us
  transfers between devices with their start and end apart: 36, of which 18 were waited for; matrix products, arithmetic and copies ran while one was open for 0% of the time, Pallas kernels for 13%

profile of v3, /device:TPU:0, one launch (start us, length us, event | category | flops | bytes accessed | tf_op | source)
XLA Modules:
  0.0 218.2 jit_solution(227690031945609484)
XLA Ops:
  0.7 1.1 copy-done
  1.8 1.0 copy-done.1
  2.8 1.0 copy-done.2
  3.9 1.0 copy-done.3
  4.9 0.7 pack.1
  5.6 3.1 %collective-permute-start = (bf16[672,384]{1,0:T(8,128)(2,1)S(1)}, bf16[672,384]{1,0:T(8,128)(2,1)S(1)}, u32[]{:S(2)}, u32[]{:S(2)}) collective-permute-start(bf16[672,384]{1,0:T(8,128)(2,1)S(1)} %get-tuple-element.83), channel_id=1, source_target_pairs={{0,8},{2,10},{4,12},{6,14},{8,16},{10,18},{12,20},{14,22},{16,24},... | collective-permute-start | bytes 1548296 | tf_op jit(solution)/shard_map/ppermute | solution.py:416
  8.7 1.6 collective-permute-start.3
  10.3 1.5 collective-permute-start.4
  11.8 1.3 collective-permute-start.1
  13.0 10.3 %collective-permute-done.refs_0_ = bf16[672,384]{1,0:T(8,128)(2,1)S(1)} collective-permute-done((bf16[672,384]{1,0:T(8,128)(2,1)S(1)}, bf16[672,384]{1,0:T(8,128)(2,1)S(1)}, u32[]{:S(2)}, u32[]{:S(2)}) %collective-permute-start) | collective-permute-done | bytes 516128 | tf_op jit(solution)/shard_map/ppermute | solution.py:416
  23.4 10.5 %collective-permute-done.3.refs_5_ = bf16[160,1536]{1,0:T(8,128)(2,1)S(1)} collective-permute-done((bf16[160,1536]{1,0:T(8,128)(2,1)S(1)}, bf16[160,1536]{1,0:T(8,128)(2,1)S(1)}, u32[]{:S(2)}, u32[]{:S(2)}) %collective-permute-start.3) | collective-permute-done | bytes 491552 | tf_op jit(solution)/shard_map/ppermute | solution.py:444
  33.9 9.7 %collective-permute-start.5 = (bf16[160,1536]{1,0:T(8,128)(2,1)S(1)}, bf16[160,1536]{1,0:T(8,128)(2,1)S(1)}, u32[]{:S(2)}, u32[]{:S(2)}) collective-permute-start(bf16[160,1536]{1,0:T(8,128)(2,1)S(1)} %collective-permute-done.3.refs_5_), channel_id=1, source_target_pairs={{0,8},{2,10},{4,12},{6,14},{8,16},{10,18},{12,20},{14,22},{16,24},... | collective-permute-start | bytes 1474568 | tf_op jit(solution)/shard_map/ppermute | solution.py:444
  43.6 1.5 collective-permute-start.6
  45.1 20.7 %collective-permute-done.1.refs_1_ = bf16[672,384]{1,0:T(8,128)(2,1)S(1)} collective-permute-done((bf16[672,384]{1,0:T(8,128)(2,1)S(1)}, bf16[672,384]{1,0:T(8,128)(2,1)S(1)}, u32[]{:S(2)}, u32[]{:S(2)}) %collective-permute-start.1) | collective-permute-done | bytes 516128 | tf_op jit(solution)/shard_map/ppermute | solution.py:416
  65.9 9.7 %collective-permute-start.7 = (bf16[160,1536]{1,0:T(8,128)(2,1)S(1)}, bf16[160,1536]{1,0:T(8,128)(2,1)S(1)}, u32[]{:S(2)}, u32[]{:S(2)}) collective-permute-start(bf16[160,1536]{1,0:T(8,128)(2,1)S(1)} %collective-permute-done.5.refs_6_), channel_id=1, source_target_pairs={{0,8},{2,10},{4,12},{6,14},{8,16},{10,18},{12,20},{14,22},{16,24},... | collective-permute-start | bytes 1474568 | tf_op jit(solution)/shard_map/ppermute | solution.py:444
  75.6 1.5 collective-permute-start.8
  77.1 1.5 collective-permute-start.9
  78.6 0.5 collective-permute-start.10
  79.1 2.6 %collective-permute-done.2.refs_2_ = bf16[672,384]{1,0:T(8,128)(2,1)S(1)} collective-permute-done((bf16[672,384]{1,0:T(8,128)(2,1)S(1)}, bf16[672,384]{1,0:T(8,128)(2,1)S(1)}, u32[]{:S(2)}, u32[]{:S(2)}) %collective-permute-start.2) | collective-permute-done | bytes 516128 | tf_op jit(solution)/shard_map/ppermute | solution.py:416
  81.8 1.6 collective-permute-start.11
  83.3 1.9 collective-permute-done.7.refs_7_
  85.2 2.2 %collective-permute-done.8.refs_10_ = bf16[160,1536]{1,0:T(8,128)(2,1)S(1)} collective-permute-done((bf16[160,1536]{1,0:T(8,128)(2,1)S(1)}, bf16[160,1536]{1,0:T(8,128)(2,1)S(1)}, u32[]{:S(2)}, u32[]{:S(2)}) %collective-permute-start.8) | collective-permute-done | bytes 491552 | tf_op jit(solution)/shard_map/ppermute | solution.py:49
  87.4 1.5 collective-permute-start.12
  88.9 0.7 stack.18.refs_0_.refs_5_
  89.7 7.9 %collective-permute-done.10.refs_1_ = bf16[512,384]{1,0:T(8,128)(2,1)S(1)} collective-permute-done((bf16[512,384]{1,0:T(8,128)(2,1)S(1)}, bf16[512,384]{1,0:T(8,128)(2,1)S(1)}, u32[]{:S(2)}, u32[]{:S(2)}) %collective-permute-start.10) | collective-permute-done | bytes 393248 | tf_op jit(solution)/shard_map/ppermute | solution.py:447
  97.6 8.4 %collective-permute-done.11.refs_2_ = bf16[512,384]{1,0:T(8,128)(2,1)S(1)} collective-permute-done((bf16[512,384]{1,0:T(8,128)(2,1)S(1)}, bf16[512,384]{1,0:T(8,128)(2,1)S(1)}, u32[]{:S(2)}, u32[]{:S(2)}) %collective-permute-start.11) | collective-permute-done | bytes 393248 | tf_op jit(solution)/shard_map/ppermute | solution.py:447
  106.0 5.8 %collective-permute-done.12.refs_3_ = bf16[512,384]{1,0:T(8,128)(2,1)S(1)} collective-permute-done((bf16[512,384]{1,0:T(8,128)(2,1)S(1)}, bf16[512,384]{1,0:T(8,128)(2,1)S(1)}, u32[]{:S(2)}, u32[]{:S(2)}) %collective-permute-start.12) | collective-permute-done | bytes 393248 | tf_op jit(solution)/shard_map/ppermute | solution.py:447
  111.8 0.7 stack.19.refs_1_.refs_6_
  112.6 0.6 collective-permute-start.15
  113.1 0.6 stack_queries.1.q_in.refs_0_
  113.7 2.2 %collective-permute-done.14.refs_3_.refs_8_ = bf16[2048,384]{1,0:T(8,128)(2,1)S(1)} collective-permute-done((bf16[2048,384]{1,0:T(8,128)(2,1)S(1)}, bf16[2048,384]{1,0:T(8,128)(2,1)S(1)}, u32[]{:S(2)}, u32[]{:S(2)}) %collective-permute-start.14) | collective-permute-done | bytes 1572896 | tf_op jit(solution)/shard_map/ppermute | solution.py:454
  116.0 10.4 %forward.1 = (bf16[3,2560,640]{2,1,0:T(8,128)(2,1)S(1)}, bf16[640,384]{1,0:T(8,128)(2,1)S(1)}, f32[3,1,640]{2,1,0:T(1,128)S(1)}) custom-call(bf16[640,384]{1,0:T(8,128)(2,1)S(1)} %stack_queries.1.q_in.refs_0_, bf16[2048,384]{1,0:T(8,128)(2,1)S(1)} %stack.18.refs_0_.refs_5_, bf16[2048,384]{1,0:T(8,128)(2,1)S(1)} %stack.19.refs_1_.refs_6_, ...), custom_call_target="tpu_custom_call" | custom-call | flops 2516582400 | bytes 9830400 | tf_op jit(solution)/shard_map/forward/pallas_call | solution.py:183
  126.4 5.5 %project.1 = (bf16[640,384]{1,0:T(8,128)(2,1)S(1)}, bf16[1536,384]{1,0:T(8,128)(2,1)S(1)}, bf16[1536,384]{1,0:T(8,128)(2,1)S(1)}) custom-call(s32[3]{0:T(128)S(1)} %pad_add_fusion.ids, bf16[640,384]{1,0:T(8,128)(2,1)S(1)} %get-tuple-element.93.attn.refs_2_, bf16[2048,384]{1,0:T(8,128)(2,1)S(1)} %stack.18.refs_0_.refs_5_, ...), custom_call_target="tpu_custom_call" | custom-call | flops 3019898880 | bytes 9633792 | tf_op jit(solution)/shard_map/project/pallas_call | solution.py:75
  131.9 3.9 %backward.3 = (bf16[160,128]{1,0:T(8,128)(2,1)S(1)}, bf16[160,128]{1,0:T(8,128)(2,1)S(1)}, bf16[160,128]{1,0:T(8,128)(2,1)S(1)}, bf16[160,128]{1,0:T(8,128)(2,1)...) custom-call(bf16[640,384]{1,0:T(8,128)(2,1)S(1)} %stack_queries.1.q_in.refs_0_, ...), custom_call_target="tpu_custom_call" | custom-call | flops 81920 | bytes 163840 | tf_op jit(solution)/shard_map/backward/pallas_call | solution.py:247
  136.4 1.6 collective-permute-done.16.other
  137.9 0.7 add_parts.5
  138.6 3.9 %backward.4 = (bf16[160,128]{1,0:T(8,128)(2,1)S(1)}, bf16[160,128]{1,0:T(8,128)(2,1)S(1)}, bf16[160,128]{1,0:T(8,128)(2,1)S(1)}, bf16[160,128]{1,0:T(8,128)(2,1)...) custom-call(bf16[640,384]{1,0:T(8,128)(2,1)S(1)} %stack_queries.1.q_in.refs_0_, ...), custom_call_target="tpu_custom_call" | custom-call | flops 81920 | bytes 163840 | tf_op jit(solution)/shard_map/backward/pallas_call | solution.py:247
  142.8 1.5 collective-permute-start.18
  144.3 8.5 %collective-permute-done.18.other = bf16[1280,128]{1,0:T(8,128)(2,1)S(1)} collective-permute-done((bf16[1280,128]{1,0:T(8,128)(2,1)S(1)}, bf16[1280,128]{1,0:T(8,128)(2,1)S(1)}, u32[]{:S(2)}, u32[]{:S(2)}) %collective-permute-start.18) | collective-permute-done | bytes 327712 | tf_op jit(solution)/shard_map/ppermute | solution.py:468
  152.8 0.6 finish.3
  153.4 0.7 add_parts.6
  154.1 4.1 %backward.5 = (bf16[160,128]{1,0:T(8,128)(2,1)S(1)}, bf16[160,128]{1,0:T(8,128)(2,1)S(1)}, bf16[160,128]{1,0:T(8,128)(2,1)S(1)}, bf16[160,128]{1,0:T(8,128)(2,1)...) custom-call(bf16[640,384]{1,0:T(8,128)(2,1)S(1)} %stack_queries.1.q_in.refs_0_, ...), custom_call_target="tpu_custom_call" | custom-call | flops 81920 | bytes 163840 | tf_op jit(solution)/shard_map/backward/pallas_call | solution.py:247
  158.3 0.8 add_parts.8
  159.2 1.6 collective-permute-start.32
  160.7 0.5 collective-permute-start.22
  161.3 0.7 add_parts.7
  162.0 1.6 collective-permute-start.27
  163.5 3.9 %collective-permute-start.20 = (bf16[480,128]{1,0:T(8,128)(2,1)S(1)}, bf16[480,128]{1,0:T(8,128)(2,1)S(1)}, u32[]{:S(2)}, u32[]{:S(2)}) collective-permute-start(bf16[480,128]{1,0:T(8,128)(2,1)S(1)} %get-tuple-element.124), channel_id=1, source_target_pairs={{0,16},{2,18},{4,20},{6,22},{8,24},{10,26},{12,28},{14,30},{16,0},... | collective-permute-start | bytes 368648 | tf_op jit(solution)/shard_map/ppermute | solution.py:416
  167.5 7.9 %collective-permute-done.32.other = bf16[768,384]{1,0:T(8,128)(2,1)S(1)} collective-permute-done((bf16[768,384]{1,0:T(8,128)(2,1)S(1)}, bf16[768,384]{1,0:T(8,128)(2,1)S(1)}, u32[]{:S(2)}, u32[]{:S(2)}) %collective-permute-start.32) | collective-permute-done | bytes 589856 | tf_op jit(solution)/shard_map/ppermute | solution.py:476
  175.4 0.7 add_parts.9
  176.0 2.5 %collective-permute-start.33 = (bf16[192,384]{1,0:T(8,128)(2,1)S(1)}, bf16[192,384]{1,0:T(8,128)(2,1)S(1)}, u32[]{:S(2)}, u32[]{:S(2)}) collective-permute-start(bf16[192,384]{1,0:T(8,128)(2,1)S(1)} %get-tuple-element.157), channel_id=1, source_target_pairs={{0,8},{2,10},{4,12},{6,14},{8,16},{10,18},{12,20},{14,22},{16,24},... | collective-permute-start | bytes 442376 | tf_op jit(solution)/shard_map/ppermute | solution.py:416
  178.6 3.8 %collective-permute-done.22.other = bf16[1280,128]{1,0:T(8,128)(2,1)S(1)} collective-permute-done((bf16[1280,128]{1,0:T(8,128)(2,1)S(1)}, bf16[1280,128]{1,0:T(8,128)(2,1)S(1)}, u32[]{:S(2)}, u32[]{:S(2)}) %collective-permute-start.22) | collective-permute-done | bytes 327712 | tf_op jit(solution)/shard_map/ppermute | solution.py:468
  182.4 0.6 finish.4
  183.0 2.5 %collective-permute-start.21 = (bf16[480,128]{1,0:T(8,128)(2,1)S(1)}, bf16[480,128]{1,0:T(8,128)(2,1)S(1)}, u32[]{:S(2)}, u32[]{:S(2)}) collective-permute-start(bf16[480,128]{1,0:T(8,128)(2,1)S(1)} %get-tuple-element.125), channel_id=1, source_target_pairs={{0,8},{2,10},{4,12},{6,14},{8,16},{10,18},{12,20},{14,22},{16,24},... | collective-permute-start | bytes 368648 | tf_op jit(solution)/shard_map/ppermute | solution.py:416
  185.6 3.4 %collective-permute-done.27.other = bf16[1280,128]{1,0:T(8,128)(2,1)S(1)} collective-permute-done((bf16[1280,128]{1,0:T(8,128)(2,1)S(1)}, bf16[1280,128]{1,0:T(8,128)(2,1)S(1)}, u32[]{:S(2)}, u32[]{:S(2)}) %collective-permute-start.27) | collective-permute-done | bytes 327712 | tf_op jit(solution)/shard_map/ppermute | solution.py:475
  189.0 0.6 finish.5
  189.6 2.5 %collective-permute-done.21.refs_3_ = bf16[480,128]{1,0:T(8,128)(2,1)S(1)} collective-permute-done((bf16[480,128]{1,0:T(8,128)(2,1)S(1)}, bf16[480,128]{1,0:T(8,128)(2,1)S(1)}, u32[]{:S(2)}, u32[]{:S(2)}) %collective-permute-start.21) | collective-permute-done | bytes 122912 | tf_op jit(solution)/shard_map/ppermute | solution.py:416
  192.1 7.3 %collective-permute-start.24 = (bf16[480,128]{1,0:T(8,128)(2,1)S(1)}, bf16[480,128]{1,0:T(8,128)(2,1)S(1)}, u32[]{:S(2)}, u32[]{:S(2)}) collective-permute-start(bf16[480,128]{1,0:T(8,128)(2,1)S(1)} %get-tuple-element.134), channel_id=1, source_target_pairs={{0,16},{2,18},{4,20},{6,22},{8,24},{10,26},{12,28},{14,30},{16,0},... | collective-permute-start | bytes 368648 | tf_op jit(solution)/shard_map/ppermute | solution.py:416
  199.7 3.5 %collective-permute-start.28 = (bf16[480,128]{1,0:T(8,128)(2,1)S(1)}, bf16[480,128]{1,0:T(8,128)(2,1)S(1)}, u32[]{:S(2)}, u32[]{:S(2)}) collective-permute-start(bf16[480,128]{1,0:T(8,128)(2,1)S(1)} %get-tuple-element.146), channel_id=1, source_target_pairs={{0,24},{2,26},{4,28},{6,30},{8,0},{10,2},{12,4},{14,6},{16,8},{18,... | collective-permute-start | bytes 368648 | tf_op jit(solution)/shard_map/ppermute | solution.py:416
  203.3 0.6 collective-permute-start.30
  203.9 1.7 join.1
  205.6 4.0 %collective-permute-done.24.refs_6_ = bf16[480,128]{1,0:T(8,128)(2,1)S(1)} collective-permute-done((bf16[480,128]{1,0:T(8,128)(2,1)S(1)}, bf16[480,128]{1,0:T(8,128)(2,1)S(1)}, u32[]{:S(2)}, u32[]{:S(2)}) %collective-permute-start.24) | collective-permute-done | bytes 122912 | tf_op jit(solution)/shard_map/ppermute | solution.py:416
  209.5 6.6 %collective-permute-done.29.refs_10_ = bf16[480,128]{1,0:T(8,128)(2,1)S(1)} collective-permute-done((bf16[480,128]{1,0:T(8,128)(2,1)S(1)}, bf16[480,128]{1,0:T(8,128)(2,1)S(1)}, u32[]{:S(2)}, u32[]{:S(2)}) %collective-permute-start.29) | collective-permute-done | bytes 122912 | tf_op jit(solution)/shard_map/ppermute | solution.py:416
  216.2 2.0 unpack.1
  (41 shorter events, 1.6 us)
Async XLA Ops:
  0.7 1.1 copy-start
  1.8 1.0 copy-start.1
  2.8 1.0 copy-start.2
  3.9 1.0 copy-start.3
  4.9 3.8 %copy-start.4 = (bf16[160,1536]{1,0:T(8,128)(2,1)S(1)}, bf16[160,1536]{1,0:T(8,128)(2,1)}, u32[]{:S(2)}) copy-start(bf16[160,1536]{1,0:T(8,128)(2,1)} %refs_4_) | copy-start | bytes 1474564
  5.6 17.8 %collective-permute-start = (bf16[672,384]{1,0:T(8,128)(2,1)S(1)}, bf16[672,384]{1,0:T(8,128)(2,1)S(1)}, u32[]{:S(2)}, u32[]{:S(2)}) collective-permute-start(bf16[672,384]{1,0:T(8,128)(2,1)S(1)} %get-tuple-element.83), channel_id=1, source_target_pairs={{0,8},{2,10},{4,12},{6,14},{8,16},{10,18},{12,20},{14,22},{16,24},... | collective-permute-start | bytes 1548296 | tf_op jit(solution)/shard_map/ppermute | solution.py:416
  8.7 25.2 %collective-permute-start.3 = (bf16[160,1536]{1,0:T(8,128)(2,1)S(1)}, bf16[160,1536]{1,0:T(8,128)(2,1)S(1)}, u32[]{:S(2)}, u32[]{:S(2)}) collective-permute-start(bf16[160,1536]{1,0:T(8,128)(2,1)S(1)} %copy-done.4), channel_id=1, source_target_pairs={{0,8},{2,10},{4,12},{6,14},{8,16},{10,18},{12,20},{14,22},{16,24},... | collective-permute-start | bytes 1474568 | tf_op jit(solution)/shard_map/ppermute | solution.py:444
  10.3 23.7 %collective-permute-start.4 = (bf16[160,1536]{1,0:T(8,128)(2,1)S(1)}, bf16[160,1536]{1,0:T(8,128)(2,1)S(1)}, u32[]{:S(2)}, u32[]{:S(2)}) collective-permute-start(bf16[160,1536]{1,0:T(8,128)(2,1)S(1)} %copy-done.4), channel_id=1, source_target_pairs={{0,1},{1,0},{2,3},{3,2},{4,5},{5,4},{6,7},{7,6},{8,9},{9,8},{10,11... | collective-permute-start | bytes 1474568 | tf_op jit(solution)/shard_map/ppermute | solution.py:49
  11.8 54.0 %collective-permute-start.1 = (bf16[672,384]{1,0:T(8,128)(2,1)S(1)}, bf16[672,384]{1,0:T(8,128)(2,1)S(1)}, u32[]{:S(2)}, u32[]{:S(2)}) collective-permute-start(bf16[672,384]{1,0:T(8,128)(2,1)S(1)} %get-tuple-element.84), channel_id=1, source_target_pairs={{0,16},{2,18},{4,20},{6,22},{8,24},{10,26},{12,28},{14,30},{16,0},... | collective-permute-start | bytes 1548296 | tf_op jit(solution)/shard_map/ppermute | solution.py:416
  33.9 31.9 %collective-permute-start.5 = (bf16[160,1536]{1,0:T(8,128)(2,1)S(1)}, bf16[160,1536]{1,0:T(8,128)(2,1)S(1)}, u32[]{:S(2)}, u32[]{:S(2)}) collective-permute-start(bf16[160,1536]{1,0:T(8,128)(2,1)S(1)} %collective-permute-done.3.refs_5_), channel_id=1, source_target_pairs={{0,8},{2,10},{4,12},{6,14},{8,16},{10,18},{12,20},{14,22},{16,24},... | collective-permute-start | bytes 1474568 | tf_op jit(solution)/shard_map/ppermute | solution.py:444
  43.6 22.3 %collective-permute-start.6 = (bf16[160,1536]{1,0:T(8,128)(2,1)S(1)}, bf16[160,1536]{1,0:T(8,128)(2,1)S(1)}, u32[]{:S(2)}, u32[]{:S(2)}) collective-permute-start(bf16[160,1536]{1,0:T(8,128)(2,1)S(1)} %collective-permute-done.3.refs_5_), channel_id=1, source_target_pairs={{0,1},{1,0},{2,3},{3,2},{4,5},{5,4},{6,7},{7,6},{8,9},{9,8},{10,11... | collective-permute-start | bytes 1474568 | tf_op jit(solution)/shard_map/ppermute | solution.py:49
  45.1 36.6 %collective-permute-start.2 = (bf16[672,384]{1,0:T(8,128)(2,1)S(1)}, bf16[672,384]{1,0:T(8,128)(2,1)S(1)}, u32[]{:S(2)}, u32[]{:S(2)}) collective-permute-start(bf16[672,384]{1,0:T(8,128)(2,1)S(1)} %get-tuple-element.85), channel_id=1, source_target_pairs={{0,24},{2,26},{4,28},{6,30},{8,0},{10,2},{12,4},{14,6},{16,8},{18,... | collective-permute-start | bytes 1548296 | tf_op jit(solution)/shard_map/ppermute | solution.py:416
  65.9 19.3 %collective-permute-start.7 = (bf16[160,1536]{1,0:T(8,128)(2,1)S(1)}, bf16[160,1536]{1,0:T(8,128)(2,1)S(1)}, u32[]{:S(2)}, u32[]{:S(2)}) collective-permute-start(bf16[160,1536]{1,0:T(8,128)(2,1)S(1)} %collective-permute-done.5.refs_6_), channel_id=1, source_target_pairs={{0,8},{2,10},{4,12},{6,14},{8,16},{10,18},{12,20},{14,22},{16,24},... | collective-permute-start | bytes 1474568 | tf_op jit(solution)/shard_map/ppermute | solution.py:444
  75.6 11.8 %collective-permute-start.8 = (bf16[160,1536]{1,0:T(8,128)(2,1)S(1)}, bf16[160,1536]{1,0:T(8,128)(2,1)S(1)}, u32[]{:S(2)}, u32[]{:S(2)}) collective-permute-start(bf16[160,1536]{1,0:T(8,128)(2,1)S(1)} %collective-permute-done.5.refs_6_), channel_id=1, source_target_pairs={{0,1},{1,0},{2,3},{3,2},{4,5},{5,4},{6,7},{7,6},{8,9},{9,8},{10,11... | collective-permute-start | bytes 1474568 | tf_op jit(solution)/shard_map/ppermute | solution.py:49
  77.1 12.5 %collective-permute-start.9 = (bf16[512,384]{1,0:T(8,128)(2,1)S(1)}, bf16[512,384]{1,0:T(8,128)(2,1)S(1)}, u32[]{:S(2)}, u32[]{:S(2)}) collective-permute-start(bf16[512,384]{1,0:T(8,128)(2,1)S(1)} %get-tuple-element.86.refs_0_), channel_id=1, source_target_pairs={{0,4},{2,6},{4,0},{6,2},{8,12},{10,14},{12,8},{14,10},{16,20},{18,... | collective-permute-start | bytes 1179656 | tf_op jit(solution)/shard_map/ppermute | solution.py:439
  78.6 19.0 %collective-permute-start.10 = (bf16[512,384]{1,0:T(8,128)(2,1)S(1)}, bf16[512,384]{1,0:T(8,128)(2,1)S(1)}, u32[]{:S(2)}, u32[]{:S(2)}) collective-permute-start(bf16[512,384]{1,0:T(8,128)(2,1)S(1)} %slice.12.refs_1_), channel_id=1, source_target_pairs={{0,4},{2,6},{4,0},{6,2},{8,12},{10,14},{12,8},{14,10},{16,20},{18,... | collective-permute-start | bytes 1179656 | tf_op jit(solution)/shard_map/ppermute | solution.py:447
  81.8 24.2 %collective-permute-start.11 = (bf16[512,384]{1,0:T(8,128)(2,1)S(1)}, bf16[512,384]{1,0:T(8,128)(2,1)S(1)}, u32[]{:S(2)}, u32[]{:S(2)}) collective-permute-start(bf16[512,384]{1,0:T(8,128)(2,1)S(1)} %slice.13.refs_2_), channel_id=1, source_target_pairs={{0,4},{2,6},{4,0},{6,2},{8,12},{10,14},{12,8},{14,10},{16,20},{18,... | collective-permute-start | bytes 1179656 | tf_op jit(solution)/shard_map/ppermute | solution.py:447
  87.4 24.4 %collective-permute-start.12 = (bf16[512,384]{1,0:T(8,128)(2,1)S(1)}, bf16[512,384]{1,0:T(8,128)(2,1)S(1)}, u32[]{:S(2)}, u32[]{:S(2)}) collective-permute-start(bf16[512,384]{1,0:T(8,128)(2,1)S(1)} %slice.14.refs_3_), channel_id=1, source_target_pairs={{0,4},{2,6},{4,0},{6,2},{8,12},{10,14},{12,8},{14,10},{16,20},{18,... | collective-permute-start | bytes 1179656 | tf_op jit(solution)/shard_map/ppermute | solution.py:447
  89.6 24.2 %collective-permute-start.13 = (bf16[2048,384]{1,0:T(8,128)(2,1)S(1)}, bf16[2048,384]{1,0:T(8,128)(2,1)S(1)}, u32[]{:S(2)}, u32[]{:S(2)}) collective-permute-start(bf16[2048,384]{1,0:T(8,128)(2,1)S(1)} %stack.18.refs_0_.refs_5_), channel_id=1, source_target_pairs={{0,2},{2,0},{4,6},{6,4},{8,10},{10,8},{12,14},{14,12},{16,18},{18,... | collective-permute-start | bytes 4718600 | tf_op jit(solution)/shard_map/ppermute | solution.py:454
  112.5 3.5 %collective-permute-start.14 = (bf16[2048,384]{1,0:T(8,128)(2,1)S(1)}, bf16[2048,384]{1,0:T(8,128)(2,1)S(1)}, u32[]{:S(2)}, u32[]{:S(2)}) collective-permute-start(bf16[2048,384]{1,0:T(8,128)(2,1)S(1)} %stack.19.refs_1_.refs_6_), channel_id=1, source_target_pairs={{0,2},{2,0},{4,6},{6,4},{8,10},{10,8},{12,14},{14,12},{16,18},{18,... | collective-permute-start | bytes 4718600 | tf_op jit(solution)/shard_map/ppermute | solution.py:454
  112.6 13.8 %collective-permute-start.15 = (bf16[160,1536]{1,0:T(8,128)(2,1)S(1)}, bf16[160,1536]{1,0:T(8,128)(2,1)S(1)}, u32[]{:S(2)}, u32[]{:S(2)}) collective-permute-start(bf16[160,1536]{1,0:T(8,128)(2,1)S(1)} %collective-permute-done.7.refs_7_), channel_id=1, source_target_pairs={{0,1},{1,0},{2,3},{3,2},{4,5},{5,4},{6,7},{7,6},{8,9},{9,8},{10,11... | collective-permute-start | bytes 1474568 | tf_op jit(solution)/shard_map/ppermute | solution.py:49
  135.8 2.2 collective-permute-start.16
  136.0 22.3 %collective-permute-start.31 = (bf16[1536,384]{1,0:T(8,128)(2,1)S(1)}, bf16[1536,384]{1,0:T(8,128)(2,1)S(1)}, u32[]{:S(2)}, u32[]{:S(2)}) collective-permute-start(bf16[1536,384]{1,0:T(8,128)(2,1)S(1)} %get-tuple-element.153), channel_id=1, source_target_pairs={{0,2},{2,0},{4,6},{6,4},{8,10},{10,8},{12,14},{14,12},{16,18},{18,... | collective-permute-start | bytes 3538952 | tf_op jit(solution)/shard_map/ppermute | solution.py:348
  142.6 10.8 %collective-permute-start.17 = (bf16[2560,128]{1,0:T(8,128)(2,1)S(1)}, bf16[2560,128]{1,0:T(8,128)(2,1)S(1)}, u32[]{:S(2)}, u32[]{:S(2)}) collective-permute-start(bf16[2560,128]{1,0:T(8,128)(2,1)S(1)} %get-tuple-element.109), channel_id=1, source_target_pairs={{0,2},{2,0},{4,6},{6,4},{8,10},{10,8},{12,14},{14,12},{16,18},{18,... | collective-permute-start | bytes 1966088 | tf_op jit(solution)/shard_map/ppermute | solution.py:348
  142.8 10.0 %collective-permute-start.18 = (bf16[1280,128]{1,0:T(8,128)(2,1)S(1)}, bf16[1280,128]{1,0:T(8,128)(2,1)S(1)}, u32[]{:S(2)}, u32[]{:S(2)}) collective-permute-start(bf16[1280,128]{1,0:T(8,128)(2,1)S(1)} %get-tuple-element.113), channel_id=1, source_target_pairs={{0,4},{2,6},{4,0},{6,2},{8,12},{10,14},{12,8},{14,10},{16,20},{18,... | collective-permute-start | bytes 983048 | tf_op jit(solution)/shard_map/ppermute | solution.py:468
  158.3 3.0 %collective-permute-start.26 = (bf16[2560,128]{1,0:T(8,128)(2,1)S(1)}, bf16[2560,128]{1,0:T(8,128)(2,1)S(1)}, u32[]{:S(2)}, u32[]{:S(2)}) collective-permute-start(bf16[2560,128]{1,0:T(8,128)(2,1)S(1)} %get-tuple-element.138), channel_id=1, source_target_pairs={{0,2},{2,0},{4,6},{6,4},{8,10},{10,8},{12,14},{14,12},{16,18},{18,... | collective-permute-start | bytes 1966088 | tf_op jit(solution)/shard_map/ppermute | solution.py:348
  159.2 16.2 %collective-permute-start.32 = (bf16[768,384]{1,0:T(8,128)(2,1)S(1)}, bf16[768,384]{1,0:T(8,128)(2,1)S(1)}, u32[]{:S(2)}, u32[]{:S(2)}) collective-permute-start(bf16[768,384]{1,0:T(8,128)(2,1)S(1)} %get-tuple-element.155), channel_id=1, source_target_pairs={{0,4},{2,6},{4,0},{6,2},{8,12},{10,14},{12,8},{14,10},{16,20},{18,... | collective-permute-start | bytes 1769480 | tf_op jit(solution)/shard_map/ppermute | solution.py:476
  160.7 21.7 %collective-permute-start.22 = (bf16[1280,128]{1,0:T(8,128)(2,1)S(1)}, bf16[1280,128]{1,0:T(8,128)(2,1)S(1)}, u32[]{:S(2)}, u32[]{:S(2)}) collective-permute-start(bf16[1280,128]{1,0:T(8,128)(2,1)S(1)} %get-tuple-element.127), channel_id=1, source_target_pairs={{0,4},{2,6},{4,0},{6,2},{8,12},{10,14},{12,8},{14,10},{16,20},{18,... | collective-permute-start | bytes 983048 | tf_op jit(solution)/shard_map/ppermute | solution.py:468
  162.0 27.0 %collective-permute-start.27 = (bf16[1280,128]{1,0:T(8,128)(2,1)S(1)}, bf16[1280,128]{1,0:T(8,128)(2,1)S(1)}, u32[]{:S(2)}, u32[]{:S(2)}) collective-permute-start(bf16[1280,128]{1,0:T(8,128)(2,1)S(1)} %get-tuple-element.140), channel_id=1, source_target_pairs={{0,4},{2,6},{4,0},{6,2},{8,12},{10,14},{12,8},{14,10},{16,20},{18,... | collective-permute-start | bytes 983048 | tf_op jit(solution)/shard_map/ppermute | solution.py:475
  163.5 15.1 %collective-permute-start.19 = (bf16[480,128]{1,0:T(8,128)(2,1)S(1)}, bf16[480,128]{1,0:T(8,128)(2,1)S(1)}, u32[]{:S(2)}, u32[]{:S(2)}) collective-permute-start(bf16[480,128]{1,0:T(8,128)(2,1)S(1)} %get-tuple-element.123), channel_id=1, source_target_pairs={{0,24},{2,26},{4,28},{6,30},{8,0},{10,2},{12,4},{14,6},{16,8},{18,... | collective-permute-start | bytes 368648 | tf_op jit(solution)/shard_map/ppermute | solution.py:416
  163.5 19.5 %collective-permute-start.20 = (bf16[480,128]{1,0:T(8,128)(2,1)S(1)}, bf16[480,128]{1,0:T(8,128)(2,1)S(1)}, u32[]{:S(2)}, u32[]{:S(2)}) collective-permute-start(bf16[480,128]{1,0:T(8,128)(2,1)S(1)} %get-tuple-element.124), channel_id=1, source_target_pairs={{0,16},{2,18},{4,20},{6,22},{8,24},{10,26},{12,28},{14,30},{16,0},... | collective-permute-start | bytes 368648 | tf_op jit(solution)/shard_map/ppermute | solution.py:416
  176.0 23.7 %collective-permute-start.33 = (bf16[192,384]{1,0:T(8,128)(2,1)S(1)}, bf16[192,384]{1,0:T(8,128)(2,1)S(1)}, u32[]{:S(2)}, u32[]{:S(2)}) collective-permute-start(bf16[192,384]{1,0:T(8,128)(2,1)S(1)} %get-tuple-element.157), channel_id=1, source_target_pairs={{0,8},{2,10},{4,12},{6,14},{8,16},{10,18},{12,20},{14,22},{16,24},... | collective-permute-start | bytes 442376 | tf_op jit(solution)/shard_map/ppermute | solution.py:416
  178.6 24.7 %collective-permute-start.34 = (bf16[192,384]{1,0:T(8,128)(2,1)S(1)}, bf16[192,384]{1,0:T(8,128)(2,1)S(1)}, u32[]{:S(2)}, u32[]{:S(2)}) collective-permute-start(bf16[192,384]{1,0:T(8,128)(2,1)S(1)} %get-tuple-element.158), channel_id=1, source_target_pairs={{0,16},{2,18},{4,20},{6,22},{8,24},{10,26},{12,28},{14,30},{16,0},... | collective-permute-start | bytes 442376 | tf_op jit(solution)/shard_map/ppermute | solution.py:416
  182.4 20.9 %collective-permute-start.35 = (bf16[192,384]{1,0:T(8,128)(2,1)S(1)}, bf16[192,384]{1,0:T(8,128)(2,1)S(1)}, u32[]{:S(2)}, u32[]{:S(2)}) collective-permute-start(bf16[192,384]{1,0:T(8,128)(2,1)S(1)} %get-tuple-element.159), channel_id=1, source_target_pairs={{0,24},{2,26},{4,28},{6,30},{8,0},{10,2},{12,4},{14,6},{16,8},{18,... | collective-permute-start | bytes 442376 | tf_op jit(solution)/shard_map/ppermute | solution.py:416
  183.0 9.1 %collective-permute-start.21 = (bf16[480,128]{1,0:T(8,128)(2,1)S(1)}, bf16[480,128]{1,0:T(8,128)(2,1)S(1)}, u32[]{:S(2)}, u32[]{:S(2)}) collective-permute-start(bf16[480,128]{1,0:T(8,128)(2,1)S(1)} %get-tuple-element.125), channel_id=1, source_target_pairs={{0,8},{2,10},{4,12},{6,14},{8,16},{10,18},{12,20},{14,22},{16,24},... | collective-permute-start | bytes 368648 | tf_op jit(solution)/shard_map/ppermute | solution.py:416
  189.0 10.4 %collective-permute-start.23 = (bf16[480,128]{1,0:T(8,128)(2,1)S(1)}, bf16[480,128]{1,0:T(8,128)(2,1)S(1)}, u32[]{:S(2)}, u32[]{:S(2)}) collective-permute-start(bf16[480,128]{1,0:T(8,128)(2,1)S(1)} %get-tuple-element.133), channel_id=1, source_target_pairs={{0,24},{2,26},{4,28},{6,30},{8,0},{10,2},{12,4},{14,6},{16,8},{18,... | collective-permute-start | bytes 368648 | tf_op jit(solution)/shard_map/ppermute | solution.py:416
  192.1 17.4 %collective-permute-start.24 = (bf16[480,128]{1,0:T(8,128)(2,1)S(1)}, bf16[480,128]{1,0:T(8,128)(2,1)S(1)}, u32[]{:S(2)}, u32[]{:S(2)}) collective-permute-start(bf16[480,128]{1,0:T(8,128)(2,1)S(1)} %get-tuple-element.134), channel_id=1, source_target_pairs={{0,16},{2,18},{4,20},{6,22},{8,24},{10,26},{12,28},{14,30},{16,0},... | collective-permute-start | bytes 368648 | tf_op jit(solution)/shard_map/ppermute | solution.py:416
  199.4 10.1 %collective-permute-start.25 = (bf16[480,128]{1,0:T(8,128)(2,1)S(1)}, bf16[480,128]{1,0:T(8,128)(2,1)S(1)}, u32[]{:S(2)}, u32[]{:S(2)}) collective-permute-start(bf16[480,128]{1,0:T(8,128)(2,1)S(1)} %get-tuple-element.135), channel_id=1, source_target_pairs={{0,8},{2,10},{4,12},{6,14},{8,16},{10,18},{12,20},{14,22},{16,24},... | collective-permute-start | bytes 368648 | tf_op jit(solution)/shard_map/ppermute | solution.py:416
  199.7 9.8 %collective-permute-start.28 = (bf16[480,128]{1,0:T(8,128)(2,1)S(1)}, bf16[480,128]{1,0:T(8,128)(2,1)S(1)}, u32[]{:S(2)}, u32[]{:S(2)}) collective-permute-start(bf16[480,128]{1,0:T(8,128)(2,1)S(1)} %get-tuple-element.146), channel_id=1, source_target_pairs={{0,24},{2,26},{4,28},{6,30},{8,0},{10,2},{12,4},{14,6},{16,8},{18,... | collective-permute-start | bytes 368648 | tf_op jit(solution)/shard_map/ppermute | solution.py:416
  203.3 12.9 %collective-permute-start.29 = (bf16[480,128]{1,0:T(8,128)(2,1)S(1)}, bf16[480,128]{1,0:T(8,128)(2,1)S(1)}, u32[]{:S(2)}, u32[]{:S(2)}) collective-permute-start(bf16[480,128]{1,0:T(8,128)(2,1)S(1)} %get-tuple-element.147), channel_id=1, source_target_pairs={{0,16},{2,18},{4,20},{6,22},{8,24},{10,26},{12,28},{14,30},{16,0},... | collective-permute-start | bytes 368648 | tf_op jit(solution)/shard_map/ppermute | solution.py:416
  203.3 12.9 %collective-permute-start.30 = (bf16[480,128]{1,0:T(8,128)(2,1)S(1)}, bf16[480,128]{1,0:T(8,128)(2,1)S(1)}, u32[]{:S(2)}, u32[]{:S(2)}) collective-permute-start(bf16[480,128]{1,0:T(8,128)(2,1)S(1)} %get-tuple-element.148), channel_id=1, source_target_pairs={{0,8},{2,10},{4,12},{6,14},{8,16},{10,18},{12,20},{14,22},{16,24},... | collective-permute-start | bytes 368648 | tf_op jit(solution)/shard_map/ppermute | solution.py:416

commit v4 on v3

--- a/solution.py
+++ b/solution.py
@@ -9,7 +9,7 @@
 from jax.sharding import PartitionSpec as P
 
 HD = 128
-VMEM_BYTES = 32 * 1024 * 1024
+VMEM_BYTES = 24 * 1024 * 1024
 BF16 = jnp.bfloat16
 F32 = jnp.float32
 
@@ -84,18 +84,27 @@
     )(*args)
 
 
-def pack_kernel(n_groups, ids, q, k, v, w, *outs):
+def pack_kernel(n_groups, ids, q, k, v, w, *refs):
+    outs, sems = refs[:-1], refs[-1]
     rows, depth = q.shape[0], w.shape[0]
     gw = q.shape[1] // n_groups
+    copies = []
     for s in range(n_groups):
         cols = pl.ds(aligned(lax.rem(ids[0] + s, n_groups) * gw, HD), gw)
-        outs[s][:rows, :] = k[:, cols]
-        outs[s][rows : 2 * rows, :] = v[:, cols]
-        outs[s][2 * rows : 2 * rows + depth, :] = w[:, cols]
-        if s == 0:
-            outs[n_groups][...] = q[:, cols]
-        else:
-            outs[s][2 * rows + depth :, :] = q[:, cols]
+        own = outs[n_groups] if s == 0 else outs[s].at[pl.ds(2 * rows + depth, rows), :]
+        for source, target in (
+            (k, outs[s].at[pl.ds(0, rows), :]),
+            (v, outs[s].at[pl.ds(rows, rows), :]),
+            (w, outs[s].at[pl.ds(2 * rows, depth), :]),
+            (q, own),
+        ):
+            copies.append(
+                pltpu.make_async_copy(source.at[:, cols], target, sems.at[len(copies)])
+            )
+    for copy in copies:
+        copy.start()
+    for copy in copies:
+        copy.wait()
 
 
 def pack(ids, q, k, v, w, n_groups):
@@ -107,7 +116,15 @@
         + [jax.ShapeDtypeStruct((shared + rows, gw), BF16)] * (n_groups - 1)
         + [jax.ShapeDtypeStruct((rows, gw), BF16)]
     )
-    return whole_call(functools.partial(pack_kernel, n_groups), shapes, (ids, q, k, v, w), "pack")
+    return pl.pallas_call(
+        functools.partial(pack_kernel, n_groups),
+        out_shape=shapes,
+        in_specs=[smem()] + [pl.BlockSpec(memory_space=pltpu.HBM)] * 4,
+        out_specs=[vmem()] * len(shapes),
+        scratch_shapes=[pltpu.SemaphoreType.DMA((4 * n_groups,))],
+        compiler_params=pltpu.CompilerParams(vmem_limit_bytes=60 * 1024 * 1024),
+        name="pack",
+    )(ids, q, k, v, w)
 
 
 def stack_kernel(n_groups, rows, ids, *refs):
@@ -237,27 +254,28 @@
         dq_outs[s][...] = dq_all[s * rows : (s + 1) * rows, :]
 
 
-def backward(head, q, blocks, part, probs, out, inverse, grad_attn, n_groups):
+def backward(head, count, q, blocks, part, probs, out, inverse, grad_attn, n_groups):
     n_q = q.shape[0]
     rows = n_q // n_groups
     seq_len = part * len(blocks)
     chunk = part if part <= 640 else math.gcd(part, 512)
     per_half = max(1, len(blocks) // 2)
-    column = pl.BlockSpec((n_q, HD), lambda i: (0, head))
+    column = pl.BlockSpec((n_q, HD), lambda i: (0, head + i))
     results = pl.pallas_call(
         functools.partial(backward_kernel, n_groups, chunk, 1.0 / math.sqrt(HD)),
-        grid=(1,),
-        out_shape=[jax.ShapeDtypeStruct((rows, HD), BF16)] * n_groups
-        + [jax.ShapeDtypeStruct((per_half * 2 * part, HD), BF16)] * 2,
+        grid=(count,),
+        out_shape=[jax.ShapeDtypeStruct((rows, count * HD), BF16)] * n_groups
+        + [jax.ShapeDtypeStruct((per_half * 2 * part, count * HD), BF16)] * 2,
         in_specs=[
             column,
-            pl.BlockSpec((1, seq_len, n_q), lambda i: (head, 0, 0)),
+            pl.BlockSpec((1, seq_len, n_q), lambda i: (head + i, 0, 0)),
             column,
-            pl.BlockSpec((1, 1, n_q), lambda i: (head, 0, 0)),
+            pl.BlockSpec((1, 1, n_q), lambda i: (head + i, 0, 0)),
             column,
         ]
-        + [pl.BlockSpec((2 * part, HD), lambda i: (0, head))] * len(blocks),
-        out_specs=[vmem()] * (n_groups + 2),
+        + [pl.BlockSpec((2 * part, HD), lambda i: (0, head + i))] * len(blocks),
+        out_specs=[pl.BlockSpec((rows, HD), lambda i: (0, i))] * n_groups
+        + [pl.BlockSpec((per_half * 2 * part, HD), lambda i: (0, i))] * 2,
         scratch_shapes=[pltpu.VMEM((n_q, HD), BF16)],
         compiler_params=params(),
         cost_estimate=pl.CostEstimate(
@@ -362,33 +380,36 @@
 
 
 def finish(ids, kept, other, dq, n_groups):
-    rows = dq[0].shape[0]
+    rows, cols = dq[0].shape
     return whole_call(
         functools.partial(finish_kernel, n_groups),
-        [jax.ShapeDtypeStruct((3 * rows, HD), BF16)] * n_groups,
+        [jax.ShapeDtypeStruct((3 * rows, cols), BF16)] * n_groups,
         (ids, kept, other, *dq),
         "finish",
     )
 
 
-def unpack_kernel(n_groups, heads, ids, *refs):
-    rows = refs[-1].shape[0]
-    for h in range(heads):
+def unpack_kernel(n_groups, ids, *refs):
+    pieces, outs = refs[:-3], refs[-3:]
+    rows, gw = outs[0].shape[0], outs[0].shape[1] // n_groups
+    before = 0
+    for c in range(0, len(pieces), n_groups):
+        cols = pieces[c].shape[1]
         for s in range(n_groups):
-            start = (lax.rem(ids[0] + s, n_groups) * heads + h) * HD
-            for i, out in enumerate(refs[-3:]):
-                piece = refs[h * n_groups + s][i * rows : (i + 1) * rows, :]
-                out[:, pl.ds(aligned(start, HD), HD)] = piece
-
-
-def unpack(ids, pieces, n_groups):
-    heads = len(pieces)
-    rows = pieces[0][0].shape[0] // 3
-    shape = jax.ShapeDtypeStruct((rows, HD * heads * n_groups), BF16)
+            start = lax.rem(ids[0] + s, n_groups) * gw + before
+            for i, out in enumerate(outs):
+                piece = pieces[c + s][i * rows : (i + 1) * rows, :]
+                out[:, pl.ds(aligned(start, HD), cols)] = piece
+        before += cols
+
+
+def unpack(ids, chunks, n_groups):
+    rows = chunks[0][0].shape[0] // 3
+    gw = sum(pieces[0].shape[1] for pieces in chunks)
     return whole_call(
-        functools.partial(unpack_kernel, n_groups, heads),
-        [shape] * 3,
-        (ids, *[p for per_head in pieces for p in per_head]),
+        functools.partial(unpack_kernel, n_groups),
+        [jax.ShapeDtypeStruct((rows, gw * n_groups), BF16)] * 3,
+        (ids, *[piece for pieces in chunks for piece in pieces]),
         "unpack",
     )
 
@@ -432,51 +453,69 @@
     frame = lax.axis_index("frame")
     ids = jnp.stack([frame // n_tok, frame % n_tok, lax.axis_index("space")]).astype(jnp.int32)
 
+    tie = lax.optimization_barrier
+    last = xor_pairs(n_frame, tok_bits[-1])
+
     *pieces, own_q = pack(ids, queries, keys, values, proj_weight.T, n_groups)
     pieces = exchange(pieces, n_groups, n_tok, 1)
     q_pieces = pieces[1:]
-    first = xor_pairs(n_frame, tok_bits[-1])
-    own, others, by_piece = [pieces[0]], [lax.ppermute(pieces[0], "frame", first)], []
-    ring = grad_out
-    for s in range(n_groups):
-        across = gather_blocks(ring, "space", n_space, space_bits)
+    own, others = [pieces[0]], [lax.ppermute(pieces[0], "frame", last)]
+    ring = [grad_out]
+    across = [gather_blocks(grad_out, "space", n_space, space_bits)]
+    for s in range(1, n_groups):
+        piece = pieces[s][:shared]
+        if s == 1:
+            ring[0], piece, others[0], *across[0] = tie((ring[0], piece, others[0], *across[0]))
+            ring.append(lax.ppermute(ring[0], "frame", shift_pairs(n_groups, n_tok, 1)))
+        own.append(piece)
+        others.append(lax.ppermute(piece, "frame", last))
+        if s == 1 and n_groups > 2:
+            ring[1], others[1], *pieces[2:] = tie((ring[1], others[1], *pieces[2:]))
+
+    for s in range(1, n_groups):
+        across.append(gather_blocks(ring[s], "space", n_space, space_bits))
         if s + 1 < n_groups:
-            ring = lax.ppermute(ring, "frame", shift_pairs(n_groups, n_tok, 1))
-            ring, piece, *across = lax.optimization_barrier((ring, pieces[s + 1][:shared], *across))
-            own.append(piece)
-            others.append(lax.ppermute(piece, "frame", first))
-        by_piece.append(across)
-    grads = [by_piece[s][r] for r in range(n_space) for s in range(n_groups)]
+            arriving = lax.ppermute(ring[s], "frame", shift_pairs(n_groups, n_tok, 1))
+            count = n_groups if s == 1 else 0
+            tied = tie((arriving, *across[s], *others[:count]))
+            arriving, across[s] = tied[0], list(tied[1 : 1 + n_space])
+            others[:count] = tied[1 + n_space :]
+            ring.append(arriving)
 
     q = stack_queries(ids, own_q, q_pieces)
     blocks = [stack(ids, own, rows), stack(ids, others, rows)]
     for bit in reversed(tok_bits[:-1]):
         blocks = blocks + [lax.ppermute(b, "frame", xor_pairs(n_frame, bit)) for b in blocks]
-
     part = n_groups * rows
     probs, out, inverse = forward(q, blocks, part)
+    grads = [across[s][r] for r in range(n_space) for s in range(n_groups)]
     grad_attn, kept, sent = project(ids, out, blocks, grads, depth, n_groups, n_tok, n_space)
-    last = xor_pairs(n_frame, tok_bits[-1])
+
+    def attention_chunk(head, count, q, *before):
+        dq, halves = backward(
+            head, count, q, blocks, part, probs, out, inverse, grad_attn, n_groups
+        )
+        kept, sent, *before = tie((*halves, *before))
+        return dq, halve(ids, kept, sent, n_frame, tok_bits), *before
+
     proj_kept, proj_sent = halve(ids, kept, sent, n_frame, tok_bits)
-    here, sums, finished = q, (), []
-    for h in range(heads):
-        if h > 0:
-            here, kept, sent, *sums = lax.optimization_barrier((q, kept, sent, *sums))
-        if h > 1:
-            finished[-1] = sums
-        if h > 0:
-            other = lax.ppermute(sent, "frame", last)
-            kept_dq = (kept, other, dq)
-        dq, halves = backward(h, here, blocks, part, probs, out, inverse, grad_attn, n_groups)
-        if h > 0:
-            sums = finish(ids, *kept_dq, n_groups)
-            finished.append(sums)
-        kept, sent = halve(ids, *halves, n_frame, tok_bits)
-    finished.append(finish(ids, kept, lax.ppermute(sent, "frame", last), dq, n_groups))
-    proj = add_parts(ids, proj_kept, lax.ppermute(proj_sent, "frame", last), n_groups)
-    proj = exchange(proj, n_groups, n_tok, 1)
+    dq, (kept, sent) = attention_chunk(0, 1, q)
+    returned = []
+    if heads > 1:
+        q, kept, sent, proj_kept, proj_sent = tie((q, kept, sent, proj_kept, proj_sent))
+        other = lax.ppermute(sent, "frame", last)
+        next_dq, (next_kept, sent), other = attention_chunk(1, heads - 1, q, other)
+        sums = finish(ids, kept, other, dq, n_groups)
+        proj_sent, *sums = tie((proj_sent, *sums))
+        returned.append(exchange(sums, n_groups, n_tok, -1))
+        dq, kept = next_dq, next_kept
+    other = lax.ppermute(proj_sent, "frame", last)
+    proj = exchange(add_parts(ids, proj_kept, other, n_groups), n_groups, n_tok, 1)
+    other = lax.ppermute(sent, "frame", last)
+    if returned:
+        other, *returned[0][1:-1] = tie((other, *returned[0][1:-1]))
+    returned.append(exchange(finish(ids, kept, other, dq, n_groups), n_groups, n_tok, -1))
     grad_proj = join(ids, proj, n_groups).T
-    returned = [exchange(sums, n_groups, n_tok, -1) for sums in finished]
     grad_queries, grad_keys, grad_values = unpack(ids, returned, n_groups)
     return (grad_queries, grad_keys, grad_values, grad_proj)
 

time: 219 us -> 225 us (1.027)
  starting transfers between devices: 62.4 us -> 81 us
  waiting for transfers between devices: 111 us -> 98.6 us
  local copies, waits for them, and re-layouts: 4.28 us -> 0.14 us
  Pallas kernels: 39.7 us -> 42 us
    ppermute x9 -> x8, starting transfers between devices: 29.1 us -> 49.4 us  [the longest x2 22.4 us: local(): arriving = lax.ppermute(ring[s], 'frame', shift_pairs(n_groups, n_tok, 1))]
    ppermute x15 -> x12, waiting for transfers between devices: 46.7 us -> 27.2 us  [exchange(): lax.ppermute(pieces[s], 'frame', shift_pairs(n_groups, n_tok, sign * s))]
    ppermute x9 -> x8, waiting for transfers between devices: 45.9 us -> 65.3 us  [the longest x1 25.3 us: local(): other = lax.ppermute(proj_sent, 'frame', last)]
    ppermute x2, waiting for transfers between devices: 12.3 us -> 0.01 us  [local(): other = lax.ppermute(sent, 'frame', last)]
    unnamed x10 -> x8, local copies, waits for them, and re-layouts: 4.16 us -> 0.02 us
    pallas_call x0 -> x1, Pallas kernels: none -> 3.73 us  [pack(): pl.pallas_call(functools.partial(pack_kernel, n_groups), out_shape=shapes...]
    ppermute x4 -> x3, waiting for transfers between devices: 1.59 us -> 4.69 us  [halve(): other = lax.ppermute(sent, 'frame', xor_pairs(n_frame, bit))]
    pallas_call x15 -> x12, Pallas kernels: 17.3 us -> 15.3 us  [whole_call(): pl.pallas_call(body, out_shape=out_shape, in_specs=[smem()] + [vmem()] *...]
  transfers between devices with their start and end apart: 36 -> 31, of which waited for: 18 -> 15; matrix products, arithmetic and copies ran while one was open for 0% -> 0% of each run, Pallas kernels for 13% -> 13%
where the time goes in v4:
time: 225 us; the launch traced here: 223 us
  waiting for transfers between devices  98.6 us (44%)
  starting transfers between devices  81 us (36%)
  Pallas kernels  42 us (19%)
    ppermute x12, waiting for transfers between devices, exchange(): lax.ppermute(pieces[s], 'frame', shift_pairs(n_groups, n_tok, sign * s))  27.2 us
    ppermute x1, waiting for transfers between devices, local(): other = lax.ppermute(proj_sent, 'frame', last)  25.3 us
    ppermute x12, starting transfers between devices, exchange(): lax.ppermute(pieces[s], 'frame', shift_pairs(n_groups, n_tok, sign * s))  24 us
    ppermute x2, starting transfers between devices, local(): arriving = lax.ppermute(ring[s], 'frame', shift_pairs(n_groups, n_tok, 1))  22.4 us
    ppermute x3, waiting for transfers between devices, local(): others.append(lax.ppermute(piece, 'frame', last))  22.4 us
    ppermute x1, starting transfers between devices, local(): ring.append(lax.ppermute(ring[0], 'frame', shift_pairs(n_groups, n_tok, 1)))  20.8 us
    pallas_call x12, Pallas kernels, whole_call(): pl.pallas_call(body, out_shape=out_shape, in_specs=[smem()] + [vmem()] *...  15.3 us
    ppermute x2, waiting for transfers between devices, local(): arriving = lax.ppermute(ring[s], 'frame', shift_pairs(n_groups, n_tok, 1))  14.5 us
  transfers between devices with their start and end apart: 31, of which 15 were waited for; matrix products, arithmetic and copies ran while one was open for 0% of the time, Pallas kernels for 13%

profile of v4, /device:TPU:0, one launch (start us, length us, event | category | flops | bytes accessed | tf_op | source)
XLA Modules:
  0.0 223.3 jit_solution(12171424660882751158)
XLA Ops:
  0.7 0.6 pad_add_fusion.ids
  1.3 3.7 %pack.1 = (bf16[512,384]{1,0:T(8,128)(2,1)}, bf16[672,384]{1,0:T(8,128)(2,1)}, bf16[672,384]{1,0:T(8,128)(2,1)}, bf16[672,384]{1,0:T(8,128)(2,1)}, bf16[160,384]{1,0:T(8,128)(2,1)}) custom-call(s32[3]{0:T(128)} %pad_add_fusion.ids, bf16[160,1536]{1,0:T(8,128)(2,1)} %q.1, bf16[160,1536]{1,0:T(8,128)(2,1)} %k.1, bf16[160,1536]{1,0:T(8,128)(2,1)} %v.1, ...), custom_call_target="tpu_custom_call" | custom-call | tf_op jit(solution)/shard_map/pack/pallas_call | solution.py:119
  5.0 0.0 copy-start
  5.0 3.1 %collective-permute-start = (bf16[672,384]{1,0:T(8,128)(2,1)}, bf16[672,384]{1,0:T(8,128)(2,1)S(1)}, u32[]{:S(2)}, u32[]{:S(2)}) collective-permute-start(bf16[672,384]{1,0:T(8,128)(2,1)} %get-tuple-element.86), channel_id=1, source_target_pairs={{0,8},{2,10},{4,12},{6,14},{8,16},{10,18},{12,20},{14,22},{16,24},... | collective-permute-start | bytes 1548296 | tf_op jit(solution)/shard_map/ppermute | solution.py:437
  8.1 1.5 collective-permute-start.4
  9.6 1.5 collective-permute-start.3
  11.1 2.6 %collective-permute-start.1 = (bf16[672,384]{1,0:T(8,128)(2,1)}, bf16[672,384]{1,0:T(8,128)(2,1)S(1)}, u32[]{:S(2)}, u32[]{:S(2)}) collective-permute-start(bf16[672,384]{1,0:T(8,128)(2,1)} %get-tuple-element.87), channel_id=1, source_target_pairs={{0,16},{2,18},{4,20},{6,22},{8,24},{10,26},{12,28},{14,30},{16,0},... | collective-permute-start | bytes 1548296 | tf_op jit(solution)/shard_map/ppermute | solution.py:437
  13.7 1.3 collective-permute-start.2
  15.0 8.0 %collective-permute-done.refs_0_ = bf16[672,384]{1,0:T(8,128)(2,1)S(1)} collective-permute-done((bf16[672,384]{1,0:T(8,128)(2,1)}, bf16[672,384]{1,0:T(8,128)(2,1)S(1)}, u32[]{:S(2)}, u32[]{:S(2)}) %collective-permute-start) | collective-permute-done | bytes 516128 | tf_op jit(solution)/shard_map/ppermute | solution.py:437
  23.1 0.0 collective-permute-done.3.refs_0_
  23.1 20.8 %collective-permute-start.5 = (bf16[160,1536]{1,0:T(8,128)(2,1)S(1)}, bf16[160,1536]{1,0:T(8,128)(2,1)S(1)}, u32[]{:S(2)}, u32[]{:S(2)}) collective-permute-start(bf16[160,1536]{1,0:T(8,128)(2,1)S(1)} %copy-done.3), channel_id=1, source_target_pairs={{0,8},{2,10},{4,12},{6,14},{8,16},{10,18},{12,20},{14,22},{16,24},... | collective-permute-start | bytes 1474568 | tf_op jit(solution)/shard_map/ppermute | solution.py:469
  43.9 1.5 collective-permute-start.6
  45.4 6.3 %collective-permute-done.6.refs_1_ = bf16[512,384]{1,0:T(8,128)(2,1)S(1)} collective-permute-done((bf16[512,384]{1,0:T(8,128)(2,1)S(1)}, bf16[512,384]{1,0:T(8,128)(2,1)S(1)}, u32[]{:S(2)}, u32[]{:S(2)}) %collective-permute-start.6) | collective-permute-done | bytes 393248 | tf_op jit(solution)/shard_map/ppermute | solution.py:471
  51.7 3.2 %collective-permute-done.5.refs_5_ = bf16[160,1536]{1,0:T(8,128)(2,1)S(1)} collective-permute-done((bf16[160,1536]{1,0:T(8,128)(2,1)S(1)}, bf16[160,1536]{1,0:T(8,128)(2,1)S(1)}, u32[]{:S(2)}, u32[]{:S(2)}) %collective-permute-start.5) | collective-permute-done | bytes 491552 | tf_op jit(solution)/shard_map/ppermute | solution.py:469
  54.9 22.0 %collective-permute-start.7 = (bf16[160,1536]{1,0:T(8,128)(2,1)S(1)}, bf16[160,1536]{1,0:T(8,128)(2,1)S(1)}, u32[]{:S(2)}, u32[]{:S(2)}) collective-permute-start(bf16[160,1536]{1,0:T(8,128)(2,1)S(1)} %collective-permute-done.5.refs_5_), channel_id=1, source_target_pairs={{0,8},{2,10},{4,12},{6,14},{8,16},{10,18},{12,20},{14,22},{16,24},... | collective-permute-start | bytes 1474568 | tf_op jit(solution)/shard_map/ppermute | solution.py:478
  76.9 1.5 collective-permute-start.8
  78.5 1.6 collective-permute-start.9
  80.1 0.5 collective-permute-start.10
  80.6 0.7 stack.18.refs_0_.refs_5_
  81.3 0.0 copy-start.1
  81.3 0.1 collective-permute-start.11
  81.4 9.2 %collective-permute-done.9.refs_2_ = bf16[512,384]{1,0:T(8,128)(2,1)S(1)} collective-permute-done((bf16[512,384]{1,0:T(8,128)(2,1)S(1)}, bf16[512,384]{1,0:T(8,128)(2,1)S(1)}, u32[]{:S(2)}, u32[]{:S(2)}) %collective-permute-start.9) | collective-permute-done | bytes 393248 | tf_op jit(solution)/shard_map/ppermute | solution.py:471
  90.7 6.9 %collective-permute-done.10.refs_3_ = bf16[512,384]{1,0:T(8,128)(2,1)S(1)} collective-permute-done((bf16[512,384]{1,0:T(8,128)(2,1)S(1)}, bf16[512,384]{1,0:T(8,128)(2,1)S(1)}, u32[]{:S(2)}, u32[]{:S(2)}) %collective-permute-start.10) | collective-permute-done | bytes 393248 | tf_op jit(solution)/shard_map/ppermute | solution.py:471
  97.5 0.7 stack.19.refs_1_.refs_6_
  98.2 0.1 collective-permute-start.12
  98.3 0.4 collective-permute-start.13
  98.7 0.5 collective-permute-start.14
  99.2 14.5 %collective-permute-done.13.refs_7_ = bf16[160,1536]{1,0:T(8,128)(2,1)S(1)} collective-permute-done((bf16[160,1536]{1,0:T(8,128)(2,1)S(1)}, bf16[160,1536]{1,0:T(8,128)(2,1)S(1)}, u32[]{:S(2)}, u32[]{:S(2)}) %collective-permute-start.13) | collective-permute-done | bytes 491552 | tf_op jit(solution)/shard_map/ppermute | solution.py:478
  113.7 0.5 collective-permute-start.15
  114.2 0.6 stack_queries.1.q_in.refs_0_
  114.8 10.2 %forward.1 = (bf16[3,2560,640]{2,1,0:T(8,128)(2,1)S(1)}, bf16[640,384]{1,0:T(8,128)(2,1)S(1)}, f32[3,1,640]{2,1,0:T(1,128)S(1)}) custom-call(bf16[640,384]{1,0:T(8,128)(2,1)S(1)} %stack_queries.1.q_in.refs_0_, bf16[2048,384]{1,0:T(8,128)(2,1)S(1)} %stack.18.refs_0_.refs_5_, bf16[2048,384]{1,0:T(8,128)(2,1)S(1)} %stack.19.refs_1_.refs_6_, ...), custom_call_target="tpu_custom_call" | custom-call | flops 2516582400 | bytes 9830400 | tf_op jit(solution)/shard_map/forward/pallas_call | solution.py:200
  125.1 1.4 collective-permute-done.15.refs_11_
  126.5 5.5 %project.1 = (bf16[640,384]{1,0:T(8,128)(2,1)S(1)}, bf16[1536,384]{1,0:T(8,128)(2,1)S(1)}, bf16[1536,384]{1,0:T(8,128)(2,1)S(1)}) custom-call(s32[3]{0:T(128)S(1)} %copy-done.2, bf16[640,384]{1,0:T(8,128)(2,1)S(1)} %get-tuple-element.102.attn.refs_2_, bf16[2048,384]{1,0:T(8,128)(2,1)S(1)} %stack.18.refs_0_.refs_5_, ...), custom_call_target="tpu_custom_call" | custom-call | flops 3019898880 | bytes 9633792 | tf_op jit(solution)/shard_map/project/pallas_call | solution.py:75
  132.0 0.1 collective-permute-start.17
  132.1 3.9 %backward.2 = (bf16[160,128]{1,0:T(8,128)(2,1)S(1)}, bf16[160,128]{1,0:T(8,128)(2,1)S(1)}, bf16[160,128]{1,0:T(8,128)(2,1)S(1)}, bf16[160,128]{1,0:T(8,128)(2,1)...) custom-call(bf16[640,384]{1,0:T(8,128)(2,1)S(1)} %stack_queries.1.q_in.refs_0_, ...), custom_call_target="tpu_custom_call" | custom-call | flops 81920 | bytes 163840 | tf_op jit(solution)/shard_map/backward/pallas_call | solution.py:264
  136.0 0.6 collective-permute-start.16
  136.5 1.7 collective-permute-done.16.other
  138.3 0.7 add_parts.4
  139.0 0.8 add_parts.5
  139.8 1.6 collective-permute-start.18
  141.4 8.8 %backward.3 = (bf16[160,256]{1,0:T(8,128)(2,1)S(1)}, bf16[160,256]{1,0:T(8,128)(2,1)S(1)}, bf16[160,256]{1,0:T(8,128)(2,1)S(1)}, bf16[160,256]{1,0:T(8,128)(2,1)...) custom-call(bf16[640,384]{1,0:T(8,128)(2,1)S(1)} %stack_queries.1.q_in.refs_0_, ...), custom_call_target="tpu_custom_call" | custom-call | flops 81920 | bytes 163840 | tf_op jit(solution)/shard_map/backward/pallas_call | solution.py:264
  150.2 0.1 collective-permute-start.19
  150.3 3.0 %collective-permute-done.19.other = bf16[2560,256]{1,0:T(8,128)(2,1)S(1)} collective-permute-done((bf16[2560,256]{1,0:T(8,128)(2,1)S(1)}, bf16[2560,256]{1,0:T(8,128)(2,1)S(1)}, u32[]{:S(2)}, u32[]{:S(2)}) %collective-permute-start.19) | collective-permute-done | bytes 1310752 | tf_op jit(solution)/shard_map/ppermute | solution.py:366
  153.3 0.8 add_parts.6
  154.2 1.1 collective-permute-start.20
  155.3 0.6 finish.2
  155.9 1.0 collective-permute-start.27
  157.0 1.4 collective-permute-start.21
  158.4 25.3 %collective-permute-done.27.other = bf16[768,384]{1,0:T(8,128)(2,1)S(1)} collective-permute-done((bf16[768,384]{1,0:T(8,128)(2,1)S(1)}, bf16[768,384]{1,0:T(8,128)(2,1)S(1)}, u32[]{:S(2)}, u32[]{:S(2)}) %collective-permute-start.27) | collective-permute-done | bytes 589856 | tf_op jit(solution)/shard_map/ppermute | solution.py:512
  183.6 0.7 add_parts.7
  184.3 0.1 collective-permute-start.28
  184.4 2.0 collective-permute-start.29
  186.4 0.7 finish.3
  187.1 1.9 collective-permute-start.24
  189.0 2.0 collective-permute-start.25
  191.0 2.0 collective-permute-done.28.refs_1_
  193.0 1.9 collective-permute-start.30
  194.8 2.9 %collective-permute-done.29.refs_2_ = bf16[192,384]{1,0:T(8,128)(2,1)S(1)} collective-permute-done((bf16[192,384]{1,0:T(8,128)(2,1)S(1)}, bf16[192,384]{1,0:T(8,128)(2,1)S(1)}, u32[]{:S(2)}, u32[]{:S(2)}) %collective-permute-start.29) | collective-permute-done | bytes 147488 | tf_op jit(solution)/shard_map/ppermute | solution.py:437
  197.7 7.8 %collective-permute-start.23 = (bf16[480,128]{1,0:T(8,128)(2,1)S(1)}, bf16[480,128]{1,0:T(8,128)(2,1)S(1)}, u32[]{:S(2)}, u32[]{:S(2)}) collective-permute-start(bf16[480,128]{1,0:T(8,128)(2,1)S(1)} %get-tuple-element.146), channel_id=1, source_target_pairs={{0,8},{2,10},{4,12},{6,14},{8,16},{10,18},{12,20},{14,22},{16,24},... | collective-permute-start | bytes 368648 | tf_op jit(solution)/shard_map/ppermute | solution.py:437
  205.5 5.2 %collective-permute-done.30.refs_3_ = bf16[192,384]{1,0:T(8,128)(2,1)S(1)} collective-permute-done((bf16[192,384]{1,0:T(8,128)(2,1)S(1)}, bf16[192,384]{1,0:T(8,128)(2,1)S(1)}, u32[]{:S(2)}, u32[]{:S(2)}) %collective-permute-start.30) | collective-permute-done | bytes 147488 | tf_op jit(solution)/shard_map/ppermute | solution.py:437
  210.7 1.7 join.1
  212.4 3.7 %collective-permute-done.23.refs_3_ = bf16[480,128]{1,0:T(8,128)(2,1)S(1)} collective-permute-done((bf16[480,128]{1,0:T(8,128)(2,1)S(1)}, bf16[480,128]{1,0:T(8,128)(2,1)S(1)}, u32[]{:S(2)}, u32[]{:S(2)}) %collective-permute-start.23) | collective-permute-done | bytes 122912 | tf_op jit(solution)/shard_map/ppermute | solution.py:437
  216.1 5.3 %collective-permute-done.25.refs_6_ = bf16[480,256]{1,0:T(8,128)(2,1)S(1)} collective-permute-done((bf16[480,256]{1,0:T(8,128)(2,1)S(1)}, bf16[480,256]{1,0:T(8,128)(2,1)S(1)}, u32[]{:S(2)}, u32[]{:S(2)}) %collective-permute-start.25) | collective-permute-done | bytes 245792 | tf_op jit(solution)/shard_map/ppermute | solution.py:437
  221.4 1.8 unpack.1
  (26 shorter events, 0.2 us)
Async XLA Ops:
  0.6 7.5 %copy-start.3 = (bf16[160,1536]{1,0:T(8,128)(2,1)S(1)}, bf16[160,1536]{1,0:T(8,128)(2,1)}, u32[]{:S(2)}) copy-start(bf16[160,1536]{1,0:T(8,128)(2,1)} %refs_4_) | copy-start | bytes 1474564
  5.0 75.7 %copy-start = (bf16[512,384]{1,0:T(8,128)(2,1)S(1)}, bf16[512,384]{1,0:T(8,128)(2,1)}, u32[]{:S(2)}) copy-start(bf16[512,384]{1,0:T(8,128)(2,1)} %get-tuple-element.89.refs_0_) | copy-start | bytes 1179652
  5.0 75.6 %copy-start.2 = (s32[3]{0:T(128)S(1)}, s32[3]{0:T(128)}, u32[]{:S(2)}) copy-start(s32[3]{0:T(128)} %pad_add_fusion.ids) | copy-start | bytes 40
  5.0 18.0 %collective-permute-start = (bf16[672,384]{1,0:T(8,128)(2,1)}, bf16[672,384]{1,0:T(8,128)(2,1)S(1)}, u32[]{:S(2)}, u32[]{:S(2)}) collective-permute-start(bf16[672,384]{1,0:T(8,128)(2,1)} %get-tuple-element.86), channel_id=1, source_target_pairs={{0,8},{2,10},{4,12},{6,14},{8,16},{10,18},{12,20},{14,22},{16,24},... | collective-permute-start | bytes 1548296 | tf_op jit(solution)/shard_map/ppermute | solution.py:437
  8.1 15.0 %collective-permute-start.4 = (bf16[160,1536]{1,0:T(8,128)(2,1)S(1)}, bf16[160,1536]{1,0:T(8,128)(2,1)S(1)}, u32[]{:S(2)}, u32[]{:S(2)}) collective-permute-start(bf16[160,1536]{1,0:T(8,128)(2,1)S(1)} %copy-done.3), channel_id=1, source_target_pairs={{0,1},{1,0},{2,3},{3,2},{4,5},{5,4},{6,7},{7,6},{8,9},{9,8},{10,11... | collective-permute-start | bytes 1474568 | tf_op jit(solution)/shard_map/ppermute | solution.py:49
  9.6 13.5 %collective-permute-start.3 = (bf16[512,384]{1,0:T(8,128)(2,1)}, bf16[512,384]{1,0:T(8,128)(2,1)S(1)}, u32[]{:S(2)}, u32[]{:S(2)}) collective-permute-start(bf16[512,384]{1,0:T(8,128)(2,1)} %get-tuple-element.89.refs_0_), channel_id=1, source_target_pairs={{0,4},{2,6},{4,0},{6,2},{8,12},{10,14},{12,8},{14,10},{16,20},{18,... | collective-permute-start | bytes 1179656 | tf_op jit(solution)/shard_map/ppermute | solution.py:462
  11.1 34.3 %collective-permute-start.1 = (bf16[672,384]{1,0:T(8,128)(2,1)}, bf16[672,384]{1,0:T(8,128)(2,1)S(1)}, u32[]{:S(2)}, u32[]{:S(2)}) collective-permute-start(bf16[672,384]{1,0:T(8,128)(2,1)} %get-tuple-element.87), channel_id=1, source_target_pairs={{0,16},{2,18},{4,20},{6,22},{8,24},{10,26},{12,28},{14,30},{16,0},... | collective-permute-start | bytes 1548296 | tf_op jit(solution)/shard_map/ppermute | solution.py:437
  13.7 31.7 %collective-permute-start.2 = (bf16[672,384]{1,0:T(8,128)(2,1)}, bf16[672,384]{1,0:T(8,128)(2,1)S(1)}, u32[]{:S(2)}, u32[]{:S(2)}) collective-permute-start(bf16[672,384]{1,0:T(8,128)(2,1)} %get-tuple-element.88), channel_id=1, source_target_pairs={{0,24},{2,26},{4,28},{6,30},{8,0},{10,2},{12,4},{14,6},{16,8},{18,... | collective-permute-start | bytes 1548296 | tf_op jit(solution)/shard_map/ppermute | solution.py:437
  23.1 31.8 %collective-permute-start.5 = (bf16[160,1536]{1,0:T(8,128)(2,1)S(1)}, bf16[160,1536]{1,0:T(8,128)(2,1)S(1)}, u32[]{:S(2)}, u32[]{:S(2)}) collective-permute-start(bf16[160,1536]{1,0:T(8,128)(2,1)S(1)} %copy-done.3), channel_id=1, source_target_pairs={{0,8},{2,10},{4,12},{6,14},{8,16},{10,18},{12,20},{14,22},{16,24},... | collective-permute-start | bytes 1474568 | tf_op jit(solution)/shard_map/ppermute | solution.py:469
  43.9 7.8 %collective-permute-start.6 = (bf16[512,384]{1,0:T(8,128)(2,1)S(1)}, bf16[512,384]{1,0:T(8,128)(2,1)S(1)}, u32[]{:S(2)}, u32[]{:S(2)}) collective-permute-start(bf16[512,384]{1,0:T(8,128)(2,1)S(1)} %slice.12.refs_1_), channel_id=1, source_target_pairs={{0,4},{2,6},{4,0},{6,2},{8,12},{10,14},{12,8},{14,10},{16,20},{18,... | collective-permute-start | bytes 1179656 | tf_op jit(solution)/shard_map/ppermute | solution.py:471
  54.9 42.6 %collective-permute-start.7 = (bf16[160,1536]{1,0:T(8,128)(2,1)S(1)}, bf16[160,1536]{1,0:T(8,128)(2,1)S(1)}, u32[]{:S(2)}, u32[]{:S(2)}) collective-permute-start(bf16[160,1536]{1,0:T(8,128)(2,1)S(1)} %collective-permute-done.5.refs_5_), channel_id=1, source_target_pairs={{0,8},{2,10},{4,12},{6,14},{8,16},{10,18},{12,20},{14,22},{16,24},... | collective-permute-start | bytes 1474568 | tf_op jit(solution)/shard_map/ppermute | solution.py:478
  76.9 20.6 %collective-permute-start.8 = (bf16[160,1536]{1,0:T(8,128)(2,1)S(1)}, bf16[160,1536]{1,0:T(8,128)(2,1)S(1)}, u32[]{:S(2)}, u32[]{:S(2)}) collective-permute-start(bf16[160,1536]{1,0:T(8,128)(2,1)S(1)} %collective-permute-done.5.refs_5_), channel_id=1, source_target_pairs={{0,1},{1,0},{2,3},{3,2},{4,5},{5,4},{6,7},{7,6},{8,9},{9,8},{10,11... | collective-permute-start | bytes 1474568 | tf_op jit(solution)/shard_map/ppermute | solution.py:49
  78.5 12.1 %collective-permute-start.9 = (bf16[512,384]{1,0:T(8,128)(2,1)S(1)}, bf16[512,384]{1,0:T(8,128)(2,1)S(1)}, u32[]{:S(2)}, u32[]{:S(2)}) collective-permute-start(bf16[512,384]{1,0:T(8,128)(2,1)S(1)} %slice.10.refs_2_), channel_id=1, source_target_pairs={{0,4},{2,6},{4,0},{6,2},{8,12},{10,14},{12,8},{14,10},{16,20},{18,... | collective-permute-start | bytes 1179656 | tf_op jit(solution)/shard_map/ppermute | solution.py:471
  80.1 17.4 %collective-permute-start.10 = (bf16[512,384]{1,0:T(8,128)(2,1)S(1)}, bf16[512,384]{1,0:T(8,128)(2,1)S(1)}, u32[]{:S(2)}, u32[]{:S(2)}) collective-permute-start(bf16[512,384]{1,0:T(8,128)(2,1)S(1)} %slice.11.refs_3_), channel_id=1, source_target_pairs={{0,4},{2,6},{4,0},{6,2},{8,12},{10,14},{12,8},{14,10},{16,20},{18,... | collective-permute-start | bytes 1179656 | tf_op jit(solution)/shard_map/ppermute | solution.py:471
  81.3 32.9 %copy-start.1 = (bf16[160,384]{1,0:T(8,128)(2,1)S(1)}, bf16[160,384]{1,0:T(8,128)(2,1)}, u32[]{:S(2)}) copy-start(bf16[160,384]{1,0:T(8,128)(2,1)} %get-tuple-element.85.own) | copy-start | bytes 368644
  81.3 33.5 %collective-permute-start.11 = (bf16[2048,384]{1,0:T(8,128)(2,1)S(1)}, bf16[2048,384]{1,0:T(8,128)(2,1)S(1)}, u32[]{:S(2)}, u32[]{:S(2)}) collective-permute-start(bf16[2048,384]{1,0:T(8,128)(2,1)S(1)} %stack.18.refs_0_.refs_5_), channel_id=1, source_target_pairs={{0,2},{2,0},{4,6},{6,4},{8,10},{10,8},{12,14},{14,12},{16,18},{18,... | collective-permute-start | bytes 4718600 | tf_op jit(solution)/shard_map/ppermute | solution.py:488
  98.2 16.6 %collective-permute-start.12 = (bf16[2048,384]{1,0:T(8,128)(2,1)S(1)}, bf16[2048,384]{1,0:T(8,128)(2,1)S(1)}, u32[]{:S(2)}, u32[]{:S(2)}) collective-permute-start(bf16[2048,384]{1,0:T(8,128)(2,1)S(1)} %stack.19.refs_1_.refs_6_), channel_id=1, source_target_pairs={{0,2},{2,0},{4,6},{6,4},{8,10},{10,8},{12,14},{14,12},{16,18},{18,... | collective-permute-start | bytes 4718600 | tf_op jit(solution)/shard_map/ppermute | solution.py:488
  98.3 15.4 %collective-permute-start.13 = (bf16[160,1536]{1,0:T(8,128)(2,1)S(1)}, bf16[160,1536]{1,0:T(8,128)(2,1)S(1)}, u32[]{:S(2)}, u32[]{:S(2)}) collective-permute-start(bf16[160,1536]{1,0:T(8,128)(2,1)S(1)} %collective-permute-done.7.refs_6_), channel_id=1, source_target_pairs={{0,8},{2,10},{4,12},{6,14},{8,16},{10,18},{12,20},{14,22},{16,24},... | collective-permute-start | bytes 1474568 | tf_op jit(solution)/shard_map/ppermute | solution.py:478
  98.7 15.0 %collective-permute-start.14 = (bf16[160,1536]{1,0:T(8,128)(2,1)S(1)}, bf16[160,1536]{1,0:T(8,128)(2,1)S(1)}, u32[]{:S(2)}, u32[]{:S(2)}) collective-permute-start(bf16[160,1536]{1,0:T(8,128)(2,1)S(1)} %collective-permute-done.7.refs_6_), channel_id=1, source_target_pairs={{0,1},{1,0},{2,3},{3,2},{4,5},{5,4},{6,7},{7,6},{8,9},{9,8},{10,11... | collective-permute-start | bytes 1474568 | tf_op jit(solution)/shard_map/ppermute | solution.py:49
  113.7 12.8 %collective-permute-start.15 = (bf16[160,1536]{1,0:T(8,128)(2,1)S(1)}, bf16[160,1536]{1,0:T(8,128)(2,1)S(1)}, u32[]{:S(2)}, u32[]{:S(2)}) collective-permute-start(bf16[160,1536]{1,0:T(8,128)(2,1)S(1)} %collective-permute-done.13.refs_7_), channel_id=1, source_target_pairs={{0,1},{1,0},{2,3},{3,2},{4,5},{5,4},{6,7},{7,6},{8,9},{9,8},{10,11... | collective-permute-start | bytes 1474568 | tf_op jit(solution)/shard_map/ppermute | solution.py:49
  132.0 7.0 %collective-permute-start.17 = (bf16[1536,384]{1,0:T(8,128)(2,1)S(1)}, bf16[1536,384]{1,0:T(8,128)(2,1)S(1)}, u32[]{:S(2)}, u32[]{:S(2)}) collective-permute-start(bf16[1536,384]{1,0:T(8,128)(2,1)S(1)} %get-tuple-element.120), channel_id=1, source_target_pairs={{0,2},{2,0},{4,6},{6,4},{8,10},{10,8},{12,14},{14,12},{16,18},{18,... | collective-permute-start | bytes 3538952 | tf_op jit(solution)/shard_map/ppermute | solution.py:366
  136.0 2.3 %collective-permute-start.16 = (bf16[2560,128]{1,0:T(8,128)(2,1)S(1)}, bf16[2560,128]{1,0:T(8,128)(2,1)S(1)}, u32[]{:S(2)}, u32[]{:S(2)}) collective-permute-start(bf16[2560,128]{1,0:T(8,128)(2,1)S(1)} %get-tuple-element.116), channel_id=1, source_target_pairs={{0,2},{2,0},{4,6},{6,4},{8,10},{10,8},{12,14},{14,12},{16,18},{18,... | collective-permute-start | bytes 1966088 | tf_op jit(solution)/shard_map/ppermute | solution.py:366
  139.8 10.4 %collective-permute-start.18 = (bf16[1280,128]{1,0:T(8,128)(2,1)S(1)}, bf16[1280,128]{1,0:T(8,128)(2,1)S(1)}, u32[]{:S(2)}, u32[]{:S(2)}) collective-permute-start(bf16[1280,128]{1,0:T(8,128)(2,1)S(1)} %get-tuple-element.128), channel_id=1, source_target_pairs={{0,4},{2,6},{4,0},{6,2},{8,12},{10,14},{12,8},{14,10},{16,20},{18,... | collective-permute-start | bytes 983048 | tf_op jit(solution)/shard_map/ppermute | solution.py:506
  150.2 3.1 %collective-permute-start.19 = (bf16[2560,256]{1,0:T(8,128)(2,1)S(1)}, bf16[2560,256]{1,0:T(8,128)(2,1)S(1)}, u32[]{:S(2)}, u32[]{:S(2)}) collective-permute-start(bf16[2560,256]{1,0:T(8,128)(2,1)S(1)} %get-tuple-element.140), channel_id=1, source_target_pairs={{0,2},{2,0},{4,6},{6,4},{8,10},{10,8},{12,14},{14,12},{16,18},{18,... | collective-permute-start | bytes 3932168 | tf_op jit(solution)/shard_map/ppermute | solution.py:366
  154.2 32.2 %collective-permute-start.20 = (bf16[1280,256]{1,0:T(8,128)(2,1)S(1)}, bf16[1280,256]{1,0:T(8,128)(2,1)S(1)}, u32[]{:S(2)}, u32[]{:S(2)}) collective-permute-start(bf16[1280,256]{1,0:T(8,128)(2,1)S(1)} %get-tuple-element.141), channel_id=1, source_target_pairs={{0,4},{2,6},{4,0},{6,2},{8,12},{10,14},{12,8},{14,10},{16,20},{18,... | collective-permute-start | bytes 1966088 | tf_op jit(solution)/shard_map/ppermute | solution.py:514
  155.9 27.7 %collective-permute-start.27 = (bf16[768,384]{1,0:T(8,128)(2,1)S(1)}, bf16[768,384]{1,0:T(8,128)(2,1)S(1)}, u32[]{:S(2)}, u32[]{:S(2)}) collective-permute-start(bf16[768,384]{1,0:T(8,128)(2,1)S(1)} %get-tuple-element.161), channel_id=1, source_target_pairs={{0,4},{2,6},{4,0},{6,2},{8,12},{10,14},{12,8},{14,10},{16,20},{18,... | collective-permute-start | bytes 1769480 | tf_op jit(solution)/shard_map/ppermute | solution.py:512
  157.0 29.4 %collective-permute-start.21 = (bf16[480,128]{1,0:T(8,128)(2,1)S(1)}, bf16[480,128]{1,0:T(8,128)(2,1)S(1)}, u32[]{:S(2)}, u32[]{:S(2)}) collective-permute-start(bf16[480,128]{1,0:T(8,128)(2,1)S(1)} %get-tuple-element.142), channel_id=1, source_target_pairs={{0,24},{2,26},{4,28},{6,30},{8,0},{10,2},{12,4},{14,6},{16,8},{18,... | collective-permute-start | bytes 368648 | tf_op jit(solution)/shard_map/ppermute | solution.py:437
  158.4 28.0 %collective-permute-start.22 = (bf16[480,128]{1,0:T(8,128)(2,1)S(1)}, bf16[480,128]{1,0:T(8,128)(2,1)S(1)}, u32[]{:S(2)}, u32[]{:S(2)}) collective-permute-start(bf16[480,128]{1,0:T(8,128)(2,1)S(1)} %get-tuple-element.143), channel_id=1, source_target_pairs={{0,16},{2,18},{4,20},{6,22},{8,24},{10,26},{12,28},{14,30},{16,0},... | collective-permute-start | bytes 368648 | tf_op jit(solution)/shard_map/ppermute | solution.py:437
  184.3 8.6 %collective-permute-start.28 = (bf16[192,384]{1,0:T(8,128)(2,1)S(1)}, bf16[192,384]{1,0:T(8,128)(2,1)S(1)}, u32[]{:S(2)}, u32[]{:S(2)}) collective-permute-start(bf16[192,384]{1,0:T(8,128)(2,1)S(1)} %get-tuple-element.163), channel_id=1, source_target_pairs={{0,8},{2,10},{4,12},{6,14},{8,16},{10,18},{12,20},{14,22},{16,24},... | collective-permute-start | bytes 442376 | tf_op jit(solution)/shard_map/ppermute | solution.py:437
  184.4 13.3 %collective-permute-start.29 = (bf16[192,384]{1,0:T(8,128)(2,1)S(1)}, bf16[192,384]{1,0:T(8,128)(2,1)S(1)}, u32[]{:S(2)}, u32[]{:S(2)}) collective-permute-start(bf16[192,384]{1,0:T(8,128)(2,1)S(1)} %get-tuple-element.164), channel_id=1, source_target_pairs={{0,16},{2,18},{4,20},{6,22},{8,24},{10,26},{12,28},{14,30},{16,0},... | collective-permute-start | bytes 442376 | tf_op jit(solution)/shard_map/ppermute | solution.py:437
  187.1 29.0 %collective-permute-start.24 = (bf16[480,256]{1,0:T(8,128)(2,1)S(1)}, bf16[480,256]{1,0:T(8,128)(2,1)S(1)}, u32[]{:S(2)}, u32[]{:S(2)}) collective-permute-start(bf16[480,256]{1,0:T(8,128)(2,1)S(1)} %get-tuple-element.154), channel_id=1, source_target_pairs={{0,24},{2,26},{4,28},{6,30},{8,0},{10,2},{12,4},{14,6},{16,8},{18,... | collective-permute-start | bytes 737288 | tf_op jit(solution)/shard_map/ppermute | solution.py:437
  189.0 32.4 %collective-permute-start.25 = (bf16[480,256]{1,0:T(8,128)(2,1)S(1)}, bf16[480,256]{1,0:T(8,128)(2,1)S(1)}, u32[]{:S(2)}, u32[]{:S(2)}) collective-permute-start(bf16[480,256]{1,0:T(8,128)(2,1)S(1)} %get-tuple-element.155), channel_id=1, source_target_pairs={{0,16},{2,18},{4,20},{6,22},{8,24},{10,26},{12,28},{14,30},{16,0},... | collective-permute-start | bytes 737288 | tf_op jit(solution)/shard_map/ppermute | solution.py:437
  191.0 30.4 %collective-permute-start.26 = (bf16[480,256]{1,0:T(8,128)(2,1)S(1)}, bf16[480,256]{1,0:T(8,128)(2,1)S(1)}, u32[]{:S(2)}, u32[]{:S(2)}) collective-permute-start(bf16[480,256]{1,0:T(8,128)(2,1)S(1)} %get-tuple-element.156), channel_id=1, source_target_pairs={{0,8},{2,10},{4,12},{6,14},{8,16},{10,18},{12,20},{14,22},{16,24},... | collective-permute-start | bytes 737288 | tf_op jit(solution)/shard_map/ppermute | solution.py:437
  193.0 17.7 %collective-permute-start.30 = (bf16[192,384]{1,0:T(8,128)(2,1)S(1)}, bf16[192,384]{1,0:T(8,128)(2,1)S(1)}, u32[]{:S(2)}, u32[]{:S(2)}) collective-permute-start(bf16[192,384]{1,0:T(8,128)(2,1)S(1)} %get-tuple-element.165), channel_id=1, source_target_pairs={{0,24},{2,26},{4,28},{6,30},{8,0},{10,2},{12,4},{14,6},{16,8},{18,... | collective-permute-start | bytes 442376 | tf_op jit(solution)/shard_map/ppermute | solution.py:437
  197.7 18.4 %collective-permute-start.23 = (bf16[480,128]{1,0:T(8,128)(2,1)S(1)}, bf16[480,128]{1,0:T(8,128)(2,1)S(1)}, u32[]{:S(2)}, u32[]{:S(2)}) collective-permute-start(bf16[480,128]{1,0:T(8,128)(2,1)S(1)} %get-tuple-element.146), channel_id=1, source_target_pairs={{0,8},{2,10},{4,12},{6,14},{8,16},{10,18},{12,20},{14,22},{16,24},... | collective-permute-start | bytes 368648 | tf_op jit(solution)/shard_map/ppermute | solution.py:437

commit v5 on v4

--- a/solution.py
+++ b/solution.py
@@ -369,64 +369,73 @@
 
 
 def finish_kernel(n_groups, ids, kept, other, *refs):
-    dq, outs = refs[:n_groups], refs[n_groups:]
-    rows = dq[0].shape[0]
+    dq, outs = refs[:n_groups], refs[-n_groups:]
+    rows, cols = dq[0].shape
     for s in range(n_groups):
-        outs[s][:rows, :] = dq[s][...]
+        outs[s][:rows, :cols] = dq[s][...]
         for i in range(2):
             at = (i * n_groups + s) * rows
             total = kept[at : at + rows, :].astype(F32) + other[at : at + rows, :].astype(F32)
-            outs[s][(i + 1) * rows : (i + 2) * rows, :] = total.astype(BF16)
-
-
-def finish(ids, kept, other, dq, n_groups):
+            outs[s][:rows, (i + 1) * cols : (i + 2) * cols] = total.astype(BF16)
+    if len(refs) > 2 * n_groups:
+        proj_kept, proj_other = refs[n_groups : n_groups + 2]
+        depth = proj_kept.shape[0] // n_groups
+        wide = proj_kept.shape[1]
+        for s in range(n_groups):
+            here = pl.ds(((n_groups - s) % n_groups) * depth, depth)
+            total = proj_kept[here, :].astype(F32) + proj_other[here, :].astype(F32)
+            outs[s][rows:, :wide] = total.astype(BF16)
+
+
+def finish(ids, kept, other, dq, n_groups, *proj):
     rows, cols = dq[0].shape
+    wide = 3 * cols
+    if proj:
+        wide = max(wide, proj[0].shape[1])
+        rows = rows + proj[0].shape[0] // n_groups
     return whole_call(
         functools.partial(finish_kernel, n_groups),
-        [jax.ShapeDtypeStruct((3 * rows, cols), BF16)] * n_groups,
-        (ids, kept, other, *dq),
+        [jax.ShapeDtypeStruct((rows, wide), BF16)] * n_groups,
+        (ids, kept, other, *dq, *proj),
         "finish",
     )
 
 
-def unpack_kernel(n_groups, ids, *refs):
+def unpack_kernel(n_groups, widths, ids, *refs):
     pieces, outs = refs[:-3], refs[-3:]
     rows, gw = outs[0].shape[0], outs[0].shape[1] // n_groups
     before = 0
-    for c in range(0, len(pieces), n_groups):
-        cols = pieces[c].shape[1]
+    for c, cols in enumerate(widths):
         for s in range(n_groups):
             start = lax.rem(ids[0] + s, n_groups) * gw + before
             for i, out in enumerate(outs):
-                piece = pieces[c + s][i * rows : (i + 1) * rows, :]
+                piece = pieces[c * n_groups + s][:rows, i * cols : (i + 1) * cols]
                 out[:, pl.ds(aligned(start, HD), cols)] = piece
         before += cols
 
 
-def unpack(ids, chunks, n_groups):
-    rows = chunks[0][0].shape[0] // 3
-    gw = sum(pieces[0].shape[1] for pieces in chunks)
+def unpack(ids, chunks, rows, gw, n_groups):
+    widths = [HD, gw - HD][: len(chunks)]
     return whole_call(
-        functools.partial(unpack_kernel, n_groups),
+        functools.partial(unpack_kernel, n_groups, widths),
         [jax.ShapeDtypeStruct((rows, gw * n_groups), BF16)] * 3,
         (ids, *[piece for pieces in chunks for piece in pieces]),
         "unpack",
     )
 
 
-def join_kernel(n_groups, ids, *refs):
+def join_kernel(n_groups, rows, gw, ids, *refs):
     pieces, out = refs[:n_groups], refs[n_groups]
-    gw = pieces[0].shape[1]
     for s in range(n_groups):
-        start = lax.rem(ids[0] - s + n_groups, n_groups) * gw
-        out[:, pl.ds(aligned(start, HD), gw)] = pieces[s][...].astype(F32)
-
-
-def join(ids, pieces, n_groups):
-    rows, gw = pieces[0].shape
+        start = lax.rem(ids[0] + s, n_groups) * gw
+        out[:, pl.ds(aligned(start, HD), gw)] = pieces[s][rows:, :gw].astype(F32)
+
+
+def join(ids, pieces, rows, gw, n_groups):
+    depth = pieces[0].shape[0] - rows
     return whole_call(
-        functools.partial(join_kernel, n_groups),
-        jax.ShapeDtypeStruct((rows, gw * n_groups), F32),
+        functools.partial(join_kernel, n_groups, rows, gw),
+        jax.ShapeDtypeStruct((depth, gw * n_groups), F32),
         (ids, *pieces),
         "join",
     )
@@ -443,6 +452,7 @@
     n_frame = lax.axis_size("frame")
     n_space = lax.axis_size("space")
     rows, width = queries.shape
+    gw = width // math.gcd(width // HD, n_frame)
     depth = proj_weight.shape[1]
     n_groups = math.gcd(width // HD, n_frame)
     n_tok = n_frame // n_groups
@@ -459,28 +469,15 @@
     *pieces, own_q = pack(ids, queries, keys, values, proj_weight.T, n_groups)
     pieces = exchange(pieces, n_groups, n_tok, 1)
     q_pieces = pieces[1:]
-    own, others = [pieces[0]], [lax.ppermute(pieces[0], "frame", last)]
-    ring = [grad_out]
-    across = [gather_blocks(grad_out, "space", n_space, space_bits)]
-    for s in range(1, n_groups):
-        piece = pieces[s][:shared]
-        if s == 1:
-            ring[0], piece, others[0], *across[0] = tie((ring[0], piece, others[0], *across[0]))
-            ring.append(lax.ppermute(ring[0], "frame", shift_pairs(n_groups, n_tok, 1)))
-        own.append(piece)
-        others.append(lax.ppermute(piece, "frame", last))
-        if s == 1 and n_groups > 2:
-            ring[1], others[1], *pieces[2:] = tie((ring[1], others[1], *pieces[2:]))
-
-    for s in range(1, n_groups):
-        across.append(gather_blocks(ring[s], "space", n_space, space_bits))
+    own, others, ring, across = [pieces[0]], [], grad_out, []
+    for s in range(n_groups):
+        others.append(lax.ppermute(own[s], "frame", last))
+        across.append(gather_blocks(ring, "space", n_space, space_bits))
         if s + 1 < n_groups:
-            arriving = lax.ppermute(ring[s], "frame", shift_pairs(n_groups, n_tok, 1))
-            count = n_groups if s == 1 else 0
-            tied = tie((arriving, *across[s], *others[:count]))
-            arriving, across[s] = tied[0], list(tied[1 : 1 + n_space])
-            others[:count] = tied[1 + n_space :]
-            ring.append(arriving)
+            ring = lax.ppermute(ring, "frame", shift_pairs(n_groups, n_tok, 1))
+            step = (ring, pieces[s + 1][:shared], others[s], *across[s])
+            ring, piece, others[s], *across[s] = tie(step)
+            own.append(piece)
 
     q = stack_queries(ids, own_q, q_pieces)
     blocks = [stack(ids, own, rows), stack(ids, others, rows)]
@@ -500,23 +497,22 @@
 
     proj_kept, proj_sent = halve(ids, kept, sent, n_frame, tok_bits)
     dq, (kept, sent) = attention_chunk(0, 1, q)
-    returned = []
+    q, kept, sent, proj_kept, proj_sent = tie((q, kept, sent, proj_kept, proj_sent))
+    other = lax.ppermute(sent, "frame", last)
+    proj_other = lax.ppermute(proj_sent, "frame", last)
     if heads > 1:
-        q, kept, sent, proj_kept, proj_sent = tie((q, kept, sent, proj_kept, proj_sent))
-        other = lax.ppermute(sent, "frame", last)
-        next_dq, (next_kept, sent), other = attention_chunk(1, heads - 1, q, other)
-        sums = finish(ids, kept, other, dq, n_groups)
-        proj_sent, *sums = tie((proj_sent, *sums))
+        dq_rest, (kept_rest, sent_rest), other, proj_other = attention_chunk(
+            1, heads - 1, q, other, proj_other
+        )
+    sums = finish(ids, kept, other, dq, n_groups, proj_kept, proj_other)
+    first = exchange(sums, n_groups, n_tok, -1)
+    returned = [first]
+    if heads > 1:
+        other = lax.ppermute(sent_rest, "frame", last)
+        sums = finish(ids, kept_rest, other, dq_rest, n_groups)
         returned.append(exchange(sums, n_groups, n_tok, -1))
-        dq, kept = next_dq, next_kept
-    other = lax.ppermute(proj_sent, "frame", last)
-    proj = exchange(add_parts(ids, proj_kept, other, n_groups), n_groups, n_tok, 1)
-    other = lax.ppermute(sent, "frame", last)
-    if returned:
-        other, *returned[0][1:-1] = tie((other, *returned[0][1:-1]))
-    returned.append(exchange(finish(ids, kept, other, dq, n_groups), n_groups, n_tok, -1))
-    grad_proj = join(ids, proj, n_groups).T
-    grad_queries, grad_keys, grad_values = unpack(ids, returned, n_groups)
+    grad_proj = join(ids, first, rows, gw, n_groups).T
+    grad_queries, grad_keys, grad_values = unpack(ids, returned, rows, gw, n_groups)
     return (grad_queries, grad_keys, grad_values, grad_proj)
 
 

time: 225 us -> 204 us (0.907)
  starting transfers between devices: 81 us -> 55.1 us
  waiting for transfers between devices: 98.6 us -> 105 us
    ppermute x8 -> x9, waiting for transfers between devices: 65.3 us -> 31.6 us  [the longest x4 11.3 us: local(): others.append(lax.ppermute(own[s], 'frame', last))]
    ppermute x12 -> x9, waiting for transfers between devices: 27.2 us -> 54.9 us  [exchange(): lax.ppermute(pieces[s], 'frame', shift_pairs(n_groups, n_tok, sign * s))]
    ppermute x8 -> x9, starting transfers between devices: 49.4 us -> 30.1 us  [the longest x3 20.9 us: local(): ring = lax.ppermute(ring, 'frame', shift_pairs(n_groups, n_tok, 1))]
    ppermute x2 -> x1, waiting for transfers between devices: 0.01 us -> 11.7 us  [local(): other = lax.ppermute(sent, 'frame', last)]
    ppermute x12 -> x9, starting transfers between devices: 24 us -> 17.6 us  [exchange(): lax.ppermute(pieces[s], 'frame', shift_pairs(n_groups, n_tok, sign * s))]
    pallas_call x12 -> x11, Pallas kernels: 15.3 us -> 14.8 us  [whole_call(): pl.pallas_call(body, out_shape=out_shape, in_specs=[smem()] + [vmem()] *...]
  transfers between devices with their start and end apart: 31 -> 28, of which waited for: 15 -> 14; matrix products, arithmetic and copies ran while one was open for 0% -> 0% of each run, Pallas kernels for 13% -> 14%
where the time goes in v5:
time: 204 us; the launch traced here: 203 us
  waiting for transfers between devices  105 us (51%)
  starting transfers between devices  55.1 us (27%)
  Pallas kernels  41.5 us (20%)
    ppermute x9, waiting for transfers between devices, exchange(): lax.ppermute(pieces[s], 'frame', shift_pairs(n_groups, n_tok, sign * s))  54.9 us
    ppermute x3, starting transfers between devices, local(): ring = lax.ppermute(ring, 'frame', shift_pairs(n_groups, n_tok, 1))  20.9 us
    ppermute x9, starting transfers between devices, exchange(): lax.ppermute(pieces[s], 'frame', shift_pairs(n_groups, n_tok, sign * s))  17.6 us
    pallas_call x11, Pallas kernels, whole_call(): pl.pallas_call(body, out_shape=out_shape, in_specs=[smem()] + [vmem()] *...  14.8 us
    pallas_call x2, Pallas kernels, backward(): pl.pallas_call(functools.partial(backward_kernel, n_groups, chunk, 1.0 /...  12.7 us
    ppermute x1, waiting for transfers between devices, local(): other = lax.ppermute(sent, 'frame', last)  11.7 us
    ppermute x4, waiting for transfers between devices, local(): others.append(lax.ppermute(own[s], 'frame', last))  11.3 us
    ppermute x3, waiting for transfers between devices, local(): ring = lax.ppermute(ring, 'frame', shift_pairs(n_groups, n_tok, 1))  10.5 us
  transfers between devices with their start and end apart: 28, of which 14 were waited for; matrix products, arithmetic and copies ran while one was open for 0% of the time, Pallas kernels for 14%

profile of v5, /device:TPU:0, one launch (start us, length us, event | category | flops | bytes accessed | tf_op | source)
XLA Modules:
  0.0 203.4 jit_solution(16876845931583185340)
XLA Ops:
  0.7 0.6 pad_add_fusion.ids
  1.2 3.7 %pack.1 = (bf16[512,384]{1,0:T(8,128)(2,1)}, bf16[672,384]{1,0:T(8,128)(2,1)}, bf16[672,384]{1,0:T(8,128)(2,1)}, bf16[672,384]{1,0:T(8,128)(2,1)}, bf16[160,384]{1,0:T(8,128)(2,1)}) custom-call(s32[3]{0:T(128)} %pad_add_fusion.ids, bf16[160,1536]{1,0:T(8,128)(2,1)} %q.1, bf16[160,1536]{1,0:T(8,128)(2,1)} %k.1, bf16[160,1536]{1,0:T(8,128)(2,1)} %v.1, ...), custom_call_target="tpu_custom_call" | custom-call | tf_op jit(solution)/shard_map/pack/pallas_call | solution.py:119
  5.0 0.0 copy-start
  5.0 3.1 %collective-permute-start = (bf16[672,384]{1,0:T(8,128)(2,1)}, bf16[672,384]{1,0:T(8,128)(2,1)S(1)}, u32[]{:S(2)}, u32[]{:S(2)}) collective-permute-start(bf16[672,384]{1,0:T(8,128)(2,1)} %get-tuple-element.71), channel_id=1, source_target_pairs={{0,8},{2,10},{4,12},{6,14},{8,16},{10,18},{12,20},{14,22},{16,24},... | collective-permute-start | bytes 1548296 | tf_op jit(solution)/shard_map/ppermute | solution.py:446
  8.1 1.6 collective-permute-start.3
  9.6 1.5 collective-permute-start.5
  11.2 1.5 collective-permute-start.4
  12.6 1.2 collective-permute-start.1
  13.9 9.1 %collective-permute-done.refs_0_ = bf16[672,384]{1,0:T(8,128)(2,1)S(1)} collective-permute-done((bf16[672,384]{1,0:T(8,128)(2,1)}, bf16[672,384]{1,0:T(8,128)(2,1)S(1)}, u32[]{:S(2)}, u32[]{:S(2)}) %collective-permute-start) | collective-permute-done | bytes 516128 | tf_op jit(solution)/shard_map/ppermute | solution.py:446
  23.0 10.5 %collective-permute-done.3.refs_5_ = bf16[160,1536]{1,0:T(8,128)(2,1)S(1)} collective-permute-done((bf16[160,1536]{1,0:T(8,128)(2,1)S(1)}, bf16[160,1536]{1,0:T(8,128)(2,1)S(1)}, u32[]{:S(2)}, u32[]{:S(2)}) %collective-permute-start.3) | collective-permute-done | bytes 491552 | tf_op jit(solution)/shard_map/ppermute | solution.py:477
  33.5 0.0 collective-permute-done.5.refs_8_
  33.5 9.7 %collective-permute-start.6 = (bf16[160,1536]{1,0:T(8,128)(2,1)S(1)}, bf16[160,1536]{1,0:T(8,128)(2,1)S(1)}, u32[]{:S(2)}, u32[]{:S(2)}) collective-permute-start(bf16[160,1536]{1,0:T(8,128)(2,1)S(1)} %collective-permute-done.3.refs_5_), channel_id=1, source_target_pairs={{0,8},{2,10},{4,12},{6,14},{8,16},{10,18},{12,20},{14,22},{16,24},... | collective-permute-start | bytes 1474568 | tf_op jit(solution)/shard_map/ppermute | solution.py:477
  43.2 1.5 collective-permute-start.8
  44.7 1.5 collective-permute-start.7
  46.2 19.2 %collective-permute-done.1.refs_1_ = bf16[672,384]{1,0:T(8,128)(2,1)S(1)} collective-permute-done((bf16[672,384]{1,0:T(8,128)(2,1)}, bf16[672,384]{1,0:T(8,128)(2,1)S(1)}, u32[]{:S(2)}, u32[]{:S(2)}) %collective-permute-start.1) | collective-permute-done | bytes 516128 | tf_op jit(solution)/shard_map/ppermute | solution.py:446
  65.4 0.0 collective-permute-done.7.refs_1_
  65.4 0.0 collective-permute-done.6.refs_6_
  65.4 9.7 %collective-permute-start.9 = (bf16[160,1536]{1,0:T(8,128)(2,1)S(1)}, bf16[160,1536]{1,0:T(8,128)(2,1)S(1)}, u32[]{:S(2)}, u32[]{:S(2)}) collective-permute-start(bf16[160,1536]{1,0:T(8,128)(2,1)S(1)} %collective-permute-done.6.refs_6_), channel_id=1, source_target_pairs={{0,8},{2,10},{4,12},{6,14},{8,16},{10,18},{12,20},{14,22},{16,24},... | collective-permute-start | bytes 1474568 | tf_op jit(solution)/shard_map/ppermute | solution.py:477
  75.1 1.5 collective-permute-start.11
  76.7 1.5 collective-permute-start.10
  78.2 3.1 %collective-permute-done.2.refs_2_ = bf16[672,384]{1,0:T(8,128)(2,1)S(1)} collective-permute-done((bf16[672,384]{1,0:T(8,128)(2,1)}, bf16[672,384]{1,0:T(8,128)(2,1)S(1)}, u32[]{:S(2)}, u32[]{:S(2)}) %collective-permute-start.2) | collective-permute-done | bytes 516128 | tf_op jit(solution)/shard_map/ppermute | solution.py:446
  81.3 4.8 %collective-permute-done.10.refs_2_ = bf16[512,384]{1,0:T(8,128)(2,1)S(1)} collective-permute-done((bf16[512,384]{1,0:T(8,128)(2,1)S(1)}, bf16[512,384]{1,0:T(8,128)(2,1)S(1)}, u32[]{:S(2)}, u32[]{:S(2)}) %collective-permute-start.10) | collective-permute-done | bytes 393248 | tf_op jit(solution)/shard_map/ppermute | solution.py:474
  86.1 0.0 collective-permute-done.9.refs_7_
  86.1 0.9 collective-permute-done.11.refs_10_
  87.0 1.5 collective-permute-start.12
  88.5 0.7 stack.18.refs_0_.refs_5_
  89.1 0.0 copy-start.1
  89.1 0.1 collective-permute-start.13
  89.2 6.5 %collective-permute-done.12.refs_3_ = bf16[512,384]{1,0:T(8,128)(2,1)S(1)} collective-permute-done((bf16[512,384]{1,0:T(8,128)(2,1)S(1)}, bf16[512,384]{1,0:T(8,128)(2,1)S(1)}, u32[]{:S(2)}, u32[]{:S(2)}) %collective-permute-start.12) | collective-permute-done | bytes 393248 | tf_op jit(solution)/shard_map/ppermute | solution.py:474
  95.7 0.7 stack.19.refs_1_.refs_6_
  96.4 0.1 collective-permute-start.14
  96.5 1.6 collective-permute-start.15
  98.1 0.6 stack_queries.1.q_in.refs_0_
  98.7 1.2 collective-permute-done.14.refs_3_.refs_8_
  99.9 10.2 %forward.1 = (bf16[3,2560,640]{2,1,0:T(8,128)(2,1)S(1)}, bf16[640,384]{1,0:T(8,128)(2,1)S(1)}, f32[3,1,640]{2,1,0:T(1,128)S(1)}) custom-call(bf16[640,384]{1,0:T(8,128)(2,1)S(1)} %stack_queries.1.q_in.refs_0_, bf16[2048,384]{1,0:T(8,128)(2,1)S(1)} %stack.18.refs_0_.refs_5_, bf16[2048,384]{1,0:T(8,128)(2,1)S(1)} %stack.19.refs_1_.refs_6_, ...), custom_call_target="tpu_custom_call" | custom-call | flops 2516582400 | bytes 9830400 | tf_op jit(solution)/shard_map/forward/pallas_call | solution.py:200
  110.1 0.0 collective-permute-done.15.refs_11_
  110.2 5.5 %project.1 = (bf16[640,384]{1,0:T(8,128)(2,1)S(1)}, bf16[1536,384]{1,0:T(8,128)(2,1)S(1)}, bf16[1536,384]{1,0:T(8,128)(2,1)S(1)}) custom-call(s32[3]{0:T(128)S(1)} %copy-done.2, bf16[640,384]{1,0:T(8,128)(2,1)S(1)} %get-tuple-element.84.attn.refs_2_, bf16[2048,384]{1,0:T(8,128)(2,1)S(1)} %stack.18.refs_0_.refs_5_, ...), custom_call_target="tpu_custom_call" | custom-call | flops 3019898880 | bytes 9633792 | tf_op jit(solution)/shard_map/project/pallas_call | solution.py:75
  115.6 0.2 collective-permute-start.17
  115.8 3.9 %backward.2 = (bf16[160,128]{1,0:T(8,128)(2,1)S(1)}, bf16[160,128]{1,0:T(8,128)(2,1)S(1)}, bf16[160,128]{1,0:T(8,128)(2,1)S(1)}, bf16[160,128]{1,0:T(8,128)(2,1)...) custom-call(bf16[640,384]{1,0:T(8,128)(2,1)S(1)} %stack_queries.1.q_in.refs_0_, ...), custom_call_target="tpu_custom_call" | custom-call | flops 81920 | bytes 163840 | tf_op jit(solution)/shard_map/backward/pallas_call | solution.py:264
  119.8 0.4 collective-permute-start.16
  120.2 1.7 collective-permute-done.16.other
  121.9 0.7 add_parts.3
  122.6 0.0 collective-permute-done.17.other
  122.6 0.8 add_parts.4
  123.5 1.6 collective-permute-start.19
  125.0 0.5 collective-permute-start.18
  125.6 8.8 %backward.3 = (bf16[160,256]{1,0:T(8,128)(2,1)S(1)}, bf16[160,256]{1,0:T(8,128)(2,1)S(1)}, bf16[160,256]{1,0:T(8,128)(2,1)S(1)}, bf16[160,256]{1,0:T(8,128)(2,1)...) custom-call(bf16[640,384]{1,0:T(8,128)(2,1)S(1)} %stack_queries.1.q_in.refs_0_, ...), custom_call_target="tpu_custom_call" | custom-call | flops 81920 | bytes 163840 | tf_op jit(solution)/shard_map/backward/pallas_call | solution.py:264
  134.4 11.7 %collective-permute-done.18.other = bf16[1280,128]{1,0:T(8,128)(2,1)S(1)} collective-permute-done((bf16[1280,128]{1,0:T(8,128)(2,1)S(1)}, bf16[1280,128]{1,0:T(8,128)(2,1)S(1)}, u32[]{:S(2)}, u32[]{:S(2)}) %collective-permute-start.18) | collective-permute-done | bytes 327712 | tf_op jit(solution)/shard_map/ppermute | solution.py:501
  146.1 3.0 %collective-permute-done.23.other = bf16[2560,256]{1,0:T(8,128)(2,1)S(1)} collective-permute-done((bf16[2560,256]{1,0:T(8,128)(2,1)S(1)}, bf16[2560,256]{1,0:T(8,128)(2,1)S(1)}, u32[]{:S(2)}, u32[]{:S(2)}) %collective-permute-start.23) | collective-permute-done | bytes 1310752 | tf_op jit(solution)/shard_map/ppermute | solution.py:366
  149.2 0.8 add_parts.5
  150.0 1.6 collective-permute-start.24
  151.6 0.8 finish.2
  152.4 2.5 %collective-permute-start.20 = (bf16[352,384]{1,0:T(8,128)(2,1)S(1)}, bf16[352,384]{1,0:T(8,128)(2,1)S(1)}, u32[]{:S(2)}, u32[]{:S(2)}) collective-permute-start(bf16[352,384]{1,0:T(8,128)(2,1)S(1)} %get-tuple-element.118), channel_id=1, source_target_pairs={{0,24},{2,26},{4,28},{6,30},{8,0},{10,2},{12,4},{14,6},{16,8},{18,... | collective-permute-start | bytes 811016 | tf_op jit(solution)/shard_map/ppermute | solution.py:446
  154.9 1.9 collective-permute-start.21
  156.8 0.2 collective-permute-start.22
  157.0 9.9 %collective-permute-done.24.other = bf16[1280,256]{1,0:T(8,128)(2,1)S(1)} collective-permute-done((bf16[1280,256]{1,0:T(8,128)(2,1)S(1)}, bf16[1280,256]{1,0:T(8,128)(2,1)S(1)}, u32[]{:S(2)}, u32[]{:S(2)}) %collective-permute-start.24) | collective-permute-done | bytes 655392 | tf_op jit(solution)/shard_map/ppermute | solution.py:511
  166.9 0.7 finish.3
  167.6 2.5 %collective-permute-start.25 = (bf16[160,768]{1,0:T(8,128)(2,1)S(1)}, bf16[160,768]{1,0:T(8,128)(2,1)S(1)}, u32[]{:S(2)}, u32[]{:S(2)}) collective-permute-start(bf16[160,768]{1,0:T(8,128)(2,1)S(1)} %get-tuple-element.130), channel_id=1, source_target_pairs={{0,24},{2,26},{4,28},{6,30},{8,0},{10,2},{12,4},{14,6},{16,8},{18,... | collective-permute-start | bytes 737288 | tf_op jit(solution)/shard_map/ppermute | solution.py:446
  170.1 1.9 collective-permute-start.26
  172.0 4.4 %collective-permute-start.27 = (bf16[160,768]{1,0:T(8,128)(2,1)S(1)}, bf16[160,768]{1,0:T(8,128)(2,1)S(1)}, u32[]{:S(2)}, u32[]{:S(2)}) collective-permute-start(bf16[160,768]{1,0:T(8,128)(2,1)S(1)} %get-tuple-element.132), channel_id=1, source_target_pairs={{0,8},{2,10},{4,12},{6,14},{8,16},{10,18},{12,20},{14,22},{16,24},... | collective-permute-start | bytes 737288 | tf_op jit(solution)/shard_map/ppermute | solution.py:446
  176.3 15.8 %collective-permute-done.21.refs_2_ = bf16[352,384]{1,0:T(8,128)(2,1)S(1)} collective-permute-done((bf16[352,384]{1,0:T(8,128)(2,1)S(1)}, bf16[352,384]{1,0:T(8,128)(2,1)S(1)}, u32[]{:S(2)}, u32[]{:S(2)}) %collective-permute-start.21) | collective-permute-done | bytes 270368 | tf_op jit(solution)/shard_map/ppermute | solution.py:446
  192.1 1.7 join.1
  193.8 7.7 %collective-permute-done.26.refs_6_ = bf16[160,768]{1,0:T(8,128)(2,1)S(1)} collective-permute-done((bf16[160,768]{1,0:T(8,128)(2,1)S(1)}, bf16[160,768]{1,0:T(8,128)(2,1)S(1)}, u32[]{:S(2)}, u32[]{:S(2)}) %collective-permute-start.26) | collective-permute-done | bytes 245792 | tf_op jit(solution)/shard_map/ppermute | solution.py:446
  201.5 1.8 unpack.1
  (19 shorter events, 0.2 us)
Async XLA Ops:
  0.6 7.4 %copy-start.3 = (bf16[160,1536]{1,0:T(8,128)(2,1)S(1)}, bf16[160,1536]{1,0:T(8,128)(2,1)}, u32[]{:S(2)}) copy-start(bf16[160,1536]{1,0:T(8,128)(2,1)} %refs_4_) | copy-start | bytes 1474564
  5.0 83.5 %copy-start = (bf16[512,384]{1,0:T(8,128)(2,1)S(1)}, bf16[512,384]{1,0:T(8,128)(2,1)}, u32[]{:S(2)}) copy-start(bf16[512,384]{1,0:T(8,128)(2,1)} %get-tuple-element.74.refs_0_) | copy-start | bytes 1179652
  5.0 83.5 %copy-start.2 = (s32[3]{0:T(128)S(1)}, s32[3]{0:T(128)}, u32[]{:S(2)}) copy-start(s32[3]{0:T(128)} %pad_add_fusion.ids) | copy-start | bytes 40
  5.0 18.0 %collective-permute-start = (bf16[672,384]{1,0:T(8,128)(2,1)}, bf16[672,384]{1,0:T(8,128)(2,1)S(1)}, u32[]{:S(2)}, u32[]{:S(2)}) collective-permute-start(bf16[672,384]{1,0:T(8,128)(2,1)} %get-tuple-element.71), channel_id=1, source_target_pairs={{0,8},{2,10},{4,12},{6,14},{8,16},{10,18},{12,20},{14,22},{16,24},... | collective-permute-start | bytes 1548296 | tf_op jit(solution)/shard_map/ppermute | solution.py:446
  8.1 25.4 %collective-permute-start.3 = (bf16[160,1536]{1,0:T(8,128)(2,1)S(1)}, bf16[160,1536]{1,0:T(8,128)(2,1)S(1)}, u32[]{:S(2)}, u32[]{:S(2)}) collective-permute-start(bf16[160,1536]{1,0:T(8,128)(2,1)S(1)} %copy-done.3), channel_id=1, source_target_pairs={{0,8},{2,10},{4,12},{6,14},{8,16},{10,18},{12,20},{14,22},{16,24},... | collective-permute-start | bytes 1474568 | tf_op jit(solution)/shard_map/ppermute | solution.py:477
  9.6 23.9 %collective-permute-start.5 = (bf16[160,1536]{1,0:T(8,128)(2,1)S(1)}, bf16[160,1536]{1,0:T(8,128)(2,1)S(1)}, u32[]{:S(2)}, u32[]{:S(2)}) collective-permute-start(bf16[160,1536]{1,0:T(8,128)(2,1)S(1)} %copy-done.3), channel_id=1, source_target_pairs={{0,1},{1,0},{2,3},{3,2},{4,5},{5,4},{6,7},{7,6},{8,9},{9,8},{10,11... | collective-permute-start | bytes 1474568 | tf_op jit(solution)/shard_map/ppermute | solution.py:49
  11.2 11.9 %collective-permute-start.4 = (bf16[512,384]{1,0:T(8,128)(2,1)}, bf16[512,384]{1,0:T(8,128)(2,1)S(1)}, u32[]{:S(2)}, u32[]{:S(2)}) collective-permute-start(bf16[512,384]{1,0:T(8,128)(2,1)} %get-tuple-element.74.refs_0_), channel_id=1, source_target_pairs={{0,4},{2,6},{4,0},{6,2},{8,12},{10,14},{12,8},{14,10},{16,20},{18,... | collective-permute-start | bytes 1179656 | tf_op jit(solution)/shard_map/ppermute | solution.py:474
  12.6 52.7 %collective-permute-start.1 = (bf16[672,384]{1,0:T(8,128)(2,1)}, bf16[672,384]{1,0:T(8,128)(2,1)S(1)}, u32[]{:S(2)}, u32[]{:S(2)}) collective-permute-start(bf16[672,384]{1,0:T(8,128)(2,1)} %get-tuple-element.72), channel_id=1, source_target_pairs={{0,16},{2,18},{4,20},{6,22},{8,24},{10,26},{12,28},{14,30},{16,0},... | collective-permute-start | bytes 1548296 | tf_op jit(solution)/shard_map/ppermute | solution.py:446
  33.5 31.9 %collective-permute-start.6 = (bf16[160,1536]{1,0:T(8,128)(2,1)S(1)}, bf16[160,1536]{1,0:T(8,128)(2,1)S(1)}, u32[]{:S(2)}, u32[]{:S(2)}) collective-permute-start(bf16[160,1536]{1,0:T(8,128)(2,1)S(1)} %collective-permute-done.3.refs_5_), channel_id=1, source_target_pairs={{0,8},{2,10},{4,12},{6,14},{8,16},{10,18},{12,20},{14,22},{16,24},... | collective-permute-start | bytes 1474568 | tf_op jit(solution)/shard_map/ppermute | solution.py:477
  43.2 22.3 %collective-permute-start.8 = (bf16[160,1536]{1,0:T(8,128)(2,1)S(1)}, bf16[160,1536]{1,0:T(8,128)(2,1)S(1)}, u32[]{:S(2)}, u32[]{:S(2)}) collective-permute-start(bf16[160,1536]{1,0:T(8,128)(2,1)S(1)} %collective-permute-done.3.refs_5_), channel_id=1, source_target_pairs={{0,1},{1,0},{2,3},{3,2},{4,5},{5,4},{6,7},{7,6},{8,9},{9,8},{10,11... | collective-permute-start | bytes 1474568 | tf_op jit(solution)/shard_map/ppermute | solution.py:49
  44.7 20.7 %collective-permute-start.7 = (bf16[512,384]{1,0:T(8,128)(2,1)S(1)}, bf16[512,384]{1,0:T(8,128)(2,1)S(1)}, u32[]{:S(2)}, u32[]{:S(2)}) collective-permute-start(bf16[512,384]{1,0:T(8,128)(2,1)S(1)} %slice.12.refs_1_), channel_id=1, source_target_pairs={{0,4},{2,6},{4,0},{6,2},{8,12},{10,14},{12,8},{14,10},{16,20},{18,... | collective-permute-start | bytes 1179656 | tf_op jit(solution)/shard_map/ppermute | solution.py:474
  46.2 35.1 %collective-permute-start.2 = (bf16[672,384]{1,0:T(8,128)(2,1)}, bf16[672,384]{1,0:T(8,128)(2,1)S(1)}, u32[]{:S(2)}, u32[]{:S(2)}) collective-permute-start(bf16[672,384]{1,0:T(8,128)(2,1)} %get-tuple-element.73), channel_id=1, source_target_pairs={{0,24},{2,26},{4,28},{6,30},{8,0},{10,2},{12,4},{14,6},{16,8},{18,... | collective-permute-start | bytes 1548296 | tf_op jit(solution)/shard_map/ppermute | solution.py:446
  65.4 20.7 %collective-permute-start.9 = (bf16[160,1536]{1,0:T(8,128)(2,1)S(1)}, bf16[160,1536]{1,0:T(8,128)(2,1)S(1)}, u32[]{:S(2)}, u32[]{:S(2)}) collective-permute-start(bf16[160,1536]{1,0:T(8,128)(2,1)S(1)} %collective-permute-done.6.refs_6_), channel_id=1, source_target_pairs={{0,8},{2,10},{4,12},{6,14},{8,16},{10,18},{12,20},{14,22},{16,24},... | collective-permute-start | bytes 1474568 | tf_op jit(solution)/shard_map/ppermute | solution.py:477
  75.1 11.8 %collective-permute-start.11 = (bf16[160,1536]{1,0:T(8,128)(2,1)S(1)}, bf16[160,1536]{1,0:T(8,128)(2,1)S(1)}, u32[]{:S(2)}, u32[]{:S(2)}) collective-permute-start(bf16[160,1536]{1,0:T(8,128)(2,1)S(1)} %collective-permute-done.6.refs_6_), channel_id=1, source_target_pairs={{0,1},{1,0},{2,3},{3,2},{4,5},{5,4},{6,7},{7,6},{8,9},{9,8},{10,11... | collective-permute-start | bytes 1474568 | tf_op jit(solution)/shard_map/ppermute | solution.py:49
  76.7 9.4 %collective-permute-start.10 = (bf16[512,384]{1,0:T(8,128)(2,1)S(1)}, bf16[512,384]{1,0:T(8,128)(2,1)S(1)}, u32[]{:S(2)}, u32[]{:S(2)}) collective-permute-start(bf16[512,384]{1,0:T(8,128)(2,1)S(1)} %slice.13.refs_2_), channel_id=1, source_target_pairs={{0,4},{2,6},{4,0},{6,2},{8,12},{10,14},{12,8},{14,10},{16,20},{18,... | collective-permute-start | bytes 1179656 | tf_op jit(solution)/shard_map/ppermute | solution.py:474
  87.0 8.8 %collective-permute-start.12 = (bf16[512,384]{1,0:T(8,128)(2,1)S(1)}, bf16[512,384]{1,0:T(8,128)(2,1)S(1)}, u32[]{:S(2)}, u32[]{:S(2)}) collective-permute-start(bf16[512,384]{1,0:T(8,128)(2,1)S(1)} %slice.14.refs_3_), channel_id=1, source_target_pairs={{0,4},{2,6},{4,0},{6,2},{8,12},{10,14},{12,8},{14,10},{16,20},{18,... | collective-permute-start | bytes 1179656 | tf_op jit(solution)/shard_map/ppermute | solution.py:474
  89.1 9.0 %copy-start.1 = (bf16[160,384]{1,0:T(8,128)(2,1)S(1)}, bf16[160,384]{1,0:T(8,128)(2,1)}, u32[]{:S(2)}) copy-start(bf16[160,384]{1,0:T(8,128)(2,1)} %get-tuple-element.70.own) | copy-start | bytes 368644
  89.1 9.5 %collective-permute-start.13 = (bf16[2048,384]{1,0:T(8,128)(2,1)S(1)}, bf16[2048,384]{1,0:T(8,128)(2,1)S(1)}, u32[]{:S(2)}, u32[]{:S(2)}) collective-permute-start(bf16[2048,384]{1,0:T(8,128)(2,1)S(1)} %stack.18.refs_0_.refs_5_), channel_id=1, source_target_pairs={{0,2},{2,0},{4,6},{6,4},{8,10},{10,8},{12,14},{14,12},{16,18},{18,... | collective-permute-start | bytes 4718600 | tf_op jit(solution)/shard_map/ppermute | solution.py:485
  96.4 3.5 %collective-permute-start.14 = (bf16[2048,384]{1,0:T(8,128)(2,1)S(1)}, bf16[2048,384]{1,0:T(8,128)(2,1)S(1)}, u32[]{:S(2)}, u32[]{:S(2)}) collective-permute-start(bf16[2048,384]{1,0:T(8,128)(2,1)S(1)} %stack.19.refs_1_.refs_6_), channel_id=1, source_target_pairs={{0,2},{2,0},{4,6},{6,4},{8,10},{10,8},{12,14},{14,12},{16,18},{18,... | collective-permute-start | bytes 4718600 | tf_op jit(solution)/shard_map/ppermute | solution.py:485
  96.5 13.6 %collective-permute-start.15 = (bf16[160,1536]{1,0:T(8,128)(2,1)S(1)}, bf16[160,1536]{1,0:T(8,128)(2,1)S(1)}, u32[]{:S(2)}, u32[]{:S(2)}) collective-permute-start(bf16[160,1536]{1,0:T(8,128)(2,1)S(1)} %collective-permute-done.9.refs_7_), channel_id=1, source_target_pairs={{0,1},{1,0},{2,3},{3,2},{4,5},{5,4},{6,7},{7,6},{8,9},{9,8},{10,11... | collective-permute-start | bytes 1474568 | tf_op jit(solution)/shard_map/ppermute | solution.py:49
  115.6 7.0 %collective-permute-start.17 = (bf16[1536,384]{1,0:T(8,128)(2,1)S(1)}, bf16[1536,384]{1,0:T(8,128)(2,1)S(1)}, u32[]{:S(2)}, u32[]{:S(2)}) collective-permute-start(bf16[1536,384]{1,0:T(8,128)(2,1)S(1)} %get-tuple-element.101), channel_id=1, source_target_pairs={{0,2},{2,0},{4,6},{6,4},{8,10},{10,8},{12,14},{14,12},{16,18},{18,... | collective-permute-start | bytes 3538952 | tf_op jit(solution)/shard_map/ppermute | solution.py:366
  119.8 2.2 %collective-permute-start.16 = (bf16[2560,128]{1,0:T(8,128)(2,1)S(1)}, bf16[2560,128]{1,0:T(8,128)(2,1)S(1)}, u32[]{:S(2)}, u32[]{:S(2)}) collective-permute-start(bf16[2560,128]{1,0:T(8,128)(2,1)S(1)} %get-tuple-element.97), channel_id=1, source_target_pairs={{0,2},{2,0},{4,6},{6,4},{8,10},{10,8},{12,14},{14,12},{16,18},{18,... | collective-permute-start | bytes 1966088 | tf_op jit(solution)/shard_map/ppermute | solution.py:366
  123.5 22.7 %collective-permute-start.19 = (bf16[768,384]{1,0:T(8,128)(2,1)S(1)}, bf16[768,384]{1,0:T(8,128)(2,1)S(1)}, u32[]{:S(2)}, u32[]{:S(2)}) collective-permute-start(bf16[768,384]{1,0:T(8,128)(2,1)S(1)} %get-tuple-element.109), channel_id=1, source_target_pairs={{0,4},{2,6},{4,0},{6,2},{8,12},{10,14},{12,8},{14,10},{16,20},{18,... | collective-permute-start | bytes 1769480 | tf_op jit(solution)/shard_map/ppermute | solution.py:502
  125.0 21.1 %collective-permute-start.18 = (bf16[1280,128]{1,0:T(8,128)(2,1)S(1)}, bf16[1280,128]{1,0:T(8,128)(2,1)S(1)}, u32[]{:S(2)}, u32[]{:S(2)}) collective-permute-start(bf16[1280,128]{1,0:T(8,128)(2,1)S(1)} %get-tuple-element.108), channel_id=1, source_target_pairs={{0,4},{2,6},{4,0},{6,2},{8,12},{10,14},{12,8},{14,10},{16,20},{18,... | collective-permute-start | bytes 983048 | tf_op jit(solution)/shard_map/ppermute | solution.py:501
  146.1 3.0 %collective-permute-start.23 = (bf16[2560,256]{1,0:T(8,128)(2,1)S(1)}, bf16[2560,256]{1,0:T(8,128)(2,1)S(1)}, u32[]{:S(2)}, u32[]{:S(2)}) collective-permute-start(bf16[2560,256]{1,0:T(8,128)(2,1)S(1)} %get-tuple-element.122), channel_id=1, source_target_pairs={{0,2},{2,0},{4,6},{6,4},{8,10},{10,8},{12,14},{14,12},{16,18},{18,... | collective-permute-start | bytes 3932168 | tf_op jit(solution)/shard_map/ppermute | solution.py:366
  150.0 16.8 %collective-permute-start.24 = (bf16[1280,256]{1,0:T(8,128)(2,1)S(1)}, bf16[1280,256]{1,0:T(8,128)(2,1)S(1)}, u32[]{:S(2)}, u32[]{:S(2)}) collective-permute-start(bf16[1280,256]{1,0:T(8,128)(2,1)S(1)} %get-tuple-element.124), channel_id=1, source_target_pairs={{0,4},{2,6},{4,0},{6,2},{8,12},{10,14},{12,8},{14,10},{16,20},{18,... | collective-permute-start | bytes 1966088 | tf_op jit(solution)/shard_map/ppermute | solution.py:511
  152.4 19.6 %collective-permute-start.20 = (bf16[352,384]{1,0:T(8,128)(2,1)S(1)}, bf16[352,384]{1,0:T(8,128)(2,1)S(1)}, u32[]{:S(2)}, u32[]{:S(2)}) collective-permute-start(bf16[352,384]{1,0:T(8,128)(2,1)S(1)} %get-tuple-element.118), channel_id=1, source_target_pairs={{0,24},{2,26},{4,28},{6,30},{8,0},{10,2},{12,4},{14,6},{16,8},{18,... | collective-permute-start | bytes 811016 | tf_op jit(solution)/shard_map/ppermute | solution.py:446
  154.9 37.2 %collective-permute-start.21 = (bf16[352,384]{1,0:T(8,128)(2,1)S(1)}, bf16[352,384]{1,0:T(8,128)(2,1)S(1)}, u32[]{:S(2)}, u32[]{:S(2)}) collective-permute-start(bf16[352,384]{1,0:T(8,128)(2,1)S(1)} %get-tuple-element.119), channel_id=1, source_target_pairs={{0,16},{2,18},{4,20},{6,22},{8,24},{10,26},{12,28},{14,30},{16,0},... | collective-permute-start | bytes 811016 | tf_op jit(solution)/shard_map/ppermute | solution.py:446
  156.8 35.3 %collective-permute-start.22 = (bf16[352,384]{1,0:T(8,128)(2,1)S(1)}, bf16[352,384]{1,0:T(8,128)(2,1)S(1)}, u32[]{:S(2)}, u32[]{:S(2)}) collective-permute-start(bf16[352,384]{1,0:T(8,128)(2,1)S(1)} %get-tuple-element.120), channel_id=1, source_target_pairs={{0,8},{2,10},{4,12},{6,14},{8,16},{10,18},{12,20},{14,22},{16,24},... | collective-permute-start | bytes 811016 | tf_op jit(solution)/shard_map/ppermute | solution.py:446
  167.6 26.2 %collective-permute-start.25 = (bf16[160,768]{1,0:T(8,128)(2,1)S(1)}, bf16[160,768]{1,0:T(8,128)(2,1)S(1)}, u32[]{:S(2)}, u32[]{:S(2)}) collective-permute-start(bf16[160,768]{1,0:T(8,128)(2,1)S(1)} %get-tuple-element.130), channel_id=1, source_target_pairs={{0,24},{2,26},{4,28},{6,30},{8,0},{10,2},{12,4},{14,6},{16,8},{18,... | collective-permute-start | bytes 737288 | tf_op jit(solution)/shard_map/ppermute | solution.py:446
  170.1 31.4 %collective-permute-start.26 = (bf16[160,768]{1,0:T(8,128)(2,1)S(1)}, bf16[160,768]{1,0:T(8,128)(2,1)S(1)}, u32[]{:S(2)}, u32[]{:S(2)}) collective-permute-start(bf16[160,768]{1,0:T(8,128)(2,1)S(1)} %get-tuple-element.131), channel_id=1, source_target_pairs={{0,16},{2,18},{4,20},{6,22},{8,24},{10,26},{12,28},{14,30},{16,0},... | collective-permute-start | bytes 737288 | tf_op jit(solution)/shard_map/ppermute | solution.py:446
  172.0 29.5 %collective-permute-start.27 = (bf16[160,768]{1,0:T(8,128)(2,1)S(1)}, bf16[160,768]{1,0:T(8,128)(2,1)S(1)}, u32[]{:S(2)}, u32[]{:S(2)}) collective-permute-start(bf16[160,768]{1,0:T(8,128)(2,1)S(1)} %get-tuple-element.132), channel_id=1, source_target_pairs={{0,8},{2,10},{4,12},{6,14},{8,16},{10,18},{12,20},{14,22},{16,24},... | collective-permute-start | bytes 737288 | tf_op jit(solution)/shard_map/ppermute | solution.py:446

commit v6 on v4

--- a/solution.py
+++ b/solution.py
@@ -293,10 +293,18 @@
     return group * n_tok + jnp.bitwise_xor(ids[1], relative_of(position, bits_of(n_tok)))
 
 
-def project_kernel(n_groups, n_tok, n_space, ids, attn, *refs):
+def tokens_of(ids, tokens, grads, n_groups, n_space):
+    rows, part = grads[0].shape
+    for r in range(n_space):
+        for s in range(n_groups):
+            tokens[s * rows : (s + 1) * rows, :] = grads[r * n_groups + s][...]
+        start = jnp.bitwise_xor(ids[2], relative_of(r, bits_of(n_space))) * part
+        yield tokens[...], pl.ds(aligned(start, 16), part)
+
+
+def attn_kernel(n_groups, n_tok, n_space, ids, *refs):
     blocks, grads = refs[:n_tok], refs[n_tok : n_tok + n_groups * n_space]
-    grad_attn, kept, sent, weight, whole, tokens = refs[n_tok + n_groups * n_space :]
-    rows, part = grads[0].shape
+    grad_attn, weight, tokens = refs[n_tok + n_groups * n_space :]
     depth = weight.shape[0] // (n_groups * n_tok)
     first = blocks[0].shape[0] - n_groups * depth
     for j in range(n_tok):
@@ -305,16 +313,39 @@
             at = first + s * depth
             weight[pl.ds(aligned(place, 16), depth), :] = blocks[j][at : at + depth, :]
     total = None
-    for r in range(n_space):
-        for s in range(n_groups):
-            tokens[s * rows : (s + 1) * rows, :] = grads[r * n_groups + s][...]
-        start = jnp.bitwise_xor(ids[2], relative_of(r, bits_of(n_space))) * part
-        block = tokens[...]
-        here = pl.ds(aligned(start, 16), part)
+    for block, here in tokens_of(ids, tokens, grads, n_groups, n_space):
         term = dot(block, weight[here, :], ((1,), (0,)))
         total = term if total is None else total + term
+    grad_attn[...] = total.astype(BF16)
+
+
+def projection_cost(n_q, total, gw):
+    return pl.CostEstimate(
+        flops=2 * n_q * total * gw,
+        bytes_accessed=2 * (n_q * total + total * gw + n_q * gw),
+        transcendentals=0,
+    )
+
+
+def attn_gradient(ids, blocks, grads, depth, n_groups, n_tok, n_space):
+    rows, part = grads[0].shape
+    n_q, gw = rows * n_groups, blocks[0].shape[1]
+    total = n_groups * n_tok * depth
+    return whole_call(
+        functools.partial(attn_kernel, n_groups, n_tok, n_space),
+        jax.ShapeDtypeStruct((n_q, gw), BF16),
+        (ids, *blocks, *grads),
+        "attn_gradient",
+        [pltpu.VMEM((total, gw), BF16), pltpu.VMEM((n_q, part), BF16)],
+        projection_cost(n_q, total, gw),
+    )
+
+
+def proj_kernel(n_groups, n_tok, n_space, ids, attn, *refs):
+    grads, (kept, sent, whole, tokens) = refs[: n_groups * n_space], refs[n_groups * n_space :]
+    depth = whole.shape[0] // (n_groups * n_tok)
+    for block, here in tokens_of(ids, tokens, grads, n_groups, n_space):
         whole[here, :] = dot(block, attn[...], ((0,), (0,))).astype(BF16)
-    grad_attn[...] = total.astype(BF16)
     per_half = max(1, n_tok // 2)
     for j in range(n_tok):
         half = sent if j >= per_half else kept
@@ -324,26 +355,18 @@
             half[at : at + depth, :] = whole[pl.ds(aligned(place, 16), depth), :]
 
 
-def project(ids, attn, blocks, grads, depth, n_groups, n_tok, n_space):
+def proj_gradient(ids, attn, grads, depth, n_groups, n_tok, n_space):
     n_q, gw = attn.shape
     part = grads[0].shape[1]
     half = n_groups * depth * max(1, n_tok // 2)
     total = n_groups * n_tok * depth
     return whole_call(
-        functools.partial(project_kernel, n_groups, n_tok, n_space),
-        [jax.ShapeDtypeStruct((n_q, gw), BF16)] + [jax.ShapeDtypeStruct((half, gw), BF16)] * 2,
-        (ids, attn, *blocks, *grads),
-        "project",
-        [
-            pltpu.VMEM((total, gw), BF16),
-            pltpu.VMEM((total, gw), BF16),
-            pltpu.VMEM((n_q, part), BF16),
-        ],
-        pl.CostEstimate(
-            flops=4 * n_q * total * gw,
-            bytes_accessed=2 * (n_q * total + 2 * total * gw + 2 * n_q * gw),
-            transcendentals=0,
-        ),
+        functools.partial(proj_kernel, n_groups, n_tok, n_space),
+        [jax.ShapeDtypeStruct((half, gw), BF16)] * 2,
+        (ids, attn, *grads),
+        "proj_gradient",
+        [pltpu.VMEM((total, gw), BF16), pltpu.VMEM((n_q, part), BF16)],
+        projection_cost(n_q, total, gw),
     )
 
 
@@ -389,25 +412,23 @@
     )
 
 
-def unpack_kernel(n_groups, ids, *refs):
+def unpack_kernel(n_groups, widths, ids, *refs):
     pieces, outs = refs[:-3], refs[-3:]
     rows, gw = outs[0].shape[0], outs[0].shape[1] // n_groups
     before = 0
-    for c in range(0, len(pieces), n_groups):
-        cols = pieces[c].shape[1]
+    for c, cols in enumerate(widths):
         for s in range(n_groups):
             start = lax.rem(ids[0] + s, n_groups) * gw + before
             for i, out in enumerate(outs):
-                piece = pieces[c + s][i * rows : (i + 1) * rows, :]
+                piece = pieces[c * n_groups + s][i * rows : (i + 1) * rows, :]
                 out[:, pl.ds(aligned(start, HD), cols)] = piece
         before += cols
 
 
-def unpack(ids, chunks, n_groups):
-    rows = chunks[0][0].shape[0] // 3
-    gw = sum(pieces[0].shape[1] for pieces in chunks)
+def unpack(ids, chunks, rows, gw, n_groups):
+    widths = [HD, gw - HD][: len(chunks)]
     return whole_call(
-        functools.partial(unpack_kernel, n_groups),
+        functools.partial(unpack_kernel, n_groups, widths),
         [jax.ShapeDtypeStruct((rows, gw * n_groups), BF16)] * 3,
         (ids, *[piece for pieces in chunks for piece in pieces]),
         "unpack",
@@ -443,6 +464,7 @@
     n_frame = lax.axis_size("frame")
     n_space = lax.axis_size("space")
     rows, width = queries.shape
+    gw = width // math.gcd(width // HD, n_frame)
     depth = proj_weight.shape[1]
     n_groups = math.gcd(width // HD, n_frame)
     n_tok = n_frame // n_groups
@@ -459,28 +481,28 @@
     *pieces, own_q = pack(ids, queries, keys, values, proj_weight.T, n_groups)
     pieces = exchange(pieces, n_groups, n_tok, 1)
     q_pieces = pieces[1:]
-    own, others = [pieces[0]], [lax.ppermute(pieces[0], "frame", last)]
-    ring = [grad_out]
-    across = [gather_blocks(grad_out, "space", n_space, space_bits)]
-    for s in range(1, n_groups):
-        piece = pieces[s][:shared]
-        if s == 1:
-            ring[0], piece, others[0], *across[0] = tie((ring[0], piece, others[0], *across[0]))
-            ring.append(lax.ppermute(ring[0], "frame", shift_pairs(n_groups, n_tok, 1)))
-        own.append(piece)
-        others.append(lax.ppermute(piece, "frame", last))
-        if s == 1 and n_groups > 2:
-            ring[1], others[1], *pieces[2:] = tie((ring[1], others[1], *pieces[2:]))
-
-    for s in range(1, n_groups):
-        across.append(gather_blocks(ring[s], "space", n_space, space_bits))
-        if s + 1 < n_groups:
-            arriving = lax.ppermute(ring[s], "frame", shift_pairs(n_groups, n_tok, 1))
-            count = n_groups if s == 1 else 0
-            tied = tie((arriving, *across[s], *others[:count]))
-            arriving, across[s] = tied[0], list(tied[1 : 1 + n_space])
-            others[:count] = tied[1 + n_space :]
-            ring.append(arriving)
+    middle = n_groups // 2
+    plan = [[middle], [s for s in range(1, n_groups) if s != middle]]
+    others, ring, across, here = [None] * n_groups, grad_out, [], [0]
+    for step in range(n_groups):
+        for s in here:
+            pieces[s] = pieces[s][:shared]
+            others[s] = lax.ppermute(pieces[s], "frame", last)
+        across.append(gather_blocks(ring, "space", n_space, space_bits))
+        if step + 1 < n_groups:
+            ring = lax.ppermute(ring, "frame", shift_pairs(n_groups, n_tok, 1))
+            coming = plan[step] if step < len(plan) else []
+            sent = here if coming else []
+            values_of = [ring, *across[step]]
+            values_of += [pieces[s] for s in coming] + [others[s] for s in sent]
+            ring, *tied = tie(tuple(values_of))
+            across[step] = tied[:n_space]
+            for s, piece in zip(coming, tied[n_space:]):
+                pieces[s] = piece
+            for s, piece in zip(sent, tied[n_space + len(coming) :]):
+                others[s] = piece
+            here = coming
+    own = pieces
 
     q = stack_queries(ids, own_q, q_pieces)
     blocks = [stack(ids, own, rows), stack(ids, others, rows)]
@@ -489,34 +511,38 @@
     part = n_groups * rows
     probs, out, inverse = forward(q, blocks, part)
     grads = [across[s][r] for r in range(n_space) for s in range(n_groups)]
-    grad_attn, kept, sent = project(ids, out, blocks, grads, depth, n_groups, n_tok, n_space)
-
-    def attention_chunk(head, count, q, *before):
-        dq, halves = backward(
-            head, count, q, blocks, part, probs, out, inverse, grad_attn, n_groups
-        )
-        kept, sent, *before = tie((*halves, *before))
-        return dq, halve(ids, kept, sent, n_frame, tok_bits), *before
-
-    proj_kept, proj_sent = halve(ids, kept, sent, n_frame, tok_bits)
-    dq, (kept, sent) = attention_chunk(0, 1, q)
-    returned = []
+    grad_attn = attn_gradient(ids, blocks, grads, depth, n_groups, n_tok, n_space)
+
+    def attention_halves(head, count, q):
+        return backward(head, count, q, blocks, part, probs, out, inverse, grad_attn, n_groups)
+
+    def across_x(piece):
+        return lax.ppermute(piece, "frame", last)
+
+    dq, (kept, sent) = attention_halves(0, 1, q)
+    out_after, kept, sent = tie((out, kept, sent))
+    kept, sent = halve(ids, kept, sent, n_frame, tok_bits)
+    proj = proj_gradient(ids, out_after, grads, depth, n_groups, n_tok, n_space)
+    q, kept, sent, *proj = tie((q, kept, sent, *proj))
+    other = across_x(sent)
+    proj_kept, proj_sent = halve(ids, *proj, n_frame, tok_bits)
     if heads > 1:
-        q, kept, sent, proj_kept, proj_sent = tie((q, kept, sent, proj_kept, proj_sent))
-        other = lax.ppermute(sent, "frame", last)
-        next_dq, (next_kept, sent), other = attention_chunk(1, heads - 1, q, other)
-        sums = finish(ids, kept, other, dq, n_groups)
-        proj_sent, *sums = tie((proj_sent, *sums))
+        dq_rest, halves = attention_halves(1, heads - 1, q)
+        other, proj_sent, *halves = tie((other, proj_sent, *halves))
+    sums = finish(ids, kept, other, dq, n_groups)
+    proj_sent, *sums = tie((proj_sent, *sums))
+    returned = [exchange(sums, n_groups, n_tok, -1)]
+    proj_other = across_x(proj_sent)
+    if heads > 1:
+        kept, sent = halve(ids, *halves, n_frame, tok_bits)
+        proj_other, sent, *returned[0][1:] = tie((proj_other, sent, *returned[0][1:]))
+    proj_pieces = exchange(add_parts(ids, proj_kept, proj_other, n_groups), n_groups, n_tok, 1)
+    if heads > 1:
+        other, *proj_pieces[1:] = tie((across_x(sent), *proj_pieces[1:]))
+        sums = finish(ids, kept, other, dq_rest, n_groups)
         returned.append(exchange(sums, n_groups, n_tok, -1))
-        dq, kept = next_dq, next_kept
-    other = lax.ppermute(proj_sent, "frame", last)
-    proj = exchange(add_parts(ids, proj_kept, other, n_groups), n_groups, n_tok, 1)
-    other = lax.ppermute(sent, "frame", last)
-    if returned:
-        other, *returned[0][1:-1] = tie((other, *returned[0][1:-1]))
-    returned.append(exchange(finish(ids, kept, other, dq, n_groups), n_groups, n_tok, -1))
-    grad_proj = join(ids, proj, n_groups).T
-    grad_queries, grad_keys, grad_values = unpack(ids, returned, n_groups)
+    grad_proj = join(ids, proj_pieces, n_groups).T
+    grad_queries, grad_keys, grad_values = unpack(ids, returned, rows, gw, n_groups)
     return (grad_queries, grad_keys, grad_values, grad_proj)
 
 

time: 225 us -> 207 us (0.920)
  starting transfers between devices: 81 us -> 32.9 us
  waiting for transfers between devices: 98.6 us -> 129 us
    ppermute x12, waiting for transfers between devices: 27.2 us -> 76.7 us  [exchange(): lax.ppermute(pieces[s], 'frame', shift_pairs(n_groups, n_tok, sign * s))]
    ppermute x10, starting transfers between devices: 52.1 us -> 10.1 us  [the longest x4 5.14 us: local(): others[s] = lax.ppermute(pieces[s], 'frame', last)]
    ppermute x10, waiting for transfers between devices: 65.4 us -> 51 us  [the longest x4 25.4 us: local(): others[s] = lax.ppermute(pieces[s], 'frame', last)]
    ppermute x12, starting transfers between devices: 24 us -> 16.5 us  [exchange(): lax.ppermute(pieces[s], 'frame', shift_pairs(n_groups, n_tok, sign * s))]
    ppermute x3, waiting for transfers between devices: 4.69 us -> 0.01 us  [halve(): other = lax.ppermute(sent, 'frame', xor_pairs(n_frame, bit))]
    pallas_call x12 -> x13, Pallas kernels: 15.3 us -> 16 us  [whole_call(): pl.pallas_call(body, out_shape=out_shape, in_specs=[smem()] + [vmem()] *...]
  transfers between devices with their start and end apart: 31 -> 31, of which waited for: 15 -> 16; matrix products, arithmetic and copies ran while one was open for 0% -> 0% of each run, Pallas kernels for 13% -> 14%
where the time goes in v6:
time: 207 us; the launch traced here: 206 us
  waiting for transfers between devices  129 us (62%)
  Pallas kernels  42.7 us (21%)
  starting transfers between devices  32.9 us (16%)
    ppermute x12, waiting for transfers between devices, exchange(): lax.ppermute(pieces[s], 'frame', shift_pairs(n_groups, n_tok, sign * s))  76.7 us
    ppermute x4, waiting for transfers between devices, local(): others[s] = lax.ppermute(pieces[s], 'frame', last)  25.4 us
    ppermute x3, waiting for transfers between devices, local(): ring = lax.ppermute(ring, 'frame', shift_pairs(n_groups, n_tok, 1))  22.4 us
    ppermute x12, starting transfers between devices, exchange(): lax.ppermute(pieces[s], 'frame', shift_pairs(n_groups, n_tok, sign * s))  16.5 us
    pallas_call x13, Pallas kernels, whole_call(): pl.pallas_call(body, out_shape=out_shape, in_specs=[smem()] + [vmem()] *...  16 us
    pallas_call x2, Pallas kernels, backward(): pl.pallas_call(functools.partial(backward_kernel, n_groups, chunk, 1.0 /...  12.7 us
    pallas_call x1, Pallas kernels, forward(): pl.pallas_call(functools.partial(forward_kernel, chunk, scale), grid=(hea...  10.2 us
    ppermute x4, starting transfers between devices, gather_blocks(): lax.ppermute(b, axis, xor_pairs(count, bit))  5.4 us
  transfers between devices with their start and end apart: 31, of which 16 were waited for; matrix products, arithmetic and copies ran while one was open for 0% of the time, Pallas kernels for 14%

profile of v6, /device:TPU:0, one launch (start us, length us, event | category | flops | bytes accessed | tf_op | source)
XLA Modules:
  0.0 206.4 jit_solution(14816150827876545947)
XLA Ops:
  0.7 0.6 pad_add_fusion.ids
  1.3 3.7 %pack.1 = (bf16[512,384]{1,0:T(8,128)(2,1)}, bf16[672,384]{1,0:T(8,128)(2,1)}, bf16[672,384]{1,0:T(8,128)(2,1)}, bf16[672,384]{1,0:T(8,128)(2,1)}, bf16[160,384]{1,0:T(8,128)(2,1)}) custom-call(s32[3]{0:T(128)} %pad_add_fusion.ids, bf16[160,1536]{1,0:T(8,128)(2,1)} %q.1, bf16[160,1536]{1,0:T(8,128)(2,1)} %k.1, bf16[160,1536]{1,0:T(8,128)(2,1)} %v.1, ...), custom_call_target="tpu_custom_call" | custom-call | tf_op jit(solution)/shard_map/pack/pallas_call | solution.py:119
  5.0 0.0 copy-start.1
  5.0 4.1 %collective-permute-start.1 = (bf16[672,384]{1,0:T(8,128)(2,1)}, bf16[672,384]{1,0:T(8,128)(2,1)S(1)}, u32[]{:S(2)}, u32[]{:S(2)}) collective-permute-start(bf16[672,384]{1,0:T(8,128)(2,1)} %get-tuple-element.89), channel_id=1, source_target_pairs={{0,16},{2,18},{4,20},{6,22},{8,24},{10,26},{12,28},{14,30},{16,0},... | collective-permute-start | bytes 1548296 | tf_op jit(solution)/shard_map/ppermute | solution.py:458
  9.1 1.6 collective-permute-start.3
  10.7 1.5 collective-permute-start.4
  12.2 1.5 collective-permute-start.5
  13.7 8.7 %collective-permute-done.5.refs_0_ = bf16[512,384]{1,0:T(8,128)(2,1)S(1)} collective-permute-done((bf16[512,384]{1,0:T(8,128)(2,1)}, bf16[512,384]{1,0:T(8,128)(2,1)S(1)}, u32[]{:S(2)}, u32[]{:S(2)}) %collective-permute-start.5) | collective-permute-done | bytes 393248 | tf_op jit(solution)/shard_map/ppermute | solution.py:490
  22.4 2.2 %collective-permute-start.2 = (bf16[672,384]{1,0:T(8,128)(2,1)}, bf16[672,384]{1,0:T(8,128)(2,1)S(1)}, u32[]{:S(2)}, u32[]{:S(2)}) collective-permute-start(bf16[672,384]{1,0:T(8,128)(2,1)} %get-tuple-element.90), channel_id=1, source_target_pairs={{0,24},{2,26},{4,28},{6,30},{8,0},{10,2},{12,4},{14,6},{16,8},{18,... | collective-permute-start | bytes 1548296 | tf_op jit(solution)/shard_map/ppermute | solution.py:458
  24.7 9.3 %collective-permute-done.3.refs_5_.refs_1_ = bf16[160,1536]{1,0:T(8,128)(2,1)S(1)} collective-permute-done((bf16[160,1536]{1,0:T(8,128)(2,1)S(1)}, bf16[160,1536]{1,0:T(8,128)(2,1)S(1)}, u32[]{:S(2)}, u32[]{:S(2)}) %collective-permute-start.3) | collective-permute-done | bytes 491552 | tf_op jit(solution)/shard_map/ppermute | solution.py:493
  34.0 20.6 %collective-permute-done.1.refs_1_ = bf16[672,384]{1,0:T(8,128)(2,1)S(1)} collective-permute-done((bf16[672,384]{1,0:T(8,128)(2,1)}, bf16[672,384]{1,0:T(8,128)(2,1)S(1)}, u32[]{:S(2)}, u32[]{:S(2)}) %collective-permute-start.1) | collective-permute-done | bytes 516128 | tf_op jit(solution)/shard_map/ppermute | solution.py:458
  54.6 1.9 collective-permute-start.7
  56.5 1.6 collective-permute-start.8
  58.1 17.2 %collective-permute-done.2.refs_2_ = bf16[672,384]{1,0:T(8,128)(2,1)S(1)} collective-permute-done((bf16[672,384]{1,0:T(8,128)(2,1)}, bf16[672,384]{1,0:T(8,128)(2,1)S(1)}, u32[]{:S(2)}, u32[]{:S(2)}) %collective-permute-start.2) | collective-permute-done | bytes 516128 | tf_op jit(solution)/shard_map/ppermute | solution.py:458
  75.4 1.6 collective-permute-start.9
  77.0 0.5 collective-permute-start.10
  77.5 0.7 stack.18.refs_0_.refs_5_
  78.2 0.0 copy-start.2
  78.2 0.1 collective-permute-start.11
  78.3 9.2 %collective-permute-done.9.refs_1_ = bf16[512,384]{1,0:T(8,128)(2,1)S(1)} collective-permute-done((bf16[512,384]{1,0:T(8,128)(2,1)S(1)}, bf16[512,384]{1,0:T(8,128)(2,1)S(1)}, u32[]{:S(2)}, u32[]{:S(2)}) %collective-permute-start.9) | collective-permute-done | bytes 393248 | tf_op jit(solution)/shard_map/ppermute | solution.py:490
  87.5 7.5 %collective-permute-done.10.refs_3_ = bf16[512,384]{1,0:T(8,128)(2,1)S(1)} collective-permute-done((bf16[512,384]{1,0:T(8,128)(2,1)S(1)}, bf16[512,384]{1,0:T(8,128)(2,1)S(1)}, u32[]{:S(2)}, u32[]{:S(2)}) %collective-permute-start.10) | collective-permute-done | bytes 393248 | tf_op jit(solution)/shard_map/ppermute | solution.py:490
  94.9 0.7 stack.19.refs_1_.refs_6_
  95.6 0.1 collective-permute-start.12
  95.7 0.8 collective-permute-start.13
  96.5 1.5 collective-permute-start.14
  98.0 13.1 %collective-permute-done.13.refs_7_.refs_3_ = bf16[160,1536]{1,0:T(8,128)(2,1)S(1)} collective-permute-done((bf16[160,1536]{1,0:T(8,128)(2,1)S(1)}, bf16[160,1536]{1,0:T(8,128)(2,1)S(1)}, u32[]{:S(2)}, u32[]{:S(2)}) %collective-permute-start.13) | collective-permute-done | bytes 491552 | tf_op jit(solution)/shard_map/ppermute | solution.py:493
  111.1 0.5 collective-permute-start.15
  111.6 0.6 stack_queries.1.q_in.refs_0_
  112.2 10.2 %forward.1 = (bf16[3,2560,640]{2,1,0:T(8,128)(2,1)S(1)}, bf16[640,384]{1,0:T(8,128)(2,1)S(1)}, f32[3,1,640]{2,1,0:T(1,128)S(1)}) custom-call(bf16[640,384]{1,0:T(8,128)(2,1)S(1)} %stack_queries.1.q_in.refs_0_, bf16[2048,384]{1,0:T(8,128)(2,1)S(1)} %stack.18.refs_0_.refs_5_, bf16[2048,384]{1,0:T(8,128)(2,1)S(1)} %stack.19.refs_1_.refs_6_, ...), custom_call_target="tpu_custom_call" | custom-call | flops 2516582400 | bytes 9830400 | tf_op jit(solution)/shard_map/forward/pallas_call | solution.py:200
  122.5 1.4 collective-permute-done.15.refs_11_.refs_7_
  123.9 3.0 %attn_gradient.1.refs_4_ = bf16[640,384]{1,0:T(8,128)(2,1)S(1)} custom-call(s32[3]{0:T(128)S(1)} %copy-done.3, bf16[2048,384]{1,0:T(8,128)(2,1)S(1)} %stack.18.refs_0_.refs_5_, bf16[2048,384]{1,0:T(8,128)(2,1)S(1)} %stack.19.refs_1_.refs_6_, bf16[2048,384]{1,0:T(8,128)(2,1)S(1)} %collective-permute-done.11.refs_2_.refs_7_, ...), custom_call_target="tpu_custom_call" | custom-call | flops 1509949440 | bytes 6782976 | tf_op jit(solution)/shard_map/attn_gradient/pallas_call | solution.py:75
  126.9 3.9 %backward.2 = (bf16[160,128]{1,0:T(8,128)(2,1)S(1)}, bf16[160,128]{1,0:T(8,128)(2,1)S(1)}, bf16[160,128]{1,0:T(8,128)(2,1)S(1)}, bf16[160,128]{1,0:T(8,128)(2,1)...) custom-call(bf16[640,384]{1,0:T(8,128)(2,1)S(1)} %stack_queries.1.q_in.refs_0_, ...), custom_call_target="tpu_custom_call" | custom-call | flops 81920 | bytes 163840 | tf_op jit(solution)/shard_map/backward/pallas_call | solution.py:264
  130.8 0.1 collective-permute-start.16
  130.9 3.3 %proj_gradient.1 = (bf16[1536,384]{1,0:T(8,128)(2,1)S(1)}, bf16[1536,384]{1,0:T(8,128)(2,1)S(1)}) custom-call(s32[3]{0:T(128)S(1)} %copy-done.3, bf16[640,384]{1,0:T(8,128)(2,1)S(1)} %get-tuple-element.115.refs_2_.attn, bf16[160,1536]{1,0:T(8,128)(2,1)S(1)} %copy-done, bf16[160,1536]{1,0:T(8,128)(2,1)S(1)} %collective-permute-done.3.refs_5_.refs_1_, ...), custom_call_target="tpu_custom_call" | custom-call | flops 1509949440 | bytes 6782976 | tf_op jit(solution)/shard_map/proj_gradient/pallas_call | solution.py:75
  134.1 0.7 add_parts.4
  134.8 0.6 collective-permute-start.18
  135.4 1.5 collective-permute-start.17
  136.9 8.8 %backward.3 = (bf16[160,256]{1,0:T(8,128)(2,1)S(1)}, bf16[160,256]{1,0:T(8,128)(2,1)S(1)}, bf16[160,256]{1,0:T(8,128)(2,1)S(1)}, bf16[160,256]{1,0:T(8,128)(2,1)...) custom-call(bf16[640,384]{1,0:T(8,128)(2,1)S(1)} %stack_queries.1.q_in.refs_0_, ...), custom_call_target="tpu_custom_call" | custom-call | flops 81920 | bytes 163840 | tf_op jit(solution)/shard_map/backward/pallas_call | solution.py:264
  145.8 0.8 add_parts.5
  146.6 0.1 collective-permute-start.20
  146.7 0.6 finish.2
  147.3 0.6 collective-permute-start.19
  147.9 1.4 collective-permute-start.21
  149.3 0.9 collective-permute-start.22
  150.2 0.6 collective-permute-start.23
  150.8 0.8 add_parts.6
  151.7 1.8 collective-permute-done.21.refs_1_
  153.5 8.0 %collective-permute-done.22.refs_2_ = bf16[480,128]{1,0:T(8,128)(2,1)S(1)} collective-permute-done((bf16[480,128]{1,0:T(8,128)(2,1)S(1)}, bf16[480,128]{1,0:T(8,128)(2,1)S(1)}, u32[]{:S(2)}, u32[]{:S(2)}) %collective-permute-start.22) | collective-permute-done | bytes 122912 | tf_op jit(solution)/shard_map/ppermute | solution.py:458
  161.5 1.6 collective-permute-done.19.other
  163.1 0.5 collective-permute-start.24
  163.6 0.7 add_parts.7
  164.3 0.9 collective-permute-start.25
  165.2 1.1 collective-permute-start.26
  166.3 2.1 %collective-permute-start.27 = (bf16[192,384]{1,0:T(8,128)(2,1)S(1)}, bf16[192,384]{1,0:T(8,128)(2,1)S(1)}, u32[]{:S(2)}, u32[]{:S(2)}) collective-permute-start(bf16[192,384]{1,0:T(8,128)(2,1)S(1)} %get-tuple-element.153), channel_id=1, source_target_pairs={{0,24},{2,26},{4,28},{6,30},{8,0},{10,2},{12,4},{14,6},{16,8},{18,... | collective-permute-start | bytes 442376 | tf_op jit(solution)/shard_map/ppermute | solution.py:458
  168.5 4.5 %collective-permute-done.25.refs_1_ = bf16[192,384]{1,0:T(8,128)(2,1)S(1)} collective-permute-done((bf16[192,384]{1,0:T(8,128)(2,1)S(1)}, bf16[192,384]{1,0:T(8,128)(2,1)S(1)}, u32[]{:S(2)}, u32[]{:S(2)}) %collective-permute-start.25) | collective-permute-done | bytes 147488 | tf_op jit(solution)/shard_map/ppermute | solution.py:458
  173.0 4.8 %collective-permute-done.26.refs_2_ = bf16[192,384]{1,0:T(8,128)(2,1)S(1)} collective-permute-done((bf16[192,384]{1,0:T(8,128)(2,1)S(1)}, bf16[192,384]{1,0:T(8,128)(2,1)S(1)}, u32[]{:S(2)}, u32[]{:S(2)}) %collective-permute-start.26) | collective-permute-done | bytes 147488 | tf_op jit(solution)/shard_map/ppermute | solution.py:458
  177.8 1.7 collective-permute-done.24.other
  179.5 0.7 finish.3
  180.2 1.7 collective-permute-start.28
  181.9 1.4 collective-permute-start.29
  183.3 1.7 join.1
  184.9 3.4 %collective-permute-done.28.refs_5_ = bf16[480,256]{1,0:T(8,128)(2,1)S(1)} collective-permute-done((bf16[480,256]{1,0:T(8,128)(2,1)S(1)}, bf16[480,256]{1,0:T(8,128)(2,1)S(1)}, u32[]{:S(2)}, u32[]{:S(2)}) %collective-permute-start.28) | collective-permute-done | bytes 245792 | tf_op jit(solution)/shard_map/ppermute | solution.py:458
  188.3 16.2 %collective-permute-done.29.refs_6_ = bf16[480,256]{1,0:T(8,128)(2,1)S(1)} collective-permute-done((bf16[480,256]{1,0:T(8,128)(2,1)S(1)}, bf16[480,256]{1,0:T(8,128)(2,1)S(1)}, u32[]{:S(2)}, u32[]{:S(2)}) %collective-permute-start.29) | collective-permute-done | bytes 245792 | tf_op jit(solution)/shard_map/ppermute | solution.py:458
  204.5 1.8 unpack.1
  (27 shorter events, 0.2 us)
Async XLA Ops:
  0.6 8.5 %copy-start = (bf16[160,1536]{1,0:T(8,128)(2,1)S(1)}, bf16[160,1536]{1,0:T(8,128)(2,1)}, u32[]{:S(2)}) copy-start(bf16[160,1536]{1,0:T(8,128)(2,1)} %refs_0_) | copy-start | bytes 1474564
  5.0 72.5 %copy-start.1 = (bf16[512,384]{1,0:T(8,128)(2,1)S(1)}, bf16[512,384]{1,0:T(8,128)(2,1)}, u32[]{:S(2)}) copy-start(bf16[512,384]{1,0:T(8,128)(2,1)} %get-tuple-element.91.refs_0_) | copy-start | bytes 1179652
  5.0 72.5 %copy-start.3 = (s32[3]{0:T(128)S(1)}, s32[3]{0:T(128)}, u32[]{:S(2)}) copy-start(s32[3]{0:T(128)} %pad_add_fusion.ids) | copy-start | bytes 40
  5.0 49.6 %collective-permute-start.1 = (bf16[672,384]{1,0:T(8,128)(2,1)}, bf16[672,384]{1,0:T(8,128)(2,1)S(1)}, u32[]{:S(2)}, u32[]{:S(2)}) collective-permute-start(bf16[672,384]{1,0:T(8,128)(2,1)} %get-tuple-element.89), channel_id=1, source_target_pairs={{0,16},{2,18},{4,20},{6,22},{8,24},{10,26},{12,28},{14,30},{16,0},... | collective-permute-start | bytes 1548296 | tf_op jit(solution)/shard_map/ppermute | solution.py:458
  9.1 24.9 %collective-permute-start.3 = (bf16[160,1536]{1,0:T(8,128)(2,1)S(1)}, bf16[160,1536]{1,0:T(8,128)(2,1)S(1)}, u32[]{:S(2)}, u32[]{:S(2)}) collective-permute-start(bf16[160,1536]{1,0:T(8,128)(2,1)S(1)} %copy-done), channel_id=1, source_target_pairs={{0,8},{2,10},{4,12},{6,14},{8,16},{10,18},{12,20},{14,22},{16,24},... | collective-permute-start | bytes 1474568 | tf_op jit(solution)/shard_map/ppermute | solution.py:493
  10.7 23.3 %collective-permute-start.4 = (bf16[160,1536]{1,0:T(8,128)(2,1)S(1)}, bf16[160,1536]{1,0:T(8,128)(2,1)S(1)}, u32[]{:S(2)}, u32[]{:S(2)}) collective-permute-start(bf16[160,1536]{1,0:T(8,128)(2,1)S(1)} %copy-done), channel_id=1, source_target_pairs={{0,1},{1,0},{2,3},{3,2},{4,5},{5,4},{6,7},{7,6},{8,9},{9,8},{10,11... | collective-permute-start | bytes 1474568 | tf_op jit(solution)/shard_map/ppermute | solution.py:49
  12.2 10.2 %collective-permute-start.5 = (bf16[512,384]{1,0:T(8,128)(2,1)}, bf16[512,384]{1,0:T(8,128)(2,1)S(1)}, u32[]{:S(2)}, u32[]{:S(2)}) collective-permute-start(bf16[512,384]{1,0:T(8,128)(2,1)} %get-tuple-element.91.refs_0_), channel_id=1, source_target_pairs={{0,4},{2,6},{4,0},{6,2},{8,12},{10,14},{12,8},{14,10},{16,20},{18,... | collective-permute-start | bytes 1179656 | tf_op jit(solution)/shard_map/ppermute | solution.py:490
  13.7 44.4 %collective-permute-start = (bf16[672,384]{1,0:T(8,128)(2,1)}, bf16[672,384]{1,0:T(8,128)(2,1)S(1)}, u32[]{:S(2)}, u32[]{:S(2)}) collective-permute-start(bf16[672,384]{1,0:T(8,128)(2,1)} %get-tuple-element.88), channel_id=1, source_target_pairs={{0,8},{2,10},{4,12},{6,14},{8,16},{10,18},{12,20},{14,22},{16,24},... | collective-permute-start | bytes 1548296 | tf_op jit(solution)/shard_map/ppermute | solution.py:458
  22.4 52.9 %collective-permute-start.2 = (bf16[672,384]{1,0:T(8,128)(2,1)}, bf16[672,384]{1,0:T(8,128)(2,1)S(1)}, u32[]{:S(2)}, u32[]{:S(2)}) collective-permute-start(bf16[672,384]{1,0:T(8,128)(2,1)} %get-tuple-element.90), channel_id=1, source_target_pairs={{0,24},{2,26},{4,28},{6,30},{8,0},{10,2},{12,4},{14,6},{16,8},{18,... | collective-permute-start | bytes 1548296 | tf_op jit(solution)/shard_map/ppermute | solution.py:458
  54.6 20.7 %collective-permute-start.6 = (bf16[160,1536]{1,0:T(8,128)(2,1)S(1)}, bf16[160,1536]{1,0:T(8,128)(2,1)S(1)}, u32[]{:S(2)}, u32[]{:S(2)}) collective-permute-start(bf16[160,1536]{1,0:T(8,128)(2,1)S(1)} %collective-permute-done.3.refs_5_.refs_1_), channel_id=1, source_target_pairs={{0,8},{2,10},{4,12},{6,14},{8,16},{10,18},{12,20},{14,22},{16,24},... | collective-permute-start | bytes 1474568 | tf_op jit(solution)/shard_map/ppermute | solution.py:493
  54.6 20.7 %collective-permute-start.7 = (bf16[160,1536]{1,0:T(8,128)(2,1)S(1)}, bf16[160,1536]{1,0:T(8,128)(2,1)S(1)}, u32[]{:S(2)}, u32[]{:S(2)}) collective-permute-start(bf16[160,1536]{1,0:T(8,128)(2,1)S(1)} %collective-permute-done.3.refs_5_.refs_1_), channel_id=1, source_target_pairs={{0,1},{1,0},{2,3},{3,2},{4,5},{5,4},{6,7},{7,6},{8,9},{9,8},{10,11... | collective-permute-start | bytes 1474568 | tf_op jit(solution)/shard_map/ppermute | solution.py:49
  56.5 18.8 %collective-permute-start.8 = (bf16[512,384]{1,0:T(8,128)(2,1)S(1)}, bf16[512,384]{1,0:T(8,128)(2,1)S(1)}, u32[]{:S(2)}, u32[]{:S(2)}) collective-permute-start(bf16[512,384]{1,0:T(8,128)(2,1)S(1)} %slice.9.refs_2_), channel_id=1, source_target_pairs={{0,4},{2,6},{4,0},{6,2},{8,12},{10,14},{12,8},{14,10},{16,20},{18,... | collective-permute-start | bytes 1179656 | tf_op jit(solution)/shard_map/ppermute | solution.py:490
  75.4 12.0 %collective-permute-start.9 = (bf16[512,384]{1,0:T(8,128)(2,1)S(1)}, bf16[512,384]{1,0:T(8,128)(2,1)S(1)}, u32[]{:S(2)}, u32[]{:S(2)}) collective-permute-start(bf16[512,384]{1,0:T(8,128)(2,1)S(1)} %slice.10.refs_1_), channel_id=1, source_target_pairs={{0,4},{2,6},{4,0},{6,2},{8,12},{10,14},{12,8},{14,10},{16,20},{18,... | collective-permute-start | bytes 1179656 | tf_op jit(solution)/shard_map/ppermute | solution.py:490
  77.0 17.9 %collective-permute-start.10 = (bf16[512,384]{1,0:T(8,128)(2,1)S(1)}, bf16[512,384]{1,0:T(8,128)(2,1)S(1)}, u32[]{:S(2)}, u32[]{:S(2)}) collective-permute-start(bf16[512,384]{1,0:T(8,128)(2,1)S(1)} %slice.11.refs_3_), channel_id=1, source_target_pairs={{0,4},{2,6},{4,0},{6,2},{8,12},{10,14},{12,8},{14,10},{16,20},{18,... | collective-permute-start | bytes 1179656 | tf_op jit(solution)/shard_map/ppermute | solution.py:490
  78.2 33.4 %copy-start.2 = (bf16[160,384]{1,0:T(8,128)(2,1)S(1)}, bf16[160,384]{1,0:T(8,128)(2,1)}, u32[]{:S(2)}) copy-start(bf16[160,384]{1,0:T(8,128)(2,1)} %get-tuple-element.87.own) | copy-start | bytes 368644
  78.2 34.0 %collective-permute-start.11 = (bf16[2048,384]{1,0:T(8,128)(2,1)S(1)}, bf16[2048,384]{1,0:T(8,128)(2,1)S(1)}, u32[]{:S(2)}, u32[]{:S(2)}) collective-permute-start(bf16[2048,384]{1,0:T(8,128)(2,1)S(1)} %stack.18.refs_0_.refs_5_), channel_id=1, source_target_pairs={{0,2},{2,0},{4,6},{6,4},{8,10},{10,8},{12,14},{14,12},{16,18},{18,... | collective-permute-start | bytes 4718600 | tf_op jit(solution)/shard_map/ppermute | solution.py:510
  95.6 16.6 %collective-permute-start.12 = (bf16[2048,384]{1,0:T(8,128)(2,1)S(1)}, bf16[2048,384]{1,0:T(8,128)(2,1)S(1)}, u32[]{:S(2)}, u32[]{:S(2)}) collective-permute-start(bf16[2048,384]{1,0:T(8,128)(2,1)S(1)} %stack.19.refs_1_.refs_6_), channel_id=1, source_target_pairs={{0,2},{2,0},{4,6},{6,4},{8,10},{10,8},{12,14},{14,12},{16,18},{18,... | collective-permute-start | bytes 4718600 | tf_op jit(solution)/shard_map/ppermute | solution.py:510
  95.7 15.4 %collective-permute-start.13 = (bf16[160,1536]{1,0:T(8,128)(2,1)S(1)}, bf16[160,1536]{1,0:T(8,128)(2,1)S(1)}, u32[]{:S(2)}, u32[]{:S(2)}) collective-permute-start(bf16[160,1536]{1,0:T(8,128)(2,1)S(1)} %collective-permute-done.6.refs_6_.refs_2_), channel_id=1, source_target_pairs={{0,8},{2,10},{4,12},{6,14},{8,16},{10,18},{12,20},{14,22},{16,24},... | collective-permute-start | bytes 1474568 | tf_op jit(solution)/shard_map/ppermute | solution.py:493
  96.5 14.6 %collective-permute-start.14 = (bf16[160,1536]{1,0:T(8,128)(2,1)S(1)}, bf16[160,1536]{1,0:T(8,128)(2,1)S(1)}, u32[]{:S(2)}, u32[]{:S(2)}) collective-permute-start(bf16[160,1536]{1,0:T(8,128)(2,1)S(1)} %collective-permute-done.6.refs_6_.refs_2_), channel_id=1, source_target_pairs={{0,1},{1,0},{2,3},{3,2},{4,5},{5,4},{6,7},{7,6},{8,9},{9,8},{10,11... | collective-permute-start | bytes 1474568 | tf_op jit(solution)/shard_map/ppermute | solution.py:49
  111.1 12.8 %collective-permute-start.15 = (bf16[160,1536]{1,0:T(8,128)(2,1)S(1)}, bf16[160,1536]{1,0:T(8,128)(2,1)S(1)}, u32[]{:S(2)}, u32[]{:S(2)}) collective-permute-start(bf16[160,1536]{1,0:T(8,128)(2,1)S(1)} %collective-permute-done.13.refs_7_.refs_3_), channel_id=1, source_target_pairs={{0,1},{1,0},{2,3},{3,2},{4,5},{5,4},{6,7},{7,6},{8,9},{9,8},{10,11... | collective-permute-start | bytes 1474568 | tf_op jit(solution)/shard_map/ppermute | solution.py:49
  130.8 3.3 %collective-permute-start.16 = (bf16[2560,128]{1,0:T(8,128)(2,1)S(1)}, bf16[2560,128]{1,0:T(8,128)(2,1)S(1)}, u32[]{:S(2)}, u32[]{:S(2)}) collective-permute-start(bf16[2560,128]{1,0:T(8,128)(2,1)S(1)} %get-tuple-element.112), channel_id=1, source_target_pairs={{0,2},{2,0},{4,6},{6,4},{8,10},{10,8},{12,14},{14,12},{16,18},{18,... | collective-permute-start | bytes 1966088 | tf_op jit(solution)/shard_map/ppermute | solution.py:389
  134.8 10.9 %collective-permute-start.18 = (bf16[1536,384]{1,0:T(8,128)(2,1)S(1)}, bf16[1536,384]{1,0:T(8,128)(2,1)S(1)}, u32[]{:S(2)}, u32[]{:S(2)}) collective-permute-start(bf16[1536,384]{1,0:T(8,128)(2,1)S(1)} %get-tuple-element.120), channel_id=1, source_target_pairs={{0,2},{2,0},{4,6},{6,4},{8,10},{10,8},{12,14},{14,12},{16,18},{18,... | collective-permute-start | bytes 3538952 | tf_op jit(solution)/shard_map/ppermute | solution.py:389
  135.4 11.2 %collective-permute-start.17 = (bf16[1280,128]{1,0:T(8,128)(2,1)S(1)}, bf16[1280,128]{1,0:T(8,128)(2,1)S(1)}, u32[]{:S(2)}, u32[]{:S(2)}) collective-permute-start(bf16[1280,128]{1,0:T(8,128)(2,1)S(1)} %get-tuple-element.118), channel_id=1, source_target_pairs={{0,4},{2,6},{4,0},{6,2},{8,12},{10,14},{12,8},{14,10},{16,20},{18,... | collective-permute-start | bytes 983048 | tf_op jit(solution)/shard_map/ppermute | solution.py:520
  146.6 4.2 %collective-permute-start.20 = (bf16[2560,256]{1,0:T(8,128)(2,1)S(1)}, bf16[2560,256]{1,0:T(8,128)(2,1)S(1)}, u32[]{:S(2)}, u32[]{:S(2)}) collective-permute-start(bf16[2560,256]{1,0:T(8,128)(2,1)S(1)} %get-tuple-element.139), channel_id=1, source_target_pairs={{0,2},{2,0},{4,6},{6,4},{8,10},{10,8},{12,14},{14,12},{16,18},{18,... | collective-permute-start | bytes 3932168 | tf_op jit(solution)/shard_map/ppermute | solution.py:389
  147.3 15.8 %collective-permute-start.19 = (bf16[768,384]{1,0:T(8,128)(2,1)S(1)}, bf16[768,384]{1,0:T(8,128)(2,1)S(1)}, u32[]{:S(2)}, u32[]{:S(2)}) collective-permute-start(bf16[768,384]{1,0:T(8,128)(2,1)S(1)} %get-tuple-element.137), channel_id=1, source_target_pairs={{0,4},{2,6},{4,0},{6,2},{8,12},{10,14},{12,8},{14,10},{16,20},{18,... | collective-permute-start | bytes 1769480 | tf_op jit(solution)/shard_map/ppermute | solution.py:520
  147.9 5.6 %collective-permute-start.21 = (bf16[480,128]{1,0:T(8,128)(2,1)S(1)}, bf16[480,128]{1,0:T(8,128)(2,1)S(1)}, u32[]{:S(2)}, u32[]{:S(2)}) collective-permute-start(bf16[480,128]{1,0:T(8,128)(2,1)S(1)} %get-tuple-element.141), channel_id=1, source_target_pairs={{0,24},{2,26},{4,28},{6,30},{8,0},{10,2},{12,4},{14,6},{16,8},{18,... | collective-permute-start | bytes 368648 | tf_op jit(solution)/shard_map/ppermute | solution.py:458
  149.3 12.2 %collective-permute-start.22 = (bf16[480,128]{1,0:T(8,128)(2,1)S(1)}, bf16[480,128]{1,0:T(8,128)(2,1)S(1)}, u32[]{:S(2)}, u32[]{:S(2)}) collective-permute-start(bf16[480,128]{1,0:T(8,128)(2,1)S(1)} %get-tuple-element.142), channel_id=1, source_target_pairs={{0,16},{2,18},{4,20},{6,22},{8,24},{10,26},{12,28},{14,30},{16,0},... | collective-permute-start | bytes 368648 | tf_op jit(solution)/shard_map/ppermute | solution.py:458
  150.2 11.3 %collective-permute-start.23 = (bf16[480,128]{1,0:T(8,128)(2,1)S(1)}, bf16[480,128]{1,0:T(8,128)(2,1)S(1)}, u32[]{:S(2)}, u32[]{:S(2)}) collective-permute-start(bf16[480,128]{1,0:T(8,128)(2,1)S(1)} %get-tuple-element.143), channel_id=1, source_target_pairs={{0,8},{2,10},{4,12},{6,14},{8,16},{10,18},{12,20},{14,22},{16,24},... | collective-permute-start | bytes 368648 | tf_op jit(solution)/shard_map/ppermute | solution.py:458
  163.1 16.3 %collective-permute-start.24 = (bf16[1280,256]{1,0:T(8,128)(2,1)S(1)}, bf16[1280,256]{1,0:T(8,128)(2,1)S(1)}, u32[]{:S(2)}, u32[]{:S(2)}) collective-permute-start(bf16[1280,256]{1,0:T(8,128)(2,1)S(1)} %get-tuple-element.148), channel_id=1, source_target_pairs={{0,4},{2,6},{4,0},{6,2},{8,12},{10,14},{12,8},{14,10},{16,20},{18,... | collective-permute-start | bytes 1966088 | tf_op jit(solution)/shard_map/ppermute | solution.py:520
  164.3 8.7 %collective-permute-start.25 = (bf16[192,384]{1,0:T(8,128)(2,1)S(1)}, bf16[192,384]{1,0:T(8,128)(2,1)S(1)}, u32[]{:S(2)}, u32[]{:S(2)}) collective-permute-start(bf16[192,384]{1,0:T(8,128)(2,1)S(1)} %get-tuple-element.151), channel_id=1, source_target_pairs={{0,8},{2,10},{4,12},{6,14},{8,16},{10,18},{12,20},{14,22},{16,24},... | collective-permute-start | bytes 442376 | tf_op jit(solution)/shard_map/ppermute | solution.py:458
  165.2 12.6 %collective-permute-start.26 = (bf16[192,384]{1,0:T(8,128)(2,1)S(1)}, bf16[192,384]{1,0:T(8,128)(2,1)S(1)}, u32[]{:S(2)}, u32[]{:S(2)}) collective-permute-start(bf16[192,384]{1,0:T(8,128)(2,1)S(1)} %get-tuple-element.152), channel_id=1, source_target_pairs={{0,16},{2,18},{4,20},{6,22},{8,24},{10,26},{12,28},{14,30},{16,0},... | collective-permute-start | bytes 442376 | tf_op jit(solution)/shard_map/ppermute | solution.py:458
  166.3 11.5 %collective-permute-start.27 = (bf16[192,384]{1,0:T(8,128)(2,1)S(1)}, bf16[192,384]{1,0:T(8,128)(2,1)S(1)}, u32[]{:S(2)}, u32[]{:S(2)}) collective-permute-start(bf16[192,384]{1,0:T(8,128)(2,1)S(1)} %get-tuple-element.153), channel_id=1, source_target_pairs={{0,24},{2,26},{4,28},{6,30},{8,0},{10,2},{12,4},{14,6},{16,8},{18,... | collective-permute-start | bytes 442376 | tf_op jit(solution)/shard_map/ppermute | solution.py:458
  180.2 8.2 %collective-permute-start.28 = (bf16[480,256]{1,0:T(8,128)(2,1)S(1)}, bf16[480,256]{1,0:T(8,128)(2,1)S(1)}, u32[]{:S(2)}, u32[]{:S(2)}) collective-permute-start(bf16[480,256]{1,0:T(8,128)(2,1)S(1)} %get-tuple-element.160), channel_id=1, source_target_pairs={{0,24},{2,26},{4,28},{6,30},{8,0},{10,2},{12,4},{14,6},{16,8},{18,... | collective-permute-start | bytes 737288 | tf_op jit(solution)/shard_map/ppermute | solution.py:458
  181.9 22.6 %collective-permute-start.29 = (bf16[480,256]{1,0:T(8,128)(2,1)S(1)}, bf16[480,256]{1,0:T(8,128)(2,1)S(1)}, u32[]{:S(2)}, u32[]{:S(2)}) collective-permute-start(bf16[480,256]{1,0:T(8,128)(2,1)S(1)} %get-tuple-element.161), channel_id=1, source_target_pairs={{0,16},{2,18},{4,20},{6,22},{8,24},{10,26},{12,28},{14,30},{16,0},... | collective-permute-start | bytes 737288 | tf_op jit(solution)/shard_map/ppermute | solution.py:458
  183.3 21.3 %collective-permute-start.30 = (bf16[480,256]{1,0:T(8,128)(2,1)S(1)}, bf16[480,256]{1,0:T(8,128)(2,1)S(1)}, u32[]{:S(2)}, u32[]{:S(2)}) collective-permute-start(bf16[480,256]{1,0:T(8,128)(2,1)S(1)} %get-tuple-element.162), channel_id=1, source_target_pairs={{0,8},{2,10},{4,12},{6,14},{8,16},{10,18},{12,20},{14,22},{16,24},... | collective-permute-start | bytes 737288 | tf_op jit(solution)/shard_map/ppermute | solution.py:458

commit v7 on v6

--- a/solution.py
+++ b/solution.py
@@ -319,10 +319,10 @@
     grad_attn[...] = total.astype(BF16)
 
 
-def projection_cost(n_q, total, gw):
+def projection_cost(n_q, gw):
     return pl.CostEstimate(
-        flops=2 * n_q * total * gw,
-        bytes_accessed=2 * (n_q * total + total * gw + n_q * gw),
+        flops=n_q * gw,
+        bytes_accessed=2 * n_q * gw,
         transcendentals=0,
     )
 
@@ -337,7 +337,7 @@
         (ids, *blocks, *grads),
         "attn_gradient",
         [pltpu.VMEM((total, gw), BF16), pltpu.VMEM((n_q, part), BF16)],
-        projection_cost(n_q, total, gw),
+        projection_cost(n_q, gw),
     )
 
 
@@ -366,7 +366,7 @@
         (ids, attn, *grads),
         "proj_gradient",
         [pltpu.VMEM((total, gw), BF16), pltpu.VMEM((n_q, part), BF16)],
-        projection_cost(n_q, total, gw),
+        projection_cost(n_q, gw),
     )
 
 
@@ -481,28 +481,15 @@
     *pieces, own_q = pack(ids, queries, keys, values, proj_weight.T, n_groups)
     pieces = exchange(pieces, n_groups, n_tok, 1)
     q_pieces = pieces[1:]
-    middle = n_groups // 2
-    plan = [[middle], [s for s in range(1, n_groups) if s != middle]]
-    others, ring, across, here = [None] * n_groups, grad_out, [], [0]
-    for step in range(n_groups):
-        for s in here:
-            pieces[s] = pieces[s][:shared]
-            others[s] = lax.ppermute(pieces[s], "frame", last)
+    own, others, ring, across = [pieces[0]], [], grad_out, []
+    for s in range(n_groups):
+        others.append(lax.ppermute(own[s], "frame", last))
         across.append(gather_blocks(ring, "space", n_space, space_bits))
-        if step + 1 < n_groups:
+        if s + 1 < n_groups:
             ring = lax.ppermute(ring, "frame", shift_pairs(n_groups, n_tok, 1))
-            coming = plan[step] if step < len(plan) else []
-            sent = here if coming else []
-            values_of = [ring, *across[step]]
-            values_of += [pieces[s] for s in coming] + [others[s] for s in sent]
-            ring, *tied = tie(tuple(values_of))
-            across[step] = tied[:n_space]
-            for s, piece in zip(coming, tied[n_space:]):
-                pieces[s] = piece
-            for s, piece in zip(sent, tied[n_space + len(coming) :]):
-                others[s] = piece
-            here = coming
-    own = pieces
+            step = (ring, pieces[s + 1][:shared], others[s], *across[s])
+            ring, piece, others[s], *across[s] = tie(step)
+            own.append(piece)
 
     q = stack_queries(ids, own_q, q_pieces)
     blocks = [stack(ids, own, rows), stack(ids, others, rows)]
@@ -519,23 +506,22 @@
     def across_x(piece):
         return lax.ppermute(piece, "frame", last)
 
-    dq, (kept, sent) = attention_halves(0, 1, q)
-    out_after, kept, sent = tie((out, kept, sent))
-    kept, sent = halve(ids, kept, sent, n_frame, tok_bits)
+    dq, halves = attention_halves(0, 1, q)
+    kept, sent = halve(ids, *halves, n_frame, tok_bits)
+    other = across_x(sent)
+    out_after, kept = tie((out, kept))
     proj = proj_gradient(ids, out_after, grads, depth, n_groups, n_tok, n_space)
-    q, kept, sent, *proj = tie((q, kept, sent, *proj))
-    other = across_x(sent)
+    other, *proj = tie((other, *proj))
     proj_kept, proj_sent = halve(ids, *proj, n_frame, tok_bits)
-    if heads > 1:
-        dq_rest, halves = attention_halves(1, heads - 1, q)
-        other, proj_sent, *halves = tie((other, proj_sent, *halves))
     sums = finish(ids, kept, other, dq, n_groups)
-    proj_sent, *sums = tie((proj_sent, *sums))
+    proj_sent, q, *sums = tie((proj_sent, q, *sums))
     returned = [exchange(sums, n_groups, n_tok, -1)]
     proj_other = across_x(proj_sent)
     if heads > 1:
-        kept, sent = halve(ids, *halves, n_frame, tok_bits)
-        proj_other, sent, *returned[0][1:] = tie((proj_other, sent, *returned[0][1:]))
+        dq_rest, halves = attention_halves(1, heads - 1, q)
+        step = (proj_other, *halves, *returned[0][1:])
+        proj_other, kept, sent, *returned[0][1:] = tie(step)
+        kept, sent = halve(ids, kept, sent, n_frame, tok_bits)
     proj_pieces = exchange(add_parts(ids, proj_kept, proj_other, n_groups), n_groups, n_tok, 1)
     if heads > 1:
         other, *proj_pieces[1:] = tie((across_x(sent), *proj_pieces[1:]))

time: 207 us -> 199 us (0.961)
  waiting for transfers between devices: 129 us -> 97.4 us
  starting transfers between devices: 32.9 us -> 56.9 us
    ppermute x12, waiting for transfers between devices: 76.7 us -> 56.5 us  [exchange(): lax.ppermute(pieces[s], 'frame', shift_pairs(n_groups, n_tok, sign * s))]
    ppermute x3, starting transfers between devices: 2.42 us -> 20.6 us  [local(): ring = lax.ppermute(ring, 'frame', shift_pairs(n_groups, n_tok, 1))]
    ppermute x3, waiting for transfers between devices: 22.4 us -> 10.5 us  [local(): ring = lax.ppermute(ring, 'frame', shift_pairs(n_groups, n_tok, 1))]
    ppermute x4, waiting for transfers between devices: 25.4 us -> 14.3 us  [local(): others.append(lax.ppermute(own[s], 'frame', last))]
    ppermute x3, waiting for transfers between devices: 0.01 us -> 7.21 us  [halve(): other = lax.ppermute(sent, 'frame', xor_pairs(n_frame, bit))]
    ppermute x12, starting transfers between devices: 16.5 us -> 20.8 us  [exchange(): lax.ppermute(pieces[s], 'frame', shift_pairs(n_groups, n_tok, sign * s))]
    ppermute x3, waiting for transfers between devices: 3.26 us -> 6.69 us  [across_x(): return lax.ppermute(piece, 'frame', last)]
    ppermute x2, waiting for transfers between devices: 0.01 us -> 2.22 us  [local(): lax.ppermute(b, 'frame', xor_pairs(n_frame, bit))]
where the time goes in v7:
time: 199 us
  waiting for transfers between devices  97.4 us (49%)
  starting transfers between devices  56.9 us (29%)
  Pallas kernels  42.7 us (21%)
    ppermute x12, waiting for transfers between devices, exchange(): lax.ppermute(pieces[s], 'frame', shift_pairs(n_groups, n_tok, sign * s))  56.5 us
    ppermute x12, starting transfers between devices, exchange(): lax.ppermute(pieces[s], 'frame', shift_pairs(n_groups, n_tok, sign * s))  20.8 us
    ppermute x3, starting transfers between devices, local(): ring = lax.ppermute(ring, 'frame', shift_pairs(n_groups, n_tok, 1))  20.6 us
    pallas_call x13, Pallas kernels, whole_call(): pl.pallas_call(body, out_shape=out_shape, in_specs=[smem()] + [vmem()] *...  16 us
    ppermute x4, waiting for transfers between devices, local(): others.append(lax.ppermute(own[s], 'frame', last))  14.3 us
    pallas_call x2, Pallas kernels, backward(): pl.pallas_call(functools.partial(backward_kernel, n_groups, chunk, 1.0 /...  12.7 us
    ppermute x3, waiting for transfers between devices, local(): ring = lax.ppermute(ring, 'frame', shift_pairs(n_groups, n_tok, 1))  10.5 us
    pallas_call x1, Pallas kernels, forward(): pl.pallas_call(functools.partial(forward_kernel, chunk, scale), grid=(hea...  10.2 us
  transfers between devices with their start and end apart: 31, of which 16 were waited for; matrix products, arithmetic and copies ran while one was open for 0% of the time, Pallas kernels for 14%

profile of v7, /device:TPU:0, one launch (start us, length us, event | category | flops | bytes accessed | tf_op | source)
XLA Modules:
  0.0 198.7 jit_solution(529413884249542349)
XLA Ops:
  0.7 0.6 pad_add_fusion.ids
  1.3 3.7 %pack.1 = (bf16[512,384]{1,0:T(8,128)(2,1)}, bf16[672,384]{1,0:T(8,128)(2,1)}, bf16[672,384]{1,0:T(8,128)(2,1)}, bf16[672,384]{1,0:T(8,128)(2,1)}, bf16[160,384]{1,0:T(8,128)(2,1)}) custom-call(s32[3]{0:T(128)} %pad_add_fusion.ids, bf16[160,1536]{1,0:T(8,128)(2,1)} %q.1, bf16[160,1536]{1,0:T(8,128)(2,1)} %k.1, bf16[160,1536]{1,0:T(8,128)(2,1)} %v.1, ...), custom_call_target="tpu_custom_call" | custom-call | tf_op jit(solution)/shard_map/pack/pallas_call | solution.py:119
  5.0 0.0 copy-start.1
  5.0 3.1 %collective-permute-start = (bf16[672,384]{1,0:T(8,128)(2,1)}, bf16[672,384]{1,0:T(8,128)(2,1)S(1)}, u32[]{:S(2)}, u32[]{:S(2)}) collective-permute-start(bf16[672,384]{1,0:T(8,128)(2,1)} %get-tuple-element.84), channel_id=1, source_target_pairs={{0,8},{2,10},{4,12},{6,14},{8,16},{10,18},{12,20},{14,22},{16,24},... | collective-permute-start | bytes 1548296 | tf_op jit(solution)/shard_map/ppermute | solution.py:458
  8.1 1.6 collective-permute-start.3
  9.7 1.5 collective-permute-start.5
  11.2 1.5 collective-permute-start.4
  12.7 1.2 collective-permute-start.1
  13.9 9.1 %collective-permute-done.refs_0_ = bf16[672,384]{1,0:T(8,128)(2,1)S(1)} collective-permute-done((bf16[672,384]{1,0:T(8,128)(2,1)}, bf16[672,384]{1,0:T(8,128)(2,1)S(1)}, u32[]{:S(2)}, u32[]{:S(2)}) %collective-permute-start) | collective-permute-done | bytes 516128 | tf_op jit(solution)/shard_map/ppermute | solution.py:458
  23.0 0.0 collective-permute-done.4.refs_0_
  23.1 10.5 %collective-permute-done.3.refs_5_.refs_1_ = bf16[160,1536]{1,0:T(8,128)(2,1)S(1)} collective-permute-done((bf16[160,1536]{1,0:T(8,128)(2,1)S(1)}, bf16[160,1536]{1,0:T(8,128)(2,1)S(1)}, u32[]{:S(2)}, u32[]{:S(2)}) %collective-permute-start.3) | collective-permute-done | bytes 491552 | tf_op jit(solution)/shard_map/ppermute | solution.py:489
  33.5 1.8 collective-permute-start.8
  35.3 9.4 %collective-permute-start.6 = (bf16[160,1536]{1,0:T(8,128)(2,1)S(1)}, bf16[160,1536]{1,0:T(8,128)(2,1)S(1)}, u32[]{:S(2)}, u32[]{:S(2)}) collective-permute-start(bf16[160,1536]{1,0:T(8,128)(2,1)S(1)} %collective-permute-done.3.refs_5_.refs_1_), channel_id=1, source_target_pairs={{0,8},{2,10},{4,12},{6,14},{8,16},{10,18},{12,20},{14,22},{16,24},... | collective-permute-start | bytes 1474568 | tf_op jit(solution)/shard_map/ppermute | solution.py:489
  44.7 1.5 collective-permute-start.7
  46.2 19.2 %collective-permute-done.1.refs_1_ = bf16[672,384]{1,0:T(8,128)(2,1)S(1)} collective-permute-done((bf16[672,384]{1,0:T(8,128)(2,1)}, bf16[672,384]{1,0:T(8,128)(2,1)S(1)}, u32[]{:S(2)}, u32[]{:S(2)}) %collective-permute-start.1) | collective-permute-done | bytes 516128 | tf_op jit(solution)/shard_map/ppermute | solution.py:458
  65.5 1.6 collective-permute-start.11
  67.1 9.6 %collective-permute-start.9 = (bf16[160,1536]{1,0:T(8,128)(2,1)S(1)}, bf16[160,1536]{1,0:T(8,128)(2,1)S(1)}, u32[]{:S(2)}, u32[]{:S(2)}) collective-permute-start(bf16[160,1536]{1,0:T(8,128)(2,1)S(1)} %collective-permute-done.6.refs_6_.refs_2_), channel_id=1, source_target_pairs={{0,8},{2,10},{4,12},{6,14},{8,16},{10,18},{12,20},{14,22},{16,24},... | collective-permute-start | bytes 1474568 | tf_op jit(solution)/shard_map/ppermute | solution.py:489
  76.7 1.5 collective-permute-start.10
  78.2 7.9 %collective-permute-done.10.refs_2_ = bf16[512,384]{1,0:T(8,128)(2,1)S(1)} collective-permute-done((bf16[512,384]{1,0:T(8,128)(2,1)S(1)}, bf16[512,384]{1,0:T(8,128)(2,1)S(1)}, u32[]{:S(2)}, u32[]{:S(2)}) %collective-permute-start.10) | collective-permute-done | bytes 393248 | tf_op jit(solution)/shard_map/ppermute | solution.py:486
  86.1 1.5 collective-permute-start.12
  87.6 0.7 stack.18.refs_0_.refs_5_
  88.3 0.0 copy-start.2
  88.3 0.1 collective-permute-start.13
  88.4 6.4 %collective-permute-done.12.refs_3_ = bf16[512,384]{1,0:T(8,128)(2,1)S(1)} collective-permute-done((bf16[512,384]{1,0:T(8,128)(2,1)S(1)}, bf16[512,384]{1,0:T(8,128)(2,1)S(1)}, u32[]{:S(2)}, u32[]{:S(2)}) %collective-permute-start.12) | collective-permute-done | bytes 393248 | tf_op jit(solution)/shard_map/ppermute | solution.py:486
  94.8 0.7 stack.19.refs_1_.refs_6_
  95.5 0.1 collective-permute-start.14
  95.6 0.6 collective-permute-start.15
  96.1 0.6 stack_queries.1.q_in.refs_0_
  96.7 2.2 %collective-permute-done.14.refs_3_.refs_8_ = bf16[2048,384]{1,0:T(8,128)(2,1)S(1)} collective-permute-done((bf16[2048,384]{1,0:T(8,128)(2,1)S(1)}, bf16[2048,384]{1,0:T(8,128)(2,1)S(1)}, u32[]{:S(2)}, u32[]{:S(2)}) %collective-permute-start.14) | collective-permute-done | bytes 1572896 | tf_op jit(solution)/shard_map/ppermute | solution.py:497
  99.0 10.2 %forward.1 = (bf16[3,2560,640]{2,1,0:T(8,128)(2,1)S(1)}, bf16[640,384]{1,0:T(8,128)(2,1)S(1)}, f32[3,1,640]{2,1,0:T(1,128)S(1)}) custom-call(bf16[640,384]{1,0:T(8,128)(2,1)S(1)} %stack_queries.1.q_in.refs_0_, bf16[2048,384]{1,0:T(8,128)(2,1)S(1)} %stack.18.refs_0_.refs_5_, bf16[2048,384]{1,0:T(8,128)(2,1)S(1)} %stack.19.refs_1_.refs_6_, ...), custom_call_target="tpu_custom_call" | custom-call | flops 2516582400 | bytes 9830400 | tf_op jit(solution)/shard_map/forward/pallas_call | solution.py:200
  109.2 3.0 %attn_gradient.1.refs_4_ = bf16[640,384]{1,0:T(8,128)(2,1)S(1)} custom-call(s32[3]{0:T(128)S(1)} %copy-done.3, bf16[2048,384]{1,0:T(8,128)(2,1)S(1)} %stack.18.refs_0_.refs_5_, bf16[2048,384]{1,0:T(8,128)(2,1)S(1)} %stack.19.refs_1_.refs_6_, bf16[2048,384]{1,0:T(8,128)(2,1)S(1)} %collective-permute-done.13.refs_2_.refs_7_, ...), custom_call_target="tpu_custom_call" | custom-call | flops 245760 | bytes 491520 | tf_op jit(solution)/shard_map/attn_gradient/pallas_call | solution.py:75
  112.2 3.9 %backward.2 = (bf16[160,128]{1,0:T(8,128)(2,1)S(1)}, bf16[160,128]{1,0:T(8,128)(2,1)S(1)}, bf16[160,128]{1,0:T(8,128)(2,1)S(1)}, bf16[160,128]{1,0:T(8,128)(2,1)...) custom-call(bf16[640,384]{1,0:T(8,128)(2,1)S(1)} %stack_queries.1.q_in.refs_0_, ...), custom_call_target="tpu_custom_call" | custom-call | flops 81920 | bytes 163840 | tf_op jit(solution)/shard_map/backward/pallas_call | solution.py:264
  116.1 0.2 collective-permute-start.16
  116.3 2.0 collective-permute-done.16.other
  118.3 0.7 add_parts.4
  119.0 1.6 collective-permute-start.17
  120.5 3.2 %proj_gradient.1 = (bf16[1536,384]{1,0:T(8,128)(2,1)S(1)}, bf16[1536,384]{1,0:T(8,128)(2,1)S(1)}) custom-call(s32[3]{0:T(128)S(1)} %copy-done.3, bf16[640,384]{1,0:T(8,128)(2,1)S(1)} %get-tuple-element.110.refs_2_.attn, bf16[160,1536]{1,0:T(8,128)(2,1)S(1)} %copy-done, bf16[160,1536]{1,0:T(8,128)(2,1)S(1)} %collective-permute-done.3.refs_5_.refs_1_, ...), custom_call_target="tpu_custom_call" | custom-call | flops 245760 | bytes 491520 | tf_op jit(solution)/shard_map/proj_gradient/pallas_call | solution.py:75
  123.8 5.0 %collective-permute-done.17.other = bf16[1280,128]{1,0:T(8,128)(2,1)S(1)} collective-permute-done((bf16[1280,128]{1,0:T(8,128)(2,1)S(1)}, bf16[1280,128]{1,0:T(8,128)(2,1)S(1)}, u32[]{:S(2)}, u32[]{:S(2)}) %collective-permute-start.17) | collective-permute-done | bytes 327712 | tf_op jit(solution)/shard_map/ppermute | solution.py:507
  128.8 0.6 finish.2
  129.4 2.2 %collective-permute-done.18.other = bf16[1536,384]{1,0:T(8,128)(2,1)S(1)} collective-permute-done((bf16[1536,384]{1,0:T(8,128)(2,1)S(1)}, bf16[1536,384]{1,0:T(8,128)(2,1)S(1)}, u32[]{:S(2)}, u32[]{:S(2)}) %collective-permute-start.18) | collective-permute-done | bytes 1179680 | tf_op jit(solution)/shard_map/ppermute | solution.py:389
  131.6 0.8 add_parts.5
  132.5 1.6 collective-permute-start.19
  134.0 4.4 %collective-permute-start.20 = (bf16[480,128]{1,0:T(8,128)(2,1)S(1)}, bf16[480,128]{1,0:T(8,128)(2,1)S(1)}, u32[]{:S(2)}, u32[]{:S(2)}) collective-permute-start(bf16[480,128]{1,0:T(8,128)(2,1)S(1)} %get-tuple-element.131), channel_id=1, source_target_pairs={{0,24},{2,26},{4,28},{6,30},{8,0},{10,2},{12,4},{14,6},{16,8},{18,... | collective-permute-start | bytes 368648 | tf_op jit(solution)/shard_map/ppermute | solution.py:458
  138.4 0.9 collective-permute-start.21
  139.3 1.1 collective-permute-start.22
  140.4 8.8 %backward.3 = (bf16[160,256]{1,0:T(8,128)(2,1)S(1)}, bf16[160,256]{1,0:T(8,128)(2,1)S(1)}, bf16[160,256]{1,0:T(8,128)(2,1)S(1)}, bf16[160,256]{1,0:T(8,128)(2,1)...) custom-call(bf16[640,384]{1,0:T(8,128)(2,1)S(1)} %stack_queries.1.q_in.refs_0_, ...), custom_call_target="tpu_custom_call" | custom-call | flops 81920 | bytes 163840 | tf_op jit(solution)/shard_map/backward/pallas_call | solution.py:264
  149.3 1.0 collective-permute-done.21.refs_2_
  150.3 3.0 %collective-permute-done.23.other = bf16[2560,256]{1,0:T(8,128)(2,1)S(1)} collective-permute-done((bf16[2560,256]{1,0:T(8,128)(2,1)S(1)}, bf16[2560,256]{1,0:T(8,128)(2,1)S(1)}, u32[]{:S(2)}, u32[]{:S(2)}) %collective-permute-start.23) | collective-permute-done | bytes 1310752 | tf_op jit(solution)/shard_map/ppermute | solution.py:389
  153.3 0.8 add_parts.6
  154.2 0.6 collective-permute-start.24
  154.8 0.7 add_parts.7
  155.5 2.5 %collective-permute-start.25 = (bf16[192,384]{1,0:T(8,128)(2,1)S(1)}, bf16[192,384]{1,0:T(8,128)(2,1)S(1)}, u32[]{:S(2)}, u32[]{:S(2)}) collective-permute-start(bf16[192,384]{1,0:T(8,128)(2,1)S(1)} %get-tuple-element.143), channel_id=1, source_target_pairs={{0,8},{2,10},{4,12},{6,14},{8,16},{10,18},{12,20},{14,22},{16,24},... | collective-permute-start | bytes 442376 | tf_op jit(solution)/shard_map/ppermute | solution.py:458
  157.9 1.1 collective-permute-start.26
  159.0 2.4 %collective-permute-start.27 = (bf16[192,384]{1,0:T(8,128)(2,1)S(1)}, bf16[192,384]{1,0:T(8,128)(2,1)S(1)}, u32[]{:S(2)}, u32[]{:S(2)}) collective-permute-start(bf16[192,384]{1,0:T(8,128)(2,1)S(1)} %get-tuple-element.145), channel_id=1, source_target_pairs={{0,24},{2,26},{4,28},{6,30},{8,0},{10,2},{12,4},{14,6},{16,8},{18,... | collective-permute-start | bytes 442376 | tf_op jit(solution)/shard_map/ppermute | solution.py:458
  161.4 2.7 %collective-permute-done.25.refs_1_ = bf16[192,384]{1,0:T(8,128)(2,1)S(1)} collective-permute-done((bf16[192,384]{1,0:T(8,128)(2,1)S(1)}, bf16[192,384]{1,0:T(8,128)(2,1)S(1)}, u32[]{:S(2)}, u32[]{:S(2)}) %collective-permute-start.25) | collective-permute-done | bytes 147488 | tf_op jit(solution)/shard_map/ppermute | solution.py:458
  164.1 5.2 %collective-permute-done.26.refs_2_ = bf16[192,384]{1,0:T(8,128)(2,1)S(1)} collective-permute-done((bf16[192,384]{1,0:T(8,128)(2,1)S(1)}, bf16[192,384]{1,0:T(8,128)(2,1)S(1)}, u32[]{:S(2)}, u32[]{:S(2)}) %collective-permute-start.26) | collective-permute-done | bytes 147488 | tf_op jit(solution)/shard_map/ppermute | solution.py:458
  169.3 1.7 collective-permute-done.24.other
  171.0 0.7 finish.3
  171.7 3.5 %collective-permute-start.28 = (bf16[480,256]{1,0:T(8,128)(2,1)S(1)}, bf16[480,256]{1,0:T(8,128)(2,1)S(1)}, u32[]{:S(2)}, u32[]{:S(2)}) collective-permute-start(bf16[480,256]{1,0:T(8,128)(2,1)S(1)} %get-tuple-element.152), channel_id=1, source_target_pairs={{0,24},{2,26},{4,28},{6,30},{8,0},{10,2},{12,4},{14,6},{16,8},{18,... | collective-permute-start | bytes 737288 | tf_op jit(solution)/shard_map/ppermute | solution.py:458
  175.2 0.6 collective-permute-start.30
  175.9 1.7 join.1
  177.5 4.2 %collective-permute-done.28.refs_5_ = bf16[480,256]{1,0:T(8,128)(2,1)S(1)} collective-permute-done((bf16[480,256]{1,0:T(8,128)(2,1)S(1)}, bf16[480,256]{1,0:T(8,128)(2,1)S(1)}, u32[]{:S(2)}, u32[]{:S(2)}) %collective-permute-start.28) | collective-permute-done | bytes 245792 | tf_op jit(solution)/shard_map/ppermute | solution.py:458
  181.7 15.2 %collective-permute-done.29.refs_6_ = bf16[480,256]{1,0:T(8,128)(2,1)S(1)} collective-permute-done((bf16[480,256]{1,0:T(8,128)(2,1)S(1)}, bf16[480,256]{1,0:T(8,128)(2,1)S(1)}, u32[]{:S(2)}, u32[]{:S(2)}) %collective-permute-start.29) | collective-permute-done | bytes 245792 | tf_op jit(solution)/shard_map/ppermute | solution.py:458
  196.8 1.8 unpack.1
  (27 shorter events, 0.2 us)
Async XLA Ops:
  0.6 7.5 %copy-start = (bf16[160,1536]{1,0:T(8,128)(2,1)S(1)}, bf16[160,1536]{1,0:T(8,128)(2,1)}, u32[]{:S(2)}) copy-start(bf16[160,1536]{1,0:T(8,128)(2,1)} %refs_0_) | copy-start | bytes 1474564
  5.0 82.6 %copy-start.1 = (bf16[512,384]{1,0:T(8,128)(2,1)S(1)}, bf16[512,384]{1,0:T(8,128)(2,1)}, u32[]{:S(2)}) copy-start(bf16[512,384]{1,0:T(8,128)(2,1)} %get-tuple-element.87.refs_0_) | copy-start | bytes 1179652
  5.0 82.6 %copy-start.3 = (s32[3]{0:T(128)S(1)}, s32[3]{0:T(128)}, u32[]{:S(2)}) copy-start(s32[3]{0:T(128)} %pad_add_fusion.ids) | copy-start | bytes 40
  5.0 18.0 %collective-permute-start = (bf16[672,384]{1,0:T(8,128)(2,1)}, bf16[672,384]{1,0:T(8,128)(2,1)S(1)}, u32[]{:S(2)}, u32[]{:S(2)}) collective-permute-start(bf16[672,384]{1,0:T(8,128)(2,1)} %get-tuple-element.84), channel_id=1, source_target_pairs={{0,8},{2,10},{4,12},{6,14},{8,16},{10,18},{12,20},{14,22},{16,24},... | collective-permute-start | bytes 1548296 | tf_op jit(solution)/shard_map/ppermute | solution.py:458
  8.1 25.4 %collective-permute-start.3 = (bf16[160,1536]{1,0:T(8,128)(2,1)S(1)}, bf16[160,1536]{1,0:T(8,128)(2,1)S(1)}, u32[]{:S(2)}, u32[]{:S(2)}) collective-permute-start(bf16[160,1536]{1,0:T(8,128)(2,1)S(1)} %copy-done), channel_id=1, source_target_pairs={{0,8},{2,10},{4,12},{6,14},{8,16},{10,18},{12,20},{14,22},{16,24},... | collective-permute-start | bytes 1474568 | tf_op jit(solution)/shard_map/ppermute | solution.py:489
  9.7 23.9 %collective-permute-start.5 = (bf16[160,1536]{1,0:T(8,128)(2,1)S(1)}, bf16[160,1536]{1,0:T(8,128)(2,1)S(1)}, u32[]{:S(2)}, u32[]{:S(2)}) collective-permute-start(bf16[160,1536]{1,0:T(8,128)(2,1)S(1)} %copy-done), channel_id=1, source_target_pairs={{0,1},{1,0},{2,3},{3,2},{4,5},{5,4},{6,7},{7,6},{8,9},{9,8},{10,11... | collective-permute-start | bytes 1474568 | tf_op jit(solution)/shard_map/ppermute | solution.py:49
  11.2 11.9 %collective-permute-start.4 = (bf16[512,384]{1,0:T(8,128)(2,1)}, bf16[512,384]{1,0:T(8,128)(2,1)S(1)}, u32[]{:S(2)}, u32[]{:S(2)}) collective-permute-start(bf16[512,384]{1,0:T(8,128)(2,1)} %get-tuple-element.87.refs_0_), channel_id=1, source_target_pairs={{0,4},{2,6},{4,0},{6,2},{8,12},{10,14},{12,8},{14,10},{16,20},{18,... | collective-permute-start | bytes 1179656 | tf_op jit(solution)/shard_map/ppermute | solution.py:486
  12.7 52.7 %collective-permute-start.1 = (bf16[672,384]{1,0:T(8,128)(2,1)}, bf16[672,384]{1,0:T(8,128)(2,1)S(1)}, u32[]{:S(2)}, u32[]{:S(2)}) collective-permute-start(bf16[672,384]{1,0:T(8,128)(2,1)} %get-tuple-element.85), channel_id=1, source_target_pairs={{0,16},{2,18},{4,20},{6,22},{8,24},{10,26},{12,28},{14,30},{16,0},... | collective-permute-start | bytes 1548296 | tf_op jit(solution)/shard_map/ppermute | solution.py:458
  33.5 31.9 %collective-permute-start.8 = (bf16[160,1536]{1,0:T(8,128)(2,1)S(1)}, bf16[160,1536]{1,0:T(8,128)(2,1)S(1)}, u32[]{:S(2)}, u32[]{:S(2)}) collective-permute-start(bf16[160,1536]{1,0:T(8,128)(2,1)S(1)} %collective-permute-done.3.refs_5_.refs_1_), channel_id=1, source_target_pairs={{0,1},{1,0},{2,3},{3,2},{4,5},{5,4},{6,7},{7,6},{8,9},{9,8},{10,11... | collective-permute-start | bytes 1474568 | tf_op jit(solution)/shard_map/ppermute | solution.py:49
  35.3 30.2 %collective-permute-start.6 = (bf16[160,1536]{1,0:T(8,128)(2,1)S(1)}, bf16[160,1536]{1,0:T(8,128)(2,1)S(1)}, u32[]{:S(2)}, u32[]{:S(2)}) collective-permute-start(bf16[160,1536]{1,0:T(8,128)(2,1)S(1)} %collective-permute-done.3.refs_5_.refs_1_), channel_id=1, source_target_pairs={{0,8},{2,10},{4,12},{6,14},{8,16},{10,18},{12,20},{14,22},{16,24},... | collective-permute-start | bytes 1474568 | tf_op jit(solution)/shard_map/ppermute | solution.py:489
  44.7 20.7 %collective-permute-start.7 = (bf16[512,384]{1,0:T(8,128)(2,1)S(1)}, bf16[512,384]{1,0:T(8,128)(2,1)S(1)}, u32[]{:S(2)}, u32[]{:S(2)}) collective-permute-start(bf16[512,384]{1,0:T(8,128)(2,1)S(1)} %slice.12.refs_1_), channel_id=1, source_target_pairs={{0,4},{2,6},{4,0},{6,2},{8,12},{10,14},{12,8},{14,10},{16,20},{18,... | collective-permute-start | bytes 1179656 | tf_op jit(solution)/shard_map/ppermute | solution.py:486
  46.2 32.0 %collective-permute-start.2 = (bf16[672,384]{1,0:T(8,128)(2,1)}, bf16[672,384]{1,0:T(8,128)(2,1)S(1)}, u32[]{:S(2)}, u32[]{:S(2)}) collective-permute-start(bf16[672,384]{1,0:T(8,128)(2,1)} %get-tuple-element.86), channel_id=1, source_target_pairs={{0,24},{2,26},{4,28},{6,30},{8,0},{10,2},{12,4},{14,6},{16,8},{18,... | collective-permute-start | bytes 1548296 | tf_op jit(solution)/shard_map/ppermute | solution.py:458
  65.5 20.6 %collective-permute-start.11 = (bf16[160,1536]{1,0:T(8,128)(2,1)S(1)}, bf16[160,1536]{1,0:T(8,128)(2,1)S(1)}, u32[]{:S(2)}, u32[]{:S(2)}) collective-permute-start(bf16[160,1536]{1,0:T(8,128)(2,1)S(1)} %collective-permute-done.6.refs_6_.refs_2_), channel_id=1, source_target_pairs={{0,1},{1,0},{2,3},{3,2},{4,5},{5,4},{6,7},{7,6},{8,9},{9,8},{10,11... | collective-permute-start | bytes 1474568 | tf_op jit(solution)/shard_map/ppermute | solution.py:49
  67.1 19.1 %collective-permute-start.9 = (bf16[160,1536]{1,0:T(8,128)(2,1)S(1)}, bf16[160,1536]{1,0:T(8,128)(2,1)S(1)}, u32[]{:S(2)}, u32[]{:S(2)}) collective-permute-start(bf16[160,1536]{1,0:T(8,128)(2,1)S(1)} %collective-permute-done.6.refs_6_.refs_2_), channel_id=1, source_target_pairs={{0,8},{2,10},{4,12},{6,14},{8,16},{10,18},{12,20},{14,22},{16,24},... | collective-permute-start | bytes 1474568 | tf_op jit(solution)/shard_map/ppermute | solution.py:489
  76.7 9.4 %collective-permute-start.10 = (bf16[512,384]{1,0:T(8,128)(2,1)S(1)}, bf16[512,384]{1,0:T(8,128)(2,1)S(1)}, u32[]{:S(2)}, u32[]{:S(2)}) collective-permute-start(bf16[512,384]{1,0:T(8,128)(2,1)S(1)} %slice.13.refs_2_), channel_id=1, source_target_pairs={{0,4},{2,6},{4,0},{6,2},{8,12},{10,14},{12,8},{14,10},{16,20},{18,... | collective-permute-start | bytes 1179656 | tf_op jit(solution)/shard_map/ppermute | solution.py:486
  86.1 8.7 %collective-permute-start.12 = (bf16[512,384]{1,0:T(8,128)(2,1)S(1)}, bf16[512,384]{1,0:T(8,128)(2,1)S(1)}, u32[]{:S(2)}, u32[]{:S(2)}) collective-permute-start(bf16[512,384]{1,0:T(8,128)(2,1)S(1)} %slice.14.refs_3_), channel_id=1, source_target_pairs={{0,4},{2,6},{4,0},{6,2},{8,12},{10,14},{12,8},{14,10},{16,20},{18,... | collective-permute-start | bytes 1179656 | tf_op jit(solution)/shard_map/ppermute | solution.py:486
  88.3 7.8 %copy-start.2 = (bf16[160,384]{1,0:T(8,128)(2,1)S(1)}, bf16[160,384]{1,0:T(8,128)(2,1)}, u32[]{:S(2)}) copy-start(bf16[160,384]{1,0:T(8,128)(2,1)} %get-tuple-element.83.own) | copy-start | bytes 368644
  88.3 8.4 %collective-permute-start.13 = (bf16[2048,384]{1,0:T(8,128)(2,1)S(1)}, bf16[2048,384]{1,0:T(8,128)(2,1)S(1)}, u32[]{:S(2)}, u32[]{:S(2)}) collective-permute-start(bf16[2048,384]{1,0:T(8,128)(2,1)S(1)} %stack.18.refs_0_.refs_5_), channel_id=1, source_target_pairs={{0,2},{2,0},{4,6},{6,4},{8,10},{10,8},{12,14},{14,12},{16,18},{18,... | collective-permute-start | bytes 4718600 | tf_op jit(solution)/shard_map/ppermute | solution.py:497
  95.5 3.5 %collective-permute-start.14 = (bf16[2048,384]{1,0:T(8,128)(2,1)S(1)}, bf16[2048,384]{1,0:T(8,128)(2,1)S(1)}, u32[]{:S(2)}, u32[]{:S(2)}) collective-permute-start(bf16[2048,384]{1,0:T(8,128)(2,1)S(1)} %stack.19.refs_1_.refs_6_), channel_id=1, source_target_pairs={{0,2},{2,0},{4,6},{6,4},{8,10},{10,8},{12,14},{14,12},{16,18},{18,... | collective-permute-start | bytes 4718600 | tf_op jit(solution)/shard_map/ppermute | solution.py:497
  95.6 13.6 %collective-permute-start.15 = (bf16[160,1536]{1,0:T(8,128)(2,1)S(1)}, bf16[160,1536]{1,0:T(8,128)(2,1)S(1)}, u32[]{:S(2)}, u32[]{:S(2)}) collective-permute-start(bf16[160,1536]{1,0:T(8,128)(2,1)S(1)} %collective-permute-done.9.refs_7_.refs_3_), channel_id=1, source_target_pairs={{0,1},{1,0},{2,3},{3,2},{4,5},{5,4},{6,7},{7,6},{8,9},{9,8},{10,11... | collective-permute-start | bytes 1474568 | tf_op jit(solution)/shard_map/ppermute | solution.py:49
  116.1 2.2 %collective-permute-start.16 = (bf16[2560,128]{1,0:T(8,128)(2,1)S(1)}, bf16[2560,128]{1,0:T(8,128)(2,1)S(1)}, u32[]{:S(2)}, u32[]{:S(2)}) collective-permute-start(bf16[2560,128]{1,0:T(8,128)(2,1)S(1)} %get-tuple-element.107), channel_id=1, source_target_pairs={{0,2},{2,0},{4,6},{6,4},{8,10},{10,8},{12,14},{14,12},{16,18},{18,... | collective-permute-start | bytes 1966088 | tf_op jit(solution)/shard_map/ppermute | solution.py:389
  119.0 9.8 %collective-permute-start.17 = (bf16[1280,128]{1,0:T(8,128)(2,1)S(1)}, bf16[1280,128]{1,0:T(8,128)(2,1)S(1)}, u32[]{:S(2)}, u32[]{:S(2)}) collective-permute-start(bf16[1280,128]{1,0:T(8,128)(2,1)S(1)} %get-tuple-element.108), channel_id=1, source_target_pairs={{0,4},{2,6},{4,0},{6,2},{8,12},{10,14},{12,8},{14,10},{16,20},{18,... | collective-permute-start | bytes 983048 | tf_op jit(solution)/shard_map/ppermute | solution.py:507
  128.8 2.8 %collective-permute-start.18 = (bf16[1536,384]{1,0:T(8,128)(2,1)S(1)}, bf16[1536,384]{1,0:T(8,128)(2,1)S(1)}, u32[]{:S(2)}, u32[]{:S(2)}) collective-permute-start(bf16[1536,384]{1,0:T(8,128)(2,1)S(1)} %get-tuple-element.114), channel_id=1, source_target_pairs={{0,2},{2,0},{4,6},{6,4},{8,10},{10,8},{12,14},{14,12},{16,18},{18,... | collective-permute-start | bytes 3538952 | tf_op jit(solution)/shard_map/ppermute | solution.py:389
  132.5 17.8 %collective-permute-start.19 = (bf16[768,384]{1,0:T(8,128)(2,1)S(1)}, bf16[768,384]{1,0:T(8,128)(2,1)S(1)}, u32[]{:S(2)}, u32[]{:S(2)}) collective-permute-start(bf16[768,384]{1,0:T(8,128)(2,1)S(1)} %get-tuple-element.127), channel_id=1, source_target_pairs={{0,4},{2,6},{4,0},{6,2},{8,12},{10,14},{12,8},{14,10},{16,20},{18,... | collective-permute-start | bytes 1769480 | tf_op jit(solution)/shard_map/ppermute | solution.py:507
  134.0 15.3 %collective-permute-start.20 = (bf16[480,128]{1,0:T(8,128)(2,1)S(1)}, bf16[480,128]{1,0:T(8,128)(2,1)S(1)}, u32[]{:S(2)}, u32[]{:S(2)}) collective-permute-start(bf16[480,128]{1,0:T(8,128)(2,1)S(1)} %get-tuple-element.131), channel_id=1, source_target_pairs={{0,24},{2,26},{4,28},{6,30},{8,0},{10,2},{12,4},{14,6},{16,8},{18,... | collective-permute-start | bytes 368648 | tf_op jit(solution)/shard_map/ppermute | solution.py:458
  138.4 11.9 %collective-permute-start.21 = (bf16[480,128]{1,0:T(8,128)(2,1)S(1)}, bf16[480,128]{1,0:T(8,128)(2,1)S(1)}, u32[]{:S(2)}, u32[]{:S(2)}) collective-permute-start(bf16[480,128]{1,0:T(8,128)(2,1)S(1)} %get-tuple-element.132), channel_id=1, source_target_pairs={{0,16},{2,18},{4,20},{6,22},{8,24},{10,26},{12,28},{14,30},{16,0},... | collective-permute-start | bytes 368648 | tf_op jit(solution)/shard_map/ppermute | solution.py:458
  139.3 11.0 %collective-permute-start.22 = (bf16[480,128]{1,0:T(8,128)(2,1)S(1)}, bf16[480,128]{1,0:T(8,128)(2,1)S(1)}, u32[]{:S(2)}, u32[]{:S(2)}) collective-permute-start(bf16[480,128]{1,0:T(8,128)(2,1)S(1)} %get-tuple-element.133), channel_id=1, source_target_pairs={{0,8},{2,10},{4,12},{6,14},{8,16},{10,18},{12,20},{14,22},{16,24},... | collective-permute-start | bytes 368648 | tf_op jit(solution)/shard_map/ppermute | solution.py:458
  150.3 3.0 %collective-permute-start.23 = (bf16[2560,256]{1,0:T(8,128)(2,1)S(1)}, bf16[2560,256]{1,0:T(8,128)(2,1)S(1)}, u32[]{:S(2)}, u32[]{:S(2)}) collective-permute-start(bf16[2560,256]{1,0:T(8,128)(2,1)S(1)} %get-tuple-element.138), channel_id=1, source_target_pairs={{0,2},{2,0},{4,6},{6,4},{8,10},{10,8},{12,14},{14,12},{16,18},{18,... | collective-permute-start | bytes 3932168 | tf_op jit(solution)/shard_map/ppermute | solution.py:389
  154.2 16.8 %collective-permute-start.24 = (bf16[1280,256]{1,0:T(8,128)(2,1)S(1)}, bf16[1280,256]{1,0:T(8,128)(2,1)S(1)}, u32[]{:S(2)}, u32[]{:S(2)}) collective-permute-start(bf16[1280,256]{1,0:T(8,128)(2,1)S(1)} %get-tuple-element.140), channel_id=1, source_target_pairs={{0,4},{2,6},{4,0},{6,2},{8,12},{10,14},{12,8},{14,10},{16,20},{18,... | collective-permute-start | bytes 1966088 | tf_op jit(solution)/shard_map/ppermute | solution.py:507
  155.5 8.7 %collective-permute-start.25 = (bf16[192,384]{1,0:T(8,128)(2,1)S(1)}, bf16[192,384]{1,0:T(8,128)(2,1)S(1)}, u32[]{:S(2)}, u32[]{:S(2)}) collective-permute-start(bf16[192,384]{1,0:T(8,128)(2,1)S(1)} %get-tuple-element.143), channel_id=1, source_target_pairs={{0,8},{2,10},{4,12},{6,14},{8,16},{10,18},{12,20},{14,22},{16,24},... | collective-permute-start | bytes 442376 | tf_op jit(solution)/shard_map/ppermute | solution.py:458
  157.9 11.4 %collective-permute-start.26 = (bf16[192,384]{1,0:T(8,128)(2,1)S(1)}, bf16[192,384]{1,0:T(8,128)(2,1)S(1)}, u32[]{:S(2)}, u32[]{:S(2)}) collective-permute-start(bf16[192,384]{1,0:T(8,128)(2,1)S(1)} %get-tuple-element.144), channel_id=1, source_target_pairs={{0,16},{2,18},{4,20},{6,22},{8,24},{10,26},{12,28},{14,30},{16,0},... | collective-permute-start | bytes 442376 | tf_op jit(solution)/shard_map/ppermute | solution.py:458
  159.0 10.3 %collective-permute-start.27 = (bf16[192,384]{1,0:T(8,128)(2,1)S(1)}, bf16[192,384]{1,0:T(8,128)(2,1)S(1)}, u32[]{:S(2)}, u32[]{:S(2)}) collective-permute-start(bf16[192,384]{1,0:T(8,128)(2,1)S(1)} %get-tuple-element.145), channel_id=1, source_target_pairs={{0,24},{2,26},{4,28},{6,30},{8,0},{10,2},{12,4},{14,6},{16,8},{18,... | collective-permute-start | bytes 442376 | tf_op jit(solution)/shard_map/ppermute | solution.py:458
  171.7 10.0 %collective-permute-start.28 = (bf16[480,256]{1,0:T(8,128)(2,1)S(1)}, bf16[480,256]{1,0:T(8,128)(2,1)S(1)}, u32[]{:S(2)}, u32[]{:S(2)}) collective-permute-start(bf16[480,256]{1,0:T(8,128)(2,1)S(1)} %get-tuple-element.152), channel_id=1, source_target_pairs={{0,24},{2,26},{4,28},{6,30},{8,0},{10,2},{12,4},{14,6},{16,8},{18,... | collective-permute-start | bytes 737288 | tf_op jit(solution)/shard_map/ppermute | solution.py:458
  175.2 21.6 %collective-permute-start.29 = (bf16[480,256]{1,0:T(8,128)(2,1)S(1)}, bf16[480,256]{1,0:T(8,128)(2,1)S(1)}, u32[]{:S(2)}, u32[]{:S(2)}) collective-permute-start(bf16[480,256]{1,0:T(8,128)(2,1)S(1)} %get-tuple-element.153), channel_id=1, source_target_pairs={{0,16},{2,18},{4,20},{6,22},{8,24},{10,26},{12,28},{14,30},{16,0},... | collective-permute-start | bytes 737288 | tf_op jit(solution)/shard_map/ppermute | solution.py:458
  175.2 21.6 %collective-permute-start.30 = (bf16[480,256]{1,0:T(8,128)(2,1)S(1)}, bf16[480,256]{1,0:T(8,128)(2,1)S(1)}, u32[]{:S(2)}, u32[]{:S(2)}) collective-permute-start(bf16[480,256]{1,0:T(8,128)(2,1)S(1)} %get-tuple-element.154), channel_id=1, source_target_pairs={{0,8},{2,10},{4,12},{6,14},{8,16},{10,18},{12,20},{14,22},{16,24},... | collective-permute-start | bytes 737288 | tf_op jit(solution)/shard_map/ppermute | solution.py:458

commit v8 on v7

--- a/solution.py
+++ b/solution.py
@@ -120,7 +120,7 @@
         functools.partial(pack_kernel, n_groups),
         out_shape=shapes,
         in_specs=[smem()] + [pl.BlockSpec(memory_space=pltpu.HBM)] * 4,
-        out_specs=[vmem()] * len(shapes),
+        out_specs=[pl.BlockSpec(memory_space=pltpu.HBM)] * len(shapes),
         scratch_shapes=[pltpu.SemaphoreType.DMA((4 * n_groups,))],
         compiler_params=pltpu.CompilerParams(vmem_limit_bytes=60 * 1024 * 1024),
         name="pack",
@@ -508,25 +508,26 @@
 
     dq, halves = attention_halves(0, 1, q)
     kept, sent = halve(ids, *halves, n_frame, tok_bits)
+    q, kept, sent = tie((q, kept, sent))
     other = across_x(sent)
-    out_after, kept = tie((out, kept))
-    proj = proj_gradient(ids, out_after, grads, depth, n_groups, n_tok, n_space)
-    other, *proj = tie((other, *proj))
-    proj_kept, proj_sent = halve(ids, *proj, n_frame, tok_bits)
-    sums = finish(ids, kept, other, dq, n_groups)
-    proj_sent, q, *sums = tie((proj_sent, q, *sums))
-    returned = [exchange(sums, n_groups, n_tok, -1)]
-    proj_other = across_x(proj_sent)
     if heads > 1:
         dq_rest, halves = attention_halves(1, heads - 1, q)
-        step = (proj_other, *halves, *returned[0][1:])
-        proj_other, kept, sent, *returned[0][1:] = tie(step)
-        kept, sent = halve(ids, kept, sent, n_frame, tok_bits)
-    proj_pieces = exchange(add_parts(ids, proj_kept, proj_other, n_groups), n_groups, n_tok, 1)
+        other, *halves = tie((other, *halves))
+    sums = finish(ids, kept, other, dq, n_groups)
+    returned = [exchange(sums, n_groups, n_tok, -1)]
+    out_after, *_ = tie((out, *sums))
+    proj = proj_gradient(ids, out_after, grads, depth, n_groups, n_tok, n_space)
     if heads > 1:
-        other, *proj_pieces[1:] = tie((across_x(sent), *proj_pieces[1:]))
+        kept, sent = halve(ids, *halves, n_frame, tok_bits)
+        other = across_x(sent)
+        other, proj, *returned[0][1:] = tie((other, tuple(proj), *returned[0][1:]))
         sums = finish(ids, kept, other, dq_rest, n_groups)
         returned.append(exchange(sums, n_groups, n_tok, -1))
+    proj_kept, proj_sent = halve(ids, *proj, n_frame, tok_bits)
+    if heads > 1:
+        proj_sent, *_ = tie((proj_sent, *sums))
+    proj = add_parts(ids, proj_kept, across_x(proj_sent), n_groups)
+    proj_pieces = exchange(proj, n_groups, n_tok, 1)
     grad_proj = join(ids, proj_pieces, n_groups).T
     grad_queries, grad_keys, grad_values = unpack(ids, returned, rows, gw, n_groups)
     return (grad_queries, grad_keys, grad_values, grad_proj)

time: 199 us -> 255 us (1.28)
  Pallas kernels: 42.7 us -> 103 us
  waiting for transfers between devices: 97.4 us -> 91.6 us
    pallas_call x1, Pallas kernels: 3.73 us -> 64.5 us  [pack(): pl.pallas_call(functools.partial(pack_kernel, n_groups), out_shape=shapes...]
    ppermute x12, waiting for transfers between devices: 56.5 us -> 48.3 us  [exchange(): lax.ppermute(pieces[s], 'frame', shift_pairs(n_groups, n_tok, sign * s))]
  transfers between devices with their start and end apart: 31 -> 31, of which waited for: 16 -> 14; matrix products, arithmetic and copies ran while one was open for 0% -> 0% of each run, Pallas kernels for 14% -> 11%
where the time goes in v8:
time: 255 us
  Pallas kernels  103 us (40%)
  waiting for transfers between devices  91.6 us (36%)
  starting transfers between devices  58.4 us (23%)
    pallas_call x1, Pallas kernels, pack(): pl.pallas_call(functools.partial(pack_kernel, n_groups), out_shape=shapes...  64.5 us
    ppermute x12, waiting for transfers between devices, exchange(): lax.ppermute(pieces[s], 'frame', shift_pairs(n_groups, n_tok, sign * s))  48.3 us
    ppermute x12, starting transfers between devices, exchange(): lax.ppermute(pieces[s], 'frame', shift_pairs(n_groups, n_tok, sign * s))  22.2 us
    ppermute x3, starting transfers between devices, local(): ring = lax.ppermute(ring, 'frame', shift_pairs(n_groups, n_tok, 1))  20.6 us
    pallas_call x13, Pallas kernels, whole_call(): pl.pallas_call(body, out_shape=out_shape, in_specs=[smem()] + [vmem()] *...  16 us
    ppermute x4, waiting for transfers between devices, local(): others.append(lax.ppermute(own[s], 'frame', last))  14.3 us
    pallas_call x2, Pallas kernels, backward(): pl.pallas_call(functools.partial(backward_kernel, n_groups, chunk, 1.0 /...  12.8 us
    ppermute x3, waiting for transfers between devices, local(): ring = lax.ppermute(ring, 'frame', shift_pairs(n_groups, n_tok, 1))  10.5 us
  transfers between devices with their start and end apart: 31, of which 14 were waited for; matrix products, arithmetic and copies ran while one was open for 0% of the time, Pallas kernels for 11%

profile of v8, /device:TPU:0, one launch (start us, length us, event | category | flops | bytes accessed | tf_op | source)
XLA Modules:
  0.0 255.0 jit_solution(17306673253551618276)
XLA Ops:
  0.7 0.6 pad_add_fusion.ids
  1.3 64.5 %pack.1 = (bf16[512,384]{1,0:T(8,128)(2,1)}, bf16[672,384]{1,0:T(8,128)(2,1)}, bf16[672,384]{1,0:T(8,128)(2,1)}, bf16[672,384]{1,0:T(8,128)(2,1)}, bf16[160,384]{1,0:T(8,128)(2,1)}) custom-call(s32[3]{0:T(128)} %pad_add_fusion.ids, bf16[160,1536]{1,0:T(8,128)(2,1)} %q.1, bf16[160,1536]{1,0:T(8,128)(2,1)} %k.1, bf16[160,1536]{1,0:T(8,128)(2,1)} %v.1, ...), custom_call_target="tpu_custom_call" | custom-call | tf_op jit(solution)/shard_map/pack/pallas_call | solution.py:119
  65.7 0.0 copy-start.1
  65.7 3.1 %collective-permute-start = (bf16[672,384]{1,0:T(8,128)(2,1)}, bf16[672,384]{1,0:T(8,128)(2,1)S(1)}, u32[]{:S(2)}, u32[]{:S(2)}) collective-permute-start(bf16[672,384]{1,0:T(8,128)(2,1)} %get-tuple-element.77), channel_id=1, source_target_pairs={{0,8},{2,10},{4,12},{6,14},{8,16},{10,18},{12,20},{14,22},{16,24},... | collective-permute-start | bytes 1548296 | tf_op jit(solution)/shard_map/ppermute | solution.py:458
  68.8 1.6 collective-permute-start.3
  70.4 1.5 collective-permute-start.5
  71.9 1.5 collective-permute-start.4
  73.4 1.2 collective-permute-start.1
  74.6 9.1 %collective-permute-done.refs_0_ = bf16[672,384]{1,0:T(8,128)(2,1)S(1)} collective-permute-done((bf16[672,384]{1,0:T(8,128)(2,1)}, bf16[672,384]{1,0:T(8,128)(2,1)S(1)}, u32[]{:S(2)}, u32[]{:S(2)}) %collective-permute-start) | collective-permute-done | bytes 516128 | tf_op jit(solution)/shard_map/ppermute | solution.py:458
  83.8 10.5 %collective-permute-done.3.refs_5_.refs_1_ = bf16[160,1536]{1,0:T(8,128)(2,1)S(1)} collective-permute-done((bf16[160,1536]{1,0:T(8,128)(2,1)S(1)}, bf16[160,1536]{1,0:T(8,128)(2,1)S(1)}, u32[]{:S(2)}, u32[]{:S(2)}) %collective-permute-start.3) | collective-permute-done | bytes 491552 | tf_op jit(solution)/shard_map/ppermute | solution.py:489
  94.3 1.8 collective-permute-start.8
  96.0 9.4 %collective-permute-start.6 = (bf16[160,1536]{1,0:T(8,128)(2,1)S(1)}, bf16[160,1536]{1,0:T(8,128)(2,1)S(1)}, u32[]{:S(2)}, u32[]{:S(2)}) collective-permute-start(bf16[160,1536]{1,0:T(8,128)(2,1)S(1)} %collective-permute-done.3.refs_5_.refs_1_), channel_id=1, source_target_pairs={{0,8},{2,10},{4,12},{6,14},{8,16},{10,18},{12,20},{14,22},{16,24},... | collective-permute-start | bytes 1474568 | tf_op jit(solution)/shard_map/ppermute | solution.py:489
  105.4 1.5 collective-permute-start.7
  106.9 19.2 %collective-permute-done.1.refs_1_ = bf16[672,384]{1,0:T(8,128)(2,1)S(1)} collective-permute-done((bf16[672,384]{1,0:T(8,128)(2,1)}, bf16[672,384]{1,0:T(8,128)(2,1)S(1)}, u32[]{:S(2)}, u32[]{:S(2)}) %collective-permute-start.1) | collective-permute-done | bytes 516128 | tf_op jit(solution)/shard_map/ppermute | solution.py:458
  126.2 1.6 collective-permute-start.11
  127.8 9.6 %collective-permute-start.9 = (bf16[160,1536]{1,0:T(8,128)(2,1)S(1)}, bf16[160,1536]{1,0:T(8,128)(2,1)S(1)}, u32[]{:S(2)}, u32[]{:S(2)}) collective-permute-start(bf16[160,1536]{1,0:T(8,128)(2,1)S(1)} %collective-permute-done.6.refs_6_.refs_2_), channel_id=1, source_target_pairs={{0,8},{2,10},{4,12},{6,14},{8,16},{10,18},{12,20},{14,22},{16,24},... | collective-permute-start | bytes 1474568 | tf_op jit(solution)/shard_map/ppermute | solution.py:489
  137.4 1.5 collective-permute-start.10
  139.0 7.9 %collective-permute-done.10.refs_2_ = bf16[512,384]{1,0:T(8,128)(2,1)S(1)} collective-permute-done((bf16[512,384]{1,0:T(8,128)(2,1)S(1)}, bf16[512,384]{1,0:T(8,128)(2,1)S(1)}, u32[]{:S(2)}, u32[]{:S(2)}) %collective-permute-start.10) | collective-permute-done | bytes 393248 | tf_op jit(solution)/shard_map/ppermute | solution.py:486
  146.8 1.5 collective-permute-start.12
  148.3 0.7 stack.18.refs_0_.refs_5_
  149.0 0.0 copy-start.2
  149.0 0.1 collective-permute-start.13
  149.1 6.4 %collective-permute-done.12.refs_3_ = bf16[512,384]{1,0:T(8,128)(2,1)S(1)} collective-permute-done((bf16[512,384]{1,0:T(8,128)(2,1)S(1)}, bf16[512,384]{1,0:T(8,128)(2,1)S(1)}, u32[]{:S(2)}, u32[]{:S(2)}) %collective-permute-start.12) | collective-permute-done | bytes 393248 | tf_op jit(solution)/shard_map/ppermute | solution.py:486
  155.5 0.7 stack.19.refs_1_.refs_6_
  156.2 0.1 collective-permute-start.14
  156.3 0.6 collective-permute-start.15
  156.9 0.6 stack_queries.1.q_in.refs_0_
  157.5 2.2 collective-permute-done.14.refs_3_.refs_8_
  159.7 10.2 %forward.1 = (bf16[3,2560,640]{2,1,0:T(8,128)(2,1)S(1)}, bf16[640,384]{1,0:T(8,128)(2,1)S(1)}, f32[3,1,640]{2,1,0:T(1,128)S(1)}) custom-call(bf16[640,384]{1,0:T(8,128)(2,1)S(1)} %stack_queries.1.q_in.refs_0_, bf16[2048,384]{1,0:T(8,128)(2,1)S(1)} %stack.18.refs_0_.refs_5_, bf16[2048,384]{1,0:T(8,128)(2,1)S(1)} %stack.19.refs_1_.refs_6_, ...), custom_call_target="tpu_custom_call" | custom-call | flops 2516582400 | bytes 9830400 | tf_op jit(solution)/shard_map/forward/pallas_call | solution.py:200
  169.9 0.0 collective-permute-done.15.refs_11_.refs_7_
  169.9 3.0 %attn_gradient.1.refs_4_ = bf16[640,384]{1,0:T(8,128)(2,1)S(1)} custom-call(s32[3]{0:T(128)S(1)} %copy-done.3, bf16[2048,384]{1,0:T(8,128)(2,1)S(1)} %stack.18.refs_0_.refs_5_, bf16[2048,384]{1,0:T(8,128)(2,1)S(1)} %stack.19.refs_1_.refs_6_, bf16[2048,384]{1,0:T(8,128)(2,1)S(1)} %collective-permute-done.13.refs_2_.refs_7_, ...), custom_call_target="tpu_custom_call" | custom-call | flops 245760 | bytes 491520 | tf_op jit(solution)/shard_map/attn_gradient/pallas_call | solution.py:75
  172.9 3.9 %backward.2 = (bf16[160,128]{1,0:T(8,128)(2,1)S(1)}, bf16[160,128]{1,0:T(8,128)(2,1)S(1)}, bf16[160,128]{1,0:T(8,128)(2,1)S(1)}, bf16[160,128]{1,0:T(8,128)(2,1)...) custom-call(bf16[640,384]{1,0:T(8,128)(2,1)S(1)} %stack_queries.1.q_in.refs_0_, ...), custom_call_target="tpu_custom_call" | custom-call | flops 81920 | bytes 163840 | tf_op jit(solution)/shard_map/backward/pallas_call | solution.py:264
  176.8 0.2 collective-permute-start.16
  177.0 2.0 collective-permute-done.16.other
  179.0 0.7 add_parts.4
  179.7 1.6 collective-permute-start.17
  181.3 8.8 %backward.3 = (bf16[160,256]{1,0:T(8,128)(2,1)S(1)}, bf16[160,256]{1,0:T(8,128)(2,1)S(1)}, bf16[160,256]{1,0:T(8,128)(2,1)S(1)}, bf16[160,256]{1,0:T(8,128)(2,1)...) custom-call(bf16[640,384]{1,0:T(8,128)(2,1)S(1)} %stack_queries.1.q_in.refs_0_, ...), custom_call_target="tpu_custom_call" | custom-call | flops 81920 | bytes 163840 | tf_op jit(solution)/shard_map/backward/pallas_call | solution.py:264
  190.1 0.1 collective-permute-start.18
  190.2 3.0 %collective-permute-done.18.other = bf16[2560,256]{1,0:T(8,128)(2,1)S(1)} collective-permute-done((bf16[2560,256]{1,0:T(8,128)(2,1)S(1)}, bf16[2560,256]{1,0:T(8,128)(2,1)S(1)}, u32[]{:S(2)}, u32[]{:S(2)}) %collective-permute-start.18) | collective-permute-done | bytes 1310752 | tf_op jit(solution)/shard_map/ppermute | solution.py:389
  193.2 0.8 add_parts.5
  194.1 0.9 collective-permute-start.19
  195.0 0.6 finish.2
  195.6 4.4 %collective-permute-start.20 = (bf16[480,128]{1,0:T(8,128)(2,1)S(1)}, bf16[480,128]{1,0:T(8,128)(2,1)S(1)}, u32[]{:S(2)}, u32[]{:S(2)}) collective-permute-start(bf16[480,128]{1,0:T(8,128)(2,1)S(1)} %get-tuple-element.117), channel_id=1, source_target_pairs={{0,24},{2,26},{4,28},{6,30},{8,0},{10,2},{12,4},{14,6},{16,8},{18,... | collective-permute-start | bytes 368648 | tf_op jit(solution)/shard_map/ppermute | solution.py:458
  200.0 0.9 collective-permute-start.21
  200.9 1.1 collective-permute-start.22
  202.1 3.2 %proj_gradient.1 = (bf16[1536,384]{1,0:T(8,128)(2,1)S(1)}, bf16[1536,384]{1,0:T(8,128)(2,1)S(1)}) custom-call(s32[3]{0:T(128)S(1)} %copy-done.3, bf16[640,384]{1,0:T(8,128)(2,1)S(1)} %get-tuple-element.120.refs_2_.attn, bf16[160,1536]{1,0:T(8,128)(2,1)S(1)} %copy-done, bf16[160,1536]{1,0:T(8,128)(2,1)S(1)} %collective-permute-done.3.refs_5_.refs_1_, ...), custom_call_target="tpu_custom_call" | custom-call | flops 245760 | bytes 491520 | tf_op jit(solution)/shard_map/proj_gradient/pallas_call | solution.py:75
  205.3 6.6 %collective-permute-done.21.refs_2_ = bf16[480,128]{1,0:T(8,128)(2,1)S(1)} collective-permute-done((bf16[480,128]{1,0:T(8,128)(2,1)S(1)}, bf16[480,128]{1,0:T(8,128)(2,1)S(1)}, u32[]{:S(2)}, u32[]{:S(2)}) %collective-permute-start.21) | collective-permute-done | bytes 122912 | tf_op jit(solution)/shard_map/ppermute | solution.py:458
  211.9 0.7 finish.3
  212.6 2.1 collective-permute-done.26.other
  214.8 0.8 add_parts.6
  215.6 1.2 collective-permute-start.27
  216.8 3.0 %collective-permute-start.23 = (bf16[480,256]{1,0:T(8,128)(2,1)S(1)}, bf16[480,256]{1,0:T(8,128)(2,1)S(1)}, u32[]{:S(2)}, u32[]{:S(2)}) collective-permute-start(bf16[480,256]{1,0:T(8,128)(2,1)S(1)} %get-tuple-element.133), channel_id=1, source_target_pairs={{0,24},{2,26},{4,28},{6,30},{8,0},{10,2},{12,4},{14,6},{16,8},{18,... | collective-permute-start | bytes 737288 | tf_op jit(solution)/shard_map/ppermute | solution.py:458
  219.9 0.9 collective-permute-start.24
  220.8 1.1 collective-permute-start.25
  221.9 9.1 %collective-permute-done.27.other = bf16[768,384]{1,0:T(8,128)(2,1)S(1)} collective-permute-done((bf16[768,384]{1,0:T(8,128)(2,1)S(1)}, bf16[768,384]{1,0:T(8,128)(2,1)S(1)}, u32[]{:S(2)}, u32[]{:S(2)}) %collective-permute-start.27) | collective-permute-done | bytes 589856 | tf_op jit(solution)/shard_map/ppermute | solution.py:507
  231.0 0.7 add_parts.7
  231.7 2.9 %collective-permute-start.28 = (bf16[192,384]{1,0:T(8,128)(2,1)S(1)}, bf16[192,384]{1,0:T(8,128)(2,1)S(1)}, u32[]{:S(2)}, u32[]{:S(2)}) collective-permute-start(bf16[192,384]{1,0:T(8,128)(2,1)S(1)} %get-tuple-element.145), channel_id=1, source_target_pairs={{0,8},{2,10},{4,12},{6,14},{8,16},{10,18},{12,20},{14,22},{16,24},... | collective-permute-start | bytes 442376 | tf_op jit(solution)/shard_map/ppermute | solution.py:458
  234.6 1.1 collective-permute-start.29
  235.7 2.4 collective-permute-start.30
  238.1 11.8 %collective-permute-done.24.refs_6_ = bf16[480,256]{1,0:T(8,128)(2,1)S(1)} collective-permute-done((bf16[480,256]{1,0:T(8,128)(2,1)S(1)}, bf16[480,256]{1,0:T(8,128)(2,1)S(1)}, u32[]{:S(2)}, u32[]{:S(2)}) %collective-permute-start.24) | collective-permute-done | bytes 245792 | tf_op jit(solution)/shard_map/ppermute | solution.py:458
  249.9 1.8 unpack.1
  251.7 1.3 collective-permute-done.29.refs_2_
  253.0 0.4 collective-permute-done.30.refs_3_
  253.4 1.7 join.1
  (27 shorter events, 0.2 us)
Async XLA Ops:
  0.6 68.2 %copy-start = (bf16[160,1536]{1,0:T(8,128)(2,1)S(1)}, bf16[160,1536]{1,0:T(8,128)(2,1)}, u32[]{:S(2)}) copy-start(bf16[160,1536]{1,0:T(8,128)(2,1)} %refs_0_) | copy-start | bytes 1474564
  65.7 82.6 %copy-start.1 = (bf16[512,384]{1,0:T(8,128)(2,1)S(1)}, bf16[512,384]{1,0:T(8,128)(2,1)}, u32[]{:S(2)}) copy-start(bf16[512,384]{1,0:T(8,128)(2,1)} %get-tuple-element.80.refs_0_) | copy-start | bytes 1179652
  65.7 82.6 %copy-start.3 = (s32[3]{0:T(128)S(1)}, s32[3]{0:T(128)}, u32[]{:S(2)}) copy-start(s32[3]{0:T(128)} %pad_add_fusion.ids) | copy-start | bytes 40
  65.7 18.0 %collective-permute-start = (bf16[672,384]{1,0:T(8,128)(2,1)}, bf16[672,384]{1,0:T(8,128)(2,1)S(1)}, u32[]{:S(2)}, u32[]{:S(2)}) collective-permute-start(bf16[672,384]{1,0:T(8,128)(2,1)} %get-tuple-element.77), channel_id=1, source_target_pairs={{0,8},{2,10},{4,12},{6,14},{8,16},{10,18},{12,20},{14,22},{16,24},... | collective-permute-start | bytes 1548296 | tf_op jit(solution)/shard_map/ppermute | solution.py:458
  68.8 25.4 %collective-permute-start.3 = (bf16[160,1536]{1,0:T(8,128)(2,1)S(1)}, bf16[160,1536]{1,0:T(8,128)(2,1)S(1)}, u32[]{:S(2)}, u32[]{:S(2)}) collective-permute-start(bf16[160,1536]{1,0:T(8,128)(2,1)S(1)} %copy-done), channel_id=1, source_target_pairs={{0,8},{2,10},{4,12},{6,14},{8,16},{10,18},{12,20},{14,22},{16,24},... | collective-permute-start | bytes 1474568 | tf_op jit(solution)/shard_map/ppermute | solution.py:489
  70.4 23.9 %collective-permute-start.5 = (bf16[160,1536]{1,0:T(8,128)(2,1)S(1)}, bf16[160,1536]{1,0:T(8,128)(2,1)S(1)}, u32[]{:S(2)}, u32[]{:S(2)}) collective-permute-start(bf16[160,1536]{1,0:T(8,128)(2,1)S(1)} %copy-done), channel_id=1, source_target_pairs={{0,1},{1,0},{2,3},{3,2},{4,5},{5,4},{6,7},{7,6},{8,9},{9,8},{10,11... | collective-permute-start | bytes 1474568 | tf_op jit(solution)/shard_map/ppermute | solution.py:49
  71.9 11.9 %collective-permute-start.4 = (bf16[512,384]{1,0:T(8,128)(2,1)}, bf16[512,384]{1,0:T(8,128)(2,1)S(1)}, u32[]{:S(2)}, u32[]{:S(2)}) collective-permute-start(bf16[512,384]{1,0:T(8,128)(2,1)} %get-tuple-element.80.refs_0_), channel_id=1, source_target_pairs={{0,4},{2,6},{4,0},{6,2},{8,12},{10,14},{12,8},{14,10},{16,20},{18,... | collective-permute-start | bytes 1179656 | tf_op jit(solution)/shard_map/ppermute | solution.py:486
  73.4 52.7 %collective-permute-start.1 = (bf16[672,384]{1,0:T(8,128)(2,1)}, bf16[672,384]{1,0:T(8,128)(2,1)S(1)}, u32[]{:S(2)}, u32[]{:S(2)}) collective-permute-start(bf16[672,384]{1,0:T(8,128)(2,1)} %get-tuple-element.78), channel_id=1, source_target_pairs={{0,16},{2,18},{4,20},{6,22},{8,24},{10,26},{12,28},{14,30},{16,0},... | collective-permute-start | bytes 1548296 | tf_op jit(solution)/shard_map/ppermute | solution.py:458
  94.3 31.9 %collective-permute-start.8 = (bf16[160,1536]{1,0:T(8,128)(2,1)S(1)}, bf16[160,1536]{1,0:T(8,128)(2,1)S(1)}, u32[]{:S(2)}, u32[]{:S(2)}) collective-permute-start(bf16[160,1536]{1,0:T(8,128)(2,1)S(1)} %collective-permute-done.3.refs_5_.refs_1_), channel_id=1, source_target_pairs={{0,1},{1,0},{2,3},{3,2},{4,5},{5,4},{6,7},{7,6},{8,9},{9,8},{10,11... | collective-permute-start | bytes 1474568 | tf_op jit(solution)/shard_map/ppermute | solution.py:49
  96.0 30.2 %collective-permute-start.6 = (bf16[160,1536]{1,0:T(8,128)(2,1)S(1)}, bf16[160,1536]{1,0:T(8,128)(2,1)S(1)}, u32[]{:S(2)}, u32[]{:S(2)}) collective-permute-start(bf16[160,1536]{1,0:T(8,128)(2,1)S(1)} %collective-permute-done.3.refs_5_.refs_1_), channel_id=1, source_target_pairs={{0,8},{2,10},{4,12},{6,14},{8,16},{10,18},{12,20},{14,22},{16,24},... | collective-permute-start | bytes 1474568 | tf_op jit(solution)/shard_map/ppermute | solution.py:489
  105.4 20.7 %collective-permute-start.7 = (bf16[512,384]{1,0:T(8,128)(2,1)S(1)}, bf16[512,384]{1,0:T(8,128)(2,1)S(1)}, u32[]{:S(2)}, u32[]{:S(2)}) collective-permute-start(bf16[512,384]{1,0:T(8,128)(2,1)S(1)} %slice.12.refs_1_), channel_id=1, source_target_pairs={{0,4},{2,6},{4,0},{6,2},{8,12},{10,14},{12,8},{14,10},{16,20},{18,... | collective-permute-start | bytes 1179656 | tf_op jit(solution)/shard_map/ppermute | solution.py:486
  106.9 32.0 %collective-permute-start.2 = (bf16[672,384]{1,0:T(8,128)(2,1)}, bf16[672,384]{1,0:T(8,128)(2,1)S(1)}, u32[]{:S(2)}, u32[]{:S(2)}) collective-permute-start(bf16[672,384]{1,0:T(8,128)(2,1)} %get-tuple-element.79), channel_id=1, source_target_pairs={{0,24},{2,26},{4,28},{6,30},{8,0},{10,2},{12,4},{14,6},{16,8},{18,... | collective-permute-start | bytes 1548296 | tf_op jit(solution)/shard_map/ppermute | solution.py:458
  126.2 20.6 %collective-permute-start.11 = (bf16[160,1536]{1,0:T(8,128)(2,1)S(1)}, bf16[160,1536]{1,0:T(8,128)(2,1)S(1)}, u32[]{:S(2)}, u32[]{:S(2)}) collective-permute-start(bf16[160,1536]{1,0:T(8,128)(2,1)S(1)} %collective-permute-done.6.refs_6_.refs_2_), channel_id=1, source_target_pairs={{0,1},{1,0},{2,3},{3,2},{4,5},{5,4},{6,7},{7,6},{8,9},{9,8},{10,11... | collective-permute-start | bytes 1474568 | tf_op jit(solution)/shard_map/ppermute | solution.py:49
  127.8 19.1 %collective-permute-start.9 = (bf16[160,1536]{1,0:T(8,128)(2,1)S(1)}, bf16[160,1536]{1,0:T(8,128)(2,1)S(1)}, u32[]{:S(2)}, u32[]{:S(2)}) collective-permute-start(bf16[160,1536]{1,0:T(8,128)(2,1)S(1)} %collective-permute-done.6.refs_6_.refs_2_), channel_id=1, source_target_pairs={{0,8},{2,10},{4,12},{6,14},{8,16},{10,18},{12,20},{14,22},{16,24},... | collective-permute-start | bytes 1474568 | tf_op jit(solution)/shard_map/ppermute | solution.py:489
  137.4 9.4 %collective-permute-start.10 = (bf16[512,384]{1,0:T(8,128)(2,1)S(1)}, bf16[512,384]{1,0:T(8,128)(2,1)S(1)}, u32[]{:S(2)}, u32[]{:S(2)}) collective-permute-start(bf16[512,384]{1,0:T(8,128)(2,1)S(1)} %slice.13.refs_2_), channel_id=1, source_target_pairs={{0,4},{2,6},{4,0},{6,2},{8,12},{10,14},{12,8},{14,10},{16,20},{18,... | collective-permute-start | bytes 1179656 | tf_op jit(solution)/shard_map/ppermute | solution.py:486
  146.8 8.7 %collective-permute-start.12 = (bf16[512,384]{1,0:T(8,128)(2,1)S(1)}, bf16[512,384]{1,0:T(8,128)(2,1)S(1)}, u32[]{:S(2)}, u32[]{:S(2)}) collective-permute-start(bf16[512,384]{1,0:T(8,128)(2,1)S(1)} %slice.14.refs_3_), channel_id=1, source_target_pairs={{0,4},{2,6},{4,0},{6,2},{8,12},{10,14},{12,8},{14,10},{16,20},{18,... | collective-permute-start | bytes 1179656 | tf_op jit(solution)/shard_map/ppermute | solution.py:486
  149.0 7.8 %copy-start.2 = (bf16[160,384]{1,0:T(8,128)(2,1)S(1)}, bf16[160,384]{1,0:T(8,128)(2,1)}, u32[]{:S(2)}) copy-start(bf16[160,384]{1,0:T(8,128)(2,1)} %get-tuple-element.76.own) | copy-start | bytes 368644
  149.0 8.4 %collective-permute-start.13 = (bf16[2048,384]{1,0:T(8,128)(2,1)S(1)}, bf16[2048,384]{1,0:T(8,128)(2,1)S(1)}, u32[]{:S(2)}, u32[]{:S(2)}) collective-permute-start(bf16[2048,384]{1,0:T(8,128)(2,1)S(1)} %stack.18.refs_0_.refs_5_), channel_id=1, source_target_pairs={{0,2},{2,0},{4,6},{6,4},{8,10},{10,8},{12,14},{14,12},{16,18},{18,... | collective-permute-start | bytes 4718600 | tf_op jit(solution)/shard_map/ppermute | solution.py:497
  156.2 3.5 %collective-permute-start.14 = (bf16[2048,384]{1,0:T(8,128)(2,1)S(1)}, bf16[2048,384]{1,0:T(8,128)(2,1)S(1)}, u32[]{:S(2)}, u32[]{:S(2)}) collective-permute-start(bf16[2048,384]{1,0:T(8,128)(2,1)S(1)} %stack.19.refs_1_.refs_6_), channel_id=1, source_target_pairs={{0,2},{2,0},{4,6},{6,4},{8,10},{10,8},{12,14},{14,12},{16,18},{18,... | collective-permute-start | bytes 4718600 | tf_op jit(solution)/shard_map/ppermute | solution.py:497
  156.3 13.6 %collective-permute-start.15 = (bf16[160,1536]{1,0:T(8,128)(2,1)S(1)}, bf16[160,1536]{1,0:T(8,128)(2,1)S(1)}, u32[]{:S(2)}, u32[]{:S(2)}) collective-permute-start(bf16[160,1536]{1,0:T(8,128)(2,1)S(1)} %collective-permute-done.9.refs_7_.refs_3_), channel_id=1, source_target_pairs={{0,1},{1,0},{2,3},{3,2},{4,5},{5,4},{6,7},{7,6},{8,9},{9,8},{10,11... | collective-permute-start | bytes 1474568 | tf_op jit(solution)/shard_map/ppermute | solution.py:49
  176.8 2.2 collective-permute-start.16
  179.7 10.4 %collective-permute-start.17 = (bf16[1280,128]{1,0:T(8,128)(2,1)S(1)}, bf16[1280,128]{1,0:T(8,128)(2,1)S(1)}, u32[]{:S(2)}, u32[]{:S(2)}) collective-permute-start(bf16[1280,128]{1,0:T(8,128)(2,1)S(1)} %get-tuple-element.104), channel_id=1, source_target_pairs={{0,4},{2,6},{4,0},{6,2},{8,12},{10,14},{12,8},{14,10},{16,20},{18,... | collective-permute-start | bytes 983048 | tf_op jit(solution)/shard_map/ppermute | solution.py:507
  190.1 3.1 %collective-permute-start.18 = (bf16[2560,256]{1,0:T(8,128)(2,1)S(1)}, bf16[2560,256]{1,0:T(8,128)(2,1)S(1)}, u32[]{:S(2)}, u32[]{:S(2)}) collective-permute-start(bf16[2560,256]{1,0:T(8,128)(2,1)S(1)} %get-tuple-element.115), channel_id=1, source_target_pairs={{0,2},{2,0},{4,6},{6,4},{8,10},{10,8},{12,14},{14,12},{16,18},{18,... | collective-permute-start | bytes 3932168 | tf_op jit(solution)/shard_map/ppermute | solution.py:389
  194.1 17.9 %collective-permute-start.19 = (bf16[1280,256]{1,0:T(8,128)(2,1)S(1)}, bf16[1280,256]{1,0:T(8,128)(2,1)S(1)}, u32[]{:S(2)}, u32[]{:S(2)}) collective-permute-start(bf16[1280,256]{1,0:T(8,128)(2,1)S(1)} %get-tuple-element.116), channel_id=1, source_target_pairs={{0,4},{2,6},{4,0},{6,2},{8,12},{10,14},{12,8},{14,10},{16,20},{18,... | collective-permute-start | bytes 1966088 | tf_op jit(solution)/shard_map/ppermute | solution.py:507
  195.6 9.7 %collective-permute-start.20 = (bf16[480,128]{1,0:T(8,128)(2,1)S(1)}, bf16[480,128]{1,0:T(8,128)(2,1)S(1)}, u32[]{:S(2)}, u32[]{:S(2)}) collective-permute-start(bf16[480,128]{1,0:T(8,128)(2,1)S(1)} %get-tuple-element.117), channel_id=1, source_target_pairs={{0,24},{2,26},{4,28},{6,30},{8,0},{10,2},{12,4},{14,6},{16,8},{18,... | collective-permute-start | bytes 368648 | tf_op jit(solution)/shard_map/ppermute | solution.py:458
  200.0 11.9 %collective-permute-start.21 = (bf16[480,128]{1,0:T(8,128)(2,1)S(1)}, bf16[480,128]{1,0:T(8,128)(2,1)S(1)}, u32[]{:S(2)}, u32[]{:S(2)}) collective-permute-start(bf16[480,128]{1,0:T(8,128)(2,1)S(1)} %get-tuple-element.118), channel_id=1, source_target_pairs={{0,16},{2,18},{4,20},{6,22},{8,24},{10,26},{12,28},{14,30},{16,0},... | collective-permute-start | bytes 368648 | tf_op jit(solution)/shard_map/ppermute | solution.py:458
  200.9 11.0 %collective-permute-start.22 = (bf16[480,128]{1,0:T(8,128)(2,1)S(1)}, bf16[480,128]{1,0:T(8,128)(2,1)S(1)}, u32[]{:S(2)}, u32[]{:S(2)}) collective-permute-start(bf16[480,128]{1,0:T(8,128)(2,1)S(1)} %get-tuple-element.119), channel_id=1, source_target_pairs={{0,8},{2,10},{4,12},{6,14},{8,16},{10,18},{12,20},{14,22},{16,24},... | collective-permute-start | bytes 368648 | tf_op jit(solution)/shard_map/ppermute | solution.py:458
  211.9 2.9 %collective-permute-start.26 = (bf16[1536,384]{1,0:T(8,128)(2,1)S(1)}, bf16[1536,384]{1,0:T(8,128)(2,1)S(1)}, u32[]{:S(2)}, u32[]{:S(2)}) collective-permute-start(bf16[1536,384]{1,0:T(8,128)(2,1)S(1)} %get-tuple-element.140), channel_id=1, source_target_pairs={{0,2},{2,0},{4,6},{6,4},{8,10},{10,8},{12,14},{14,12},{16,18},{18,... | collective-permute-start | bytes 3538952 | tf_op jit(solution)/shard_map/ppermute | solution.py:389
  215.6 15.4 %collective-permute-start.27 = (bf16[768,384]{1,0:T(8,128)(2,1)S(1)}, bf16[768,384]{1,0:T(8,128)(2,1)S(1)}, u32[]{:S(2)}, u32[]{:S(2)}) collective-permute-start(bf16[768,384]{1,0:T(8,128)(2,1)S(1)} %get-tuple-element.143), channel_id=1, source_target_pairs={{0,4},{2,6},{4,0},{6,2},{8,12},{10,14},{12,8},{14,10},{16,20},{18,... | collective-permute-start | bytes 1769480 | tf_op jit(solution)/shard_map/ppermute | solution.py:507
  216.8 18.9 %collective-permute-start.23 = (bf16[480,256]{1,0:T(8,128)(2,1)S(1)}, bf16[480,256]{1,0:T(8,128)(2,1)S(1)}, u32[]{:S(2)}, u32[]{:S(2)}) collective-permute-start(bf16[480,256]{1,0:T(8,128)(2,1)S(1)} %get-tuple-element.133), channel_id=1, source_target_pairs={{0,24},{2,26},{4,28},{6,30},{8,0},{10,2},{12,4},{14,6},{16,8},{18,... | collective-permute-start | bytes 737288 | tf_op jit(solution)/shard_map/ppermute | solution.py:458
  219.9 30.0 %collective-permute-start.24 = (bf16[480,256]{1,0:T(8,128)(2,1)S(1)}, bf16[480,256]{1,0:T(8,128)(2,1)S(1)}, u32[]{:S(2)}, u32[]{:S(2)}) collective-permute-start(bf16[480,256]{1,0:T(8,128)(2,1)S(1)} %get-tuple-element.134), channel_id=1, source_target_pairs={{0,16},{2,18},{4,20},{6,22},{8,24},{10,26},{12,28},{14,30},{16,0},... | collective-permute-start | bytes 737288 | tf_op jit(solution)/shard_map/ppermute | solution.py:458
  220.8 29.1 %collective-permute-start.25 = (bf16[480,256]{1,0:T(8,128)(2,1)S(1)}, bf16[480,256]{1,0:T(8,128)(2,1)S(1)}, u32[]{:S(2)}, u32[]{:S(2)}) collective-permute-start(bf16[480,256]{1,0:T(8,128)(2,1)S(1)} %get-tuple-element.135), channel_id=1, source_target_pairs={{0,8},{2,10},{4,12},{6,14},{8,16},{10,18},{12,20},{14,22},{16,24},... | collective-permute-start | bytes 737288 | tf_op jit(solution)/shard_map/ppermute | solution.py:458
  231.7 20.0 %collective-permute-start.28 = (bf16[192,384]{1,0:T(8,128)(2,1)S(1)}, bf16[192,384]{1,0:T(8,128)(2,1)S(1)}, u32[]{:S(2)}, u32[]{:S(2)}) collective-permute-start(bf16[192,384]{1,0:T(8,128)(2,1)S(1)} %get-tuple-element.145), channel_id=1, source_target_pairs={{0,8},{2,10},{4,12},{6,14},{8,16},{10,18},{12,20},{14,22},{16,24},... | collective-permute-start | bytes 442376 | tf_op jit(solution)/shard_map/ppermute | solution.py:458
  234.6 18.4 %collective-permute-start.29 = (bf16[192,384]{1,0:T(8,128)(2,1)S(1)}, bf16[192,384]{1,0:T(8,128)(2,1)S(1)}, u32[]{:S(2)}, u32[]{:S(2)}) collective-permute-start(bf16[192,384]{1,0:T(8,128)(2,1)S(1)} %get-tuple-element.146), channel_id=1, source_target_pairs={{0,16},{2,18},{4,20},{6,22},{8,24},{10,26},{12,28},{14,30},{16,0},... | collective-permute-start | bytes 442376 | tf_op jit(solution)/shard_map/ppermute | solution.py:458
  235.7 17.7 %collective-permute-start.30 = (bf16[192,384]{1,0:T(8,128)(2,1)S(1)}, bf16[192,384]{1,0:T(8,128)(2,1)S(1)}, u32[]{:S(2)}, u32[]{:S(2)}) collective-permute-start(bf16[192,384]{1,0:T(8,128)(2,1)S(1)} %get-tuple-element.147), channel_id=1, source_target_pairs={{0,24},{2,26},{4,28},{6,30},{8,0},{10,2},{12,4},{14,6},{16,8},{18,... | collective-permute-start | bytes 442376 | tf_op jit(solution)/shard_map/ppermute | solution.py:458

commit v9 on v8

--- a/solution.py
+++ b/solution.py
@@ -120,7 +120,7 @@
         functools.partial(pack_kernel, n_groups),
         out_shape=shapes,
         in_specs=[smem()] + [pl.BlockSpec(memory_space=pltpu.HBM)] * 4,
-        out_specs=[pl.BlockSpec(memory_space=pltpu.HBM)] * len(shapes),
+        out_specs=[vmem()] * len(shapes),
         scratch_shapes=[pltpu.SemaphoreType.DMA((4 * n_groups,))],
         compiler_params=pltpu.CompilerParams(vmem_limit_bytes=60 * 1024 * 1024),
         name="pack",

time: 255 us -> 194 us (0.76)
  Pallas kernels: 103 us -> 42.7 us
    pallas_call x1, Pallas kernels: 64.5 us -> 3.73 us  [pack(): pl.pallas_call(functools.partial(pack_kernel, n_groups), out_shape=shapes...]
  transfers between devices with their start and end apart: 31 -> 31, of which waited for: 14 -> 14; matrix products, arithmetic and copies ran while one was open for 0% -> 0% of each run, Pallas kernels for 11% -> 14%
where the time goes in v9:
time: 194 us
  waiting for transfers between devices  91.6 us (47%)
  starting transfers between devices  58.4 us (30%)
  Pallas kernels  42.7 us (22%)
    ppermute x12, waiting for transfers between devices, exchange(): lax.ppermute(pieces[s], 'frame', shift_pairs(n_groups, n_tok, sign * s))  48.3 us
    ppermute x12, starting transfers between devices, exchange(): lax.ppermute(pieces[s], 'frame', shift_pairs(n_groups, n_tok, sign * s))  22.2 us
    ppermute x3, starting transfers between devices, local(): ring = lax.ppermute(ring, 'frame', shift_pairs(n_groups, n_tok, 1))  20.6 us
    pallas_call x13, Pallas kernels, whole_call(): pl.pallas_call(body, out_shape=out_shape, in_specs=[smem()] + [vmem()] *...  16 us
    ppermute x4, waiting for transfers between devices, local(): others.append(lax.ppermute(own[s], 'frame', last))  14.3 us
    pallas_call x2, Pallas kernels, backward(): pl.pallas_call(functools.partial(backward_kernel, n_groups, chunk, 1.0 /...  12.8 us
    ppermute x3, waiting for transfers between devices, local(): ring = lax.ppermute(ring, 'frame', shift_pairs(n_groups, n_tok, 1))  10.5 us
    pallas_call x1, Pallas kernels, forward(): pl.pallas_call(functools.partial(forward_kernel, chunk, scale), grid=(hea...  10.2 us
  transfers between devices with their start and end apart: 31, of which 14 were waited for; matrix products, arithmetic and copies ran while one was open for 0% of the time, Pallas kernels for 14%

profile of v9, /device:TPU:0, one launch (start us, length us, event | category | flops | bytes accessed | tf_op | source)
XLA Modules:
  0.0 194.3 jit_solution(11037221720772383948)
XLA Ops:
  0.7 0.6 pad_add_fusion.ids
  1.3 3.7 %pack.1 = (bf16[512,384]{1,0:T(8,128)(2,1)}, bf16[672,384]{1,0:T(8,128)(2,1)}, bf16[672,384]{1,0:T(8,128)(2,1)}, bf16[672,384]{1,0:T(8,128)(2,1)}, bf16[160,384]{1,0:T(8,128)(2,1)}) custom-call(s32[3]{0:T(128)} %pad_add_fusion.ids, bf16[160,1536]{1,0:T(8,128)(2,1)} %q.1, bf16[160,1536]{1,0:T(8,128)(2,1)} %k.1, bf16[160,1536]{1,0:T(8,128)(2,1)} %v.1, ...), custom_call_target="tpu_custom_call" | custom-call | tf_op jit(solution)/shard_map/pack/pallas_call | solution.py:119
  5.0 0.0 copy-start.1
  5.0 3.1 %collective-permute-start = (bf16[672,384]{1,0:T(8,128)(2,1)}, bf16[672,384]{1,0:T(8,128)(2,1)S(1)}, u32[]{:S(2)}, u32[]{:S(2)}) collective-permute-start(bf16[672,384]{1,0:T(8,128)(2,1)} %get-tuple-element.77), channel_id=1, source_target_pairs={{0,8},{2,10},{4,12},{6,14},{8,16},{10,18},{12,20},{14,22},{16,24},... | collective-permute-start | bytes 1548296 | tf_op jit(solution)/shard_map/ppermute | solution.py:458
  8.1 1.6 collective-permute-start.3
  9.7 1.5 collective-permute-start.5
  11.2 1.5 collective-permute-start.4
  12.7 1.2 collective-permute-start.1
  13.9 9.1 %collective-permute-done.refs_0_ = bf16[672,384]{1,0:T(8,128)(2,1)S(1)} collective-permute-done((bf16[672,384]{1,0:T(8,128)(2,1)}, bf16[672,384]{1,0:T(8,128)(2,1)S(1)}, u32[]{:S(2)}, u32[]{:S(2)}) %collective-permute-start) | collective-permute-done | bytes 516128 | tf_op jit(solution)/shard_map/ppermute | solution.py:458
  23.0 0.0 collective-permute-done.4.refs_0_
  23.1 10.5 %collective-permute-done.3.refs_5_.refs_1_ = bf16[160,1536]{1,0:T(8,128)(2,1)S(1)} collective-permute-done((bf16[160,1536]{1,0:T(8,128)(2,1)S(1)}, bf16[160,1536]{1,0:T(8,128)(2,1)S(1)}, u32[]{:S(2)}, u32[]{:S(2)}) %collective-permute-start.3) | collective-permute-done | bytes 491552 | tf_op jit(solution)/shard_map/ppermute | solution.py:489
  33.5 1.8 collective-permute-start.8
  35.3 9.4 %collective-permute-start.6 = (bf16[160,1536]{1,0:T(8,128)(2,1)S(1)}, bf16[160,1536]{1,0:T(8,128)(2,1)S(1)}, u32[]{:S(2)}, u32[]{:S(2)}) collective-permute-start(bf16[160,1536]{1,0:T(8,128)(2,1)S(1)} %collective-permute-done.3.refs_5_.refs_1_), channel_id=1, source_target_pairs={{0,8},{2,10},{4,12},{6,14},{8,16},{10,18},{12,20},{14,22},{16,24},... | collective-permute-start | bytes 1474568 | tf_op jit(solution)/shard_map/ppermute | solution.py:489
  44.7 1.5 collective-permute-start.7
  46.2 19.2 %collective-permute-done.1.refs_1_ = bf16[672,384]{1,0:T(8,128)(2,1)S(1)} collective-permute-done((bf16[672,384]{1,0:T(8,128)(2,1)}, bf16[672,384]{1,0:T(8,128)(2,1)S(1)}, u32[]{:S(2)}, u32[]{:S(2)}) %collective-permute-start.1) | collective-permute-done | bytes 516128 | tf_op jit(solution)/shard_map/ppermute | solution.py:458
  65.5 1.6 collective-permute-start.11
  67.1 9.6 %collective-permute-start.9 = (bf16[160,1536]{1,0:T(8,128)(2,1)S(1)}, bf16[160,1536]{1,0:T(8,128)(2,1)S(1)}, u32[]{:S(2)}, u32[]{:S(2)}) collective-permute-start(bf16[160,1536]{1,0:T(8,128)(2,1)S(1)} %collective-permute-done.6.refs_6_.refs_2_), channel_id=1, source_target_pairs={{0,8},{2,10},{4,12},{6,14},{8,16},{10,18},{12,20},{14,22},{16,24},... | collective-permute-start | bytes 1474568 | tf_op jit(solution)/shard_map/ppermute | solution.py:489
  76.7 1.5 collective-permute-start.10
  78.2 7.9 %collective-permute-done.10.refs_2_ = bf16[512,384]{1,0:T(8,128)(2,1)S(1)} collective-permute-done((bf16[512,384]{1,0:T(8,128)(2,1)S(1)}, bf16[512,384]{1,0:T(8,128)(2,1)S(1)}, u32[]{:S(2)}, u32[]{:S(2)}) %collective-permute-start.10) | collective-permute-done | bytes 393248 | tf_op jit(solution)/shard_map/ppermute | solution.py:486
  86.1 1.5 collective-permute-start.12
  87.6 0.7 stack.18.refs_0_.refs_5_
  88.3 0.0 copy-start.2
  88.3 0.1 collective-permute-start.13
  88.4 6.4 %collective-permute-done.12.refs_3_ = bf16[512,384]{1,0:T(8,128)(2,1)S(1)} collective-permute-done((bf16[512,384]{1,0:T(8,128)(2,1)S(1)}, bf16[512,384]{1,0:T(8,128)(2,1)S(1)}, u32[]{:S(2)}, u32[]{:S(2)}) %collective-permute-start.12) | collective-permute-done | bytes 393248 | tf_op jit(solution)/shard_map/ppermute | solution.py:486
  94.8 0.7 stack.19.refs_1_.refs_6_
  95.5 0.1 collective-permute-start.14
  95.6 0.6 collective-permute-start.15
  96.1 0.6 stack_queries.1.q_in.refs_0_
  96.7 2.2 %collective-permute-done.14.refs_3_.refs_8_ = bf16[2048,384]{1,0:T(8,128)(2,1)S(1)} collective-permute-done((bf16[2048,384]{1,0:T(8,128)(2,1)S(1)}, bf16[2048,384]{1,0:T(8,128)(2,1)S(1)}, u32[]{:S(2)}, u32[]{:S(2)}) %collective-permute-start.14) | collective-permute-done | bytes 1572896 | tf_op jit(solution)/shard_map/ppermute | solution.py:497
  99.0 10.2 %forward.1 = (bf16[3,2560,640]{2,1,0:T(8,128)(2,1)S(1)}, bf16[640,384]{1,0:T(8,128)(2,1)S(1)}, f32[3,1,640]{2,1,0:T(1,128)S(1)}) custom-call(bf16[640,384]{1,0:T(8,128)(2,1)S(1)} %stack_queries.1.q_in.refs_0_, bf16[2048,384]{1,0:T(8,128)(2,1)S(1)} %stack.18.refs_0_.refs_5_, bf16[2048,384]{1,0:T(8,128)(2,1)S(1)} %stack.19.refs_1_.refs_6_, ...), custom_call_target="tpu_custom_call" | custom-call | flops 2516582400 | bytes 9830400 | tf_op jit(solution)/shard_map/forward/pallas_call | solution.py:200
  109.2 3.0 %attn_gradient.1.refs_4_ = bf16[640,384]{1,0:T(8,128)(2,1)S(1)} custom-call(s32[3]{0:T(128)S(1)} %copy-done.3, bf16[2048,384]{1,0:T(8,128)(2,1)S(1)} %stack.18.refs_0_.refs_5_, bf16[2048,384]{1,0:T(8,128)(2,1)S(1)} %stack.19.refs_1_.refs_6_, bf16[2048,384]{1,0:T(8,128)(2,1)S(1)} %collective-permute-done.13.refs_2_.refs_7_, ...), custom_call_target="tpu_custom_call" | custom-call | flops 245760 | bytes 491520 | tf_op jit(solution)/shard_map/attn_gradient/pallas_call | solution.py:75
  112.2 3.9 %backward.2 = (bf16[160,128]{1,0:T(8,128)(2,1)S(1)}, bf16[160,128]{1,0:T(8,128)(2,1)S(1)}, bf16[160,128]{1,0:T(8,128)(2,1)S(1)}, bf16[160,128]{1,0:T(8,128)(2,1)...) custom-call(bf16[640,384]{1,0:T(8,128)(2,1)S(1)} %stack_queries.1.q_in.refs_0_, ...), custom_call_target="tpu_custom_call" | custom-call | flops 81920 | bytes 163840 | tf_op jit(solution)/shard_map/backward/pallas_call | solution.py:264
  116.1 0.2 collective-permute-start.16
  116.3 2.0 %collective-permute-done.16.other = bf16[2560,128]{1,0:T(8,128)(2,1)S(1)} collective-permute-done((bf16[2560,128]{1,0:T(8,128)(2,1)S(1)}, bf16[2560,128]{1,0:T(8,128)(2,1)S(1)}, u32[]{:S(2)}, u32[]{:S(2)}) %collective-permute-start.16) | collective-permute-done | bytes 655392 | tf_op jit(solution)/shard_map/ppermute | solution.py:389
  118.3 0.7 add_parts.4
  119.0 1.6 collective-permute-start.17
  120.5 8.8 %backward.3 = (bf16[160,256]{1,0:T(8,128)(2,1)S(1)}, bf16[160,256]{1,0:T(8,128)(2,1)S(1)}, bf16[160,256]{1,0:T(8,128)(2,1)S(1)}, bf16[160,256]{1,0:T(8,128)(2,1)...) custom-call(bf16[640,384]{1,0:T(8,128)(2,1)S(1)} %stack_queries.1.q_in.refs_0_, ...), custom_call_target="tpu_custom_call" | custom-call | flops 81920 | bytes 163840 | tf_op jit(solution)/shard_map/backward/pallas_call | solution.py:264
  129.4 0.1 collective-permute-start.18
  129.5 3.0 %collective-permute-done.18.other = bf16[2560,256]{1,0:T(8,128)(2,1)S(1)} collective-permute-done((bf16[2560,256]{1,0:T(8,128)(2,1)S(1)}, bf16[2560,256]{1,0:T(8,128)(2,1)S(1)}, u32[]{:S(2)}, u32[]{:S(2)}) %collective-permute-start.18) | collective-permute-done | bytes 1310752 | tf_op jit(solution)/shard_map/ppermute | solution.py:389
  132.5 0.8 add_parts.5
  133.3 0.9 collective-permute-start.19
  134.2 0.6 finish.2
  134.9 4.4 %collective-permute-start.20 = (bf16[480,128]{1,0:T(8,128)(2,1)S(1)}, bf16[480,128]{1,0:T(8,128)(2,1)S(1)}, u32[]{:S(2)}, u32[]{:S(2)}) collective-permute-start(bf16[480,128]{1,0:T(8,128)(2,1)S(1)} %get-tuple-element.117), channel_id=1, source_target_pairs={{0,24},{2,26},{4,28},{6,30},{8,0},{10,2},{12,4},{14,6},{16,8},{18,... | collective-permute-start | bytes 368648 | tf_op jit(solution)/shard_map/ppermute | solution.py:458
  139.3 0.9 collective-permute-start.21
  140.2 1.1 collective-permute-start.22
  141.3 3.2 %proj_gradient.1 = (bf16[1536,384]{1,0:T(8,128)(2,1)S(1)}, bf16[1536,384]{1,0:T(8,128)(2,1)S(1)}) custom-call(s32[3]{0:T(128)S(1)} %copy-done.3, bf16[640,384]{1,0:T(8,128)(2,1)S(1)} %get-tuple-element.120.refs_2_.attn, bf16[160,1536]{1,0:T(8,128)(2,1)S(1)} %copy-done, bf16[160,1536]{1,0:T(8,128)(2,1)S(1)} %collective-permute-done.3.refs_5_.refs_1_, ...), custom_call_target="tpu_custom_call" | custom-call | flops 245760 | bytes 491520 | tf_op jit(solution)/shard_map/proj_gradient/pallas_call | solution.py:75
  144.6 6.6 %collective-permute-done.21.refs_2_ = bf16[480,128]{1,0:T(8,128)(2,1)S(1)} collective-permute-done((bf16[480,128]{1,0:T(8,128)(2,1)S(1)}, bf16[480,128]{1,0:T(8,128)(2,1)S(1)}, u32[]{:S(2)}, u32[]{:S(2)}) %collective-permute-start.21) | collective-permute-done | bytes 122912 | tf_op jit(solution)/shard_map/ppermute | solution.py:458
  151.2 0.7 finish.3
  151.9 2.1 %collective-permute-done.26.other = bf16[1536,384]{1,0:T(8,128)(2,1)S(1)} collective-permute-done((bf16[1536,384]{1,0:T(8,128)(2,1)S(1)}, bf16[1536,384]{1,0:T(8,128)(2,1)S(1)}, u32[]{:S(2)}, u32[]{:S(2)}) %collective-permute-start.26) | collective-permute-done | bytes 1179680 | tf_op jit(solution)/shard_map/ppermute | solution.py:389
  154.0 0.8 add_parts.6
  154.9 1.2 collective-permute-start.27
  156.1 3.0 %collective-permute-start.23 = (bf16[480,256]{1,0:T(8,128)(2,1)S(1)}, bf16[480,256]{1,0:T(8,128)(2,1)S(1)}, u32[]{:S(2)}, u32[]{:S(2)}) collective-permute-start(bf16[480,256]{1,0:T(8,128)(2,1)S(1)} %get-tuple-element.133), channel_id=1, source_target_pairs={{0,24},{2,26},{4,28},{6,30},{8,0},{10,2},{12,4},{14,6},{16,8},{18,... | collective-permute-start | bytes 737288 | tf_op jit(solution)/shard_map/ppermute | solution.py:458
  159.2 0.9 collective-permute-start.24
  160.1 1.1 collective-permute-start.25
  161.2 9.1 %collective-permute-done.27.other = bf16[768,384]{1,0:T(8,128)(2,1)S(1)} collective-permute-done((bf16[768,384]{1,0:T(8,128)(2,1)S(1)}, bf16[768,384]{1,0:T(8,128)(2,1)S(1)}, u32[]{:S(2)}, u32[]{:S(2)}) %collective-permute-start.27) | collective-permute-done | bytes 589856 | tf_op jit(solution)/shard_map/ppermute | solution.py:507
  170.3 0.7 add_parts.7
  171.0 2.9 %collective-permute-start.28 = (bf16[192,384]{1,0:T(8,128)(2,1)S(1)}, bf16[192,384]{1,0:T(8,128)(2,1)S(1)}, u32[]{:S(2)}, u32[]{:S(2)}) collective-permute-start(bf16[192,384]{1,0:T(8,128)(2,1)S(1)} %get-tuple-element.145), channel_id=1, source_target_pairs={{0,8},{2,10},{4,12},{6,14},{8,16},{10,18},{12,20},{14,22},{16,24},... | collective-permute-start | bytes 442376 | tf_op jit(solution)/shard_map/ppermute | solution.py:458
  173.9 1.1 collective-permute-start.29
  175.0 2.4 %collective-permute-start.30 = (bf16[192,384]{1,0:T(8,128)(2,1)S(1)}, bf16[192,384]{1,0:T(8,128)(2,1)S(1)}, u32[]{:S(2)}, u32[]{:S(2)}) collective-permute-start(bf16[192,384]{1,0:T(8,128)(2,1)S(1)} %get-tuple-element.147), channel_id=1, source_target_pairs={{0,24},{2,26},{4,28},{6,30},{8,0},{10,2},{12,4},{14,6},{16,8},{18,... | collective-permute-start | bytes 442376 | tf_op jit(solution)/shard_map/ppermute | solution.py:458
  177.3 11.8 %collective-permute-done.24.refs_6_ = bf16[480,256]{1,0:T(8,128)(2,1)S(1)} collective-permute-done((bf16[480,256]{1,0:T(8,128)(2,1)S(1)}, bf16[480,256]{1,0:T(8,128)(2,1)S(1)}, u32[]{:S(2)}, u32[]{:S(2)}) %collective-permute-start.24) | collective-permute-done | bytes 245792 | tf_op jit(solution)/shard_map/ppermute | solution.py:458
  189.1 1.8 unpack.1
  191.0 1.3 collective-permute-done.29.refs_2_
  192.2 0.4 collective-permute-done.30.refs_3_
  192.6 1.7 join.1
  (27 shorter events, 0.2 us)
Async XLA Ops:
  0.6 7.5 %copy-start = (bf16[160,1536]{1,0:T(8,128)(2,1)S(1)}, bf16[160,1536]{1,0:T(8,128)(2,1)}, u32[]{:S(2)}) copy-start(bf16[160,1536]{1,0:T(8,128)(2,1)} %refs_0_) | copy-start | bytes 1474564
  5.0 82.6 %copy-start.1 = (bf16[512,384]{1,0:T(8,128)(2,1)S(1)}, bf16[512,384]{1,0:T(8,128)(2,1)}, u32[]{:S(2)}) copy-start(bf16[512,384]{1,0:T(8,128)(2,1)} %get-tuple-element.80.refs_0_) | copy-start | bytes 1179652
  5.0 82.6 %copy-start.3 = (s32[3]{0:T(128)S(1)}, s32[3]{0:T(128)}, u32[]{:S(2)}) copy-start(s32[3]{0:T(128)} %pad_add_fusion.ids) | copy-start | bytes 40
  5.0 18.0 %collective-permute-start = (bf16[672,384]{1,0:T(8,128)(2,1)}, bf16[672,384]{1,0:T(8,128)(2,1)S(1)}, u32[]{:S(2)}, u32[]{:S(2)}) collective-permute-start(bf16[672,384]{1,0:T(8,128)(2,1)} %get-tuple-element.77), channel_id=1, source_target_pairs={{0,8},{2,10},{4,12},{6,14},{8,16},{10,18},{12,20},{14,22},{16,24},... | collective-permute-start | bytes 1548296 | tf_op jit(solution)/shard_map/ppermute | solution.py:458
  8.1 25.4 %collective-permute-start.3 = (bf16[160,1536]{1,0:T(8,128)(2,1)S(1)}, bf16[160,1536]{1,0:T(8,128)(2,1)S(1)}, u32[]{:S(2)}, u32[]{:S(2)}) collective-permute-start(bf16[160,1536]{1,0:T(8,128)(2,1)S(1)} %copy-done), channel_id=1, source_target_pairs={{0,8},{2,10},{4,12},{6,14},{8,16},{10,18},{12,20},{14,22},{16,24},... | collective-permute-start | bytes 1474568 | tf_op jit(solution)/shard_map/ppermute | solution.py:489
  9.7 23.9 %collective-permute-start.5 = (bf16[160,1536]{1,0:T(8,128)(2,1)S(1)}, bf16[160,1536]{1,0:T(8,128)(2,1)S(1)}, u32[]{:S(2)}, u32[]{:S(2)}) collective-permute-start(bf16[160,1536]{1,0:T(8,128)(2,1)S(1)} %copy-done), channel_id=1, source_target_pairs={{0,1},{1,0},{2,3},{3,2},{4,5},{5,4},{6,7},{7,6},{8,9},{9,8},{10,11... | collective-permute-start | bytes 1474568 | tf_op jit(solution)/shard_map/ppermute | solution.py:49
  11.2 11.9 %collective-permute-start.4 = (bf16[512,384]{1,0:T(8,128)(2,1)}, bf16[512,384]{1,0:T(8,128)(2,1)S(1)}, u32[]{:S(2)}, u32[]{:S(2)}) collective-permute-start(bf16[512,384]{1,0:T(8,128)(2,1)} %get-tuple-element.80.refs_0_), channel_id=1, source_target_pairs={{0,4},{2,6},{4,0},{6,2},{8,12},{10,14},{12,8},{14,10},{16,20},{18,... | collective-permute-start | bytes 1179656 | tf_op jit(solution)/shard_map/ppermute | solution.py:486
  12.7 52.7 %collective-permute-start.1 = (bf16[672,384]{1,0:T(8,128)(2,1)}, bf16[672,384]{1,0:T(8,128)(2,1)S(1)}, u32[]{:S(2)}, u32[]{:S(2)}) collective-permute-start(bf16[672,384]{1,0:T(8,128)(2,1)} %get-tuple-element.78), channel_id=1, source_target_pairs={{0,16},{2,18},{4,20},{6,22},{8,24},{10,26},{12,28},{14,30},{16,0},... | collective-permute-start | bytes 1548296 | tf_op jit(solution)/shard_map/ppermute | solution.py:458
  33.5 31.9 %collective-permute-start.8 = (bf16[160,1536]{1,0:T(8,128)(2,1)S(1)}, bf16[160,1536]{1,0:T(8,128)(2,1)S(1)}, u32[]{:S(2)}, u32[]{:S(2)}) collective-permute-start(bf16[160,1536]{1,0:T(8,128)(2,1)S(1)} %collective-permute-done.3.refs_5_.refs_1_), channel_id=1, source_target_pairs={{0,1},{1,0},{2,3},{3,2},{4,5},{5,4},{6,7},{7,6},{8,9},{9,8},{10,11... | collective-permute-start | bytes 1474568 | tf_op jit(solution)/shard_map/ppermute | solution.py:49
  35.3 30.2 %collective-permute-start.6 = (bf16[160,1536]{1,0:T(8,128)(2,1)S(1)}, bf16[160,1536]{1,0:T(8,128)(2,1)S(1)}, u32[]{:S(2)}, u32[]{:S(2)}) collective-permute-start(bf16[160,1536]{1,0:T(8,128)(2,1)S(1)} %collective-permute-done.3.refs_5_.refs_1_), channel_id=1, source_target_pairs={{0,8},{2,10},{4,12},{6,14},{8,16},{10,18},{12,20},{14,22},{16,24},... | collective-permute-start | bytes 1474568 | tf_op jit(solution)/shard_map/ppermute | solution.py:489
  44.7 20.7 %collective-permute-start.7 = (bf16[512,384]{1,0:T(8,128)(2,1)S(1)}, bf16[512,384]{1,0:T(8,128)(2,1)S(1)}, u32[]{:S(2)}, u32[]{:S(2)}) collective-permute-start(bf16[512,384]{1,0:T(8,128)(2,1)S(1)} %slice.12.refs_1_), channel_id=1, source_target_pairs={{0,4},{2,6},{4,0},{6,2},{8,12},{10,14},{12,8},{14,10},{16,20},{18,... | collective-permute-start | bytes 1179656 | tf_op jit(solution)/shard_map/ppermute | solution.py:486
  46.2 32.0 %collective-permute-start.2 = (bf16[672,384]{1,0:T(8,128)(2,1)}, bf16[672,384]{1,0:T(8,128)(2,1)S(1)}, u32[]{:S(2)}, u32[]{:S(2)}) collective-permute-start(bf16[672,384]{1,0:T(8,128)(2,1)} %get-tuple-element.79), channel_id=1, source_target_pairs={{0,24},{2,26},{4,28},{6,30},{8,0},{10,2},{12,4},{14,6},{16,8},{18,... | collective-permute-start | bytes 1548296 | tf_op jit(solution)/shard_map/ppermute | solution.py:458
  65.5 20.6 %collective-permute-start.11 = (bf16[160,1536]{1,0:T(8,128)(2,1)S(1)}, bf16[160,1536]{1,0:T(8,128)(2,1)S(1)}, u32[]{:S(2)}, u32[]{:S(2)}) collective-permute-start(bf16[160,1536]{1,0:T(8,128)(2,1)S(1)} %collective-permute-done.6.refs_6_.refs_2_), channel_id=1, source_target_pairs={{0,1},{1,0},{2,3},{3,2},{4,5},{5,4},{6,7},{7,6},{8,9},{9,8},{10,11... | collective-permute-start | bytes 1474568 | tf_op jit(solution)/shard_map/ppermute | solution.py:49
  67.1 19.1 %collective-permute-start.9 = (bf16[160,1536]{1,0:T(8,128)(2,1)S(1)}, bf16[160,1536]{1,0:T(8,128)(2,1)S(1)}, u32[]{:S(2)}, u32[]{:S(2)}) collective-permute-start(bf16[160,1536]{1,0:T(8,128)(2,1)S(1)} %collective-permute-done.6.refs_6_.refs_2_), channel_id=1, source_target_pairs={{0,8},{2,10},{4,12},{6,14},{8,16},{10,18},{12,20},{14,22},{16,24},... | collective-permute-start | bytes 1474568 | tf_op jit(solution)/shard_map/ppermute | solution.py:489
  76.7 9.4 %collective-permute-start.10 = (bf16[512,384]{1,0:T(8,128)(2,1)S(1)}, bf16[512,384]{1,0:T(8,128)(2,1)S(1)}, u32[]{:S(2)}, u32[]{:S(2)}) collective-permute-start(bf16[512,384]{1,0:T(8,128)(2,1)S(1)} %slice.13.refs_2_), channel_id=1, source_target_pairs={{0,4},{2,6},{4,0},{6,2},{8,12},{10,14},{12,8},{14,10},{16,20},{18,... | collective-permute-start | bytes 1179656 | tf_op jit(solution)/shard_map/ppermute | solution.py:486
  86.1 8.7 %collective-permute-start.12 = (bf16[512,384]{1,0:T(8,128)(2,1)S(1)}, bf16[512,384]{1,0:T(8,128)(2,1)S(1)}, u32[]{:S(2)}, u32[]{:S(2)}) collective-permute-start(bf16[512,384]{1,0:T(8,128)(2,1)S(1)} %slice.14.refs_3_), channel_id=1, source_target_pairs={{0,4},{2,6},{4,0},{6,2},{8,12},{10,14},{12,8},{14,10},{16,20},{18,... | collective-permute-start | bytes 1179656 | tf_op jit(solution)/shard_map/ppermute | solution.py:486
  88.3 7.8 %copy-start.2 = (bf16[160,384]{1,0:T(8,128)(2,1)S(1)}, bf16[160,384]{1,0:T(8,128)(2,1)}, u32[]{:S(2)}) copy-start(bf16[160,384]{1,0:T(8,128)(2,1)} %get-tuple-element.76.own) | copy-start | bytes 368644
  88.3 8.4 %collective-permute-start.13 = (bf16[2048,384]{1,0:T(8,128)(2,1)S(1)}, bf16[2048,384]{1,0:T(8,128)(2,1)S(1)}, u32[]{:S(2)}, u32[]{:S(2)}) collective-permute-start(bf16[2048,384]{1,0:T(8,128)(2,1)S(1)} %stack.18.refs_0_.refs_5_), channel_id=1, source_target_pairs={{0,2},{2,0},{4,6},{6,4},{8,10},{10,8},{12,14},{14,12},{16,18},{18,... | collective-permute-start | bytes 4718600 | tf_op jit(solution)/shard_map/ppermute | solution.py:497
  95.5 3.5 %collective-permute-start.14 = (bf16[2048,384]{1,0:T(8,128)(2,1)S(1)}, bf16[2048,384]{1,0:T(8,128)(2,1)S(1)}, u32[]{:S(2)}, u32[]{:S(2)}) collective-permute-start(bf16[2048,384]{1,0:T(8,128)(2,1)S(1)} %stack.19.refs_1_.refs_6_), channel_id=1, source_target_pairs={{0,2},{2,0},{4,6},{6,4},{8,10},{10,8},{12,14},{14,12},{16,18},{18,... | collective-permute-start | bytes 4718600 | tf_op jit(solution)/shard_map/ppermute | solution.py:497
  95.6 13.6 %collective-permute-start.15 = (bf16[160,1536]{1,0:T(8,128)(2,1)S(1)}, bf16[160,1536]{1,0:T(8,128)(2,1)S(1)}, u32[]{:S(2)}, u32[]{:S(2)}) collective-permute-start(bf16[160,1536]{1,0:T(8,128)(2,1)S(1)} %collective-permute-done.9.refs_7_.refs_3_), channel_id=1, source_target_pairs={{0,1},{1,0},{2,3},{3,2},{4,5},{5,4},{6,7},{7,6},{8,9},{9,8},{10,11... | collective-permute-start | bytes 1474568 | tf_op jit(solution)/shard_map/ppermute | solution.py:49
  116.1 2.2 %collective-permute-start.16 = (bf16[2560,128]{1,0:T(8,128)(2,1)S(1)}, bf16[2560,128]{1,0:T(8,128)(2,1)S(1)}, u32[]{:S(2)}, u32[]{:S(2)}) collective-permute-start(bf16[2560,128]{1,0:T(8,128)(2,1)S(1)} %get-tuple-element.100), channel_id=1, source_target_pairs={{0,2},{2,0},{4,6},{6,4},{8,10},{10,8},{12,14},{14,12},{16,18},{18,... | collective-permute-start | bytes 1966088 | tf_op jit(solution)/shard_map/ppermute | solution.py:389
  119.0 10.4 %collective-permute-start.17 = (bf16[1280,128]{1,0:T(8,128)(2,1)S(1)}, bf16[1280,128]{1,0:T(8,128)(2,1)S(1)}, u32[]{:S(2)}, u32[]{:S(2)}) collective-permute-start(bf16[1280,128]{1,0:T(8,128)(2,1)S(1)} %get-tuple-element.104), channel_id=1, source_target_pairs={{0,4},{2,6},{4,0},{6,2},{8,12},{10,14},{12,8},{14,10},{16,20},{18,... | collective-permute-start | bytes 983048 | tf_op jit(solution)/shard_map/ppermute | solution.py:507
  129.4 3.1 %collective-permute-start.18 = (bf16[2560,256]{1,0:T(8,128)(2,1)S(1)}, bf16[2560,256]{1,0:T(8,128)(2,1)S(1)}, u32[]{:S(2)}, u32[]{:S(2)}) collective-permute-start(bf16[2560,256]{1,0:T(8,128)(2,1)S(1)} %get-tuple-element.115), channel_id=1, source_target_pairs={{0,2},{2,0},{4,6},{6,4},{8,10},{10,8},{12,14},{14,12},{16,18},{18,... | collective-permute-start | bytes 3932168 | tf_op jit(solution)/shard_map/ppermute | solution.py:389
  133.3 17.9 %collective-permute-start.19 = (bf16[1280,256]{1,0:T(8,128)(2,1)S(1)}, bf16[1280,256]{1,0:T(8,128)(2,1)S(1)}, u32[]{:S(2)}, u32[]{:S(2)}) collective-permute-start(bf16[1280,256]{1,0:T(8,128)(2,1)S(1)} %get-tuple-element.116), channel_id=1, source_target_pairs={{0,4},{2,6},{4,0},{6,2},{8,12},{10,14},{12,8},{14,10},{16,20},{18,... | collective-permute-start | bytes 1966088 | tf_op jit(solution)/shard_map/ppermute | solution.py:507
  134.9 9.7 %collective-permute-start.20 = (bf16[480,128]{1,0:T(8,128)(2,1)S(1)}, bf16[480,128]{1,0:T(8,128)(2,1)S(1)}, u32[]{:S(2)}, u32[]{:S(2)}) collective-permute-start(bf16[480,128]{1,0:T(8,128)(2,1)S(1)} %get-tuple-element.117), channel_id=1, source_target_pairs={{0,24},{2,26},{4,28},{6,30},{8,0},{10,2},{12,4},{14,6},{16,8},{18,... | collective-permute-start | bytes 368648 | tf_op jit(solution)/shard_map/ppermute | solution.py:458
  139.3 11.9 %collective-permute-start.21 = (bf16[480,128]{1,0:T(8,128)(2,1)S(1)}, bf16[480,128]{1,0:T(8,128)(2,1)S(1)}, u32[]{:S(2)}, u32[]{:S(2)}) collective-permute-start(bf16[480,128]{1,0:T(8,128)(2,1)S(1)} %get-tuple-element.118), channel_id=1, source_target_pairs={{0,16},{2,18},{4,20},{6,22},{8,24},{10,26},{12,28},{14,30},{16,0},... | collective-permute-start | bytes 368648 | tf_op jit(solution)/shard_map/ppermute | solution.py:458
  140.2 11.0 %collective-permute-start.22 = (bf16[480,128]{1,0:T(8,128)(2,1)S(1)}, bf16[480,128]{1,0:T(8,128)(2,1)S(1)}, u32[]{:S(2)}, u32[]{:S(2)}) collective-permute-start(bf16[480,128]{1,0:T(8,128)(2,1)S(1)} %get-tuple-element.119), channel_id=1, source_target_pairs={{0,8},{2,10},{4,12},{6,14},{8,16},{10,18},{12,20},{14,22},{16,24},... | collective-permute-start | bytes 368648 | tf_op jit(solution)/shard_map/ppermute | solution.py:458
  151.2 2.9 %collective-permute-start.26 = (bf16[1536,384]{1,0:T(8,128)(2,1)S(1)}, bf16[1536,384]{1,0:T(8,128)(2,1)S(1)}, u32[]{:S(2)}, u32[]{:S(2)}) collective-permute-start(bf16[1536,384]{1,0:T(8,128)(2,1)S(1)} %get-tuple-element.140), channel_id=1, source_target_pairs={{0,2},{2,0},{4,6},{6,4},{8,10},{10,8},{12,14},{14,12},{16,18},{18,... | collective-permute-start | bytes 3538952 | tf_op jit(solution)/shard_map/ppermute | solution.py:389
  154.9 15.4 %collective-permute-start.27 = (bf16[768,384]{1,0:T(8,128)(2,1)S(1)}, bf16[768,384]{1,0:T(8,128)(2,1)S(1)}, u32[]{:S(2)}, u32[]{:S(2)}) collective-permute-start(bf16[768,384]{1,0:T(8,128)(2,1)S(1)} %get-tuple-element.143), channel_id=1, source_target_pairs={{0,4},{2,6},{4,0},{6,2},{8,12},{10,14},{12,8},{14,10},{16,20},{18,... | collective-permute-start | bytes 1769480 | tf_op jit(solution)/shard_map/ppermute | solution.py:507
  156.1 18.9 %collective-permute-start.23 = (bf16[480,256]{1,0:T(8,128)(2,1)S(1)}, bf16[480,256]{1,0:T(8,128)(2,1)S(1)}, u32[]{:S(2)}, u32[]{:S(2)}) collective-permute-start(bf16[480,256]{1,0:T(8,128)(2,1)S(1)} %get-tuple-element.133), channel_id=1, source_target_pairs={{0,24},{2,26},{4,28},{6,30},{8,0},{10,2},{12,4},{14,6},{16,8},{18,... | collective-permute-start | bytes 737288 | tf_op jit(solution)/shard_map/ppermute | solution.py:458
  159.2 30.0 %collective-permute-start.24 = (bf16[480,256]{1,0:T(8,128)(2,1)S(1)}, bf16[480,256]{1,0:T(8,128)(2,1)S(1)}, u32[]{:S(2)}, u32[]{:S(2)}) collective-permute-start(bf16[480,256]{1,0:T(8,128)(2,1)S(1)} %get-tuple-element.134), channel_id=1, source_target_pairs={{0,16},{2,18},{4,20},{6,22},{8,24},{10,26},{12,28},{14,30},{16,0},... | collective-permute-start | bytes 737288 | tf_op jit(solution)/shard_map/ppermute | solution.py:458
  160.1 29.1 %collective-permute-start.25 = (bf16[480,256]{1,0:T(8,128)(2,1)S(1)}, bf16[480,256]{1,0:T(8,128)(2,1)S(1)}, u32[]{:S(2)}, u32[]{:S(2)}) collective-permute-start(bf16[480,256]{1,0:T(8,128)(2,1)S(1)} %get-tuple-element.135), channel_id=1, source_target_pairs={{0,8},{2,10},{4,12},{6,14},{8,16},{10,18},{12,20},{14,22},{16,24},... | collective-permute-start | bytes 737288 | tf_op jit(solution)/shard_map/ppermute | solution.py:458
  171.0 20.0 %collective-permute-start.28 = (bf16[192,384]{1,0:T(8,128)(2,1)S(1)}, bf16[192,384]{1,0:T(8,128)(2,1)S(1)}, u32[]{:S(2)}, u32[]{:S(2)}) collective-permute-start(bf16[192,384]{1,0:T(8,128)(2,1)S(1)} %get-tuple-element.145), channel_id=1, source_target_pairs={{0,8},{2,10},{4,12},{6,14},{8,16},{10,18},{12,20},{14,22},{16,24},... | collective-permute-start | bytes 442376 | tf_op jit(solution)/shard_map/ppermute | solution.py:458
  173.9 18.4 %collective-permute-start.29 = (bf16[192,384]{1,0:T(8,128)(2,1)S(1)}, bf16[192,384]{1,0:T(8,128)(2,1)S(1)}, u32[]{:S(2)}, u32[]{:S(2)}) collective-permute-start(bf16[192,384]{1,0:T(8,128)(2,1)S(1)} %get-tuple-element.146), channel_id=1, source_target_pairs={{0,16},{2,18},{4,20},{6,22},{8,24},{10,26},{12,28},{14,30},{16,0},... | collective-permute-start | bytes 442376 | tf_op jit(solution)/shard_map/ppermute | solution.py:458
  175.0 17.7 %collective-permute-start.30 = (bf16[192,384]{1,0:T(8,128)(2,1)S(1)}, bf16[192,384]{1,0:T(8,128)(2,1)S(1)}, u32[]{:S(2)}, u32[]{:S(2)}) collective-permute-start(bf16[192,384]{1,0:T(8,128)(2,1)S(1)} %get-tuple-element.147), channel_id=1, source_target_pairs={{0,24},{2,26},{4,28},{6,30},{8,0},{10,2},{12,4},{14,6},{16,8},{18,... | collective-permute-start | bytes 442376 | tf_op jit(solution)/shard_map/ppermute | solution.py:458

commit v10 on v9

--- a/solution.py
+++ b/solution.py
@@ -295,16 +295,20 @@
 
 def tokens_of(ids, tokens, grads, n_groups, n_space):
     rows, part = grads[0].shape
+    count = len(grads) // n_space
     for r in range(n_space):
-        for s in range(n_groups):
-            tokens[s * rows : (s + 1) * rows, :] = grads[r * n_groups + s][...]
+        tokens[:rows, :] = grads[r * count][...]
+        for s in range(1, n_groups):
+            above, below = grads[r * count + 2 * s - 1 : r * count + 2 * s + 1]
+            here = slice(s * rows, (s + 1) * rows)
+            tokens[here, :] = jnp.where(ids[0] >= s, above[...], below[...])
         start = jnp.bitwise_xor(ids[2], relative_of(r, bits_of(n_space))) * part
         yield tokens[...], pl.ds(aligned(start, 16), part)
 
 
 def attn_kernel(n_groups, n_tok, n_space, ids, *refs):
-    blocks, grads = refs[:n_tok], refs[n_tok : n_tok + n_groups * n_space]
-    grad_attn, weight, tokens = refs[n_tok + n_groups * n_space :]
+    blocks, grads = refs[:n_tok], refs[n_tok:-3]
+    grad_attn, weight, tokens = refs[-3:]
     depth = weight.shape[0] // (n_groups * n_tok)
     first = blocks[0].shape[0] - n_groups * depth
     for j in range(n_tok):
@@ -342,7 +346,7 @@
 
 
 def proj_kernel(n_groups, n_tok, n_space, ids, attn, *refs):
-    grads, (kept, sent, whole, tokens) = refs[: n_groups * n_space], refs[n_groups * n_space :]
+    grads, (kept, sent, whole, tokens) = refs[:-4], refs[-4:]
     depth = whole.shape[0] // (n_groups * n_tok)
     for block, here in tokens_of(ids, tokens, grads, n_groups, n_space):
         whole[here, :] = dot(block, attn[...], ((0,), (0,))).astype(BF16)
@@ -478,17 +482,40 @@
     tie = lax.optimization_barrier
     last = xor_pairs(n_frame, tok_bits[-1])
 
+    def across_y(piece, first, end):
+        groups = range(first * n_tok, end * n_tok)
+        blocks = [piece]
+        for bit in reversed(space_bits):
+            pairs = [(f * n_space + y, f * n_space + (y ^ bit)) for f in groups for y in range(n_space)]
+            blocks = blocks + [lax.ppermute(b, ("frame", "space"), pairs) for b in blocks]
+        return blocks
+
+    def along_z(piece, first, end, step):
+        groups = range(first * n_tok, end * n_tok)
+        return lax.ppermute(piece, "frame", [(f, f + step * n_tok) for f in groups])
+
     *pieces, own_q = pack(ids, queries, keys, values, proj_weight.T, n_groups)
     pieces = exchange(pieces, n_groups, n_tok, 1)
     q_pieces = pieces[1:]
-    own, others, ring, across = [pieces[0]], [], grad_out, []
+    own, others = [pieces[0]], []
+    up, down, across = [grad_out], [grad_out], []
     for s in range(n_groups):
         others.append(lax.ppermute(own[s], "frame", last))
-        across.append(gather_blocks(ring, "space", n_space, space_bits))
+        if s == 0:
+            arrived = across_y(grad_out, 0, n_groups)
+        else:
+            arrived = across_y(up[s], s, n_groups) + across_y(down[s], 0, n_groups - s)
+        across.append(arrived)
         if s + 1 < n_groups:
-            ring = lax.ppermute(ring, "frame", shift_pairs(n_groups, n_tok, 1))
-            step = (ring, pieces[s + 1][:shared], others[s], *across[s])
-            ring, piece, others[s], *across[s] = tie(step)
+            going_up = along_z(up[s], s, n_groups - 1, 1)
+            going_down = along_z(down[s], 1, n_groups - s, -1)
+            step = (going_up, going_down, pieces[s + 1][:shared], others[s])
+            if s + 2 < n_groups:
+                step = (*step, *arrived)
+            going_up, going_down, piece, others[s], *arrived = tie(step)
+            across[s] = arrived or across[s]
+            up.append(going_up)
+            down.append(going_down)
             own.append(piece)
 
     q = stack_queries(ids, own_q, q_pieces)
@@ -497,7 +524,11 @@
         blocks = blocks + [lax.ppermute(b, "frame", xor_pairs(n_frame, bit)) for b in blocks]
     part = n_groups * rows
     probs, out, inverse = forward(q, blocks, part)
-    grads = [across[s][r] for r in range(n_space) for s in range(n_groups)]
+    grads = []
+    for r in range(n_space):
+        grads.append(across[0][r])
+        for s in range(1, n_groups):
+            grads += [across[s][r], across[n_groups - s][n_space + r]]
     grad_attn = attn_gradient(ids, blocks, grads, depth, n_groups, n_tok, n_space)
 
     def attention_halves(head, count, q):

time: 194 us -> 207 us (1.067); the launches traced: 194 us -> 205 us
  waiting for transfers between devices: 91.6 us -> 113 us
  starting transfers between devices: 58.4 us -> 47.1 us
    ppermute x4, waiting for transfers between devices: 14.3 us -> 24.2 us  [local(): others.append(lax.ppermute(own[s], 'frame', last))]
    ppermute x12, starting transfers between devices: 22.2 us -> 14.2 us  [exchange(): lax.ppermute(pieces[s], 'frame', shift_pairs(n_groups, n_tok, sign * s))]
    ppermute x3, waiting for transfers between devices: 9.12 us -> 15.9 us  [across_x(): return lax.ppermute(piece, 'frame', last)]
    ppermute x7 -> x13, waiting for transfers between devices: 10.5 us -> 16.9 us  [the longest x6 8.51 us: along_z(): return lax.ppermute(piece, 'frame', [(f, f + step * n_tok) for f in groups])]
    ppermute x7 -> x13, starting transfers between devices: 26.1 us -> 22.9 us  [the longest x7 13.1 us: across_y(): lax.ppermute(b, ('frame', 'space'), pairs)]
    ppermute x2, waiting for transfers between devices: 2.22 us -> 0.01 us  [local(): lax.ppermute(b, 'frame', xor_pairs(n_frame, bit))]
  transfers between devices with their start and end apart: 31 -> 37, of which waited for: 14 -> 17; matrix products, arithmetic and copies ran while one was open for 0% -> 0% of each run, Pallas kernels for 14% -> 14%
where the time goes in v10:
time: 207 us; the launch traced here: 205 us
  waiting for transfers between devices  113 us (55%)
  starting transfers between devices  47.1 us (23%)
  Pallas kernels  42.7 us (21%)
    ppermute x12, waiting for transfers between devices, exchange(): lax.ppermute(pieces[s], 'frame', shift_pairs(n_groups, n_tok, sign * s))  48.8 us
    ppermute x4, waiting for transfers between devices, local(): others.append(lax.ppermute(own[s], 'frame', last))  24.2 us
    pallas_call x13, Pallas kernels, whole_call(): pl.pallas_call(body, out_shape=out_shape, in_specs=[smem()] + [vmem()] *...  16 us
    ppermute x3, waiting for transfers between devices, across_x(): return lax.ppermute(piece, 'frame', last)  15.9 us
    ppermute x12, starting transfers between devices, exchange(): lax.ppermute(pieces[s], 'frame', shift_pairs(n_groups, n_tok, sign * s))  14.2 us
    ppermute x7, starting transfers between devices, across_y(): lax.ppermute(b, ('frame', 'space'), pairs)  13.1 us
    pallas_call x2, Pallas kernels, backward(): pl.pallas_call(functools.partial(backward_kernel, n_groups, chunk, 1.0 /...  12.7 us
    pallas_call x1, Pallas kernels, forward(): pl.pallas_call(functools.partial(forward_kernel, chunk, scale), grid=(hea...  10.3 us
  transfers between devices with their start and end apart: 37, of which 17 were waited for; matrix products, arithmetic and copies ran while one was open for 0% of the time, Pallas kernels for 14%

profile of v10, /device:TPU:0, one launch (start us, length us, event | category | flops | bytes accessed | tf_op | source)
XLA Modules:
  0.0 204.7 jit_solution(17433510221973452101)
XLA Ops:
  0.7 0.6 pad_add_fusion.ids
  1.2 3.7 %pack.1 = (bf16[512,384]{1,0:T(8,128)(2,1)}, bf16[672,384]{1,0:T(8,128)(2,1)}, bf16[672,384]{1,0:T(8,128)(2,1)}, bf16[672,384]{1,0:T(8,128)(2,1)}, bf16[160,384]{1,0:T(8,128)(2,1)}) custom-call(s32[3]{0:T(128)} %pad_add_fusion.ids, bf16[160,1536]{1,0:T(8,128)(2,1)} %q.1, bf16[160,1536]{1,0:T(8,128)(2,1)} %k.1, bf16[160,1536]{1,0:T(8,128)(2,1)} %v.1, ...), custom_call_target="tpu_custom_call" | custom-call | tf_op jit(solution)/shard_map/pack/pallas_call | solution.py:119
  5.0 3.1 %collective-permute-start = (bf16[672,384]{1,0:T(8,128)(2,1)}, bf16[672,384]{1,0:T(8,128)(2,1)S(1)}, u32[]{:S(2)}, u32[]{:S(2)}) collective-permute-start(bf16[672,384]{1,0:T(8,128)(2,1)} %get-tuple-element.80), channel_id=1, source_target_pairs={{0,8},{2,10},{4,12},{6,14},{8,16},{10,18},{12,20},{14,22},{16,24},... | collective-permute-start | bytes 1548296 | tf_op jit(solution)/shard_map/ppermute | solution.py:462
  8.1 1.3 collective-permute-start.4
  9.3 4.6 %collective-permute-start.3 = (bf16[160,1536]{1,0:T(8,128)(2,1)S(1)}, bf16[160,1536]{1,0:T(8,128)(2,1)S(1)}, u32[]{:S(2)}, u32[]{:S(2)}) collective-permute-start(bf16[160,1536]{1,0:T(8,128)(2,1)S(1)} %copy-done), channel_id=1, source_target_pairs={{0,8},{2,10},{4,12},{6,14},{8,16},{10,18},{12,20},{14,22},{16,24},... | collective-permute-start | bytes 1474568 | tf_op jit(solution)/shard_map/ppermute | solution.py:495
  13.9 1.6 collective-permute-start.6
  15.5 2.6 %collective-permute-start.1 = (bf16[672,384]{1,0:T(8,128)(2,1)}, bf16[672,384]{1,0:T(8,128)(2,1)S(1)}, u32[]{:S(2)}, u32[]{:S(2)}) collective-permute-start(bf16[672,384]{1,0:T(8,128)(2,1)} %get-tuple-element.81), channel_id=1, source_target_pairs={{0,16},{2,18},{4,20},{6,22},{8,24},{10,26},{12,28},{14,30},{16,0},... | collective-permute-start | bytes 1548296 | tf_op jit(solution)/shard_map/ppermute | solution.py:462
  18.1 4.8 %collective-permute-done.refs_0_ = bf16[672,384]{1,0:T(8,128)(2,1)S(1)} collective-permute-done((bf16[672,384]{1,0:T(8,128)(2,1)}, bf16[672,384]{1,0:T(8,128)(2,1)S(1)}, u32[]{:S(2)}, u32[]{:S(2)}) %collective-permute-start) | collective-permute-done | bytes 516128 | tf_op jit(solution)/shard_map/ppermute | solution.py:462
  22.9 1.7 collective-permute-start.5
  24.7 7.9 %collective-permute-done.5.refs_0_ = bf16[512,384]{1,0:T(8,128)(2,1)S(1)} collective-permute-done((bf16[512,384]{1,0:T(8,128)(2,1)}, bf16[512,384]{1,0:T(8,128)(2,1)S(1)}, u32[]{:S(2)}, u32[]{:S(2)}) %collective-permute-start.5) | collective-permute-done | bytes 393248 | tf_op jit(solution)/shard_map/ppermute | solution.py:503
  32.6 0.7 collective-permute-start.10
  33.3 0.7 collective-permute-start.7
  34.0 3.4 %collective-permute-start.11 = (bf16[160,1536]{1,0:T(8,128)(2,1)S(1)}, bf16[160,1536]{1,0:T(8,128)(2,1)S(1)}, u32[]{:S(2)}, u32[]{:S(2)}) collective-permute-start(bf16[160,1536]{1,0:T(8,128)(2,1)S(1)} %collective-permute-done.4.refs_10_.refs_6_), channel_id=1, source_target_pairs={{0,1},{1,0},{2,3},{3,2},{4,5},{5,4},{6,7},{7,6},{8,9},{9,8},{10,11... | collective-permute-start | bytes 1474568 | tf_op jit(solution)/shard_map/ppermute | solution.py:490
  37.4 1.3 collective-permute-start.8
  38.7 16.1 %collective-permute-done.1.refs_1_ = bf16[672,384]{1,0:T(8,128)(2,1)S(1)} collective-permute-done((bf16[672,384]{1,0:T(8,128)(2,1)}, bf16[672,384]{1,0:T(8,128)(2,1)S(1)}, u32[]{:S(2)}, u32[]{:S(2)}) %collective-permute-start.1) | collective-permute-done | bytes 516128 | tf_op jit(solution)/shard_map/ppermute | solution.py:462
  54.8 1.5 collective-permute-start.9
  56.3 9.5 %collective-permute-done.9.refs_1_ = bf16[512,384]{1,0:T(8,128)(2,1)S(1)} collective-permute-done((bf16[512,384]{1,0:T(8,128)(2,1)S(1)}, bf16[512,384]{1,0:T(8,128)(2,1)S(1)}, u32[]{:S(2)}, u32[]{:S(2)}) %collective-permute-start.9) | collective-permute-done | bytes 393248 | tf_op jit(solution)/shard_map/ppermute | solution.py:503
  65.8 0.6 collective-permute-start.2
  66.4 0.7 collective-permute-start.12
  67.1 1.3 collective-permute-start.13
  68.4 1.6 collective-permute-start.14
  70.0 10.7 %collective-permute-done.2.refs_2_ = bf16[672,384]{1,0:T(8,128)(2,1)S(1)} collective-permute-done((bf16[672,384]{1,0:T(8,128)(2,1)}, bf16[672,384]{1,0:T(8,128)(2,1)S(1)}, u32[]{:S(2)}, u32[]{:S(2)}) %collective-permute-start.2) | collective-permute-done | bytes 516128 | tf_op jit(solution)/shard_map/ppermute | solution.py:462
  80.7 8.5 %collective-permute-done.13.refs_6_.refs_2_ = bf16[160,1536]{1,0:T(8,128)(2,1)S(1)} collective-permute-done((bf16[160,1536]{1,0:T(8,128)(2,1)S(1)}, bf16[160,1536]{1,0:T(8,128)(2,1)S(1)}, u32[]{:S(2)}, u32[]{:S(2)}) %collective-permute-start.13) | collective-permute-done | bytes 491552 | tf_op jit(solution)/shard_map/ppermute | solution.py:495
  89.2 1.5 collective-permute-start.15
  90.7 0.7 stack.18.refs_0_.refs_5_
  91.5 6.9 %collective-permute-done.15.refs_3_ = bf16[512,384]{1,0:T(8,128)(2,1)S(1)} collective-permute-done((bf16[512,384]{1,0:T(8,128)(2,1)S(1)}, bf16[512,384]{1,0:T(8,128)(2,1)S(1)}, u32[]{:S(2)}, u32[]{:S(2)}) %collective-permute-start.15) | collective-permute-done | bytes 393248 | tf_op jit(solution)/shard_map/ppermute | solution.py:503
  98.4 0.7 stack.19.refs_1_.refs_6_
  99.2 0.7 collective-permute-start.19
  99.9 3.4 %collective-permute-start.20 = (bf16[160,1536]{1,0:T(8,128)(2,1)S(1)}, bf16[160,1536]{1,0:T(8,128)(2,1)S(1)}, u32[]{:S(2)}, u32[]{:S(2)}) collective-permute-start(bf16[160,1536]{1,0:T(8,128)(2,1)S(1)} %collective-permute-done.8.refs_8_.refs_4_), channel_id=1, source_target_pairs={{0,1},{1,0},{2,3},{3,2},{4,5},{5,4},{6,7},{7,6},{8,9},{9,8},{10,11... | collective-permute-start | bytes 1474568 | tf_op jit(solution)/shard_map/ppermute | solution.py:490
  103.3 2.4 %collective-permute-start.18 = (bf16[160,1536]{1,0:T(8,128)(2,1)S(1)}, bf16[160,1536]{1,0:T(8,128)(2,1)S(1)}, u32[]{:S(2)}, u32[]{:S(2)}) collective-permute-start(bf16[160,1536]{1,0:T(8,128)(2,1)S(1)} %collective-permute-done.13.refs_6_.refs_2_), channel_id=1, source_target_pairs={{0,1},{1,0},{2,3},{3,2},{4,5},{5,4},{6,7},{7,6}} | collective-permute-start | bytes 1474568 | tf_op jit(solution)/shard_map/ppermute | solution.py:490
  105.7 0.9 collective-permute-start.21
  106.6 0.6 stack_queries.1.q_in.refs_0_
  107.2 10.3 %forward.1 = (bf16[3,2560,640]{2,1,0:T(8,128)(2,1)S(1)}, bf16[640,384]{1,0:T(8,128)(2,1)S(1)}, f32[3,1,640]{2,1,0:T(1,128)S(1)}) custom-call(bf16[640,384]{1,0:T(8,128)(2,1)S(1)} %stack_queries.1.q_in.refs_0_, bf16[2048,384]{1,0:T(8,128)(2,1)S(1)} %stack.18.refs_0_.refs_5_, bf16[2048,384]{1,0:T(8,128)(2,1)S(1)} %stack.19.refs_1_.refs_6_, ...), custom_call_target="tpu_custom_call" | custom-call | flops 2516582400 | bytes 9830400 | tf_op jit(solution)/shard_map/forward/pallas_call | solution.py:200
  117.5 8.4 %collective-permute-done.18.refs_13_.refs_9_ = bf16[160,1536]{1,0:T(8,128)(2,1)S(1)} collective-permute-done((bf16[160,1536]{1,0:T(8,128)(2,1)S(1)}, bf16[160,1536]{1,0:T(8,128)(2,1)S(1)}, u32[]{:S(2)}, u32[]{:S(2)}) %collective-permute-start.18) | collective-permute-done | bytes 491552 | tf_op jit(solution)/shard_map/ppermute | solution.py:490
  125.9 3.0 %attn_gradient.1.refs_4_ = bf16[640,384]{1,0:T(8,128)(2,1)S(1)} custom-call(s32[3]{0:T(128)S(1)} %copy-done.3, bf16[2048,384]{1,0:T(8,128)(2,1)S(1)} %stack.18.refs_0_.refs_5_, bf16[2048,384]{1,0:T(8,128)(2,1)S(1)} %stack.19.refs_1_.refs_6_, bf16[2048,384]{1,0:T(8,128)(2,1)S(1)} %collective-permute-done.16.refs_2_.refs_7_, ...), custom_call_target="tpu_custom_call" | custom-call | flops 245760 | bytes 491520 | tf_op jit(solution)/shard_map/attn_gradient/pallas_call | solution.py:75
  128.9 3.9 %backward.2 = (bf16[160,128]{1,0:T(8,128)(2,1)S(1)}, bf16[160,128]{1,0:T(8,128)(2,1)S(1)}, bf16[160,128]{1,0:T(8,128)(2,1)S(1)}, bf16[160,128]{1,0:T(8,128)(2,1)...) custom-call(bf16[640,384]{1,0:T(8,128)(2,1)S(1)} %stack_queries.1.q_in.refs_0_, ...), custom_call_target="tpu_custom_call" | custom-call | flops 81920 | bytes 163840 | tf_op jit(solution)/shard_map/backward/pallas_call | solution.py:264
  132.9 2.1 %collective-permute-done.22.other = bf16[2560,128]{1,0:T(8,128)(2,1)S(1)} collective-permute-done((bf16[2560,128]{1,0:T(8,128)(2,1)S(1)}, bf16[2560,128]{1,0:T(8,128)(2,1)S(1)}, u32[]{:S(2)}, u32[]{:S(2)}) %collective-permute-start.22) | collective-permute-done | bytes 655392 | tf_op jit(solution)/shard_map/ppermute | solution.py:393
  134.9 0.7 add_parts.4
  135.6 1.6 collective-permute-start.23
  137.2 8.8 %backward.3 = (bf16[160,256]{1,0:T(8,128)(2,1)S(1)}, bf16[160,256]{1,0:T(8,128)(2,1)S(1)}, bf16[160,256]{1,0:T(8,128)(2,1)S(1)}, bf16[160,256]{1,0:T(8,128)(2,1)...) custom-call(bf16[640,384]{1,0:T(8,128)(2,1)S(1)} %stack_queries.1.q_in.refs_0_, ...), custom_call_target="tpu_custom_call" | custom-call | flops 81920 | bytes 163840 | tf_op jit(solution)/shard_map/backward/pallas_call | solution.py:264
  146.1 3.0 %collective-permute-done.24.other = bf16[2560,256]{1,0:T(8,128)(2,1)S(1)} collective-permute-done((bf16[2560,256]{1,0:T(8,128)(2,1)S(1)}, bf16[2560,256]{1,0:T(8,128)(2,1)S(1)}, u32[]{:S(2)}, u32[]{:S(2)}) %collective-permute-start.24) | collective-permute-done | bytes 1310752 | tf_op jit(solution)/shard_map/ppermute | solution.py:393
  149.1 0.8 add_parts.5
  150.0 0.9 collective-permute-start.25
  150.9 0.6 finish.2
  151.5 0.9 collective-permute-start.26
  152.4 1.2 collective-permute-start.28
  153.6 3.2 %proj_gradient.1 = (bf16[1536,384]{1,0:T(8,128)(2,1)S(1)}, bf16[1536,384]{1,0:T(8,128)(2,1)S(1)}) custom-call(s32[3]{0:T(128)S(1)} %copy-done.3, bf16[640,384]{1,0:T(8,128)(2,1)S(1)} %get-tuple-element.126.refs_2_.attn, bf16[160,1536]{1,0:T(8,128)(2,1)S(1)} %copy-done, bf16[160,1536]{1,0:T(8,128)(2,1)S(1)} %collective-permute-done.3.refs_5_.refs_1_, ...), custom_call_target="tpu_custom_call" | custom-call | flops 245760 | bytes 491520 | tf_op jit(solution)/shard_map/proj_gradient/pallas_call | solution.py:75
  156.9 0.5 collective-permute-done.26.refs_1_
  157.4 6.0 %collective-permute-done.27.refs_2_ = bf16[480,128]{1,0:T(8,128)(2,1)S(1)} collective-permute-done((bf16[480,128]{1,0:T(8,128)(2,1)S(1)}, bf16[480,128]{1,0:T(8,128)(2,1)S(1)}, u32[]{:S(2)}, u32[]{:S(2)}) %collective-permute-start.27) | collective-permute-done | bytes 122912 | tf_op jit(solution)/shard_map/ppermute | solution.py:462
  163.4 3.4 %collective-permute-done.25.other = bf16[1280,256]{1,0:T(8,128)(2,1)S(1)} collective-permute-done((bf16[1280,256]{1,0:T(8,128)(2,1)S(1)}, bf16[1280,256]{1,0:T(8,128)(2,1)S(1)}, u32[]{:S(2)}, u32[]{:S(2)}) %collective-permute-start.25) | collective-permute-done | bytes 655392 | tf_op jit(solution)/shard_map/ppermute | solution.py:538
  166.8 0.7 finish.3
  167.5 2.1 %collective-permute-done.32.other = bf16[1536,384]{1,0:T(8,128)(2,1)S(1)} collective-permute-done((bf16[1536,384]{1,0:T(8,128)(2,1)S(1)}, bf16[1536,384]{1,0:T(8,128)(2,1)S(1)}, u32[]{:S(2)}, u32[]{:S(2)}) %collective-permute-start.32) | collective-permute-done | bytes 1179680 | tf_op jit(solution)/shard_map/ppermute | solution.py:393
  169.7 0.8 add_parts.6
  170.5 0.9 collective-permute-start.33
  171.4 0.8 collective-permute-start.29
  172.3 1.2 collective-permute-start.31
  173.4 12.5 %collective-permute-done.33.other = bf16[768,384]{1,0:T(8,128)(2,1)S(1)} collective-permute-done((bf16[768,384]{1,0:T(8,128)(2,1)S(1)}, bf16[768,384]{1,0:T(8,128)(2,1)S(1)}, u32[]{:S(2)}, u32[]{:S(2)}) %collective-permute-start.33) | collective-permute-done | bytes 589856 | tf_op jit(solution)/shard_map/ppermute | solution.py:538
  185.9 0.7 add_parts.7
  186.7 1.4 collective-permute-start.35
  188.1 2.4 %collective-permute-start.36 = (bf16[192,384]{1,0:T(8,128)(2,1)S(1)}, bf16[192,384]{1,0:T(8,128)(2,1)S(1)}, u32[]{:S(2)}, u32[]{:S(2)}) collective-permute-start(bf16[192,384]{1,0:T(8,128)(2,1)S(1)} %get-tuple-element.153), channel_id=1, source_target_pairs={{0,24},{2,26},{4,28},{6,30},{8,0},{10,2},{12,4},{14,6},{16,8},{18,... | collective-permute-start | bytes 442376 | tf_op jit(solution)/shard_map/ppermute | solution.py:462
  190.5 9.3 %collective-permute-done.30.refs_6_ = bf16[480,256]{1,0:T(8,128)(2,1)S(1)} collective-permute-done((bf16[480,256]{1,0:T(8,128)(2,1)S(1)}, bf16[480,256]{1,0:T(8,128)(2,1)S(1)}, u32[]{:S(2)}, u32[]{:S(2)}) %collective-permute-start.30) | collective-permute-done | bytes 245792 | tf_op jit(solution)/shard_map/ppermute | solution.py:462
  199.9 1.8 unpack.1
  201.7 1.3 collective-permute-done.35.refs_2_
  203.0 1.7 join.1
  (39 shorter events, 0.5 us)
Async XLA Ops:
  0.6 7.4 %copy-start = (bf16[160,1536]{1,0:T(8,128)(2,1)S(1)}, bf16[160,1536]{1,0:T(8,128)(2,1)}, u32[]{:S(2)}) copy-start(bf16[160,1536]{1,0:T(8,128)(2,1)} %refs_0_) | copy-start | bytes 1474564
  5.0 85.8 %copy-start.1 = (bf16[512,384]{1,0:T(8,128)(2,1)S(1)}, bf16[512,384]{1,0:T(8,128)(2,1)}, u32[]{:S(2)}) copy-start(bf16[512,384]{1,0:T(8,128)(2,1)} %get-tuple-element.83.refs_0_) | copy-start | bytes 1179652
  5.0 85.8 %copy-start.3 = (s32[3]{0:T(128)S(1)}, s32[3]{0:T(128)}, u32[]{:S(2)}) copy-start(s32[3]{0:T(128)} %pad_add_fusion.ids) | copy-start | bytes 40
  5.0 17.9 %collective-permute-start = (bf16[672,384]{1,0:T(8,128)(2,1)}, bf16[672,384]{1,0:T(8,128)(2,1)S(1)}, u32[]{:S(2)}, u32[]{:S(2)}) collective-permute-start(bf16[672,384]{1,0:T(8,128)(2,1)} %get-tuple-element.80), channel_id=1, source_target_pairs={{0,8},{2,10},{4,12},{6,14},{8,16},{10,18},{12,20},{14,22},{16,24},... | collective-permute-start | bytes 1548296 | tf_op jit(solution)/shard_map/ppermute | solution.py:462
  8.1 24.5 %collective-permute-start.4 = (bf16[160,1536]{1,0:T(8,128)(2,1)S(1)}, bf16[160,1536]{1,0:T(8,128)(2,1)S(1)}, u32[]{:S(2)}, u32[]{:S(2)}) collective-permute-start(bf16[160,1536]{1,0:T(8,128)(2,1)S(1)} %copy-done), channel_id=1, source_target_pairs={{8,0},{10,2},{12,4},{14,6},{16,8},{18,10},{20,12},{22,14},{24,16},... | collective-permute-start | bytes 1474568 | tf_op jit(solution)/shard_map/ppermute | solution.py:495
  9.3 23.3 %collective-permute-start.3 = (bf16[160,1536]{1,0:T(8,128)(2,1)S(1)}, bf16[160,1536]{1,0:T(8,128)(2,1)S(1)}, u32[]{:S(2)}, u32[]{:S(2)}) collective-permute-start(bf16[160,1536]{1,0:T(8,128)(2,1)S(1)} %copy-done), channel_id=1, source_target_pairs={{0,8},{2,10},{4,12},{6,14},{8,16},{10,18},{12,20},{14,22},{16,24},... | collective-permute-start | bytes 1474568 | tf_op jit(solution)/shard_map/ppermute | solution.py:495
  13.9 18.7 %collective-permute-start.6 = (bf16[160,1536]{1,0:T(8,128)(2,1)S(1)}, bf16[160,1536]{1,0:T(8,128)(2,1)S(1)}, u32[]{:S(2)}, u32[]{:S(2)}) collective-permute-start(bf16[160,1536]{1,0:T(8,128)(2,1)S(1)} %copy-done), channel_id=1, source_target_pairs={{0,1},{1,0},{2,3},{3,2},{4,5},{5,4},{6,7},{7,6},{8,9},{9,8},{10,11... | collective-permute-start | bytes 1474568 | tf_op jit(solution)/shard_map/ppermute | solution.py:490
  15.5 39.3 %collective-permute-start.1 = (bf16[672,384]{1,0:T(8,128)(2,1)}, bf16[672,384]{1,0:T(8,128)(2,1)S(1)}, u32[]{:S(2)}, u32[]{:S(2)}) collective-permute-start(bf16[672,384]{1,0:T(8,128)(2,1)} %get-tuple-element.81), channel_id=1, source_target_pairs={{0,16},{2,18},{4,20},{6,22},{8,24},{10,26},{12,28},{14,30},{16,0},... | collective-permute-start | bytes 1548296 | tf_op jit(solution)/shard_map/ppermute | solution.py:462
  22.9 9.7 %collective-permute-start.5 = (bf16[512,384]{1,0:T(8,128)(2,1)}, bf16[512,384]{1,0:T(8,128)(2,1)S(1)}, u32[]{:S(2)}, u32[]{:S(2)}) collective-permute-start(bf16[512,384]{1,0:T(8,128)(2,1)} %get-tuple-element.83.refs_0_), channel_id=1, source_target_pairs={{0,4},{2,6},{4,0},{6,2},{8,12},{10,14},{12,8},{14,10},{16,20},{18,... | collective-permute-start | bytes 1179656 | tf_op jit(solution)/shard_map/ppermute | solution.py:503
  32.6 33.8 %collective-permute-start.10 = (bf16[160,1536]{1,0:T(8,128)(2,1)S(1)}, bf16[160,1536]{1,0:T(8,128)(2,1)S(1)}, u32[]{:S(2)}, u32[]{:S(2)}) collective-permute-start(bf16[160,1536]{1,0:T(8,128)(2,1)S(1)} %collective-permute-done.3.refs_5_.refs_1_), channel_id=1, source_target_pairs={{8,9},{9,8},{10,11},{11,10},{12,13},{13,12},{14,15},{15,14},{16,17... | collective-permute-start | bytes 1474568 | tf_op jit(solution)/shard_map/ppermute | solution.py:490
  33.3 33.1 %collective-permute-start.7 = (bf16[160,1536]{1,0:T(8,128)(2,1)S(1)}, bf16[160,1536]{1,0:T(8,128)(2,1)S(1)}, u32[]{:S(2)}, u32[]{:S(2)}) collective-permute-start(bf16[160,1536]{1,0:T(8,128)(2,1)S(1)} %collective-permute-done.3.refs_5_.refs_1_), channel_id=1, source_target_pairs={{8,16},{10,18},{12,20},{14,22},{16,24},{18,26},{20,28},{22,30},{9,... | collective-permute-start | bytes 1474568 | tf_op jit(solution)/shard_map/ppermute | solution.py:495
  34.0 32.4 %collective-permute-start.11 = (bf16[160,1536]{1,0:T(8,128)(2,1)S(1)}, bf16[160,1536]{1,0:T(8,128)(2,1)S(1)}, u32[]{:S(2)}, u32[]{:S(2)}) collective-permute-start(bf16[160,1536]{1,0:T(8,128)(2,1)S(1)} %collective-permute-done.4.refs_10_.refs_6_), channel_id=1, source_target_pairs={{0,1},{1,0},{2,3},{3,2},{4,5},{5,4},{6,7},{7,6},{8,9},{9,8},{10,11... | collective-permute-start | bytes 1474568 | tf_op jit(solution)/shard_map/ppermute | solution.py:490
  37.4 29.0 %collective-permute-start.8 = (bf16[160,1536]{1,0:T(8,128)(2,1)S(1)}, bf16[160,1536]{1,0:T(8,128)(2,1)S(1)}, u32[]{:S(2)}, u32[]{:S(2)}) collective-permute-start(bf16[160,1536]{1,0:T(8,128)(2,1)S(1)} %collective-permute-done.4.refs_10_.refs_6_), channel_id=1, source_target_pairs={{8,0},{10,2},{12,4},{14,6},{16,8},{18,10},{20,12},{22,14},{9,1},{1... | collective-permute-start | bytes 1474568 | tf_op jit(solution)/shard_map/ppermute | solution.py:495
  54.8 10.9 %collective-permute-start.9 = (bf16[512,384]{1,0:T(8,128)(2,1)S(1)}, bf16[512,384]{1,0:T(8,128)(2,1)S(1)}, u32[]{:S(2)}, u32[]{:S(2)}) collective-permute-start(bf16[512,384]{1,0:T(8,128)(2,1)S(1)} %slice.12.refs_1_), channel_id=1, source_target_pairs={{0,4},{2,6},{4,0},{6,2},{8,12},{10,14},{12,8},{14,10},{16,20},{18,... | collective-permute-start | bytes 1179656 | tf_op jit(solution)/shard_map/ppermute | solution.py:503
  65.8 14.9 %collective-permute-start.2 = (bf16[672,384]{1,0:T(8,128)(2,1)}, bf16[672,384]{1,0:T(8,128)(2,1)S(1)}, u32[]{:S(2)}, u32[]{:S(2)}) collective-permute-start(bf16[672,384]{1,0:T(8,128)(2,1)} %get-tuple-element.82), channel_id=1, source_target_pairs={{0,24},{2,26},{4,28},{6,30},{8,0},{10,2},{12,4},{14,6},{16,8},{18,... | collective-permute-start | bytes 1548296 | tf_op jit(solution)/shard_map/ppermute | solution.py:462
  66.4 14.3 %collective-permute-start.12 = (bf16[160,1536]{1,0:T(8,128)(2,1)S(1)}, bf16[160,1536]{1,0:T(8,128)(2,1)S(1)}, u32[]{:S(2)}, u32[]{:S(2)}) collective-permute-start(bf16[160,1536]{1,0:T(8,128)(2,1)S(1)} %collective-permute-done.7.refs_7_.refs_3_), channel_id=1, source_target_pairs={{16,24},{18,26},{20,28},{22,30},{17,25},{19,27},{21,29},{23,31}} | collective-permute-start | bytes 1474568 | tf_op jit(solution)/shard_map/ppermute | solution.py:495
  67.1 22.1 %collective-permute-start.13 = (bf16[160,1536]{1,0:T(8,128)(2,1)S(1)}, bf16[160,1536]{1,0:T(8,128)(2,1)S(1)}, u32[]{:S(2)}, u32[]{:S(2)}) collective-permute-start(bf16[160,1536]{1,0:T(8,128)(2,1)S(1)} %collective-permute-done.8.refs_8_.refs_4_), channel_id=1, source_target_pairs={{8,0},{10,2},{12,4},{14,6},{9,1},{11,3},{13,5},{15,7}} | collective-permute-start | bytes 1474568 | tf_op jit(solution)/shard_map/ppermute | solution.py:495
  68.4 12.3 %collective-permute-start.14 = (bf16[512,384]{1,0:T(8,128)(2,1)S(1)}, bf16[512,384]{1,0:T(8,128)(2,1)S(1)}, u32[]{:S(2)}, u32[]{:S(2)}) collective-permute-start(bf16[512,384]{1,0:T(8,128)(2,1)S(1)} %slice.13.refs_2_), channel_id=1, source_target_pairs={{0,4},{2,6},{4,0},{6,2},{8,12},{10,14},{12,8},{14,10},{16,20},{18,... | collective-permute-start | bytes 1179656 | tf_op jit(solution)/shard_map/ppermute | solution.py:503
  89.2 9.2 %collective-permute-start.15 = (bf16[512,384]{1,0:T(8,128)(2,1)S(1)}, bf16[512,384]{1,0:T(8,128)(2,1)S(1)}, u32[]{:S(2)}, u32[]{:S(2)}) collective-permute-start(bf16[512,384]{1,0:T(8,128)(2,1)S(1)} %slice.14.refs_3_), channel_id=1, source_target_pairs={{0,4},{2,6},{4,0},{6,2},{8,12},{10,14},{12,8},{14,10},{16,20},{18,... | collective-permute-start | bytes 1179656 | tf_op jit(solution)/shard_map/ppermute | solution.py:503
  91.4 15.2 %copy-start.2 = (bf16[160,384]{1,0:T(8,128)(2,1)S(1)}, bf16[160,384]{1,0:T(8,128)(2,1)}, u32[]{:S(2)}) copy-start(bf16[160,384]{1,0:T(8,128)(2,1)} %get-tuple-element.79.own) | copy-start | bytes 368644
  91.4 14.3 %collective-permute-start.16 = (bf16[2048,384]{1,0:T(8,128)(2,1)S(1)}, bf16[2048,384]{1,0:T(8,128)(2,1)S(1)}, u32[]{:S(2)}, u32[]{:S(2)}) collective-permute-start(bf16[2048,384]{1,0:T(8,128)(2,1)S(1)} %stack.18.refs_0_.refs_5_), channel_id=1, source_target_pairs={{0,2},{2,0},{4,6},{6,4},{8,10},{10,8},{12,14},{14,12},{16,18},{18,... | collective-permute-start | bytes 4718600 | tf_op jit(solution)/shard_map/ppermute | solution.py:524
  99.1 8.1 %collective-permute-start.17 = (bf16[2048,384]{1,0:T(8,128)(2,1)S(1)}, bf16[2048,384]{1,0:T(8,128)(2,1)S(1)}, u32[]{:S(2)}, u32[]{:S(2)}) collective-permute-start(bf16[2048,384]{1,0:T(8,128)(2,1)S(1)} %stack.19.refs_1_.refs_6_), channel_id=1, source_target_pairs={{0,2},{2,0},{4,6},{6,4},{8,10},{10,8},{12,14},{14,12},{16,18},{18,... | collective-permute-start | bytes 4718600 | tf_op jit(solution)/shard_map/ppermute | solution.py:524
  99.2 18.3 %collective-permute-start.19 = (bf16[160,1536]{1,0:T(8,128)(2,1)S(1)}, bf16[160,1536]{1,0:T(8,128)(2,1)S(1)}, u32[]{:S(2)}, u32[]{:S(2)}) collective-permute-start(bf16[160,1536]{1,0:T(8,128)(2,1)S(1)} %collective-permute-done.7.refs_7_.refs_3_), channel_id=1, source_target_pairs={{16,17},{17,16},{18,19},{19,18},{20,21},{21,20},{22,23},{23,22},{2... | collective-permute-start | bytes 1474568 | tf_op jit(solution)/shard_map/ppermute | solution.py:490
  99.9 17.6 %collective-permute-start.20 = (bf16[160,1536]{1,0:T(8,128)(2,1)S(1)}, bf16[160,1536]{1,0:T(8,128)(2,1)S(1)}, u32[]{:S(2)}, u32[]{:S(2)}) collective-permute-start(bf16[160,1536]{1,0:T(8,128)(2,1)S(1)} %collective-permute-done.8.refs_8_.refs_4_), channel_id=1, source_target_pairs={{0,1},{1,0},{2,3},{3,2},{4,5},{5,4},{6,7},{7,6},{8,9},{9,8},{10,11... | collective-permute-start | bytes 1474568 | tf_op jit(solution)/shard_map/ppermute | solution.py:490
  103.3 22.6 %collective-permute-start.18 = (bf16[160,1536]{1,0:T(8,128)(2,1)S(1)}, bf16[160,1536]{1,0:T(8,128)(2,1)S(1)}, u32[]{:S(2)}, u32[]{:S(2)}) collective-permute-start(bf16[160,1536]{1,0:T(8,128)(2,1)S(1)} %collective-permute-done.13.refs_6_.refs_2_), channel_id=1, source_target_pairs={{0,1},{1,0},{2,3},{3,2},{4,5},{5,4},{6,7},{7,6}} | collective-permute-start | bytes 1474568 | tf_op jit(solution)/shard_map/ppermute | solution.py:490
  105.7 20.2 %collective-permute-start.21 = (bf16[160,1536]{1,0:T(8,128)(2,1)S(1)}, bf16[160,1536]{1,0:T(8,128)(2,1)S(1)}, u32[]{:S(2)}, u32[]{:S(2)}) collective-permute-start(bf16[160,1536]{1,0:T(8,128)(2,1)S(1)} %collective-permute-done.12.refs_9_.refs_5_), channel_id=1, source_target_pairs={{24,25},{25,24},{26,27},{27,26},{28,29},{29,28},{30,31},{31,30}} | collective-permute-start | bytes 1474568 | tf_op jit(solution)/shard_map/ppermute | solution.py:490
  132.8 2.2 %collective-permute-start.22 = (bf16[2560,128]{1,0:T(8,128)(2,1)S(1)}, bf16[2560,128]{1,0:T(8,128)(2,1)S(1)}, u32[]{:S(2)}, u32[]{:S(2)}) collective-permute-start(bf16[2560,128]{1,0:T(8,128)(2,1)S(1)} %get-tuple-element.106), channel_id=1, source_target_pairs={{0,2},{2,0},{4,6},{6,4},{8,10},{10,8},{12,14},{14,12},{16,18},{18,... | collective-permute-start | bytes 1966088 | tf_op jit(solution)/shard_map/ppermute | solution.py:393
  135.6 10.4 %collective-permute-start.23 = (bf16[1280,128]{1,0:T(8,128)(2,1)S(1)}, bf16[1280,128]{1,0:T(8,128)(2,1)S(1)}, u32[]{:S(2)}, u32[]{:S(2)}) collective-permute-start(bf16[1280,128]{1,0:T(8,128)(2,1)S(1)} %get-tuple-element.110), channel_id=1, source_target_pairs={{0,4},{2,6},{4,0},{6,2},{8,12},{10,14},{12,8},{14,10},{16,20},{18,... | collective-permute-start | bytes 983048 | tf_op jit(solution)/shard_map/ppermute | solution.py:538
  146.0 3.1 %collective-permute-start.24 = (bf16[2560,256]{1,0:T(8,128)(2,1)S(1)}, bf16[2560,256]{1,0:T(8,128)(2,1)S(1)}, u32[]{:S(2)}, u32[]{:S(2)}) collective-permute-start(bf16[2560,256]{1,0:T(8,128)(2,1)S(1)} %get-tuple-element.121), channel_id=1, source_target_pairs={{0,2},{2,0},{4,6},{6,4},{8,10},{10,8},{12,14},{14,12},{16,18},{18,... | collective-permute-start | bytes 3932168 | tf_op jit(solution)/shard_map/ppermute | solution.py:393
  150.0 16.8 %collective-permute-start.25 = (bf16[1280,256]{1,0:T(8,128)(2,1)S(1)}, bf16[1280,256]{1,0:T(8,128)(2,1)S(1)}, u32[]{:S(2)}, u32[]{:S(2)}) collective-permute-start(bf16[1280,256]{1,0:T(8,128)(2,1)S(1)} %get-tuple-element.122), channel_id=1, source_target_pairs={{0,4},{2,6},{4,0},{6,2},{8,12},{10,14},{12,8},{14,10},{16,20},{18,... | collective-permute-start | bytes 1966088 | tf_op jit(solution)/shard_map/ppermute | solution.py:538
  151.5 5.9 %collective-permute-start.26 = (bf16[480,128]{1,0:T(8,128)(2,1)S(1)}, bf16[480,128]{1,0:T(8,128)(2,1)S(1)}, u32[]{:S(2)}, u32[]{:S(2)}) collective-permute-start(bf16[480,128]{1,0:T(8,128)(2,1)S(1)} %get-tuple-element.123), channel_id=1, source_target_pairs={{0,24},{2,26},{4,28},{6,30},{8,0},{10,2},{12,4},{14,6},{16,8},{18,... | collective-permute-start | bytes 368648 | tf_op jit(solution)/shard_map/ppermute | solution.py:462
  152.4 11.0 %collective-permute-start.27 = (bf16[480,128]{1,0:T(8,128)(2,1)S(1)}, bf16[480,128]{1,0:T(8,128)(2,1)S(1)}, u32[]{:S(2)}, u32[]{:S(2)}) collective-permute-start(bf16[480,128]{1,0:T(8,128)(2,1)S(1)} %get-tuple-element.124), channel_id=1, source_target_pairs={{0,16},{2,18},{4,20},{6,22},{8,24},{10,26},{12,28},{14,30},{16,0},... | collective-permute-start | bytes 368648 | tf_op jit(solution)/shard_map/ppermute | solution.py:462
  152.4 11.0 %collective-permute-start.28 = (bf16[480,128]{1,0:T(8,128)(2,1)S(1)}, bf16[480,128]{1,0:T(8,128)(2,1)S(1)}, u32[]{:S(2)}, u32[]{:S(2)}) collective-permute-start(bf16[480,128]{1,0:T(8,128)(2,1)S(1)} %get-tuple-element.125), channel_id=1, source_target_pairs={{0,8},{2,10},{4,12},{6,14},{8,16},{10,18},{12,20},{14,22},{16,24},... | collective-permute-start | bytes 368648 | tf_op jit(solution)/shard_map/ppermute | solution.py:462
  166.8 2.8 %collective-permute-start.32 = (bf16[1536,384]{1,0:T(8,128)(2,1)S(1)}, bf16[1536,384]{1,0:T(8,128)(2,1)S(1)}, u32[]{:S(2)}, u32[]{:S(2)}) collective-permute-start(bf16[1536,384]{1,0:T(8,128)(2,1)S(1)} %get-tuple-element.146), channel_id=1, source_target_pairs={{0,2},{2,0},{4,6},{6,4},{8,10},{10,8},{12,14},{14,12},{16,18},{18,... | collective-permute-start | bytes 3538952 | tf_op jit(solution)/shard_map/ppermute | solution.py:393
  170.5 15.4 %collective-permute-start.33 = (bf16[768,384]{1,0:T(8,128)(2,1)S(1)}, bf16[768,384]{1,0:T(8,128)(2,1)S(1)}, u32[]{:S(2)}, u32[]{:S(2)}) collective-permute-start(bf16[768,384]{1,0:T(8,128)(2,1)S(1)} %get-tuple-element.149), channel_id=1, source_target_pairs={{0,4},{2,6},{4,0},{6,2},{8,12},{10,14},{12,8},{14,10},{16,20},{18,... | collective-permute-start | bytes 1769480 | tf_op jit(solution)/shard_map/ppermute | solution.py:538
  171.4 16.7 %collective-permute-start.29 = (bf16[480,256]{1,0:T(8,128)(2,1)S(1)}, bf16[480,256]{1,0:T(8,128)(2,1)S(1)}, u32[]{:S(2)}, u32[]{:S(2)}) collective-permute-start(bf16[480,256]{1,0:T(8,128)(2,1)S(1)} %get-tuple-element.139), channel_id=1, source_target_pairs={{0,24},{2,26},{4,28},{6,30},{8,0},{10,2},{12,4},{14,6},{16,8},{18,... | collective-permute-start | bytes 737288 | tf_op jit(solution)/shard_map/ppermute | solution.py:462
  172.3 27.6 %collective-permute-start.30 = (bf16[480,256]{1,0:T(8,128)(2,1)S(1)}, bf16[480,256]{1,0:T(8,128)(2,1)S(1)}, u32[]{:S(2)}, u32[]{:S(2)}) collective-permute-start(bf16[480,256]{1,0:T(8,128)(2,1)S(1)} %get-tuple-element.140), channel_id=1, source_target_pairs={{0,16},{2,18},{4,20},{6,22},{8,24},{10,26},{12,28},{14,30},{16,0},... | collective-permute-start | bytes 737288 | tf_op jit(solution)/shard_map/ppermute | solution.py:462
  172.3 27.6 %collective-permute-start.31 = (bf16[480,256]{1,0:T(8,128)(2,1)S(1)}, bf16[480,256]{1,0:T(8,128)(2,1)S(1)}, u32[]{:S(2)}, u32[]{:S(2)}) collective-permute-start(bf16[480,256]{1,0:T(8,128)(2,1)S(1)} %get-tuple-element.141), channel_id=1, source_target_pairs={{0,8},{2,10},{4,12},{6,14},{8,16},{10,18},{12,20},{14,22},{16,24},... | collective-permute-start | bytes 737288 | tf_op jit(solution)/shard_map/ppermute | solution.py:462
  186.6 15.1 %collective-permute-start.34 = (bf16[192,384]{1,0:T(8,128)(2,1)S(1)}, bf16[192,384]{1,0:T(8,128)(2,1)S(1)}, u32[]{:S(2)}, u32[]{:S(2)}) collective-permute-start(bf16[192,384]{1,0:T(8,128)(2,1)S(1)} %get-tuple-element.151), channel_id=1, source_target_pairs={{0,8},{2,10},{4,12},{6,14},{8,16},{10,18},{12,20},{14,22},{16,24},... | collective-permute-start | bytes 442376 | tf_op jit(solution)/shard_map/ppermute | solution.py:462
  186.7 16.3 %collective-permute-start.35 = (bf16[192,384]{1,0:T(8,128)(2,1)S(1)}, bf16[192,384]{1,0:T(8,128)(2,1)S(1)}, u32[]{:S(2)}, u32[]{:S(2)}) collective-permute-start(bf16[192,384]{1,0:T(8,128)(2,1)S(1)} %get-tuple-element.152), channel_id=1, source_target_pairs={{0,16},{2,18},{4,20},{6,22},{8,24},{10,26},{12,28},{14,30},{16,0},... | collective-permute-start | bytes 442376 | tf_op jit(solution)/shard_map/ppermute | solution.py:462
  188.1 14.9 %collective-permute-start.36 = (bf16[192,384]{1,0:T(8,128)(2,1)S(1)}, bf16[192,384]{1,0:T(8,128)(2,1)S(1)}, u32[]{:S(2)}, u32[]{:S(2)}) collective-permute-start(bf16[192,384]{1,0:T(8,128)(2,1)S(1)} %get-tuple-element.153), channel_id=1, source_target_pairs={{0,24},{2,26},{4,28},{6,30},{8,0},{10,2},{12,4},{14,6},{16,8},{18,... | collective-permute-start | bytes 442376 | tf_op jit(solution)/shard_map/ppermute | solution.py:462

commit v11 on v9

--- a/solution.py
+++ b/solution.py
@@ -520,12 +520,12 @@
     if heads > 1:
         kept, sent = halve(ids, *halves, n_frame, tok_bits)
         other = across_x(sent)
-        other, proj, *returned[0][1:] = tie((other, tuple(proj), *returned[0][1:]))
+    proj_kept, proj_sent = halve(ids, *proj, n_frame, tok_bits)
+    if heads > 1:
+        step = (other, proj_kept, proj_sent, *returned[0][1:])
+        other, proj_kept, proj_sent, *returned[0][1:] = tie(step)
         sums = finish(ids, kept, other, dq_rest, n_groups)
         returned.append(exchange(sums, n_groups, n_tok, -1))
-    proj_kept, proj_sent = halve(ids, *proj, n_frame, tok_bits)
-    if heads > 1:
-        proj_sent, *_ = tie((proj_sent, *sums))
     proj = add_parts(ids, proj_kept, across_x(proj_sent), n_groups)
     proj_pieces = exchange(proj, n_groups, n_tok, 1)
     grad_proj = join(ids, proj_pieces, n_groups).T

time: 194 us -> 192 us (0.990)
  waiting for transfers between devices: 91.6 us -> 87.1 us
    ppermute x3, waiting for transfers between devices: 7.12 us -> 1.97 us  [halve(): other = lax.ppermute(sent, 'frame', xor_pairs(n_frame, bit))]
    ppermute x12, waiting for transfers between devices: 48.3 us -> 51.4 us  [exchange(): lax.ppermute(pieces[s], 'frame', shift_pairs(n_groups, n_tok, sign * s))]
    ppermute x3, waiting for transfers between devices: 9.12 us -> 6.7 us  [across_x(): return lax.ppermute(piece, 'frame', last)]
  transfers between devices with their start and end apart: 31 -> 31, of which waited for: 14 -> 12; matrix products, arithmetic and copies ran while one was open for 0% -> 0% of each run, Pallas kernels for 14% -> 16%
where the time goes in v11:
time: 192 us
  waiting for transfers between devices  87.1 us (45%)
  starting transfers between devices  60.2 us (31%)
  Pallas kernels  42.7 us (22%)
    ppermute x12, waiting for transfers between devices, exchange(): lax.ppermute(pieces[s], 'frame', shift_pairs(n_groups, n_tok, sign * s))  51.4 us
    ppermute x12, starting transfers between devices, exchange(): lax.ppermute(pieces[s], 'frame', shift_pairs(n_groups, n_tok, sign * s))  23.6 us
    ppermute x3, starting transfers between devices, local(): ring = lax.ppermute(ring, 'frame', shift_pairs(n_groups, n_tok, 1))  20.6 us
    pallas_call x13, Pallas kernels, whole_call(): pl.pallas_call(body, out_shape=out_shape, in_specs=[smem()] + [vmem()] *...  16 us
    ppermute x4, waiting for transfers between devices, local(): others.append(lax.ppermute(own[s], 'frame', last))  14.3 us
    pallas_call x2, Pallas kernels, backward(): pl.pallas_call(functools.partial(backward_kernel, n_groups, chunk, 1.0 /...  12.7 us
    ppermute x3, waiting for transfers between devices, local(): ring = lax.ppermute(ring, 'frame', shift_pairs(n_groups, n_tok, 1))  10.5 us
    pallas_call x1, Pallas kernels, forward(): pl.pallas_call(functools.partial(forward_kernel, chunk, scale), grid=(hea...  10.2 us
  transfers between devices with their start and end apart: 31, of which 12 were waited for; matrix products, arithmetic and copies ran while one was open for 0% of the time, Pallas kernels for 16%

profile of v11, /device:TPU:0, one launch (start us, length us, event | category | flops | bytes accessed | tf_op | source)
XLA Modules:
  0.0 191.7 jit_solution(1813287328774796548)
XLA Ops:
  0.7 0.6 pad_add_fusion.ids
  1.3 3.7 %pack.1 = (bf16[512,384]{1,0:T(8,128)(2,1)}, bf16[672,384]{1,0:T(8,128)(2,1)}, bf16[672,384]{1,0:T(8,128)(2,1)}, bf16[672,384]{1,0:T(8,128)(2,1)}, bf16[160,384]{1,0:T(8,128)(2,1)}) custom-call(s32[3]{0:T(128)} %pad_add_fusion.ids, bf16[160,1536]{1,0:T(8,128)(2,1)} %q.1, bf16[160,1536]{1,0:T(8,128)(2,1)} %k.1, bf16[160,1536]{1,0:T(8,128)(2,1)} %v.1, ...), custom_call_target="tpu_custom_call" | custom-call | tf_op jit(solution)/shard_map/pack/pallas_call | solution.py:119
  5.0 0.0 copy-start.1
  5.0 3.1 %collective-permute-start = (bf16[672,384]{1,0:T(8,128)(2,1)}, bf16[672,384]{1,0:T(8,128)(2,1)S(1)}, u32[]{:S(2)}, u32[]{:S(2)}) collective-permute-start(bf16[672,384]{1,0:T(8,128)(2,1)} %get-tuple-element.76), channel_id=1, source_target_pairs={{0,8},{2,10},{4,12},{6,14},{8,16},{10,18},{12,20},{14,22},{16,24},... | collective-permute-start | bytes 1548296 | tf_op jit(solution)/shard_map/ppermute | solution.py:458
  8.1 1.6 collective-permute-start.3
  9.7 1.5 collective-permute-start.5
  11.2 1.5 collective-permute-start.4
  12.7 1.2 collective-permute-start.1
  13.9 9.1 %collective-permute-done.refs_0_ = bf16[672,384]{1,0:T(8,128)(2,1)S(1)} collective-permute-done((bf16[672,384]{1,0:T(8,128)(2,1)}, bf16[672,384]{1,0:T(8,128)(2,1)S(1)}, u32[]{:S(2)}, u32[]{:S(2)}) %collective-permute-start) | collective-permute-done | bytes 516128 | tf_op jit(solution)/shard_map/ppermute | solution.py:458
  23.1 10.5 %collective-permute-done.3.refs_5_.refs_1_ = bf16[160,1536]{1,0:T(8,128)(2,1)S(1)} collective-permute-done((bf16[160,1536]{1,0:T(8,128)(2,1)S(1)}, bf16[160,1536]{1,0:T(8,128)(2,1)S(1)}, u32[]{:S(2)}, u32[]{:S(2)}) %collective-permute-start.3) | collective-permute-done | bytes 491552 | tf_op jit(solution)/shard_map/ppermute | solution.py:489
  33.5 0.0 collective-permute-done.5.refs_8_.refs_4_
  33.5 1.8 collective-permute-start.8
  35.3 9.4 %collective-permute-start.6 = (bf16[160,1536]{1,0:T(8,128)(2,1)S(1)}, bf16[160,1536]{1,0:T(8,128)(2,1)S(1)}, u32[]{:S(2)}, u32[]{:S(2)}) collective-permute-start(bf16[160,1536]{1,0:T(8,128)(2,1)S(1)} %collective-permute-done.3.refs_5_.refs_1_), channel_id=1, source_target_pairs={{0,8},{2,10},{4,12},{6,14},{8,16},{10,18},{12,20},{14,22},{16,24},... | collective-permute-start | bytes 1474568 | tf_op jit(solution)/shard_map/ppermute | solution.py:489
  44.7 1.5 collective-permute-start.7
  46.2 19.2 %collective-permute-done.1.refs_1_ = bf16[672,384]{1,0:T(8,128)(2,1)S(1)} collective-permute-done((bf16[672,384]{1,0:T(8,128)(2,1)}, bf16[672,384]{1,0:T(8,128)(2,1)S(1)}, u32[]{:S(2)}, u32[]{:S(2)}) %collective-permute-start.1) | collective-permute-done | bytes 516128 | tf_op jit(solution)/shard_map/ppermute | solution.py:458
  65.4 0.0 collective-permute-done.7.refs_1_
  65.5 1.6 collective-permute-start.11
  67.1 9.6 %collective-permute-start.9 = (bf16[160,1536]{1,0:T(8,128)(2,1)S(1)}, bf16[160,1536]{1,0:T(8,128)(2,1)S(1)}, u32[]{:S(2)}, u32[]{:S(2)}) collective-permute-start(bf16[160,1536]{1,0:T(8,128)(2,1)S(1)} %collective-permute-done.6.refs_6_.refs_2_), channel_id=1, source_target_pairs={{0,8},{2,10},{4,12},{6,14},{8,16},{10,18},{12,20},{14,22},{16,24},... | collective-permute-start | bytes 1474568 | tf_op jit(solution)/shard_map/ppermute | solution.py:489
  76.7 1.5 collective-permute-start.10
  78.2 7.9 %collective-permute-done.10.refs_2_ = bf16[512,384]{1,0:T(8,128)(2,1)S(1)} collective-permute-done((bf16[512,384]{1,0:T(8,128)(2,1)S(1)}, bf16[512,384]{1,0:T(8,128)(2,1)S(1)}, u32[]{:S(2)}, u32[]{:S(2)}) %collective-permute-start.10) | collective-permute-done | bytes 393248 | tf_op jit(solution)/shard_map/ppermute | solution.py:486
  86.1 1.5 collective-permute-start.12
  87.6 0.7 stack.18.refs_0_.refs_5_
  88.3 0.0 copy-start.2
  88.3 0.1 collective-permute-start.13
  88.4 6.4 %collective-permute-done.12.refs_3_ = bf16[512,384]{1,0:T(8,128)(2,1)S(1)} collective-permute-done((bf16[512,384]{1,0:T(8,128)(2,1)S(1)}, bf16[512,384]{1,0:T(8,128)(2,1)S(1)}, u32[]{:S(2)}, u32[]{:S(2)}) %collective-permute-start.12) | collective-permute-done | bytes 393248 | tf_op jit(solution)/shard_map/ppermute | solution.py:486
  94.8 0.7 stack.19.refs_1_.refs_6_
  95.5 0.1 collective-permute-start.14
  95.6 0.6 collective-permute-start.15
  96.1 0.6 stack_queries.1.q_in.refs_0_
  96.7 2.2 %collective-permute-done.14.refs_3_.refs_8_ = bf16[2048,384]{1,0:T(8,128)(2,1)S(1)} collective-permute-done((bf16[2048,384]{1,0:T(8,128)(2,1)S(1)}, bf16[2048,384]{1,0:T(8,128)(2,1)S(1)}, u32[]{:S(2)}, u32[]{:S(2)}) %collective-permute-start.14) | collective-permute-done | bytes 1572896 | tf_op jit(solution)/shard_map/ppermute | solution.py:497
  99.0 10.2 %forward.1 = (bf16[3,2560,640]{2,1,0:T(8,128)(2,1)S(1)}, bf16[640,384]{1,0:T(8,128)(2,1)S(1)}, f32[3,1,640]{2,1,0:T(1,128)S(1)}) custom-call(bf16[640,384]{1,0:T(8,128)(2,1)S(1)} %stack_queries.1.q_in.refs_0_, bf16[2048,384]{1,0:T(8,128)(2,1)S(1)} %stack.18.refs_0_.refs_5_, bf16[2048,384]{1,0:T(8,128)(2,1)S(1)} %stack.19.refs_1_.refs_6_, ...), custom_call_target="tpu_custom_call" | custom-call | flops 2516582400 | bytes 9830400 | tf_op jit(solution)/shard_map/forward/pallas_call | solution.py:200
  109.2 3.0 %attn_gradient.1.refs_4_ = bf16[640,384]{1,0:T(8,128)(2,1)S(1)} custom-call(s32[3]{0:T(128)S(1)} %copy-done.3, bf16[2048,384]{1,0:T(8,128)(2,1)S(1)} %stack.18.refs_0_.refs_5_, bf16[2048,384]{1,0:T(8,128)(2,1)S(1)} %stack.19.refs_1_.refs_6_, bf16[2048,384]{1,0:T(8,128)(2,1)S(1)} %collective-permute-done.13.refs_2_.refs_7_, ...), custom_call_target="tpu_custom_call" | custom-call | flops 245760 | bytes 491520 | tf_op jit(solution)/shard_map/attn_gradient/pallas_call | solution.py:75
  112.2 3.9 %backward.2 = (bf16[160,128]{1,0:T(8,128)(2,1)S(1)}, bf16[160,128]{1,0:T(8,128)(2,1)S(1)}, bf16[160,128]{1,0:T(8,128)(2,1)S(1)}, bf16[160,128]{1,0:T(8,128)(2,1)...) custom-call(bf16[640,384]{1,0:T(8,128)(2,1)S(1)} %stack_queries.1.q_in.refs_0_, ...), custom_call_target="tpu_custom_call" | custom-call | flops 81920 | bytes 163840 | tf_op jit(solution)/shard_map/backward/pallas_call | solution.py:264
  116.1 0.2 collective-permute-start.16
  116.3 2.0 %collective-permute-done.16.other = bf16[2560,128]{1,0:T(8,128)(2,1)S(1)} collective-permute-done((bf16[2560,128]{1,0:T(8,128)(2,1)S(1)}, bf16[2560,128]{1,0:T(8,128)(2,1)S(1)}, u32[]{:S(2)}, u32[]{:S(2)}) %collective-permute-start.16) | collective-permute-done | bytes 655392 | tf_op jit(solution)/shard_map/ppermute | solution.py:389
  118.3 0.7 add_parts.4
  119.0 1.6 collective-permute-start.17
  120.5 8.8 %backward.3 = (bf16[160,256]{1,0:T(8,128)(2,1)S(1)}, bf16[160,256]{1,0:T(8,128)(2,1)S(1)}, bf16[160,256]{1,0:T(8,128)(2,1)S(1)}, bf16[160,256]{1,0:T(8,128)(2,1)...) custom-call(bf16[640,384]{1,0:T(8,128)(2,1)S(1)} %stack_queries.1.q_in.refs_0_, ...), custom_call_target="tpu_custom_call" | custom-call | flops 81920 | bytes 163840 | tf_op jit(solution)/shard_map/backward/pallas_call | solution.py:264
  129.4 0.1 collective-permute-start.18
  129.4 0.6 finish.2
  130.1 3.2 %proj_gradient.1 = (bf16[1536,384]{1,0:T(8,128)(2,1)S(1)}, bf16[1536,384]{1,0:T(8,128)(2,1)S(1)}) custom-call(s32[3]{0:T(128)S(1)} %copy-done.3, bf16[640,384]{1,0:T(8,128)(2,1)S(1)} %get-tuple-element.119.refs_2_.attn, bf16[160,1536]{1,0:T(8,128)(2,1)S(1)} %copy-done, bf16[160,1536]{1,0:T(8,128)(2,1)S(1)} %collective-permute-done.3.refs_5_.refs_1_, ...), custom_call_target="tpu_custom_call" | custom-call | flops 245760 | bytes 491520 | tf_op jit(solution)/shard_map/proj_gradient/pallas_call | solution.py:75
  133.3 0.6 collective-permute-start.20
  133.9 0.8 add_parts.5
  134.7 0.9 collective-permute-start.19
  135.7 4.4 %collective-permute-start.21 = (bf16[480,128]{1,0:T(8,128)(2,1)S(1)}, bf16[480,128]{1,0:T(8,128)(2,1)S(1)}, u32[]{:S(2)}, u32[]{:S(2)}) collective-permute-start(bf16[480,128]{1,0:T(8,128)(2,1)S(1)} %get-tuple-element.116), channel_id=1, source_target_pairs={{0,24},{2,26},{4,28},{6,30},{8,0},{10,2},{12,4},{14,6},{16,8},{18,... | collective-permute-start | bytes 368648 | tf_op jit(solution)/shard_map/ppermute | solution.py:458
  140.0 0.9 collective-permute-start.22
  140.9 1.1 collective-permute-start.23
  142.1 0.8 add_parts.6
  142.9 0.9 collective-permute-done.21.refs_1_
  143.8 8.0 %collective-permute-done.22.refs_2_ = bf16[480,128]{1,0:T(8,128)(2,1)S(1)} collective-permute-done((bf16[480,128]{1,0:T(8,128)(2,1)S(1)}, bf16[480,128]{1,0:T(8,128)(2,1)S(1)}, u32[]{:S(2)}, u32[]{:S(2)}) %collective-permute-start.22) | collective-permute-done | bytes 122912 | tf_op jit(solution)/shard_map/ppermute | solution.py:458
  151.8 1.2 collective-permute-start.27
  153.0 0.7 finish.3
  153.7 3.8 %collective-permute-start.24 = (bf16[480,256]{1,0:T(8,128)(2,1)S(1)}, bf16[480,256]{1,0:T(8,128)(2,1)S(1)}, u32[]{:S(2)}, u32[]{:S(2)}) collective-permute-start(bf16[480,256]{1,0:T(8,128)(2,1)S(1)} %get-tuple-element.134), channel_id=1, source_target_pairs={{0,24},{2,26},{4,28},{6,30},{8,0},{10,2},{12,4},{14,6},{16,8},{18,... | collective-permute-start | bytes 737288 | tf_op jit(solution)/shard_map/ppermute | solution.py:458
  157.5 0.9 collective-permute-start.25
  158.4 1.1 collective-permute-start.26
  159.5 6.7 %collective-permute-done.27.other = bf16[768,384]{1,0:T(8,128)(2,1)S(1)} collective-permute-done((bf16[768,384]{1,0:T(8,128)(2,1)S(1)}, bf16[768,384]{1,0:T(8,128)(2,1)S(1)}, u32[]{:S(2)}, u32[]{:S(2)}) %collective-permute-start.27) | collective-permute-done | bytes 589856 | tf_op jit(solution)/shard_map/ppermute | solution.py:507
  166.2 0.7 add_parts.7
  166.9 3.6 %collective-permute-start.28 = (bf16[192,384]{1,0:T(8,128)(2,1)S(1)}, bf16[192,384]{1,0:T(8,128)(2,1)S(1)}, u32[]{:S(2)}, u32[]{:S(2)}) collective-permute-start(bf16[192,384]{1,0:T(8,128)(2,1)S(1)} %get-tuple-element.143), channel_id=1, source_target_pairs={{0,8},{2,10},{4,12},{6,14},{8,16},{10,18},{12,20},{14,22},{16,24},... | collective-permute-start | bytes 442376 | tf_op jit(solution)/shard_map/ppermute | solution.py:458
  170.5 1.1 collective-permute-start.29
  171.6 2.4 %collective-permute-start.30 = (bf16[192,384]{1,0:T(8,128)(2,1)S(1)}, bf16[192,384]{1,0:T(8,128)(2,1)S(1)}, u32[]{:S(2)}, u32[]{:S(2)}) collective-permute-start(bf16[192,384]{1,0:T(8,128)(2,1)S(1)} %get-tuple-element.145), channel_id=1, source_target_pairs={{0,24},{2,26},{4,28},{6,30},{8,0},{10,2},{12,4},{14,6},{16,8},{18,... | collective-permute-start | bytes 442376 | tf_op jit(solution)/shard_map/ppermute | solution.py:458
  173.9 13.5 %collective-permute-done.25.refs_6_ = bf16[480,256]{1,0:T(8,128)(2,1)S(1)} collective-permute-done((bf16[480,256]{1,0:T(8,128)(2,1)S(1)}, bf16[480,256]{1,0:T(8,128)(2,1)S(1)}, u32[]{:S(2)}, u32[]{:S(2)}) %collective-permute-start.25) | collective-permute-done | bytes 245792 | tf_op jit(solution)/shard_map/ppermute | solution.py:458
  187.4 1.8 unpack.1
  189.3 0.8 collective-permute-done.29.refs_2_
  190.0 1.7 join.1
  (27 shorter events, 0.2 us)
Async XLA Ops:
  0.6 7.5 %copy-start = (bf16[160,1536]{1,0:T(8,128)(2,1)S(1)}, bf16[160,1536]{1,0:T(8,128)(2,1)}, u32[]{:S(2)}) copy-start(bf16[160,1536]{1,0:T(8,128)(2,1)} %refs_0_) | copy-start | bytes 1474564
  5.0 82.6 %copy-start.1 = (bf16[512,384]{1,0:T(8,128)(2,1)S(1)}, bf16[512,384]{1,0:T(8,128)(2,1)}, u32[]{:S(2)}) copy-start(bf16[512,384]{1,0:T(8,128)(2,1)} %get-tuple-element.79.refs_0_) | copy-start | bytes 1179652
  5.0 82.6 %copy-start.3 = (s32[3]{0:T(128)S(1)}, s32[3]{0:T(128)}, u32[]{:S(2)}) copy-start(s32[3]{0:T(128)} %pad_add_fusion.ids) | copy-start | bytes 40
  5.0 18.0 %collective-permute-start = (bf16[672,384]{1,0:T(8,128)(2,1)}, bf16[672,384]{1,0:T(8,128)(2,1)S(1)}, u32[]{:S(2)}, u32[]{:S(2)}) collective-permute-start(bf16[672,384]{1,0:T(8,128)(2,1)} %get-tuple-element.76), channel_id=1, source_target_pairs={{0,8},{2,10},{4,12},{6,14},{8,16},{10,18},{12,20},{14,22},{16,24},... | collective-permute-start | bytes 1548296 | tf_op jit(solution)/shard_map/ppermute | solution.py:458
  8.1 25.4 %collective-permute-start.3 = (bf16[160,1536]{1,0:T(8,128)(2,1)S(1)}, bf16[160,1536]{1,0:T(8,128)(2,1)S(1)}, u32[]{:S(2)}, u32[]{:S(2)}) collective-permute-start(bf16[160,1536]{1,0:T(8,128)(2,1)S(1)} %copy-done), channel_id=1, source_target_pairs={{0,8},{2,10},{4,12},{6,14},{8,16},{10,18},{12,20},{14,22},{16,24},... | collective-permute-start | bytes 1474568 | tf_op jit(solution)/shard_map/ppermute | solution.py:489
  9.7 23.9 %collective-permute-start.5 = (bf16[160,1536]{1,0:T(8,128)(2,1)S(1)}, bf16[160,1536]{1,0:T(8,128)(2,1)S(1)}, u32[]{:S(2)}, u32[]{:S(2)}) collective-permute-start(bf16[160,1536]{1,0:T(8,128)(2,1)S(1)} %copy-done), channel_id=1, source_target_pairs={{0,1},{1,0},{2,3},{3,2},{4,5},{5,4},{6,7},{7,6},{8,9},{9,8},{10,11... | collective-permute-start | bytes 1474568 | tf_op jit(solution)/shard_map/ppermute | solution.py:49
  11.2 11.9 %collective-permute-start.4 = (bf16[512,384]{1,0:T(8,128)(2,1)}, bf16[512,384]{1,0:T(8,128)(2,1)S(1)}, u32[]{:S(2)}, u32[]{:S(2)}) collective-permute-start(bf16[512,384]{1,0:T(8,128)(2,1)} %get-tuple-element.79.refs_0_), channel_id=1, source_target_pairs={{0,4},{2,6},{4,0},{6,2},{8,12},{10,14},{12,8},{14,10},{16,20},{18,... | collective-permute-start | bytes 1179656 | tf_op jit(solution)/shard_map/ppermute | solution.py:486
  12.7 52.7 %collective-permute-start.1 = (bf16[672,384]{1,0:T(8,128)(2,1)}, bf16[672,384]{1,0:T(8,128)(2,1)S(1)}, u32[]{:S(2)}, u32[]{:S(2)}) collective-permute-start(bf16[672,384]{1,0:T(8,128)(2,1)} %get-tuple-element.77), channel_id=1, source_target_pairs={{0,16},{2,18},{4,20},{6,22},{8,24},{10,26},{12,28},{14,30},{16,0},... | collective-permute-start | bytes 1548296 | tf_op jit(solution)/shard_map/ppermute | solution.py:458
  33.5 31.9 %collective-permute-start.8 = (bf16[160,1536]{1,0:T(8,128)(2,1)S(1)}, bf16[160,1536]{1,0:T(8,128)(2,1)S(1)}, u32[]{:S(2)}, u32[]{:S(2)}) collective-permute-start(bf16[160,1536]{1,0:T(8,128)(2,1)S(1)} %collective-permute-done.3.refs_5_.refs_1_), channel_id=1, source_target_pairs={{0,1},{1,0},{2,3},{3,2},{4,5},{5,4},{6,7},{7,6},{8,9},{9,8},{10,11... | collective-permute-start | bytes 1474568 | tf_op jit(solution)/shard_map/ppermute | solution.py:49
  35.3 30.2 %collective-permute-start.6 = (bf16[160,1536]{1,0:T(8,128)(2,1)S(1)}, bf16[160,1536]{1,0:T(8,128)(2,1)S(1)}, u32[]{:S(2)}, u32[]{:S(2)}) collective-permute-start(bf16[160,1536]{1,0:T(8,128)(2,1)S(1)} %collective-permute-done.3.refs_5_.refs_1_), channel_id=1, source_target_pairs={{0,8},{2,10},{4,12},{6,14},{8,16},{10,18},{12,20},{14,22},{16,24},... | collective-permute-start | bytes 1474568 | tf_op jit(solution)/shard_map/ppermute | solution.py:489
  44.7 20.7 %collective-permute-start.7 = (bf16[512,384]{1,0:T(8,128)(2,1)S(1)}, bf16[512,384]{1,0:T(8,128)(2,1)S(1)}, u32[]{:S(2)}, u32[]{:S(2)}) collective-permute-start(bf16[512,384]{1,0:T(8,128)(2,1)S(1)} %slice.12.refs_1_), channel_id=1, source_target_pairs={{0,4},{2,6},{4,0},{6,2},{8,12},{10,14},{12,8},{14,10},{16,20},{18,... | collective-permute-start | bytes 1179656 | tf_op jit(solution)/shard_map/ppermute | solution.py:486
  46.2 32.0 %collective-permute-start.2 = (bf16[672,384]{1,0:T(8,128)(2,1)}, bf16[672,384]{1,0:T(8,128)(2,1)S(1)}, u32[]{:S(2)}, u32[]{:S(2)}) collective-permute-start(bf16[672,384]{1,0:T(8,128)(2,1)} %get-tuple-element.78), channel_id=1, source_target_pairs={{0,24},{2,26},{4,28},{6,30},{8,0},{10,2},{12,4},{14,6},{16,8},{18,... | collective-permute-start | bytes 1548296 | tf_op jit(solution)/shard_map/ppermute | solution.py:458
  65.5 20.6 %collective-permute-start.11 = (bf16[160,1536]{1,0:T(8,128)(2,1)S(1)}, bf16[160,1536]{1,0:T(8,128)(2,1)S(1)}, u32[]{:S(2)}, u32[]{:S(2)}) collective-permute-start(bf16[160,1536]{1,0:T(8,128)(2,1)S(1)} %collective-permute-done.6.refs_6_.refs_2_), channel_id=1, source_target_pairs={{0,1},{1,0},{2,3},{3,2},{4,5},{5,4},{6,7},{7,6},{8,9},{9,8},{10,11... | collective-permute-start | bytes 1474568 | tf_op jit(solution)/shard_map/ppermute | solution.py:49
  67.1 19.1 %collective-permute-start.9 = (bf16[160,1536]{1,0:T(8,128)(2,1)S(1)}, bf16[160,1536]{1,0:T(8,128)(2,1)S(1)}, u32[]{:S(2)}, u32[]{:S(2)}) collective-permute-start(bf16[160,1536]{1,0:T(8,128)(2,1)S(1)} %collective-permute-done.6.refs_6_.refs_2_), channel_id=1, source_target_pairs={{0,8},{2,10},{4,12},{6,14},{8,16},{10,18},{12,20},{14,22},{16,24},... | collective-permute-start | bytes 1474568 | tf_op jit(solution)/shard_map/ppermute | solution.py:489
  76.7 9.4 %collective-permute-start.10 = (bf16[512,384]{1,0:T(8,128)(2,1)S(1)}, bf16[512,384]{1,0:T(8,128)(2,1)S(1)}, u32[]{:S(2)}, u32[]{:S(2)}) collective-permute-start(bf16[512,384]{1,0:T(8,128)(2,1)S(1)} %slice.13.refs_2_), channel_id=1, source_target_pairs={{0,4},{2,6},{4,0},{6,2},{8,12},{10,14},{12,8},{14,10},{16,20},{18,... | collective-permute-start | bytes 1179656 | tf_op jit(solution)/shard_map/ppermute | solution.py:486
  86.1 8.7 %collective-permute-start.12 = (bf16[512,384]{1,0:T(8,128)(2,1)S(1)}, bf16[512,384]{1,0:T(8,128)(2,1)S(1)}, u32[]{:S(2)}, u32[]{:S(2)}) collective-permute-start(bf16[512,384]{1,0:T(8,128)(2,1)S(1)} %slice.14.refs_3_), channel_id=1, source_target_pairs={{0,4},{2,6},{4,0},{6,2},{8,12},{10,14},{12,8},{14,10},{16,20},{18,... | collective-permute-start | bytes 1179656 | tf_op jit(solution)/shard_map/ppermute | solution.py:486
  88.3 7.8 %copy-start.2 = (bf16[160,384]{1,0:T(8,128)(2,1)S(1)}, bf16[160,384]{1,0:T(8,128)(2,1)}, u32[]{:S(2)}) copy-start(bf16[160,384]{1,0:T(8,128)(2,1)} %get-tuple-element.75.own) | copy-start | bytes 368644
  88.3 8.4 %collective-permute-start.13 = (bf16[2048,384]{1,0:T(8,128)(2,1)S(1)}, bf16[2048,384]{1,0:T(8,128)(2,1)S(1)}, u32[]{:S(2)}, u32[]{:S(2)}) collective-permute-start(bf16[2048,384]{1,0:T(8,128)(2,1)S(1)} %stack.18.refs_0_.refs_5_), channel_id=1, source_target_pairs={{0,2},{2,0},{4,6},{6,4},{8,10},{10,8},{12,14},{14,12},{16,18},{18,... | collective-permute-start | bytes 4718600 | tf_op jit(solution)/shard_map/ppermute | solution.py:497
  95.5 3.5 %collective-permute-start.14 = (bf16[2048,384]{1,0:T(8,128)(2,1)S(1)}, bf16[2048,384]{1,0:T(8,128)(2,1)S(1)}, u32[]{:S(2)}, u32[]{:S(2)}) collective-permute-start(bf16[2048,384]{1,0:T(8,128)(2,1)S(1)} %stack.19.refs_1_.refs_6_), channel_id=1, source_target_pairs={{0,2},{2,0},{4,6},{6,4},{8,10},{10,8},{12,14},{14,12},{16,18},{18,... | collective-permute-start | bytes 4718600 | tf_op jit(solution)/shard_map/ppermute | solution.py:497
  95.6 13.6 %collective-permute-start.15 = (bf16[160,1536]{1,0:T(8,128)(2,1)S(1)}, bf16[160,1536]{1,0:T(8,128)(2,1)S(1)}, u32[]{:S(2)}, u32[]{:S(2)}) collective-permute-start(bf16[160,1536]{1,0:T(8,128)(2,1)S(1)} %collective-permute-done.9.refs_7_.refs_3_), channel_id=1, source_target_pairs={{0,1},{1,0},{2,3},{3,2},{4,5},{5,4},{6,7},{7,6},{8,9},{9,8},{10,11... | collective-permute-start | bytes 1474568 | tf_op jit(solution)/shard_map/ppermute | solution.py:49
  116.1 2.2 %collective-permute-start.16 = (bf16[2560,128]{1,0:T(8,128)(2,1)S(1)}, bf16[2560,128]{1,0:T(8,128)(2,1)S(1)}, u32[]{:S(2)}, u32[]{:S(2)}) collective-permute-start(bf16[2560,128]{1,0:T(8,128)(2,1)S(1)} %get-tuple-element.99), channel_id=1, source_target_pairs={{0,2},{2,0},{4,6},{6,4},{8,10},{10,8},{12,14},{14,12},{16,18},{18,... | collective-permute-start | bytes 1966088 | tf_op jit(solution)/shard_map/ppermute | solution.py:389
  119.0 10.4 %collective-permute-start.17 = (bf16[1280,128]{1,0:T(8,128)(2,1)S(1)}, bf16[1280,128]{1,0:T(8,128)(2,1)S(1)}, u32[]{:S(2)}, u32[]{:S(2)}) collective-permute-start(bf16[1280,128]{1,0:T(8,128)(2,1)S(1)} %get-tuple-element.103), channel_id=1, source_target_pairs={{0,4},{2,6},{4,0},{6,2},{8,12},{10,14},{12,8},{14,10},{16,20},{18,... | collective-permute-start | bytes 983048 | tf_op jit(solution)/shard_map/ppermute | solution.py:507
  129.4 4.5 %collective-permute-start.18 = (bf16[2560,256]{1,0:T(8,128)(2,1)S(1)}, bf16[2560,256]{1,0:T(8,128)(2,1)S(1)}, u32[]{:S(2)}, u32[]{:S(2)}) collective-permute-start(bf16[2560,256]{1,0:T(8,128)(2,1)S(1)} %get-tuple-element.114), channel_id=1, source_target_pairs={{0,2},{2,0},{4,6},{6,4},{8,10},{10,8},{12,14},{14,12},{16,18},{18,... | collective-permute-start | bytes 3932168 | tf_op jit(solution)/shard_map/ppermute | solution.py:389
  133.3 8.7 %collective-permute-start.20 = (bf16[1536,384]{1,0:T(8,128)(2,1)S(1)}, bf16[1536,384]{1,0:T(8,128)(2,1)S(1)}, u32[]{:S(2)}, u32[]{:S(2)}) collective-permute-start(bf16[1536,384]{1,0:T(8,128)(2,1)S(1)} %get-tuple-element.121), channel_id=1, source_target_pairs={{0,2},{2,0},{4,6},{6,4},{8,10},{10,8},{12,14},{14,12},{16,18},{18,... | collective-permute-start | bytes 3538952 | tf_op jit(solution)/shard_map/ppermute | solution.py:389
  134.7 17.1 %collective-permute-start.19 = (bf16[1280,256]{1,0:T(8,128)(2,1)S(1)}, bf16[1280,256]{1,0:T(8,128)(2,1)S(1)}, u32[]{:S(2)}, u32[]{:S(2)}) collective-permute-start(bf16[1280,256]{1,0:T(8,128)(2,1)S(1)} %get-tuple-element.115), channel_id=1, source_target_pairs={{0,4},{2,6},{4,0},{6,2},{8,12},{10,14},{12,8},{14,10},{16,20},{18,... | collective-permute-start | bytes 1966088 | tf_op jit(solution)/shard_map/ppermute | solution.py:507
  135.7 8.2 %collective-permute-start.21 = (bf16[480,128]{1,0:T(8,128)(2,1)S(1)}, bf16[480,128]{1,0:T(8,128)(2,1)S(1)}, u32[]{:S(2)}, u32[]{:S(2)}) collective-permute-start(bf16[480,128]{1,0:T(8,128)(2,1)S(1)} %get-tuple-element.116), channel_id=1, source_target_pairs={{0,24},{2,26},{4,28},{6,30},{8,0},{10,2},{12,4},{14,6},{16,8},{18,... | collective-permute-start | bytes 368648 | tf_op jit(solution)/shard_map/ppermute | solution.py:458
  140.0 11.7 %collective-permute-start.22 = (bf16[480,128]{1,0:T(8,128)(2,1)S(1)}, bf16[480,128]{1,0:T(8,128)(2,1)S(1)}, u32[]{:S(2)}, u32[]{:S(2)}) collective-permute-start(bf16[480,128]{1,0:T(8,128)(2,1)S(1)} %get-tuple-element.117), channel_id=1, source_target_pairs={{0,16},{2,18},{4,20},{6,22},{8,24},{10,26},{12,28},{14,30},{16,0},... | collective-permute-start | bytes 368648 | tf_op jit(solution)/shard_map/ppermute | solution.py:458
  140.9 10.8 %collective-permute-start.23 = (bf16[480,128]{1,0:T(8,128)(2,1)S(1)}, bf16[480,128]{1,0:T(8,128)(2,1)S(1)}, u32[]{:S(2)}, u32[]{:S(2)}) collective-permute-start(bf16[480,128]{1,0:T(8,128)(2,1)S(1)} %get-tuple-element.118), channel_id=1, source_target_pairs={{0,8},{2,10},{4,12},{6,14},{8,16},{10,18},{12,20},{14,22},{16,24},... | collective-permute-start | bytes 368648 | tf_op jit(solution)/shard_map/ppermute | solution.py:458
  151.8 14.4 %collective-permute-start.27 = (bf16[768,384]{1,0:T(8,128)(2,1)S(1)}, bf16[768,384]{1,0:T(8,128)(2,1)S(1)}, u32[]{:S(2)}, u32[]{:S(2)}) collective-permute-start(bf16[768,384]{1,0:T(8,128)(2,1)S(1)} %get-tuple-element.141), channel_id=1, source_target_pairs={{0,4},{2,6},{4,0},{6,2},{8,12},{10,14},{12,8},{14,10},{16,20},{18,... | collective-permute-start | bytes 1769480 | tf_op jit(solution)/shard_map/ppermute | solution.py:507
  153.7 17.9 %collective-permute-start.24 = (bf16[480,256]{1,0:T(8,128)(2,1)S(1)}, bf16[480,256]{1,0:T(8,128)(2,1)S(1)}, u32[]{:S(2)}, u32[]{:S(2)}) collective-permute-start(bf16[480,256]{1,0:T(8,128)(2,1)S(1)} %get-tuple-element.134), channel_id=1, source_target_pairs={{0,24},{2,26},{4,28},{6,30},{8,0},{10,2},{12,4},{14,6},{16,8},{18,... | collective-permute-start | bytes 737288 | tf_op jit(solution)/shard_map/ppermute | solution.py:458
  157.5 30.0 %collective-permute-start.25 = (bf16[480,256]{1,0:T(8,128)(2,1)S(1)}, bf16[480,256]{1,0:T(8,128)(2,1)S(1)}, u32[]{:S(2)}, u32[]{:S(2)}) collective-permute-start(bf16[480,256]{1,0:T(8,128)(2,1)S(1)} %get-tuple-element.135), channel_id=1, source_target_pairs={{0,16},{2,18},{4,20},{6,22},{8,24},{10,26},{12,28},{14,30},{16,0},... | collective-permute-start | bytes 737288 | tf_op jit(solution)/shard_map/ppermute | solution.py:458
  158.4 29.1 %collective-permute-start.26 = (bf16[480,256]{1,0:T(8,128)(2,1)S(1)}, bf16[480,256]{1,0:T(8,128)(2,1)S(1)}, u32[]{:S(2)}, u32[]{:S(2)}) collective-permute-start(bf16[480,256]{1,0:T(8,128)(2,1)S(1)} %get-tuple-element.136), channel_id=1, source_target_pairs={{0,8},{2,10},{4,12},{6,14},{8,16},{10,18},{12,20},{14,22},{16,24},... | collective-permute-start | bytes 737288 | tf_op jit(solution)/shard_map/ppermute | solution.py:458
  166.9 22.4 %collective-permute-start.28 = (bf16[192,384]{1,0:T(8,128)(2,1)S(1)}, bf16[192,384]{1,0:T(8,128)(2,1)S(1)}, u32[]{:S(2)}, u32[]{:S(2)}) collective-permute-start(bf16[192,384]{1,0:T(8,128)(2,1)S(1)} %get-tuple-element.143), channel_id=1, source_target_pairs={{0,8},{2,10},{4,12},{6,14},{8,16},{10,18},{12,20},{14,22},{16,24},... | collective-permute-start | bytes 442376 | tf_op jit(solution)/shard_map/ppermute | solution.py:458
  170.5 19.6 %collective-permute-start.29 = (bf16[192,384]{1,0:T(8,128)(2,1)S(1)}, bf16[192,384]{1,0:T(8,128)(2,1)S(1)}, u32[]{:S(2)}, u32[]{:S(2)}) collective-permute-start(bf16[192,384]{1,0:T(8,128)(2,1)S(1)} %get-tuple-element.144), channel_id=1, source_target_pairs={{0,16},{2,18},{4,20},{6,22},{8,24},{10,26},{12,28},{14,30},{16,0},... | collective-permute-start | bytes 442376 | tf_op jit(solution)/shard_map/ppermute | solution.py:458
  171.6 18.5 %collective-permute-start.30 = (bf16[192,384]{1,0:T(8,128)(2,1)S(1)}, bf16[192,384]{1,0:T(8,128)(2,1)S(1)}, u32[]{:S(2)}, u32[]{:S(2)}) collective-permute-start(bf16[192,384]{1,0:T(8,128)(2,1)S(1)} %get-tuple-element.145), channel_id=1, source_target_pairs={{0,24},{2,26},{4,28},{6,30},{8,0},{10,2},{12,4},{14,6},{16,8},{18,... | collective-permute-start | bytes 442376 | tf_op jit(solution)/shard_map/ppermute | solution.py:458

commit v12 on v11

--- a/solution.py
+++ b/solution.py
@@ -426,7 +426,7 @@
 
 
 def unpack(ids, chunks, rows, gw, n_groups):
-    widths = [HD, gw - HD][: len(chunks)]
+    widths = [max(HD, gw - HD), HD][: len(chunks)]
     return whole_call(
         functools.partial(unpack_kernel, n_groups, widths),
         [jax.ShapeDtypeStruct((rows, gw * n_groups), BF16)] * 3,
@@ -506,12 +506,12 @@
     def across_x(piece):
         return lax.ppermute(piece, "frame", last)
 
-    dq, halves = attention_halves(0, 1, q)
+    dq, halves = attention_halves(0, max(1, heads - 1), q)
     kept, sent = halve(ids, *halves, n_frame, tok_bits)
     q, kept, sent = tie((q, kept, sent))
     other = across_x(sent)
     if heads > 1:
-        dq_rest, halves = attention_halves(1, heads - 1, q)
+        dq_rest, halves = attention_halves(heads - 1, 1, q)
         other, *halves = tie((other, *halves))
     sums = finish(ids, kept, other, dq, n_groups)
     returned = [exchange(sums, n_groups, n_tok, -1)]

time: 192 us -> 220 us (1.15)
  waiting for transfers between devices: 87.1 us -> 122 us
  starting transfers between devices: 60.2 us -> 54 us
    ppermute x3, waiting for transfers between devices: 6.7 us -> 24.4 us  [across_x(): return lax.ppermute(piece, 'frame', last)]
    ppermute x12, waiting for transfers between devices: 51.4 us -> 64.2 us  [exchange(): lax.ppermute(pieces[s], 'frame', shift_pairs(n_groups, n_tok, sign * s))]
    ppermute x12, starting transfers between devices: 23.6 us -> 17.4 us  [exchange(): lax.ppermute(pieces[s], 'frame', shift_pairs(n_groups, n_tok, sign * s))]
    ppermute x3, waiting for transfers between devices: 1.97 us -> 6.18 us  [halve(): other = lax.ppermute(sent, 'frame', xor_pairs(n_frame, bit))]
  transfers between devices with their start and end apart: 31 -> 31, of which waited for: 12 -> 13; matrix products, arithmetic and copies ran while one was open for 0% -> 0% of each run, Pallas kernels for 16% -> 9%
where the time goes in v12:
time: 220 us
  waiting for transfers between devices  122 us (55%)
  starting transfers between devices  54 us (25%)
  Pallas kernels  42.9 us (20%)
    ppermute x12, waiting for transfers between devices, exchange(): lax.ppermute(pieces[s], 'frame', shift_pairs(n_groups, n_tok, sign * s))  64.2 us
    ppermute x3, waiting for transfers between devices, across_x(): return lax.ppermute(piece, 'frame', last)  24.4 us
    ppermute x3, starting transfers between devices, local(): ring = lax.ppermute(ring, 'frame', shift_pairs(n_groups, n_tok, 1))  20.6 us
    ppermute x12, starting transfers between devices, exchange(): lax.ppermute(pieces[s], 'frame', shift_pairs(n_groups, n_tok, sign * s))  17.4 us
    pallas_call x13, Pallas kernels, whole_call(): pl.pallas_call(body, out_shape=out_shape, in_specs=[smem()] + [vmem()] *...  16 us
    ppermute x4, waiting for transfers between devices, local(): others.append(lax.ppermute(own[s], 'frame', last))  14.3 us
    pallas_call x2, Pallas kernels, backward(): pl.pallas_call(functools.partial(backward_kernel, n_groups, chunk, 1.0 /...  12.9 us
    ppermute x3, waiting for transfers between devices, local(): ring = lax.ppermute(ring, 'frame', shift_pairs(n_groups, n_tok, 1))  10.5 us
  transfers between devices with their start and end apart: 31, of which 13 were waited for; matrix products, arithmetic and copies ran while one was open for 0% of the time, Pallas kernels for 9%

profile of v12, /device:TPU:0, one launch (start us, length us, event | category | flops | bytes accessed | tf_op | source)
XLA Modules:
  0.0 220.3 jit_solution(15622734575301510681)
XLA Ops:
  0.7 0.6 pad_add_fusion.ids
  1.3 3.7 %pack.1 = (bf16[512,384]{1,0:T(8,128)(2,1)}, bf16[672,384]{1,0:T(8,128)(2,1)}, bf16[672,384]{1,0:T(8,128)(2,1)}, bf16[672,384]{1,0:T(8,128)(2,1)}, bf16[160,384]{1,0:T(8,128)(2,1)}) custom-call(s32[3]{0:T(128)} %pad_add_fusion.ids, bf16[160,1536]{1,0:T(8,128)(2,1)} %q.1, bf16[160,1536]{1,0:T(8,128)(2,1)} %k.1, bf16[160,1536]{1,0:T(8,128)(2,1)} %v.1, ...), custom_call_target="tpu_custom_call" | custom-call | tf_op jit(solution)/shard_map/pack/pallas_call | solution.py:119
  5.0 0.0 copy-start.1
  5.0 3.1 %collective-permute-start = (bf16[672,384]{1,0:T(8,128)(2,1)}, bf16[672,384]{1,0:T(8,128)(2,1)S(1)}, u32[]{:S(2)}, u32[]{:S(2)}) collective-permute-start(bf16[672,384]{1,0:T(8,128)(2,1)} %get-tuple-element.76), channel_id=1, source_target_pairs={{0,8},{2,10},{4,12},{6,14},{8,16},{10,18},{12,20},{14,22},{16,24},... | collective-permute-start | bytes 1548296 | tf_op jit(solution)/shard_map/ppermute | solution.py:458
  8.1 1.6 collective-permute-start.3
  9.7 1.5 collective-permute-start.5
  11.2 1.5 collective-permute-start.4
  12.7 1.2 collective-permute-start.1
  13.9 9.1 %collective-permute-done.refs_0_ = bf16[672,384]{1,0:T(8,128)(2,1)S(1)} collective-permute-done((bf16[672,384]{1,0:T(8,128)(2,1)}, bf16[672,384]{1,0:T(8,128)(2,1)S(1)}, u32[]{:S(2)}, u32[]{:S(2)}) %collective-permute-start) | collective-permute-done | bytes 516128 | tf_op jit(solution)/shard_map/ppermute | solution.py:458
  23.1 10.5 %collective-permute-done.3.refs_5_.refs_1_ = bf16[160,1536]{1,0:T(8,128)(2,1)S(1)} collective-permute-done((bf16[160,1536]{1,0:T(8,128)(2,1)S(1)}, bf16[160,1536]{1,0:T(8,128)(2,1)S(1)}, u32[]{:S(2)}, u32[]{:S(2)}) %collective-permute-start.3) | collective-permute-done | bytes 491552 | tf_op jit(solution)/shard_map/ppermute | solution.py:489
  33.5 1.8 collective-permute-start.8
  35.3 9.4 %collective-permute-start.6 = (bf16[160,1536]{1,0:T(8,128)(2,1)S(1)}, bf16[160,1536]{1,0:T(8,128)(2,1)S(1)}, u32[]{:S(2)}, u32[]{:S(2)}) collective-permute-start(bf16[160,1536]{1,0:T(8,128)(2,1)S(1)} %collective-permute-done.3.refs_5_.refs_1_), channel_id=1, source_target_pairs={{0,8},{2,10},{4,12},{6,14},{8,16},{10,18},{12,20},{14,22},{16,24},... | collective-permute-start | bytes 1474568 | tf_op jit(solution)/shard_map/ppermute | solution.py:489
  44.7 1.5 collective-permute-start.7
  46.2 19.2 %collective-permute-done.1.refs_1_ = bf16[672,384]{1,0:T(8,128)(2,1)S(1)} collective-permute-done((bf16[672,384]{1,0:T(8,128)(2,1)}, bf16[672,384]{1,0:T(8,128)(2,1)S(1)}, u32[]{:S(2)}, u32[]{:S(2)}) %collective-permute-start.1) | collective-permute-done | bytes 516128 | tf_op jit(solution)/shard_map/ppermute | solution.py:458
  65.4 0.0 collective-permute-done.7.refs_1_
  65.5 0.0 collective-permute-done.6.refs_6_.refs_2_
  65.5 1.6 collective-permute-start.11
  67.1 9.6 %collective-permute-start.9 = (bf16[160,1536]{1,0:T(8,128)(2,1)S(1)}, bf16[160,1536]{1,0:T(8,128)(2,1)S(1)}, u32[]{:S(2)}, u32[]{:S(2)}) collective-permute-start(bf16[160,1536]{1,0:T(8,128)(2,1)S(1)} %collective-permute-done.6.refs_6_.refs_2_), channel_id=1, source_target_pairs={{0,8},{2,10},{4,12},{6,14},{8,16},{10,18},{12,20},{14,22},{16,24},... | collective-permute-start | bytes 1474568 | tf_op jit(solution)/shard_map/ppermute | solution.py:489
  76.7 1.5 collective-permute-start.10
  78.2 7.9 %collective-permute-done.10.refs_2_ = bf16[512,384]{1,0:T(8,128)(2,1)S(1)} collective-permute-done((bf16[512,384]{1,0:T(8,128)(2,1)S(1)}, bf16[512,384]{1,0:T(8,128)(2,1)S(1)}, u32[]{:S(2)}, u32[]{:S(2)}) %collective-permute-start.10) | collective-permute-done | bytes 393248 | tf_op jit(solution)/shard_map/ppermute | solution.py:486
  86.1 1.5 collective-permute-start.12
  87.6 0.7 stack.18.refs_0_.refs_5_
  88.3 0.0 copy-start.2
  88.3 0.1 collective-permute-start.13
  88.4 6.4 %collective-permute-done.12.refs_3_ = bf16[512,384]{1,0:T(8,128)(2,1)S(1)} collective-permute-done((bf16[512,384]{1,0:T(8,128)(2,1)S(1)}, bf16[512,384]{1,0:T(8,128)(2,1)S(1)}, u32[]{:S(2)}, u32[]{:S(2)}) %collective-permute-start.12) | collective-permute-done | bytes 393248 | tf_op jit(solution)/shard_map/ppermute | solution.py:486
  94.8 0.7 stack.19.refs_1_.refs_6_
  95.5 0.1 collective-permute-start.14
  95.6 0.6 collective-permute-start.15
  96.1 0.6 stack_queries.1.q_in.refs_0_
  96.7 2.2 %collective-permute-done.14.refs_3_.refs_8_ = bf16[2048,384]{1,0:T(8,128)(2,1)S(1)} collective-permute-done((bf16[2048,384]{1,0:T(8,128)(2,1)S(1)}, bf16[2048,384]{1,0:T(8,128)(2,1)S(1)}, u32[]{:S(2)}, u32[]{:S(2)}) %collective-permute-start.14) | collective-permute-done | bytes 1572896 | tf_op jit(solution)/shard_map/ppermute | solution.py:497
  99.0 10.2 %forward.1 = (bf16[3,2560,640]{2,1,0:T(8,128)(2,1)S(1)}, bf16[640,384]{1,0:T(8,128)(2,1)S(1)}, f32[3,1,640]{2,1,0:T(1,128)S(1)}) custom-call(bf16[640,384]{1,0:T(8,128)(2,1)S(1)} %stack_queries.1.q_in.refs_0_, bf16[2048,384]{1,0:T(8,128)(2,1)S(1)} %stack.18.refs_0_.refs_5_, bf16[2048,384]{1,0:T(8,128)(2,1)S(1)} %stack.19.refs_1_.refs_6_, ...), custom_call_target="tpu_custom_call" | custom-call | flops 2516582400 | bytes 9830400 | tf_op jit(solution)/shard_map/forward/pallas_call | solution.py:200
  109.2 3.0 %attn_gradient.1.refs_4_ = bf16[640,384]{1,0:T(8,128)(2,1)S(1)} custom-call(s32[3]{0:T(128)S(1)} %copy-done.3, bf16[2048,384]{1,0:T(8,128)(2,1)S(1)} %stack.18.refs_0_.refs_5_, bf16[2048,384]{1,0:T(8,128)(2,1)S(1)} %stack.19.refs_1_.refs_6_, bf16[2048,384]{1,0:T(8,128)(2,1)S(1)} %collective-permute-done.13.refs_2_.refs_7_, ...), custom_call_target="tpu_custom_call" | custom-call | flops 245760 | bytes 491520 | tf_op jit(solution)/shard_map/attn_gradient/pallas_call | solution.py:75
  112.2 9.0 %backward.2 = (bf16[160,256]{1,0:T(8,128)(2,1)S(1)}, bf16[160,256]{1,0:T(8,128)(2,1)S(1)}, bf16[160,256]{1,0:T(8,128)(2,1)S(1)}, bf16[160,256]{1,0:T(8,128)(2,1)...) custom-call(bf16[640,384]{1,0:T(8,128)(2,1)S(1)} %stack_queries.1.q_in.refs_0_, ...), custom_call_target="tpu_custom_call" | custom-call | flops 81920 | bytes 163840 | tf_op jit(solution)/shard_map/backward/pallas_call | solution.py:264
  121.2 0.2 collective-permute-start.16
  121.4 2.9 %collective-permute-done.16.other = bf16[2560,256]{1,0:T(8,128)(2,1)S(1)} collective-permute-done((bf16[2560,256]{1,0:T(8,128)(2,1)S(1)}, bf16[2560,256]{1,0:T(8,128)(2,1)S(1)}, u32[]{:S(2)}, u32[]{:S(2)}) %collective-permute-start.16) | collective-permute-done | bytes 1310752 | tf_op jit(solution)/shard_map/ppermute | solution.py:389
  124.3 0.8 add_parts.4
  125.2 1.6 collective-permute-start.17
  126.7 3.9 %backward.3 = (bf16[160,128]{1,0:T(8,128)(2,1)S(1)}, bf16[160,128]{1,0:T(8,128)(2,1)S(1)}, bf16[160,128]{1,0:T(8,128)(2,1)S(1)}, bf16[160,128]{1,0:T(8,128)(2,1)...) custom-call(bf16[640,384]{1,0:T(8,128)(2,1)S(1)} %stack_queries.1.q_in.refs_0_, ...), custom_call_target="tpu_custom_call" | custom-call | flops 81920 | bytes 163840 | tf_op jit(solution)/shard_map/backward/pallas_call | solution.py:264
  130.6 11.4 %collective-permute-done.17.other = bf16[1280,256]{1,0:T(8,128)(2,1)S(1)} collective-permute-done((bf16[1280,256]{1,0:T(8,128)(2,1)S(1)}, bf16[1280,256]{1,0:T(8,128)(2,1)S(1)}, u32[]{:S(2)}, u32[]{:S(2)}) %collective-permute-start.17) | collective-permute-done | bytes 655392 | tf_op jit(solution)/shard_map/ppermute | solution.py:507
  142.0 0.7 finish.2
  142.7 3.2 %proj_gradient.1 = (bf16[1536,384]{1,0:T(8,128)(2,1)S(1)}, bf16[1536,384]{1,0:T(8,128)(2,1)S(1)}) custom-call(s32[3]{0:T(128)S(1)} %copy-done.3, bf16[640,384]{1,0:T(8,128)(2,1)S(1)} %get-tuple-element.119.refs_2_.attn, bf16[160,1536]{1,0:T(8,128)(2,1)S(1)} %copy-done, bf16[160,1536]{1,0:T(8,128)(2,1)S(1)} %collective-permute-done.3.refs_5_.refs_1_, ...), custom_call_target="tpu_custom_call" | custom-call | flops 245760 | bytes 491520 | tf_op jit(solution)/shard_map/proj_gradient/pallas_call | solution.py:75
  145.9 0.1 collective-permute-start.20
  146.0 0.5 collective-permute-start.18
  146.5 3.3 %collective-permute-done.18.other = bf16[2560,128]{1,0:T(8,128)(2,1)S(1)} collective-permute-done((bf16[2560,128]{1,0:T(8,128)(2,1)S(1)}, bf16[2560,128]{1,0:T(8,128)(2,1)S(1)}, u32[]{:S(2)}, u32[]{:S(2)}) %collective-permute-start.18) | collective-permute-done | bytes 655392 | tf_op jit(solution)/shard_map/ppermute | solution.py:389
  149.8 0.7 add_parts.5
  150.5 1.6 collective-permute-start.19
  152.0 4.4 %collective-permute-start.21 = (bf16[480,256]{1,0:T(8,128)(2,1)S(1)}, bf16[480,256]{1,0:T(8,128)(2,1)S(1)}, u32[]{:S(2)}, u32[]{:S(2)}) collective-permute-start(bf16[480,256]{1,0:T(8,128)(2,1)S(1)} %get-tuple-element.116), channel_id=1, source_target_pairs={{0,24},{2,26},{4,28},{6,30},{8,0},{10,2},{12,4},{14,6},{16,8},{18,... | collective-permute-start | bytes 737288 | tf_op jit(solution)/shard_map/ppermute | solution.py:458
  156.4 0.9 collective-permute-start.22
  157.3 1.1 collective-permute-start.23
  158.5 0.8 add_parts.6
  159.3 3.6 %collective-permute-done.21.refs_1_ = bf16[480,256]{1,0:T(8,128)(2,1)S(1)} collective-permute-done((bf16[480,256]{1,0:T(8,128)(2,1)S(1)}, bf16[480,256]{1,0:T(8,128)(2,1)S(1)}, u32[]{:S(2)}, u32[]{:S(2)}) %collective-permute-start.21) | collective-permute-done | bytes 245792 | tf_op jit(solution)/shard_map/ppermute | solution.py:458
  162.9 15.9 %collective-permute-done.22.refs_2_ = bf16[480,256]{1,0:T(8,128)(2,1)S(1)} collective-permute-done((bf16[480,256]{1,0:T(8,128)(2,1)S(1)}, bf16[480,256]{1,0:T(8,128)(2,1)S(1)}, u32[]{:S(2)}, u32[]{:S(2)}) %collective-permute-start.22) | collective-permute-done | bytes 245792 | tf_op jit(solution)/shard_map/ppermute | solution.py:458
  178.8 0.5 collective-permute-start.27
  179.4 0.6 finish.3
  180.0 0.1 collective-permute-start.24
  180.1 13.0 %collective-permute-done.27.other = bf16[768,384]{1,0:T(8,128)(2,1)S(1)} collective-permute-done((bf16[768,384]{1,0:T(8,128)(2,1)S(1)}, bf16[768,384]{1,0:T(8,128)(2,1)S(1)}, u32[]{:S(2)}, u32[]{:S(2)}) %collective-permute-start.27) | collective-permute-done | bytes 589856 | tf_op jit(solution)/shard_map/ppermute | solution.py:507
  193.1 0.7 add_parts.7
  193.8 1.2 collective-permute-start.28
  195.0 2.0 collective-permute-start.29
  197.0 2.8 %collective-permute-start.30 = (bf16[192,384]{1,0:T(8,128)(2,1)S(1)}, bf16[192,384]{1,0:T(8,128)(2,1)S(1)}, u32[]{:S(2)}, u32[]{:S(2)}) collective-permute-start(bf16[192,384]{1,0:T(8,128)(2,1)S(1)} %get-tuple-element.145), channel_id=1, source_target_pairs={{0,24},{2,26},{4,28},{6,30},{8,0},{10,2},{12,4},{14,6},{16,8},{18,... | collective-permute-start | bytes 442376 | tf_op jit(solution)/shard_map/ppermute | solution.py:458
  199.8 0.6 collective-permute-start.26
  200.4 16.4 %collective-permute-done.25.refs_6_ = bf16[480,128]{1,0:T(8,128)(2,1)S(1)} collective-permute-done((bf16[480,128]{1,0:T(8,128)(2,1)S(1)}, bf16[480,128]{1,0:T(8,128)(2,1)S(1)}, u32[]{:S(2)}, u32[]{:S(2)}) %collective-permute-start.25) | collective-permute-done | bytes 122912 | tf_op jit(solution)/shard_map/ppermute | solution.py:458
  216.8 1.8 unpack.1
  218.7 1.7 join.1
  (27 shorter events, 0.2 us)
Async XLA Ops:
  0.6 7.5 %copy-start = (bf16[160,1536]{1,0:T(8,128)(2,1)S(1)}, bf16[160,1536]{1,0:T(8,128)(2,1)}, u32[]{:S(2)}) copy-start(bf16[160,1536]{1,0:T(8,128)(2,1)} %refs_0_) | copy-start | bytes 1474564
  5.0 82.6 %copy-start.1 = (bf16[512,384]{1,0:T(8,128)(2,1)S(1)}, bf16[512,384]{1,0:T(8,128)(2,1)}, u32[]{:S(2)}) copy-start(bf16[512,384]{1,0:T(8,128)(2,1)} %get-tuple-element.79.refs_0_) | copy-start | bytes 1179652
  5.0 82.6 %copy-start.3 = (s32[3]{0:T(128)S(1)}, s32[3]{0:T(128)}, u32[]{:S(2)}) copy-start(s32[3]{0:T(128)} %pad_add_fusion.ids) | copy-start | bytes 40
  5.0 18.0 %collective-permute-start = (bf16[672,384]{1,0:T(8,128)(2,1)}, bf16[672,384]{1,0:T(8,128)(2,1)S(1)}, u32[]{:S(2)}, u32[]{:S(2)}) collective-permute-start(bf16[672,384]{1,0:T(8,128)(2,1)} %get-tuple-element.76), channel_id=1, source_target_pairs={{0,8},{2,10},{4,12},{6,14},{8,16},{10,18},{12,20},{14,22},{16,24},... | collective-permute-start | bytes 1548296 | tf_op jit(solution)/shard_map/ppermute | solution.py:458
  8.1 25.4 %collective-permute-start.3 = (bf16[160,1536]{1,0:T(8,128)(2,1)S(1)}, bf16[160,1536]{1,0:T(8,128)(2,1)S(1)}, u32[]{:S(2)}, u32[]{:S(2)}) collective-permute-start(bf16[160,1536]{1,0:T(8,128)(2,1)S(1)} %copy-done), channel_id=1, source_target_pairs={{0,8},{2,10},{4,12},{6,14},{8,16},{10,18},{12,20},{14,22},{16,24},... | collective-permute-start | bytes 1474568 | tf_op jit(solution)/shard_map/ppermute | solution.py:489
  9.7 23.9 %collective-permute-start.5 = (bf16[160,1536]{1,0:T(8,128)(2,1)S(1)}, bf16[160,1536]{1,0:T(8,128)(2,1)S(1)}, u32[]{:S(2)}, u32[]{:S(2)}) collective-permute-start(bf16[160,1536]{1,0:T(8,128)(2,1)S(1)} %copy-done), channel_id=1, source_target_pairs={{0,1},{1,0},{2,3},{3,2},{4,5},{5,4},{6,7},{7,6},{8,9},{9,8},{10,11... | collective-permute-start | bytes 1474568 | tf_op jit(solution)/shard_map/ppermute | solution.py:49
  11.2 11.9 %collective-permute-start.4 = (bf16[512,384]{1,0:T(8,128)(2,1)}, bf16[512,384]{1,0:T(8,128)(2,1)S(1)}, u32[]{:S(2)}, u32[]{:S(2)}) collective-permute-start(bf16[512,384]{1,0:T(8,128)(2,1)} %get-tuple-element.79.refs_0_), channel_id=1, source_target_pairs={{0,4},{2,6},{4,0},{6,2},{8,12},{10,14},{12,8},{14,10},{16,20},{18,... | collective-permute-start | bytes 1179656 | tf_op jit(solution)/shard_map/ppermute | solution.py:486
  12.7 52.7 %collective-permute-start.1 = (bf16[672,384]{1,0:T(8,128)(2,1)}, bf16[672,384]{1,0:T(8,128)(2,1)S(1)}, u32[]{:S(2)}, u32[]{:S(2)}) collective-permute-start(bf16[672,384]{1,0:T(8,128)(2,1)} %get-tuple-element.77), channel_id=1, source_target_pairs={{0,16},{2,18},{4,20},{6,22},{8,24},{10,26},{12,28},{14,30},{16,0},... | collective-permute-start | bytes 1548296 | tf_op jit(solution)/shard_map/ppermute | solution.py:458
  33.5 31.9 %collective-permute-start.8 = (bf16[160,1536]{1,0:T(8,128)(2,1)S(1)}, bf16[160,1536]{1,0:T(8,128)(2,1)S(1)}, u32[]{:S(2)}, u32[]{:S(2)}) collective-permute-start(bf16[160,1536]{1,0:T(8,128)(2,1)S(1)} %collective-permute-done.3.refs_5_.refs_1_), channel_id=1, source_target_pairs={{0,1},{1,0},{2,3},{3,2},{4,5},{5,4},{6,7},{7,6},{8,9},{9,8},{10,11... | collective-permute-start | bytes 1474568 | tf_op jit(solution)/shard_map/ppermute | solution.py:49
  35.3 30.2 %collective-permute-start.6 = (bf16[160,1536]{1,0:T(8,128)(2,1)S(1)}, bf16[160,1536]{1,0:T(8,128)(2,1)S(1)}, u32[]{:S(2)}, u32[]{:S(2)}) collective-permute-start(bf16[160,1536]{1,0:T(8,128)(2,1)S(1)} %collective-permute-done.3.refs_5_.refs_1_), channel_id=1, source_target_pairs={{0,8},{2,10},{4,12},{6,14},{8,16},{10,18},{12,20},{14,22},{16,24},... | collective-permute-start | bytes 1474568 | tf_op jit(solution)/shard_map/ppermute | solution.py:489
  44.7 20.7 %collective-permute-start.7 = (bf16[512,384]{1,0:T(8,128)(2,1)S(1)}, bf16[512,384]{1,0:T(8,128)(2,1)S(1)}, u32[]{:S(2)}, u32[]{:S(2)}) collective-permute-start(bf16[512,384]{1,0:T(8,128)(2,1)S(1)} %slice.12.refs_1_), channel_id=1, source_target_pairs={{0,4},{2,6},{4,0},{6,2},{8,12},{10,14},{12,8},{14,10},{16,20},{18,... | collective-permute-start | bytes 1179656 | tf_op jit(solution)/shard_map/ppermute | solution.py:486
  46.2 32.0 %collective-permute-start.2 = (bf16[672,384]{1,0:T(8,128)(2,1)}, bf16[672,384]{1,0:T(8,128)(2,1)S(1)}, u32[]{:S(2)}, u32[]{:S(2)}) collective-permute-start(bf16[672,384]{1,0:T(8,128)(2,1)} %get-tuple-element.78), channel_id=1, source_target_pairs={{0,24},{2,26},{4,28},{6,30},{8,0},{10,2},{12,4},{14,6},{16,8},{18,... | collective-permute-start | bytes 1548296 | tf_op jit(solution)/shard_map/ppermute | solution.py:458
  65.5 20.6 %collective-permute-start.11 = (bf16[160,1536]{1,0:T(8,128)(2,1)S(1)}, bf16[160,1536]{1,0:T(8,128)(2,1)S(1)}, u32[]{:S(2)}, u32[]{:S(2)}) collective-permute-start(bf16[160,1536]{1,0:T(8,128)(2,1)S(1)} %collective-permute-done.6.refs_6_.refs_2_), channel_id=1, source_target_pairs={{0,1},{1,0},{2,3},{3,2},{4,5},{5,4},{6,7},{7,6},{8,9},{9,8},{10,11... | collective-permute-start | bytes 1474568 | tf_op jit(solution)/shard_map/ppermute | solution.py:49
  67.1 19.1 %collective-permute-start.9 = (bf16[160,1536]{1,0:T(8,128)(2,1)S(1)}, bf16[160,1536]{1,0:T(8,128)(2,1)S(1)}, u32[]{:S(2)}, u32[]{:S(2)}) collective-permute-start(bf16[160,1536]{1,0:T(8,128)(2,1)S(1)} %collective-permute-done.6.refs_6_.refs_2_), channel_id=1, source_target_pairs={{0,8},{2,10},{4,12},{6,14},{8,16},{10,18},{12,20},{14,22},{16,24},... | collective-permute-start | bytes 1474568 | tf_op jit(solution)/shard_map/ppermute | solution.py:489
  76.7 9.4 %collective-permute-start.10 = (bf16[512,384]{1,0:T(8,128)(2,1)S(1)}, bf16[512,384]{1,0:T(8,128)(2,1)S(1)}, u32[]{:S(2)}, u32[]{:S(2)}) collective-permute-start(bf16[512,384]{1,0:T(8,128)(2,1)S(1)} %slice.13.refs_2_), channel_id=1, source_target_pairs={{0,4},{2,6},{4,0},{6,2},{8,12},{10,14},{12,8},{14,10},{16,20},{18,... | collective-permute-start | bytes 1179656 | tf_op jit(solution)/shard_map/ppermute | solution.py:486
  86.1 8.7 %collective-permute-start.12 = (bf16[512,384]{1,0:T(8,128)(2,1)S(1)}, bf16[512,384]{1,0:T(8,128)(2,1)S(1)}, u32[]{:S(2)}, u32[]{:S(2)}) collective-permute-start(bf16[512,384]{1,0:T(8,128)(2,1)S(1)} %slice.14.refs_3_), channel_id=1, source_target_pairs={{0,4},{2,6},{4,0},{6,2},{8,12},{10,14},{12,8},{14,10},{16,20},{18,... | collective-permute-start | bytes 1179656 | tf_op jit(solution)/shard_map/ppermute | solution.py:486
  88.3 7.8 %copy-start.2 = (bf16[160,384]{1,0:T(8,128)(2,1)S(1)}, bf16[160,384]{1,0:T(8,128)(2,1)}, u32[]{:S(2)}) copy-start(bf16[160,384]{1,0:T(8,128)(2,1)} %get-tuple-element.75.own) | copy-start | bytes 368644
  88.3 8.4 %collective-permute-start.13 = (bf16[2048,384]{1,0:T(8,128)(2,1)S(1)}, bf16[2048,384]{1,0:T(8,128)(2,1)S(1)}, u32[]{:S(2)}, u32[]{:S(2)}) collective-permute-start(bf16[2048,384]{1,0:T(8,128)(2,1)S(1)} %stack.18.refs_0_.refs_5_), channel_id=1, source_target_pairs={{0,2},{2,0},{4,6},{6,4},{8,10},{10,8},{12,14},{14,12},{16,18},{18,... | collective-permute-start | bytes 4718600 | tf_op jit(solution)/shard_map/ppermute | solution.py:497
  95.5 3.5 %collective-permute-start.14 = (bf16[2048,384]{1,0:T(8,128)(2,1)S(1)}, bf16[2048,384]{1,0:T(8,128)(2,1)S(1)}, u32[]{:S(2)}, u32[]{:S(2)}) collective-permute-start(bf16[2048,384]{1,0:T(8,128)(2,1)S(1)} %stack.19.refs_1_.refs_6_), channel_id=1, source_target_pairs={{0,2},{2,0},{4,6},{6,4},{8,10},{10,8},{12,14},{14,12},{16,18},{18,... | collective-permute-start | bytes 4718600 | tf_op jit(solution)/shard_map/ppermute | solution.py:497
  95.6 13.6 %collective-permute-start.15 = (bf16[160,1536]{1,0:T(8,128)(2,1)S(1)}, bf16[160,1536]{1,0:T(8,128)(2,1)S(1)}, u32[]{:S(2)}, u32[]{:S(2)}) collective-permute-start(bf16[160,1536]{1,0:T(8,128)(2,1)S(1)} %collective-permute-done.9.refs_7_.refs_3_), channel_id=1, source_target_pairs={{0,1},{1,0},{2,3},{3,2},{4,5},{5,4},{6,7},{7,6},{8,9},{9,8},{10,11... | collective-permute-start | bytes 1474568 | tf_op jit(solution)/shard_map/ppermute | solution.py:49
  121.2 3.1 %collective-permute-start.16 = (bf16[2560,256]{1,0:T(8,128)(2,1)S(1)}, bf16[2560,256]{1,0:T(8,128)(2,1)S(1)}, u32[]{:S(2)}, u32[]{:S(2)}) collective-permute-start(bf16[2560,256]{1,0:T(8,128)(2,1)S(1)} %get-tuple-element.99), channel_id=1, source_target_pairs={{0,2},{2,0},{4,6},{6,4},{8,10},{10,8},{12,14},{14,12},{16,18},{18,... | collective-permute-start | bytes 3932168 | tf_op jit(solution)/shard_map/ppermute | solution.py:389
  125.2 16.8 %collective-permute-start.17 = (bf16[1280,256]{1,0:T(8,128)(2,1)S(1)}, bf16[1280,256]{1,0:T(8,128)(2,1)S(1)}, u32[]{:S(2)}, u32[]{:S(2)}) collective-permute-start(bf16[1280,256]{1,0:T(8,128)(2,1)S(1)} %get-tuple-element.103), channel_id=1, source_target_pairs={{0,4},{2,6},{4,0},{6,2},{8,12},{10,14},{12,8},{14,10},{16,20},{18,... | collective-permute-start | bytes 1966088 | tf_op jit(solution)/shard_map/ppermute | solution.py:507
  145.9 12.5 %collective-permute-start.20 = (bf16[1536,384]{1,0:T(8,128)(2,1)S(1)}, bf16[1536,384]{1,0:T(8,128)(2,1)S(1)}, u32[]{:S(2)}, u32[]{:S(2)}) collective-permute-start(bf16[1536,384]{1,0:T(8,128)(2,1)S(1)} %get-tuple-element.121), channel_id=1, source_target_pairs={{0,2},{2,0},{4,6},{6,4},{8,10},{10,8},{12,14},{14,12},{16,18},{18,... | collective-permute-start | bytes 3538952 | tf_op jit(solution)/shard_map/ppermute | solution.py:389
  146.0 3.8 %collective-permute-start.18 = (bf16[2560,128]{1,0:T(8,128)(2,1)S(1)}, bf16[2560,128]{1,0:T(8,128)(2,1)S(1)}, u32[]{:S(2)}, u32[]{:S(2)}) collective-permute-start(bf16[2560,128]{1,0:T(8,128)(2,1)S(1)} %get-tuple-element.114), channel_id=1, source_target_pairs={{0,2},{2,0},{4,6},{6,4},{8,10},{10,8},{12,14},{14,12},{16,18},{18,... | collective-permute-start | bytes 1966088 | tf_op jit(solution)/shard_map/ppermute | solution.py:389
  150.5 28.4 %collective-permute-start.19 = (bf16[1280,128]{1,0:T(8,128)(2,1)S(1)}, bf16[1280,128]{1,0:T(8,128)(2,1)S(1)}, u32[]{:S(2)}, u32[]{:S(2)}) collective-permute-start(bf16[1280,128]{1,0:T(8,128)(2,1)S(1)} %get-tuple-element.115), channel_id=1, source_target_pairs={{0,4},{2,6},{4,0},{6,2},{8,12},{10,14},{12,8},{14,10},{16,20},{18,... | collective-permute-start | bytes 983048 | tf_op jit(solution)/shard_map/ppermute | solution.py:507
  152.0 10.8 %collective-permute-start.21 = (bf16[480,256]{1,0:T(8,128)(2,1)S(1)}, bf16[480,256]{1,0:T(8,128)(2,1)S(1)}, u32[]{:S(2)}, u32[]{:S(2)}) collective-permute-start(bf16[480,256]{1,0:T(8,128)(2,1)S(1)} %get-tuple-element.116), channel_id=1, source_target_pairs={{0,24},{2,26},{4,28},{6,30},{8,0},{10,2},{12,4},{14,6},{16,8},{18,... | collective-permute-start | bytes 737288 | tf_op jit(solution)/shard_map/ppermute | solution.py:458
  156.4 22.4 %collective-permute-start.22 = (bf16[480,256]{1,0:T(8,128)(2,1)S(1)}, bf16[480,256]{1,0:T(8,128)(2,1)S(1)}, u32[]{:S(2)}, u32[]{:S(2)}) collective-permute-start(bf16[480,256]{1,0:T(8,128)(2,1)S(1)} %get-tuple-element.117), channel_id=1, source_target_pairs={{0,16},{2,18},{4,20},{6,22},{8,24},{10,26},{12,28},{14,30},{16,0},... | collective-permute-start | bytes 737288 | tf_op jit(solution)/shard_map/ppermute | solution.py:458
  157.3 21.5 %collective-permute-start.23 = (bf16[480,256]{1,0:T(8,128)(2,1)S(1)}, bf16[480,256]{1,0:T(8,128)(2,1)S(1)}, u32[]{:S(2)}, u32[]{:S(2)}) collective-permute-start(bf16[480,256]{1,0:T(8,128)(2,1)S(1)} %get-tuple-element.118), channel_id=1, source_target_pairs={{0,8},{2,10},{4,12},{6,14},{8,16},{10,18},{12,20},{14,22},{16,24},... | collective-permute-start | bytes 737288 | tf_op jit(solution)/shard_map/ppermute | solution.py:458
  178.8 14.2 %collective-permute-start.27 = (bf16[768,384]{1,0:T(8,128)(2,1)S(1)}, bf16[768,384]{1,0:T(8,128)(2,1)S(1)}, u32[]{:S(2)}, u32[]{:S(2)}) collective-permute-start(bf16[768,384]{1,0:T(8,128)(2,1)S(1)} %get-tuple-element.141), channel_id=1, source_target_pairs={{0,4},{2,6},{4,0},{6,2},{8,12},{10,14},{12,8},{14,10},{16,20},{18,... | collective-permute-start | bytes 1769480 | tf_op jit(solution)/shard_map/ppermute | solution.py:507
  180.0 19.8 %collective-permute-start.24 = (bf16[480,128]{1,0:T(8,128)(2,1)S(1)}, bf16[480,128]{1,0:T(8,128)(2,1)S(1)}, u32[]{:S(2)}, u32[]{:S(2)}) collective-permute-start(bf16[480,128]{1,0:T(8,128)(2,1)S(1)} %get-tuple-element.134), channel_id=1, source_target_pairs={{0,24},{2,26},{4,28},{6,30},{8,0},{10,2},{12,4},{14,6},{16,8},{18,... | collective-permute-start | bytes 368648 | tf_op jit(solution)/shard_map/ppermute | solution.py:458
  193.8 24.9 %collective-permute-start.28 = (bf16[192,384]{1,0:T(8,128)(2,1)S(1)}, bf16[192,384]{1,0:T(8,128)(2,1)S(1)}, u32[]{:S(2)}, u32[]{:S(2)}) collective-permute-start(bf16[192,384]{1,0:T(8,128)(2,1)S(1)} %get-tuple-element.143), channel_id=1, source_target_pairs={{0,8},{2,10},{4,12},{6,14},{8,16},{10,18},{12,20},{14,22},{16,24},... | collective-permute-start | bytes 442376 | tf_op jit(solution)/shard_map/ppermute | solution.py:458
  195.0 23.7 %collective-permute-start.29 = (bf16[192,384]{1,0:T(8,128)(2,1)S(1)}, bf16[192,384]{1,0:T(8,128)(2,1)S(1)}, u32[]{:S(2)}, u32[]{:S(2)}) collective-permute-start(bf16[192,384]{1,0:T(8,128)(2,1)S(1)} %get-tuple-element.144), channel_id=1, source_target_pairs={{0,16},{2,18},{4,20},{6,22},{8,24},{10,26},{12,28},{14,30},{16,0},... | collective-permute-start | bytes 442376 | tf_op jit(solution)/shard_map/ppermute | solution.py:458
  197.0 21.7 %collective-permute-start.30 = (bf16[192,384]{1,0:T(8,128)(2,1)S(1)}, bf16[192,384]{1,0:T(8,128)(2,1)S(1)}, u32[]{:S(2)}, u32[]{:S(2)}) collective-permute-start(bf16[192,384]{1,0:T(8,128)(2,1)S(1)} %get-tuple-element.145), channel_id=1, source_target_pairs={{0,24},{2,26},{4,28},{6,30},{8,0},{10,2},{12,4},{14,6},{16,8},{18,... | collective-permute-start | bytes 442376 | tf_op jit(solution)/shard_map/ppermute | solution.py:458
  199.8 17.0 %collective-permute-start.25 = (bf16[480,128]{1,0:T(8,128)(2,1)S(1)}, bf16[480,128]{1,0:T(8,128)(2,1)S(1)}, u32[]{:S(2)}, u32[]{:S(2)}) collective-permute-start(bf16[480,128]{1,0:T(8,128)(2,1)S(1)} %get-tuple-element.135), channel_id=1, source_target_pairs={{0,16},{2,18},{4,20},{6,22},{8,24},{10,26},{12,28},{14,30},{16,0},... | collective-permute-start | bytes 368648 | tf_op jit(solution)/shard_map/ppermute | solution.py:458
  199.8 17.0 %collective-permute-start.26 = (bf16[480,128]{1,0:T(8,128)(2,1)S(1)}, bf16[480,128]{1,0:T(8,128)(2,1)S(1)}, u32[]{:S(2)}, u32[]{:S(2)}) collective-permute-start(bf16[480,128]{1,0:T(8,128)(2,1)S(1)} %get-tuple-element.136), channel_id=1, source_target_pairs={{0,8},{2,10},{4,12},{6,14},{8,16},{10,18},{12,20},{14,22},{16,24},... | collective-permute-start | bytes 368648 | tf_op jit(solution)/shard_map/ppermute | solution.py:458
